TPU v7x, 32 devices: a whole 2x2x4 slice. The times are simulated.
32 devices in a mesh: groups: 2 (over x), expert: 8 (over z, y), dp: 2 (over core).
Axes of the slice: x: 2, y: 2, z: 4, core: 2. Of those that a mesh axis runs over, the one named last changes fastest.
Arguments:
- tokens: bfloat16 [4, 1024, 6144], P(('groups', 'dp'), 'expert'), parts along dimension 0, may hold values from -6 to 6
- output_gradient: bfloat16 [4, 1024, 6144], P(('groups', 'dp'), 'expert'), parts along dimension 0, may hold values from -12 to 12
- token_expert_choice: int32 [4, 1024, 4], P(('groups', 'dp'), 'expert'), parts along dimension 0, may hold values from 0 to 15, as said below
- routing_weight_table: bfloat16 [4, 1024, 4], P(('groups', 'dp'), 'expert'), parts along dimension 0, may hold values from 0.049804688 to 0.59765625
- stored_gate_rows: bfloat16 [4, 288, 6144], P(('groups', 'dp'), None, 'expert'), parts along dimension 0, may hold values from -9 to 9
- stored_up_rows: bfloat16 [4, 288, 6144], P(('groups', 'dp'), None, 'expert'), parts along dimension 0, may hold values from -6 to 6
- gate_weight: bfloat16 [6144, 6144], P(None, 'expert'), may hold values from -0.078125 to 0.078125
- up_weight: bfloat16 [6144, 6144], P(None, 'expert'), may hold values from -0.078125 to 0.078125
- down_weight: bfloat16 [6144, 6144], P('expert'), may hold values from -0.078125 to 0.078125
- adapter_down_factor: bfloat16 [128, 6144], P('groups'), parts along dimension 0, may hold values from -0.078125 to 0.078125
- adapter_gate_factor: bfloat16 [128, 6144], P('groups', 'expert'), parts along dimension 0, may hold values from -0.75 to 0.75
- adapter_up_factor: bfloat16 [128, 6144], P('groups', 'expert'), parts along dimension 0, may hold values from -0.75 to 0.75
Outputs:
- input_gradient: bfloat16 [4, 1024, 6144], P(('groups', 'dp'), 'expert'), parts along dimension 0
- grad_lora_down: float32 [128, 6144], P('groups', 'expert'), parts along dimension 0
- grad_lora_gate: float32 [128, 6144], P('groups', 'expert'), parts along dimension 0
- grad_lora_up: float32 [128, 6144], P('groups', 'expert'), parts along dimension 0
There are 2 independent parts, one for each index of `groups`. A program takes and returns all parts, laid end to end along the dimension named above; an argument that names none is the same for every part. Nothing has to cross between parts.
Inputs may be any that keep to these rules, and one draw needn't show every extreme that they name: `token_expert_choice`: each token names 4 different experts. Within the 128 tokens of one device (aligned blocks along the token dimension of each replica) expert 0 is named by 1 to 36 tokens, and in every replica some device's tokens name it exactly 36 times.
All inputs are finite; a program needn't handle non-finite values.
Results may differ from a plain program's by a relative error of at most 0.018.
Values may be sent and summed in bfloat16 or wider, within the bound.
No kernel may reach another device: no remote copies, remote signals or barrier semaphores. Data moves between devices by JAX's collectives and lax.ppermute only.
A program may use at most 128 MiB of HBM per device.

v0:
```python
import jax
import jax.numpy as jnp
from jax import lax
from jax.sharding import PartitionSpec as P

SCALE = 0.25


def activation_grads(pre_gate, pre_up, grad_hidden):
    sigma = jax.nn.sigmoid(pre_gate)
    slope = sigma * (1.0 + pre_gate * (1.0 - sigma))
    gate_gradient = (grad_hidden * pre_up * slope).astype(jnp.bfloat16)
    up_gradient = (grad_hidden * pre_gate * sigma).astype(jnp.bfloat16)
    return (gate_gradient, up_gradient)


def on_device(
    tokens,
    output_gradient,
    token_expert_choice,
    routing_weight_table,
    stored_gate_rows,
    stored_up_rows,
    gate_weight,
    up_weight,
    down_weight,
    adapter_down_factor,
    adapter_gate_factor,
    adapter_up_factor,
):
    members = lax.axis_size("expert")
    own_count = tokens.shape[1]
    model_width = tokens.shape[2]
    capacity = stored_gate_rows.shape[1] // members
    adapter_rank_width = adapter_down_factor.shape[0]
    input_rows = tokens[0]
    grad_local = output_gradient[0]
    selected_mask = token_expert_choice[0]
    token_weight_rows = routing_weight_table[0]
    adapter_product = jnp.dot(
        input_rows, adapter_down_factor.T, preferred_element_type=jnp.float32
    ).astype(jnp.bfloat16)
    hit = selected_mask == 0
    named = jnp.any(hit, axis=1)
    weight_tok = jnp.sum(
        jnp.where(hit, token_weight_rows, jnp.zeros_like(token_weight_rows)), axis=1
    )
    slot = jnp.cumsum(named.astype(jnp.int32)) - 1
    row = jnp.where(named, slot, capacity)
    source_table = (
        jnp.full((capacity + 1,), own_count, jnp.int32)
        .at[row]
        .set(jnp.arange(own_count, dtype=jnp.int32))[:capacity]
    )
    gate_table = jnp.zeros((capacity + 1,), jnp.bfloat16).at[row].set(weight_tok)[:capacity]
    grad_padded = jnp.concatenate([grad_local, jnp.zeros((1, model_width), jnp.bfloat16)], axis=0)
    low_padded = jnp.concatenate(
        [adapter_product, jnp.zeros((1, adapter_rank_width), jnp.bfloat16)], axis=0
    )
    grad_block = grad_padded[source_table]
    low_block = low_padded[source_table]
    rows_all, low_all, weight_all = (
        lax.all_gather(grad_block, "expert", axis=0, tiled=True),
        lax.all_gather(low_block, "expert", axis=0, tiled=True),
        lax.all_gather(gate_table, "expert", axis=0, tiled=True),
    )
    grad_hidden = (
        jnp.dot(rows_all, down_weight.T, preferred_element_type=jnp.float32)
        * weight_all.astype(jnp.float32)[:, None]
    )
    gate_gradient, up_gradient = activation_grads(
        stored_gate_rows[0].astype(jnp.float32), stored_up_rows[0].astype(jnp.float32), grad_hidden
    )
    part_term = jnp.dot(gate_gradient, gate_weight.T, preferred_element_type=jnp.float32) + jnp.dot(
        up_gradient, up_weight.T, preferred_element_type=jnp.float32
    )
    low_term = SCALE * (
        jnp.dot(gate_gradient, adapter_gate_factor.T, preferred_element_type=jnp.float32)
        + jnp.dot(up_gradient, adapter_up_factor.T, preferred_element_type=jnp.float32)
    )
    gate_local = SCALE * jnp.dot(low_all.T, gate_gradient, preferred_element_type=jnp.float32)
    up_local = SCALE * jnp.dot(low_all.T, up_gradient, preferred_element_type=jnp.float32)
    back_part, back_low = (
        lax.psum_scatter(
            part_term.astype(jnp.bfloat16), "expert", scatter_dimension=0, tiled=True
        ).astype(jnp.float32),
        lax.psum_scatter(
            low_term.astype(jnp.bfloat16), "expert", scatter_dimension=0, tiled=True
        ).astype(jnp.float32),
    )
    picked = jnp.minimum(row, capacity - 1)
    mask = named[:, None]
    reduced_total = jnp.where(mask, back_part[picked], jnp.float32(0.0))
    low_summed = jnp.where(mask, back_low[picked], jnp.float32(0.0))
    adapter_rank_sum = low_summed.astype(jnp.bfloat16)
    input_gradient = (
        reduced_total
        + jnp.dot(adapter_rank_sum, adapter_down_factor, preferred_element_type=jnp.float32)
    ).astype(jnp.bfloat16)
    down_local = jnp.dot(adapter_rank_sum.T, input_rows, preferred_element_type=jnp.float32)
    down_shard = lax.psum_scatter(
        down_local.astype(jnp.bfloat16), "expert", scatter_dimension=1, tiled=True
    )
    grad_down, grad_gate, grad_up = (
        lax.psum(down_shard, "dp").astype(jnp.float32),
        lax.psum(gate_local.astype(jnp.bfloat16), "dp").astype(jnp.float32),
        lax.psum(up_local.astype(jnp.bfloat16), "dp").astype(jnp.float32),
    )
    return (input_gradient[None], grad_down, grad_gate, grad_up)


def solution(mesh):
    placed = (
        P(("groups", "dp"), "expert", None),
        P(("groups", "dp"), "expert", None),
        P(("groups", "dp"), "expert", None),
        P(("groups", "dp"), "expert", None),
        P(("groups", "dp"), None, "expert"),
        P(("groups", "dp"), None, "expert"),
        P(None, "expert"),
        P(None, "expert"),
        P("expert", None),
        P("groups", None),
        P("groups", "expert"),
        P("groups", "expert"),
    )
    return jax.shard_map(
        on_device,
        mesh=mesh,
        in_specs=placed,
        out_specs=(
            P(("groups", "dp"), "expert", None),
            P("groups", "expert"),
            P("groups", "expert"),
            P("groups", "expert"),
        ),
        check_vma=False,
    )
```

profile of v0, /device:TPU:0, one launch (start us, length us, event | category | flops | bytes accessed | tf_op | source)
XLA Modules:
  0.0 309.0 jit_solution(13248152031340831306)
XLA Ops:
  9.7 1.6 concatenate.6
  11.2 1.6 gather_fusion
  12.9 1.3 scatter_custom_fusion.1
  15.8 23.3 %all-reduce.2 = bf16[288]{0:T(512)(128)(2,1)S(1)} all-reduce(bf16[288]{0:T(512)(128)(2,1)S(1)} %dynamic-update-slice), channel_id=1, replica_groups=mesh['groups'=2,'expert'=8,'dp'=2] {'expert'}, use_global_device_ids=true, to_apply=%add.2 | all-reduce | flops 288 | bytes 1152
  39.1 46.9 %all-gather.6.cloned.1.call-done = bf16[8,36,6144]{2,1,0:T(8,128)(2,1)} async-done(((bf16[1,36,6144]{2,1,0:T(8,128)(2,1)}), bf16[8,36,6144]{2,1,0:T(8,128)(2,1)}) %all-gather.6.cloned.1.call-update) | async-done | bytes 3538960 | tf_op jit(solution)/shard_map/all_gather | solution.py:63
  86.0 4.8 %reshape.123 = bf16[288,6144]{1,0:T(8,128)(2,1)} reshape(bf16[8,36,6144]{2,1,0:T(8,128)(2,1)} %all-gather.6.cloned.1.call-done) | data formatting | bytes 7077888
  90.8 8.2 %fusion.22 = (bf16[288,768]{1,0:T(8,128)(2,1)S(1)}, bf16[288,768]{1,0:T(8,128)(2,1)S(1)}) fusion(bf16[1,288,768]{2,1,0:T(8,128)(2,1)} %param.16, bf16[1,288,768]{2,1,0:T(8,128)(2,1)} %param.17, f32[288]{0:T(512)S(1)} %convert_element_type.73, bf16[288,6144]{1,0:T(8,128)(2,1)} %reshape.123, bf16[768,6144]{1,0:T(8,128)(2,1)} %param.20), kind=kOutput, calls=%fused_computation.34 | convolution fusion | flops 2721447936 | bytes 14746752 | tf_op jit(solution)/shard_map/dot_general | solution.py:68
  99.4 5.0 %fusion.32 = f32[288,6144]{1,0:T(8,128)} fusion(bf16[288,768]{1,0:T(8,128)(2,1)S(1)} %get-tuple-element.16, bf16[6144,768]{1,0:T(8,128)(2,1)S(1)} %bitcast.48), kind=kOutput, calls=%fused_computation.56 | convolution fusion | flops 2717908992 | bytes 16957440 | tf_op jit(solution)/shard_map/dot_general | solution.py:74
  104.6 12.4 %fusion.2 = bf16[288,6144]{1,0:T(8,128)(2,1)} fusion(f32[288,6144]{1,0:T(8,128)} %fusion.32, bf16[288,768]{1,0:T(8,128)(2,1)S(1)} %get-tuple-element.15, bf16[6144,768]{1,0:T(8,128)(2,1)} %param.19), kind=kOutput, calls=%fused_computation.7 | convolution fusion | flops 2721447936 | bytes 20496384 | tf_op jit(solution)/shard_map/dot_general | solution.py:74
  117.0 84.6 %fusion.30 = (bf16[40,6144]{1,0:T(8,128)(2,1)S(1)}, bf16[48,64]{1,0:T(8,128)(2,1)S(1)}) fusion(bf16[288,6144]{1,0:T(8,128)(2,1)} %fusion.2, bf16[288,64]{1,0:T(8,128)(2,1)S(1)} %fusion.10), kind=kCustom, calls=%all-reduce-scatter.2 | all-reduce-scatter fusion | flops 1990658 | bytes 4073984
  201.6 1.3 collective-permute-start.1
  202.9 2.4 collective-permute-start.2
  207.8 1.4 convolution_convert_fusion
  209.8 1.8 fusion.11
  212.4 33.0 %all-gather.3 = bf16[8,36,64]{2,1,0:T(8,128)(2,1)S(1)} all-gather(bf16[1,36,64]{2,1,0:T(8,128)(2,1)S(1)} %bitcast.51), channel_id=3, replica_groups=mesh['groups'=2,'expert'=8,'dp'=2] {'expert'}, dimensions={0}, use_global_device_ids=true | all-gather | bytes 41472 | tf_op jit(solution)/shard_map/all_gather | solution.py:64
  245.5 1.3 collective-permute-start
  248.6 4.0 %collective-permute-done = bf16[28,6144]{1,0:T(8,128)(2,1)S(1)} collective-permute-done((bf16[28,6144]{1,0:T(8,128)(2,1)S(1)}, bf16[28,6144]{1,0:T(8,128)(2,1)S(1)}, u32[]{:S(2)}, u32[]{:S(2)}) %collective-permute-start) | collective-permute-done | bytes 344096
  253.3 23.7 %reduce-scatter.6.cloned.1.call-done = bf16[64,768]{1,0:T(8,128)(2,1)} async-done(((bf16[64,6144]{1,0:T(8,128)(2,1)}), bf16[64,768]{1,0:T(8,128)(2,1)}) %reduce-scatter.6.cloned.1.call-update) | async-done | bytes 98320 | tf_op jit(solution)/shard_map/reduce_scatter | solution.py:101
  277.2 3.2 %gather_fusion.1 = f32[128,6144]{1,0:T(8,128)} fusion(f32[36,6144]{1,0:T(8,128)S(1)} %dynamic-slice_convert_fusion, s32[1024]{0:T(1024)S(1)} %pad_clamp_fusion), kind=kCustom, calls=%fused_computation.1 | custom fusion | bytes 6291968 | tf_op jit(solution)/shard_map/gather | solution.py:93
  280.4 3.6 %fusion.3 = bf16[1,128,6144]{2,1,0:T(8,128)(2,1)} fusion(f32[128,6144]{1,0:T(8,128)} %gather_fusion.1, pred[128]{0:T(512)(128)(4,1)S(1)} %reduce_or.11, bf16[64,6144]{1,0:T(8,128)(2,1)S(1)} %copy-done.1, bf16[128,64]{1,0:T(8,128)(2,1)S(1)} %gather_fusion.2), kind=kOutput, calls=%fused_computation.10 | convolution fusion | flops 103030784 | bytes 5521536 | tf_op jit(solution)/shard_map/dot_general | solution.py:98
  284.0 13.7 %all-reduce.11.cloned.1.call-done = (bf16[64,768]{1,0:T(8,128)(2,1)}, bf16[64,768]{1,0:T(8,128)(2,1)}, bf16[64,768]{1,0:T(8,128)(2,1)}) async-done(((bf16[64,768]{1,0:T(8,128)(2,1)}, bf16[64,768]{1,0:T(8,128)(2,1)}, bf16[64,768]{1,0:T(8,128)(2,1)}), (bf16[64,768]{1,0:T(8,128)(2,1)}, bf16[64,768]{1,0:T(8,128)(2,1)}, bf16[64,768]{1,0:T(8,128)(2,1)})) %all-reduce.11.cloned.1.call-update) | async-done | bytes 294928 | tf_op jit(solution)/shard_map/psum | solution.py:105
  297.7 1.6 convert_element_type.87
  299.3 1.6 convert_element_type.90
  300.9 1.6 convert_element_type.92
  (56 shorter events, 9.2 us)
Async XLA Ops:
  7.2 200.6 %copy-start = (bf16[1,128,6144]{2,1,0:T(8,128)(2,1)S(1)}, bf16[1,128,6144]{2,1,0:T(8,128)(2,1)}, u32[]{:S(2)}) copy-start(bf16[1,128,6144]{2,1,0:T(8,128)(2,1)} %param.12) | copy-start | bytes 4718596
  7.2 78.8 %all-gather.6.cloned.1.call-start = ((), (), s32[]{:S(2)}) async-start(), calls=%async_computation.2 | async-start | bytes 4423680 | tf_op jit(solution)/shard_map/all_gather | solution.py:63
  9.6 4.6 %copy-start.4 = (u32[32]{0:T(128)S(1)}, u32[32]{0:T(128)}, u32[]{:S(2)}) copy-start(u32[32]{0:T(128)} %constant.48) | copy-start | bytes 388
  12.8 264.2 %reduce-scatter.6.cloned.1.call-start = ((), (), s32[]{:S(2)}) async-start(), calls=%async_computation.1 | async-start | bytes 884736 | tf_op jit(solution)/shard_map/reduce_scatter | solution.py:101
  86.0 13.3 %slice-start = ((s8[9437184]{0:T(1024)(128)(4,1)}), s8[1048576]{0:T(1024)(128)(4,1)S(1)}, s32[]{:S(2)}) async-start(s8[9437184]{0:T(1024)(128)(4,1)} %bitcast.47), calls=%async_computation.4 | async-start | bytes 2097152
  90.8 8.2 %copy-start.3 = (bf16[64,768]{1,0:T(8,128)(2,1)S(1)}, bf16[64,768]{1,0:T(8,128)(2,1)}, u32[]{:S(2)}) copy-start(bf16[64,768]{1,0:T(8,128)(2,1)} %param.22) | copy-start | bytes 294916
  90.8 8.5 %slice-start.1 = ((s8[9437184]{0:T(1024)(128)(4,1)}), s8[4194304]{0:T(1024)(128)(4,1)S(1)}, s32[]{:S(2)}) async-start(s8[9437184]{0:T(1024)(128)(4,1)} %bitcast.47), calls=%async_computation.5 | async-start | bytes 8388608
  90.8 8.5 %slice-start.2 = ((s8[9437184]{0:T(1024)(128)(4,1)}), s8[4194304]{0:T(1024)(128)(4,1)S(1)}, s32[]{:S(2)}) async-start(s8[9437184]{0:T(1024)(128)(4,1)} %bitcast.47), calls=%async_computation.6 | async-start | bytes 8388608
  99.4 5.0 %copy-start.2 = (bf16[64,768]{1,0:T(8,128)(2,1)S(1)}, bf16[64,768]{1,0:T(8,128)(2,1)}, u32[]{:S(2)}) copy-start(bf16[64,768]{1,0:T(8,128)(2,1)} %param.23) | copy-start | bytes 294916
  201.6 5.0 %collective-permute-start.1 = (bf16[48,64]{1,0:T(8,128)(2,1)S(1)}, bf16[48,64]{1,0:T(8,128)(2,1)S(1)}, u32[]{:S(2)}, u32[]{:S(2)}) collective-permute-start(bf16[48,64]{1,0:T(8,128)(2,1)S(1)} %get-tuple-element.12), channel_id=1, source_target_pairs={{0,2},{2,4},{4,6},{6,8},{8,10},{10,12},{12,14},{1,3},{3,5},{5,7},{... | collective-permute-start | bytes 18440
  202.9 3.7 %collective-permute-start.2 = (bf16[36,64]{1,0:T(8,128)(2,1)S(1)}, bf16[36,64]{1,0:T(8,128)(2,1)S(1)}, u32[]{:S(2)}, u32[]{:S(2)}) collective-permute-start(bf16[36,64]{1,0:T(8,128)(2,1)S(1)} %slice.17), channel_id=1, source_target_pairs={{0,4},{2,6},{4,8},{6,10},{8,12},{10,14},{1,5},{3,7},{5,9},{7,11},{... | collective-permute-start | bytes 13832
  209.1 88.6 %all-reduce.11.cloned.1.call-start = ((), (), s32[]{:S(2)}) async-start(), calls=%async_computation.3 | async-start | bytes 589824 | tf_op jit(solution)/shard_map/psum | solution.py:105
  245.5 7.1 %collective-permute-start = (bf16[28,6144]{1,0:T(8,128)(2,1)S(1)}, bf16[28,6144]{1,0:T(8,128)(2,1)S(1)}, u32[]{:S(2)}, u32[]{:S(2)}) collective-permute-start(bf16[28,6144]{1,0:T(8,128)(2,1)S(1)} %slice.16), channel_id=1, source_target_pairs={{0,2},{2,4},{4,6},{6,8},{8,10},{10,12},{12,14},{1,3},{3,5},{5,7},{... | collective-permute-start | bytes 1032200
  277.2 3.2 %copy-start.1 = (bf16[64,6144]{1,0:T(8,128)(2,1)S(1)}, bf16[64,6144]{1,0:T(8,128)(2,1)}, u32[]{:S(2)}) copy-start(bf16[64,6144]{1,0:T(8,128)(2,1)} %param.21) | copy-start | bytes 2359300
Sparse Core Ops, SparseCore 0:
  13.0 73.0 all-gather.5
  209.3 67.7 reduce-scatter.5
  280.3 17.3 all-reduce.10
where the time goes:
time: 310 us; the launch traced here: 309 us
  blocking collectives  141 us (45%)
  waiting for transfers between devices  89.1 us (29%)
  matrix products  34.7 us (11%)
  local copies, waits for them, and re-layouts  17.3 us (6%)
  between operations  16 us (5%)
  other arithmetic  6.02 us (2%)
  starting transfers between devices  5.1 us (2%)
    unnamed x2, blocking collectives  108 us
    all_gather x1, waiting for transfers between devices, on_device(): lax.all_gather(grad_block, 'expert', axis=0, tiled=True)  46.9 us
    all_gather x1, blocking collectives, on_device(): lax.all_gather(low_block, 'expert', axis=0, tiled=True)  33 us
    reduce_scatter x1, waiting for transfers between devices, on_device(): lax.psum_scatter(down_local.astype(jnp.bfloat16), 'expert', scatter_dimen...  23.7 us
    psum x1, waiting for transfers between devices, on_device(): lax.psum(down_shard, 'dp').astype(jnp.float32)  13.7 us
    dot_general x1, matrix products, on_device(): jnp.dot(up_gradient, up_weight.T, preferred_element_type=jnp.float32)  12.4 us
    dot_general x1, matrix products, on_device(): jnp.dot(rows_all, down_weight.T, preferred_element_type=jnp.float32)  8.18 us
    unnamed x26, local copies, waits for them, and re-layouts  7.02 us
  transfers between devices with their start and end apart: 6, of which 5 were waited for; matrix products, arithmetic and copies ran while one was open for 5% of the time, Pallas kernels for 0%

commit v1 on v0

v1 whole, which is shorter than its diff:
```python
import functools

import jax
import jax.numpy as jnp
from jax import lax
from jax.experimental import pallas as pl
from jax.experimental.pallas import tpu as pltpu
from jax.sharding import PartitionSpec as P

SCALE = 0.25
NT = (((1,), (1,)), ((), ()))
TN = (((0,), (0,)), ((), ()))
BF = jnp.bfloat16
F32 = jnp.float32
VMEM_LIMIT = 48 * 1024 * 1024


def ring_order(mesh):
    count = mesh.shape["expert"]
    plain = list(range(count))
    if count < 4 or count % 2:
        return plain
    snake = list(range(0, count, 2)) + list(range(count - 1, 0, -2))
    spots = [getattr(d, "coords", None) for d in mesh.devices[0, :, 0]]
    if any(s is None for s in spots):
        return snake if count == 8 else plain

    def length(order):
        hops = zip(order, order[1:] + order[:1])
        return sum(sum(abs(a - b) for a, b in zip(spots[i], spots[j])) for i, j in hops)

    return min((plain, snake), key=length)


def dot(a, b, dims=None):
    if dims is None:
        dims = (((1,), (0,)), ((), ()))
    return lax.dot_general(a, b, dims, preferred_element_type=F32)


def pick_rows(choice, capacity):
    tokens = choice.shape[1]
    named = jnp.max((choice == 0).astype(F32), axis=0, keepdims=True)
    before = lax.broadcasted_iota(jnp.int32, (tokens, tokens), 0)
    after = lax.broadcasted_iota(jnp.int32, (tokens, tokens), 1)
    upto = (before <= after).astype(BF)
    count = dot(jnp.broadcast_to(named, (8, tokens)).astype(BF), upto)[:1]
    slot = jnp.where(named > 0, count - 1.0, -1000.0).astype(jnp.int32)
    row = lax.broadcasted_iota(jnp.int32, (2 * capacity, tokens), 0)
    return (row == slot).astype(BF), (row - capacity == slot).astype(BF)


def prepare_kernel(capacity, choice_ref, weight_ref, grad_ref, tokens_ref, down_ref, block_ref):
    half = grad_ref.shape[1] // 2
    rank = down_ref.shape[0]
    choice = choice_ref[...]
    upper, lower = pick_rows(choice, capacity)
    block_ref[:, :half] = (dot(upper, grad_ref[:, :half]) + dot(lower, grad_ref[:, half:])).astype(BF)
    low = dot(tokens_ref[...], down_ref[...], NT).astype(BF)
    weight = jnp.sum(
        jnp.where(choice == 0, weight_ref[...].astype(F32), 0.0), axis=0, keepdims=True
    )
    column = jnp.sum(upper.astype(F32) * weight, axis=1, keepdims=True)
    block_ref[:, half : half + rank] = dot(upper, low).astype(BF)
    block_ref[:, half + rank :] = jnp.broadcast_to(column, (2 * capacity, rank)).astype(BF)


def hidden_kernel(capacity, slot, count, *refs):
    blocks, (gate_ref, up_ref, down_ref, dgate_ref, dup_ref, rows) = refs[:count], refs[count:]
    half = down_ref.shape[1] // 2
    rank = (blocks[0].shape[1] - half) // 2
    tall = rows.shape[0] // count

    @pl.when(pl.program_id(0) == 0)
    def _():
        for i, block in enumerate(blocks):
            rows[i * tall : i * tall + 2 * capacity, :] = block[:, :half]

    first = dot(rows[...], down_ref[:, :half], NT)
    second = dot(rows[...], down_ref[:, half:], NT)
    live = lax.broadcasted_iota(jnp.int32, (slot, first.shape[1]), 0) < capacity
    for i, block in enumerate(blocks):
        at = i * tall
        weight = block[:, half:].astype(F32)[:slot, rank : rank + 1]
        grad = (first[at : at + slot] + second[at + capacity : at + capacity + slot]) * weight
        grad = jnp.where(live, grad, 0.0)
        gate = gate_ref[i].astype(F32)
        up = up_ref[i].astype(F32)
        sig = 1.0 / (1.0 + jnp.exp(-gate))
        dgate_ref[i] = (grad * up * (sig * (1.0 + gate * (1.0 - sig)))).astype(BF)
        dup_ref[i] = (grad * gate * sig).astype(BF)


def partial_kernel(capacity, slot, groups, cut, *refs):
    members = sum(groups)
    pieces = len(groups)
    dgates, refs = refs[:pieces], refs[pieces:]
    dups, refs = refs[:pieces], refs[pieces:]
    extras, refs = refs[:members], refs[members:]
    (gate_a, gate_b, up_a, up_b, lora_gate, lora_up), refs = refs[:6], refs[6:]
    outs, refs = refs[: members + 1], refs[members + 1 :]
    low_out, lora_out, dgate, dup, low, tile = refs
    rank = lora_gate.shape[0]

    @pl.when(pl.program_id(0) == 0)
    def _():
        at = 0
        for size, dgate_ref, dup_ref in zip(groups, dgates, dups):
            for i in range(size):
                dgate[at : at + slot, :] = dgate_ref[i]
                dup[at : at + slot, :] = dup_ref[i]
                low[at : at + slot, :] = extras[at // slot][:slot, :rank]
                at += slot
        low_out[...] = SCALE * (dot(dgate[...], lora_gate[...], NT) + dot(dup[...], lora_up[...], NT))
        lora_out[:rank, :] = (SCALE * dot(low[...], dgate[...], TN)).astype(BF)
        lora_out[rank:, :] = (SCALE * dot(low[...], dup[...], TN)).astype(BF)

    first = dot(dgate[...], gate_a[...], NT) + dot(dup[...], up_a[...], NT)
    second = dot(dgate[...], gate_b[...], NT) + dot(dup[...], up_b[...], NT)
    for i in range(members):
        at = i * slot
        tile[:capacity, :] = first[at : at + capacity]
        tile[capacity:, :] = second[at : at + capacity]
        if i < members - 1:
            outs[i][...] = tile[...].astype(BF)
        else:
            outs[i][...] = tile[:cut, :].astype(BF)
            outs[i + 1][...] = tile[cut:, :].astype(BF)


def adapter_kernel(capacity, owner_ref, choice_ref, low_ref, tokens_ref, out_ref):
    upper, _ = pick_rows(choice_ref[...], capacity)
    low = dot(upper[: low_ref.shape[0]], low_ref[...], TN).astype(BF)
    out_ref[0] = dot(low, tokens_ref[...], TN).astype(BF)


def finish_kernel(capacity, choice_ref, left_ref, right_ref, own_ref, low_ref, down_ref, out_ref, low_tall):
    half = left_ref.shape[1]
    upper, lower = pick_rows(choice_ref[...], capacity)
    low = low_ref[...].astype(F32)[:capacity]
    zero = jnp.zeros_like(low)
    low_tall[:capacity, :] = low
    low_tall[capacity:, :] = zero
    low_upper = low_tall[...].astype(BF)
    low_tall[:capacity, :] = zero
    low_tall[capacity:, :] = low
    low_lower = low_tall[...].astype(BF)
    total = left_ref[...].astype(F32) + right_ref[...].astype(F32) + own_ref[...].astype(F32)
    total += dot(low_upper, down_ref[:, :half]) + dot(low_lower, down_ref[:, half:])
    total = total.astype(BF)
    out_ref[:, :half] = dot(upper, total, TN).astype(BF)
    out_ref[:, half:] = dot(lower, total, TN).astype(BF)


def params():
    return pltpu.CompilerParams(vmem_limit_bytes=VMEM_LIMIT)


def cost(flops, moved):
    return pl.CostEstimate(flops=int(flops), bytes_accessed=int(moved), transcendentals=0)


def on_device(
    ring,
    tokens,
    output_gradient,
    token_expert_choice,
    routing_weight_table,
    stored_gate_rows,
    stored_up_rows,
    gate_weight,
    up_weight,
    down_weight,
    adapter_down_factor,
    adapter_gate_factor,
    adapter_up_factor,
):
    n = len(ring)
    tokens, output_gradient = tokens[0], output_gradient[0]
    own_count, width = tokens.shape
    half = width // 2
    capacity = stored_gate_rows.shape[1] // n
    hidden = stored_gate_rows.shape[2]
    rank = adapter_down_factor.shape[0]
    tall = -(-2 * capacity // 16) * 16
    slot = -(-capacity // 8) * 8
    cut = capacity // 16 * 16
    wide = half + 2 * rank
    middle = n // 2
    choice = token_expert_choice[0].T
    weights = routing_weight_table[0].T

    me = lax.axis_index("expert")
    core = lax.axis_index("dp")
    place = [0] * n
    for i, e in enumerate(ring):
        place[e] = i
    to_right = [(ring[i], ring[(i + 1) % n]) for i in range(n)]
    to_left = [(ring[i], ring[(i - 1) % n]) for i in range(n)]
    passes = [[0, -1, 1]] + [[-s, s] for s in range(2, middle)] + [[middle]]
    order = [r for group in passes for r in group]
    owners = jnp.array(
        [[ring[(place[e] + r) % n] for r in order] for e in range(n)], jnp.int32
    )[me]
    paired = jnp.array(
        [[[(place[e ^ x] - place[e] - r) % n for r in order].index(0) for x in range(n)] for e in range(n)],
        jnp.int32,
    )[me]

    block = pl.pallas_call(
        functools.partial(prepare_kernel, capacity),
        out_shape=jax.ShapeDtypeStruct((2 * capacity, wide), BF),
        compiler_params=params(),
        cost_estimate=cost(4e8, 4.5e6),
        name="prepare",
    )(choice, weights, output_gradient, tokens, adapter_down_factor)

    def in_order(stored):
        rows = stored[0].reshape(n, capacity, hidden)[owners]
        return jnp.pad(rows, ((0, 0), (0, slot - capacity), (0, 0)))

    gate_rows, up_rows = in_order(stored_gate_rows), in_order(stored_up_rows)

    got = {0: block}
    rightward = leftward = block
    for s in range(1, middle):
        rightward = lax.ppermute(rightward, "expert", to_right)
        leftward = lax.ppermute(leftward, "expert", to_left)
        got[-s], got[s] = rightward, leftward
    got[middle] = jnp.concatenate(
        [
            lax.ppermute(rightward[:cut], "expert", to_right),
            lax.ppermute(leftward[cut:], "expert", to_left),
        ],
        axis=0,
    )

    columns = 256
    dgates, dups = [], []
    start = 0
    for group in passes:
        size = len(group)
        grads = jax.ShapeDtypeStruct((size, slot, hidden), BF)
        row_spec = pl.BlockSpec((size, slot, columns), lambda i: (0, 0, i))
        dgate, dup = pl.pallas_call(
            functools.partial(hidden_kernel, capacity, slot, size),
            grid=(hidden // columns,),
            in_specs=[pl.BlockSpec((2 * capacity, wide), lambda i: (0, 0))] * size
            + [row_spec, row_spec, pl.BlockSpec((columns, width), lambda i: (i, 0))],
            out_specs=[row_spec, row_spec],
            out_shape=[grads, grads],
            scratch_shapes=[pltpu.VMEM((size * tall, half), BF)],
            compiler_params=params(),
            cost_estimate=cost(2 * size * tall * width * hidden, 2 * hidden * width),
            name="hidden_rows",
        )(
            *[got[r] for r in group],
            gate_rows[start : start + size],
            up_rows[start : start + size],
            down_weight,
        )
        dgates.append(dgate)
        dups.append(dup)
        start += size

    steps = half // columns
    sizes = [len(group) for group in passes]
    whole = lambda shape: pl.BlockSpec(shape, lambda i: (0,) * len(shape))
    part_a = pl.BlockSpec((columns, hidden), lambda i: (i, 0))
    part_b = pl.BlockSpec((columns, hidden), lambda i: (i + steps, 0))
    heights = [2 * capacity] * (n - 1) + [cut, 2 * capacity - cut]
    results = pl.pallas_call(
        functools.partial(partial_kernel, capacity, slot, sizes, cut),
        grid=(steps,),
        in_specs=[whole((s, slot, hidden)) for s in sizes] * 2
        + [pl.BlockSpec((2 * capacity, 2 * rank), lambda i: (0, half // (2 * rank)))] * n
        + [part_a, part_b, part_a, part_b]
        + [whole((rank, hidden))] * 2,
        out_specs=[pl.BlockSpec((h, columns), lambda i: (0, i)) for h in heights]
        + [whole((n * slot, rank)), whole((2 * rank, hidden))],
        out_shape=[jax.ShapeDtypeStruct((h, half), BF) for h in heights]
        + [
            jax.ShapeDtypeStruct((n * slot, rank), F32),
            jax.ShapeDtypeStruct((2 * rank, hidden), BF),
        ],
        scratch_shapes=[
            pltpu.VMEM((n * slot, hidden), BF),
            pltpu.VMEM((n * slot, hidden), BF),
            pltpu.VMEM((n * slot, rank), BF),
            pltpu.VMEM((2 * capacity, columns), F32),
        ],
        compiler_params=params(),
        cost_estimate=cost(4 * n * slot * width * hidden, 4 * hidden * width),
        name="partials",
    )(
        *dgates,
        *dups,
        *[got[r] for r in order],
        gate_weight,
        gate_weight,
        up_weight,
        up_weight,
        adapter_gate_factor,
        adapter_up_factor,
    )
    own = dict(zip(order[:-1], results))
    last_a, last_b, low_part, lora_local = results[n - 1 :]

    def add(a, b):
        return (a.astype(F32) + b.astype(F32)).astype(BF)

    going_right = lax.ppermute(last_a, "expert", to_right)
    going_left = lax.ppermute(last_b, "expert", to_left)

    low = low_part.reshape(n, slot, rank)[paired]
    bit = 1
    while bit < n:
        pairs = low.reshape(low.shape[0] // 2, 2, slot, rank)
        other = lax.ppermute(pairs[:, 1], "expert", [(e, e ^ bit) for e in range(n)])
        low = pairs[:, 0] + other
        bit *= 2
    low = low[0].astype(BF)

    own_right = own[middle - 1]
    own_left = own[-(middle - 1)]
    going_right = jnp.concatenate(
        [add(own_right[:cut], going_right), own_right[cut:]], axis=0
    )
    going_left = jnp.concatenate([own_left[:cut], add(own_left[cut:], going_left)], axis=0)
    for s in range(middle - 1, 0, -1):
        going_right = lax.ppermute(going_right, "expert", to_right)
        going_left = lax.ppermute(going_left, "expert", to_left)
        if s > 1:
            going_right = add(going_right, own[s - 1])
            going_left = add(going_left, own[-(s - 1)])

    share = width // n
    columns_of = jnp.arange(n, dtype=jnp.int32) ^ me
    if share % 128 == 0:
        down = pl.pallas_call(
            functools.partial(adapter_kernel, capacity),
            grid_spec=pltpu.PrefetchScalarGridSpec(
                num_scalar_prefetch=1,
                grid=(n,),
                in_specs=[
                    pl.BlockSpec(choice.shape, lambda i, o: (0, 0)),
                    pl.BlockSpec((slot, rank), lambda i, o: (0, 0)),
                    pl.BlockSpec((own_count, share), lambda i, o: (0, o[i])),
                ],
                out_specs=pl.BlockSpec((1, rank, share), lambda i, o: (i, 0, 0)),
            ),
            out_shape=jax.ShapeDtypeStruct((n, rank, share), BF),
            compiler_params=params(),
            cost_estimate=cost(2 * own_count * rank * width, 2 * own_count * width),
            name="adapter_gradient",
        )(columns_of, choice, low, tokens)
    else:
        upper, _ = pick_rows(choice, capacity)
        low_tokens = dot(upper[:slot], low, TN).astype(BF)
        down = dot(low_tokens, tokens, TN).astype(BF).reshape(rank, n, share)
        down = down.transpose(1, 0, 2)[columns_of]

    swap = [(0, 1), (1, 0)]
    part = rank // 2
    keep = jnp.where(core == 0, down[:, :part], down[:, part:])
    send = jnp.where(core == 0, down[:, part:], down[:, :part])
    down = add(keep, lax.ppermute(send, "dp", swap))
    lora = lora_local.astype(F32) + lax.ppermute(lora_local, "dp", swap).astype(F32)
    bit = 1
    while bit < n:
        pairs = down.reshape(down.shape[0] // 2, 2, part, share)
        other = lax.ppermute(pairs[:, 1], "expert", [(e, e ^ bit) for e in range(n)])
        down = add(pairs[:, 0], other)
        bit *= 2
    down = down[0]
    there = lax.ppermute(down, "dp", swap)
    grad_down = jnp.where(
        core == 0, jnp.concatenate([down, there]), jnp.concatenate([there, down])
    ).astype(F32)

    input_gradient = pl.pallas_call(
        functools.partial(finish_kernel, capacity),
        out_shape=jax.ShapeDtypeStruct((own_count, width), BF),
        scratch_shapes=[pltpu.VMEM((2 * capacity, rank), F32)],
        compiler_params=params(),
        cost_estimate=cost(4e8, 4.5e6),
        name="finish",
    )(choice, going_right, going_left, own[0], low, adapter_down_factor)
    return (input_gradient[None], grad_down, lora[:rank], lora[rank:])


def solution(mesh):
    placed = (
        P(("groups", "dp"), "expert", None),
        P(("groups", "dp"), "expert", None),
        P(("groups", "dp"), "expert", None),
        P(("groups", "dp"), "expert", None),
        P(("groups", "dp"), None, "expert"),
        P(("groups", "dp"), None, "expert"),
        P(None, "expert"),
        P(None, "expert"),
        P("expert", None),
        P("groups", None),
        P("groups", "expert"),
        P("groups", "expert"),
    )
    return jax.shard_map(
        functools.partial(on_device, ring_order(mesh)),
        mesh=mesh,
        in_specs=placed,
        out_specs=(
            P(("groups", "dp"), "expert", None),
            P("groups", "expert"),
            P("groups", "expert"),
            P("groups", "expert"),
        ),
        check_vma=False,
    )
```

time: 310 us -> 153 us (0.49)
  blocking collectives: 141 us -> 0 us
  Pallas kernels: 0 us -> 48 us
  waiting for transfers between devices: 89.1 us -> 50 us
  matrix products: 34.7 us -> 0 us
  starting transfers between devices: 5.1 us -> 30.3 us
  between operations: 16 us -> 1.14 us
    unnamed x2 -> x0, blocking collectives: 108 us -> none
    ppermute x0 -> x25, waiting for transfers between devices: none -> 50 us  [the longest x3 17.1 us: on_device(): rightward = lax.ppermute(rightward, 'expert', to_right)]
    pallas_call x0 -> x8, Pallas kernels: none -> 48 us  [the longest x4 24.9 us: on_device(): pl.pallas_call(functools.partial(hidden_kernel, capacity, slot, size), gr...]
    all_gather x1 -> x0, waiting for transfers between devices: 46.9 us -> none  [on_device(): lax.all_gather(grad_block, 'expert', axis=0, tiled=True)]
    dot_general x10 -> x0, matrix products: 34.7 us -> none  [the longest x1 12.4 us: on_device(): jnp.dot(up_gradient, up_weight.T, preferred_element_type=jnp.float32)]
    all_gather x1 -> x0, blocking collectives: 33 us -> none  [on_device(): lax.all_gather(low_block, 'expert', axis=0, tiled=True)]
    ppermute x0 -> x25, starting transfers between devices: none -> 30.3 us  [the longest x6 9.34 us: on_device(): lax.ppermute(pairs[:, 1], 'expert', [(e, e ^ bit) for e in range(n)])]
    reduce_scatter x1 -> x0, waiting for transfers between devices: 23.7 us -> none  [on_device(): lax.psum_scatter(down_local.astype(jnp.bfloat16), 'expert', scatter_dimen...]
  transfers between devices with their start and end apart: 6 -> 25, of which waited for: 5 -> 15; matrix products, arithmetic and copies ran while one was open for 5% -> 5% of each run, Pallas kernels for 0% -> 16%
where the time goes in v1:
time: 153 us; the launch traced here: 152 us
  waiting for transfers between devices  50 us (33%)
  Pallas kernels  48 us (31%)
  starting transfers between devices  30.3 us (20%)
  local copies, waits for them, and re-layouts  17.8 us (12%)
  other arithmetic  4.86 us (3%)
    pallas_call x4, Pallas kernels, on_device(): pl.pallas_call(functools.partial(hidden_kernel, capacity, slot, size), gr...  24.9 us
    ppermute x3, waiting for transfers between devices, on_device(): rightward = lax.ppermute(rightward, 'expert', to_right)  17.1 us
    ppermute x6, waiting for transfers between devices, on_device(): lax.ppermute(pairs[:, 1], 'expert', [(e, e ^ bit) for e in range(n)])  16.7 us
    pallas_call x1, Pallas kernels, on_device(): pl.pallas_call(functools.partial(partial_kernel, capacity, slot, sizes, c...  15 us
    ppermute x3, waiting for transfers between devices, on_device(): going_right = lax.ppermute(going_right, 'expert', to_right)  11.3 us
    unnamed x59, local copies, waits for them, and re-layouts  11.3 us
    ppermute x6, starting transfers between devices, on_device(): lax.ppermute(pairs[:, 1], 'expert', [(e, e ^ bit) for e in range(n)])  9.34 us
    ppermute x3, starting transfers between devices, on_device(): rightward = lax.ppermute(rightward, 'expert', to_right)  6.35 us
  transfers between devices with their start and end apart: 25, of which 15 were waited for; matrix products, arithmetic and copies ran while one was open for 5% of the time, Pallas kernels for 16%

profile of v1, /device:TPU:0, one launch (start us, length us, event | category | flops | bytes accessed | tf_op | source)
XLA Modules:
  0.0 152.0 jit_solution(17772334888478495647)
XLA Ops:
  7.0 3.1 %collective-permute-start = (bf16[72,3200]{1,0:T(8,128)(2,1)S(1)}, bf16[72,3200]{1,0:T(8,128)(2,1)S(1)}, u32[]{:S(2)}, u32[]{:S(2)}) collective-permute-start(bf16[72,3200]{1,0:T(8,128)(2,1)S(1)} %prepare.1.refs_0_.refs_8_), channel_id=1, source_target_pairs={{0,4},{4,8},{8,12},{12,14},{14,10},{10,6},{6,2},{2,0},{1,5},{5,9},... | collective-permute-start | bytes 1382408 | tf_op jit(solution)/shard_map/ppermute | solution.py:227
  13.7 6.9 %collective-permute-done.refs_1_.refs_9_ = bf16[72,3200]{1,0:T(8,128)(2,1)S(1)} collective-permute-done((bf16[72,3200]{1,0:T(8,128)(2,1)S(1)}, bf16[72,3200]{1,0:T(8,128)(2,1)S(1)}, u32[]{:S(2)}, u32[]{:S(2)}) %collective-permute-start) | collective-permute-done | bytes 460832 | tf_op jit(solution)/shard_map/ppermute | solution.py:227
  20.6 1.8 %collective-permute-start.2 = (bf16[72,3200]{1,0:T(8,128)(2,1)S(1)}, bf16[72,3200]{1,0:T(8,128)(2,1)S(1)}, u32[]{:S(2)}, u32[]{:S(2)}) collective-permute-start(bf16[72,3200]{1,0:T(8,128)(2,1)S(1)} %collective-permute-done.refs_1_.refs_9_), channel_id=1, source_target_pairs={{0,4},{4,8},{8,12},{12,14},{14,10},{10,6},{6,2},{2,0},{1,5},{5,9},... | collective-permute-start | bytes 1382408 | tf_op jit(solution)/shard_map/ppermute | solution.py:227
  24.0 8.4 %collective-permute-done.2.refs_0_.refs_11_ = bf16[72,3200]{1,0:T(8,128)(2,1)S(1)} collective-permute-done((bf16[72,3200]{1,0:T(8,128)(2,1)S(1)}, bf16[72,3200]{1,0:T(8,128)(2,1)S(1)}, u32[]{:S(2)}, u32[]{:S(2)}) %collective-permute-start.2) | collective-permute-done | bytes 460832 | tf_op jit(solution)/shard_map/ppermute | solution.py:227
  35.4 6.0 %hidden_rows.4 = (bf16[3,40,768]{2,1,0:T(8,128)(2,1)S(1)}, bf16[3,40,768]{2,1,0:T(8,128)(2,1)S(1)}) custom-call(bf16[72,3200]{1,0:T(8,128)(2,1)S(1)} %prepare.1.refs_0_.refs_8_, bf16[72,3200]{1,0:T(8,128)(2,1)S(1)} %collective-permute-done.refs_1_.refs_9_, bf16[72,3200]{1,0:T(8,128)(2,1)S(1)} %collective-permute-done.1.refs_2_.refs_10_, ...), custom_call_target="tpu_custom_call" | custom-call | flops 2264924160 | bytes 9437184 | tf_op jit(solution)/shard_map/hidden_rows/pallas_call | solution.py:245
  44.6 6.3 %hidden_rows.5 = (bf16[2,40,768]{2,1,0:T(8,128)(2,1)S(1)}, bf16[2,40,768]{2,1,0:T(8,128)(2,1)S(1)}) custom-call(bf16[72,3200]{1,0:T(8,128)(2,1)S(1)} %collective-permute-done.2.refs_0_.refs_11_, bf16[72,3200]{1,0:T(8,128)(2,1)S(1)} %collective-permute-done.3.refs_1_.refs_12_, bf16[2,40,768]{2,1,0:T(8,128)(2,1)S(1)} %get-tuple-element.45.refs_2_, ...), custom_call_target="tpu_custom_call" | custom-call | flops 1509949440 | bytes 9437184 | tf_op jit(solution)/shard_map/hidden_rows/pallas_call | solution.py:245
  51.7 6.3 %hidden_rows.6 = (bf16[2,40,768]{2,1,0:T(8,128)(2,1)S(1)}, bf16[2,40,768]{2,1,0:T(8,128)(2,1)S(1)}) custom-call(bf16[72,3200]{1,0:T(8,128)(2,1)S(1)} %collective-permute-done.4.refs_0_.refs_13_, bf16[72,3200]{1,0:T(8,128)(2,1)S(1)} %collective-permute-done.5.refs_1_.refs_14_, bf16[2,40,768]{2,1,0:T(8,128)(2,1)S(1)} %get-tuple-element.44.refs_2_, ...), custom_call_target="tpu_custom_call" | custom-call | flops 1509949440 | bytes 9437184 | tf_op jit(solution)/shard_map/hidden_rows/pallas_call | solution.py:245
  58.2 6.2 %hidden_rows.7 = (bf16[1,40,768]{2,1,0:T(8,128)(2,1)S(1)}, bf16[1,40,768]{2,1,0:T(8,128)(2,1)S(1)}) custom-call(bf16[72,3200]{1,0:T(8,128)(2,1)S(1)} %constant_dynamic-update-slice_fusion.refs_0_.refs_15_, bf16[1,40,768]{2,1,0:T(8,128)(2,1)S(1)} %pad_slice_fusion.4.refs_1_, bf16[1,40,768]{2,1,0:T(8,128)(2,1)S(1)} %pad_slice_fusion.refs_2_, ...), custom_call_target="tpu_custom_call" | custom-call | flops 754974720 | bytes 9437184 | tf_op jit(solution)/shard_map/hidden_rows/pallas_call | solution.py:245
  64.5 15.0 %partials.1 = (bf16[72,3072]{1,0:T(8,128)(2,1)S(1)}, bf16[72,3072]{1,0:T(8,128)(2,1)S(1)}, bf16[72,3072]{1,0:T(8,128)(2,1)S(1)}, bf16[72,3072]{1,0:T(8,128)(2,1)...) custom-call(bf16[3,40,768]{2,1,0:T(8,128)(2,1)S(1)} %get-tuple-eleme, ...), custom_call_target="tpu_custom_call" | custom-call | flops 6039797760 | bytes 18874368 | tf_op jit(solution)/shard_map/partials/pallas_call | solution.py:272
  88.9 3.2 %collective-permute-done.16 = f32[4,40,64]{2,1,0:T(8,128)S(1)} collective-permute-done((f32[4,40,64]{2,1,0:T(8,128)S(1)}, f32[4,40,64]{2,1,0:T(8,128)S(1)}, u32[]{:S(2)}, u32[]{:S(2)}) %collective-permute-start.16) | collective-permute-done | bytes 40992 | tf_op jit(solution)/shard_map/ppermute | solution.py:319
  94.3 2.7 %collective-permute-done.17 = f32[2,40,64]{2,1,0:T(8,128)S(1)} collective-permute-done((f32[2,40,64]{2,1,0:T(8,128)S(1)}, f32[2,40,64]{2,1,0:T(8,128)S(1)}, u32[]{:S(2)}, u32[]{:S(2)}) %collective-permute-start.17) | collective-permute-done | bytes 20512 | tf_op jit(solution)/shard_map/ppermute | solution.py:319
  97.0 2.4 %collective-permute-start.18 = (f32[1,40,64]{2,1,0:T(8,128)S(1)}, f32[1,40,64]{2,1,0:T(8,128)S(1)}, u32[]{:S(2)}, u32[]{:S(2)}) collective-permute-start(f32[1,40,64]{2,1,0:T(8,128)S(1)} %slice_bitcast_fusion.10), channel_id=1, source_target_pairs={{0,8},{2,10},{4,12},{6,14},{8,0},{10,2},{12,4},{14,6},{1,9},{3,11}... | collective-permute-start | bytes 30728 | tf_op jit(solution)/shard_map/ppermute | solution.py:319
  99.5 1.9 %collective-permute-start.8 = (bf16[32,3072]{1,0:T(8,128)(2,1)}, bf16[32,3072]{1,0:T(8,128)(2,1)S(1)}, u32[]{:S(2)}, u32[]{:S(2)}) collective-permute-start(bf16[32,3072]{1,0:T(8,128)(2,1)} %copy-done.28), channel_id=1, source_target_pairs={{0,4},{4,8},{8,12},{12,14},{14,10},{10,6},{6,2},{2,0},{1,5},{5,9},... | collective-permute-start | bytes 589832 | tf_op jit(solution)/shard_map/ppermute | solution.py:312
  101.8 4.9 %adapter_gradient.1 = bf16[8,64,768]{2,1,0:T(8,128)(2,1)S(1)} custom-call(s32[8]{0:T(128)S(1)} %iota_xor_fusion.owner_ref, s32[4,128]{1,0:T(4,128)S(1)} %bitcast.92, bf16[40,64]{1,0:T(8,128)(2,1)S(1)} %fusion.11.low_ref, bf16[128,6144]{1,0:T(8,128)(2,1)S(1)} %bitcast.88), custom_call_target="tpu_custom_call" | custom-call | flops 100663296 | bytes 1572864 | tf_op jit(solution)/shard_map/adapter_gradient/pallas_call | solution.py:340
  112.2 8.0 %collective-permute-done.9 = bf16[72,3072]{1,0:T(8,128)(2,1)S(1)} collective-permute-done((bf16[72,3072]{1,0:T(8,128)(2,1)S(1)}, bf16[72,3072]{1,0:T(8,128)(2,1)S(1)}, u32[]{:S(2)}, u32[]{:S(2)}) %collective-permute-start.9) | collective-permute-done | bytes 442400 | tf_op jit(solution)/shard_map/ppermute | solution.py:331
  121.5 2.9 %collective-permute-done.20 = bf16[4,32,768]{2,1,0:T(8,128)(2,1)S(1)} collective-permute-done((bf16[4,32,768]{2,1,0:T(8,128)(2,1)S(1)}, bf16[4,32,768]{2,1,0:T(8,128)(2,1)S(1)}, u32[]{:S(2)}, u32[]{:S(2)}) %collective-permute-start.20) | collective-permute-done | bytes 196640 | tf_op jit(solution)/shard_map/ppermute | solution.py:372
  124.7 2.4 %collective-permute-start.14 = (bf16[72,3072]{1,0:T(8,128)(2,1)S(1)}, bf16[72,3072]{1,0:T(8,128)(2,1)S(1)}, u32[]{:S(2)}, u32[]{:S(2)}) collective-permute-start(bf16[72,3072]{1,0:T(8,128)(2,1)S(1)} %add_convert_fusion.1), channel_id=1, source_target_pairs={{0,2},{4,0},{8,4},{12,8},{14,12},{10,14},{6,10},{2,6},{1,3},{5,1},... | collective-permute-start | bytes 1327112 | tf_op jit(solution)/shard_map/ppermute | solution.py:332
  127.1 5.7 %collective-permute-done.21 = bf16[2,32,768]{2,1,0:T(8,128)(2,1)S(1)} collective-permute-done((bf16[2,32,768]{2,1,0:T(8,128)(2,1)S(1)}, bf16[2,32,768]{2,1,0:T(8,128)(2,1)S(1)}, u32[]{:S(2)}, u32[]{:S(2)}) %collective-permute-start.21) | collective-permute-done | bytes 98336 | tf_op jit(solution)/shard_map/ppermute | solution.py:372
  132.8 2.7 %collective-permute-start.22 = (bf16[1,32,768]{2,1,0:T(8,128)(2,1)S(1)}, bf16[1,32,768]{2,1,0:T(8,128)(2,1)S(1)}, u32[]{:S(2)}, u32[]{:S(2)}) collective-permute-start(bf16[1,32,768]{2,1,0:T(8,128)(2,1)S(1)} %slice_bitcast_fusion.6), channel_id=1, source_target_pairs={{0,8},{2,10},{4,12},{6,14},{8,0},{10,2},{12,4},{14,6},{1,9},{3,11}... | collective-permute-start | bytes 147464 | tf_op jit(solution)/shard_map/ppermute | solution.py:372
  135.6 2.5 %collective-permute-start.11 = (bf16[72,3072]{1,0:T(8,128)(2,1)S(1)}, bf16[72,3072]{1,0:T(8,128)(2,1)S(1)}, u32[]{:S(2)}, u32[]{:S(2)}) collective-permute-start(bf16[72,3072]{1,0:T(8,128)(2,1)S(1)} %add_convert_fusion.2), channel_id=1, source_target_pairs={{0,4},{4,8},{8,12},{12,14},{14,10},{10,6},{6,2},{2,0},{1,5},{5,9},... | collective-permute-start | bytes 1327112 | tf_op jit(solution)/shard_map/ppermute | solution.py:331
  139.2 2.2 %collective-permute-done.22 = bf16[1,32,768]{2,1,0:T(8,128)(2,1)S(1)} collective-permute-done((bf16[1,32,768]{2,1,0:T(8,128)(2,1)S(1)}, bf16[1,32,768]{2,1,0:T(8,128)(2,1)S(1)}, u32[]{:S(2)}, u32[]{:S(2)}) %collective-permute-start.22) | collective-permute-done | bytes 49184 | tf_op jit(solution)/shard_map/ppermute | solution.py:372
  143.4 3.2 %collective-permute-done.11.left_ref = bf16[72,3072]{1,0:T(8,128)(2,1)S(1)} collective-permute-done((bf16[72,3072]{1,0:T(8,128)(2,1)S(1)}, bf16[72,3072]{1,0:T(8,128)(2,1)S(1)}, u32[]{:S(2)}, u32[]{:S(2)}) %collective-permute-start.11) | collective-permute-done | bytes 442400 | tf_op jit(solution)/shard_map/ppermute | solution.py:331
  146.6 3.4 %collective-permute-done.15.right_ref = bf16[72,3072]{1,0:T(8,128)(2,1)S(1)} collective-permute-done((bf16[72,3072]{1,0:T(8,128)(2,1)S(1)}, bf16[72,3072]{1,0:T(8,128)(2,1)S(1)}, u32[]{:S(2)}, u32[]{:S(2)}) %collective-permute-start.15) | collective-permute-done | bytes 442400 | tf_op jit(solution)/shard_map/ppermute | solution.py:332
  150.0 2.0 %finish.1 = bf16[128,6144]{1,0:T(8,128)(2,1)} custom-call(s32[4,128]{1,0:T(4,128)S(1)} %bitcast.93, bf16[72,3072]{1,0:T(8,128)(2,1)S(1)} %collective-permute-done.11.left_ref, bf16[72,3072]{1,0:T(8,128)(2,1)S(1)} %collective-permute-done.15.right_ref, bf16[72,3072]{1,0:T(8,128)(2,1)S(1)} %copy-done.20, bf16[40,64]{1,0:T(8,128)(2,1)S(1)} %fusion.11.low_ref, ...), custom_call_target="tpu_custom_call" | custom-call | flops 400000000 | bytes 4500000 | tf_op jit(solution)/shard_map/finish/pallas_call | solution.py:381
  (138 shorter events, 40.7 us)
Async XLA Ops:
  7.0 13.6 %collective-permute-start = (bf16[72,3200]{1,0:T(8,128)(2,1)S(1)}, bf16[72,3200]{1,0:T(8,128)(2,1)S(1)}, u32[]{:S(2)}, u32[]{:S(2)}) collective-permute-start(bf16[72,3200]{1,0:T(8,128)(2,1)S(1)} %prepare.1.refs_0_.refs_8_), channel_id=1, source_target_pairs={{0,4},{4,8},{8,12},{12,14},{14,10},{10,6},{6,2},{2,0},{1,5},{5,9},... | collective-permute-start | bytes 1382408 | tf_op jit(solution)/shard_map/ppermute | solution.py:227
  10.1 13.5 %collective-permute-start.1 = (bf16[72,3200]{1,0:T(8,128)(2,1)S(1)}, bf16[72,3200]{1,0:T(8,128)(2,1)S(1)}, u32[]{:S(2)}, u32[]{:S(2)}) collective-permute-start(bf16[72,3200]{1,0:T(8,128)(2,1)S(1)} %prepare.1.refs_0_.refs_8_), channel_id=1, source_target_pairs={{0,2},{4,0},{8,4},{12,8},{14,12},{10,14},{6,10},{2,6},{1,3},{5,1},... | collective-permute-start | bytes 1382408 | tf_op jit(solution)/shard_map/ppermute | solution.py:228
  20.6 11.7 %collective-permute-start.2 = (bf16[72,3200]{1,0:T(8,128)(2,1)S(1)}, bf16[72,3200]{1,0:T(8,128)(2,1)S(1)}, u32[]{:S(2)}, u32[]{:S(2)}) collective-permute-start(bf16[72,3200]{1,0:T(8,128)(2,1)S(1)} %collective-permute-done.refs_1_.refs_9_), channel_id=1, source_target_pairs={{0,4},{4,8},{8,12},{12,14},{14,10},{10,6},{6,2},{2,0},{1,5},{5,9},... | collective-permute-start | bytes 1382408 | tf_op jit(solution)/shard_map/ppermute | solution.py:227
  23.6 11.2 %collective-permute-start.3 = (bf16[72,3200]{1,0:T(8,128)(2,1)S(1)}, bf16[72,3200]{1,0:T(8,128)(2,1)S(1)}, u32[]{:S(2)}, u32[]{:S(2)}) collective-permute-start(bf16[72,3200]{1,0:T(8,128)(2,1)S(1)} %collective-permute-done.1.refs_2_.refs_10_), channel_id=1, source_target_pairs={{0,2},{4,0},{8,4},{12,8},{14,12},{10,14},{6,10},{2,6},{1,3},{5,1},... | collective-permute-start | bytes 1382408 | tf_op jit(solution)/shard_map/ppermute | solution.py:228
  32.4 10.8 %collective-permute-start.4 = (bf16[72,3200]{1,0:T(8,128)(2,1)S(1)}, bf16[72,3200]{1,0:T(8,128)(2,1)S(1)}, u32[]{:S(2)}, u32[]{:S(2)}) collective-permute-start(bf16[72,3200]{1,0:T(8,128)(2,1)S(1)} %collective-permute-done.2.refs_0_.refs_11_), channel_id=1, source_target_pairs={{0,4},{4,8},{8,12},{12,14},{14,10},{10,6},{6,2},{2,0},{1,5},{5,9},... | collective-permute-start | bytes 1382408 | tf_op jit(solution)/shard_map/ppermute | solution.py:227
  34.9 16.1 %collective-permute-start.5 = (bf16[72,3200]{1,0:T(8,128)(2,1)S(1)}, bf16[72,3200]{1,0:T(8,128)(2,1)S(1)}, u32[]{:S(2)}, u32[]{:S(2)}) collective-permute-start(bf16[72,3200]{1,0:T(8,128)(2,1)S(1)} %collective-permute-done.3.refs_1_.refs_12_), channel_id=1, source_target_pairs={{0,2},{4,0},{8,4},{12,8},{14,12},{10,14},{6,10},{2,6},{1,3},{5,1},... | collective-permute-start | bytes 1382408 | tf_op jit(solution)/shard_map/ppermute | solution.py:228
  43.2 14.9 %collective-permute-start.6 = (bf16[32,3200]{1,0:T(8,128)(2,1)S(1)}, bf16[32,3200]{1,0:T(8,128)(2,1)S(1)}, u32[]{:S(2)}, u32[]{:S(2)}) collective-permute-start(bf16[32,3200]{1,0:T(8,128)(2,1)S(1)} %slice.128), channel_id=1, source_target_pairs={{0,4},{4,8},{8,12},{12,14},{14,10},{10,6},{6,2},{2,0},{1,5},{5,9},... | collective-permute-start | bytes 614408 | tf_op jit(solution)/shard_map/ppermute | solution.py:232
  51.0 7.2 %collective-permute-start.7 = (bf16[40,3200]{1,0:T(8,128)(2,1)S(1)}, bf16[40,3200]{1,0:T(8,128)(2,1)S(1)}, u32[]{:S(2)}, u32[]{:S(2)}) collective-permute-start(bf16[40,3200]{1,0:T(8,128)(2,1)S(1)} %slice.129), channel_id=1, source_target_pairs={{0,2},{4,0},{8,4},{12,8},{14,12},{10,14},{6,10},{2,6},{1,3},{5,1},... | collective-permute-start | bytes 768008 | tf_op jit(solution)/shard_map/ppermute | solution.py:233
  87.6 4.4 %collective-permute-start.16 = (f32[4,40,64]{2,1,0:T(8,128)S(1)}, f32[4,40,64]{2,1,0:T(8,128)S(1)}, u32[]{:S(2)}, u32[]{:S(2)}) collective-permute-start(f32[4,40,64]{2,1,0:T(8,128)S(1)} %slice_bitcast_fusion.4), channel_id=1, source_target_pairs={{0,2},{2,0},{4,6},{6,4},{8,10},{10,8},{12,14},{14,12},{1,3},{3,1},... | collective-permute-start | bytes 122888 | tf_op jit(solution)/shard_map/ppermute | solution.py:319
  93.0 4.1 %collective-permute-start.17 = (f32[2,40,64]{2,1,0:T(8,128)S(1)}, f32[2,40,64]{2,1,0:T(8,128)S(1)}, u32[]{:S(2)}, u32[]{:S(2)}) collective-permute-start(f32[2,40,64]{2,1,0:T(8,128)S(1)} %slice_bitcast_fusion.8), channel_id=1, source_target_pairs={{0,4},{2,6},{4,0},{6,2},{8,12},{10,14},{12,8},{14,10},{1,5},{3,7},... | collective-permute-start | bytes 61448 | tf_op jit(solution)/shard_map/ppermute | solution.py:319
  97.0 4.7 %collective-permute-start.18 = (f32[1,40,64]{2,1,0:T(8,128)S(1)}, f32[1,40,64]{2,1,0:T(8,128)S(1)}, u32[]{:S(2)}, u32[]{:S(2)}) collective-permute-start(f32[1,40,64]{2,1,0:T(8,128)S(1)} %slice_bitcast_fusion.10), channel_id=1, source_target_pairs={{0,8},{2,10},{4,12},{6,14},{8,0},{10,2},{12,4},{14,6},{1,9},{3,11}... | collective-permute-start | bytes 30728 | tf_op jit(solution)/shard_map/ppermute | solution.py:319
  99.5 7.6 %collective-permute-start.8 = (bf16[32,3072]{1,0:T(8,128)(2,1)}, bf16[32,3072]{1,0:T(8,128)(2,1)S(1)}, u32[]{:S(2)}, u32[]{:S(2)}) collective-permute-start(bf16[32,3072]{1,0:T(8,128)(2,1)} %copy-done.28), channel_id=1, source_target_pairs={{0,4},{4,8},{8,12},{12,14},{14,10},{10,6},{6,2},{2,0},{1,5},{5,9},... | collective-permute-start | bytes 589832 | tf_op jit(solution)/shard_map/ppermute | solution.py:312
  101.4 7.6 %collective-permute-start.24 = (bf16[128,768]{1,0:T(8,128)(2,1)}, bf16[128,768]{1,0:T(8,128)(2,1)S(1)}, u32[]{:S(2)}, u32[]{:S(2)}) collective-permute-start(bf16[128,768]{1,0:T(8,128)(2,1)} %copy-done.21), channel_id=1, source_target_pairs={{0,1},{1,0},{2,3},{3,2},{4,5},{5,4},{6,7},{7,6},{8,9},{9,8},{10,11... | collective-permute-start | bytes 589832 | tf_op jit(solution)/shard_map/ppermute | solution.py:368
  101.5 8.6 %collective-permute-start.12 = (bf16[40,3072]{1,0:T(8,128)(2,1)}, bf16[40,3072]{1,0:T(8,128)(2,1)S(1)}, u32[]{:S(2)}, u32[]{:S(2)}) collective-permute-start(bf16[40,3072]{1,0:T(8,128)(2,1)} %copy-done.27), channel_id=1, source_target_pairs={{0,2},{4,0},{8,4},{12,8},{14,12},{10,14},{6,10},{2,6},{1,3},{5,1},... | collective-permute-start | bytes 737288 | tf_op jit(solution)/shard_map/ppermute | solution.py:313
  106.8 3.6 %collective-permute-start.19 = (bf16[8,32,768]{2,1,0:T(8,128)(2,1)S(1)}, bf16[8,32,768]{2,1,0:T(8,128)(2,1)S(1)}, u32[]{:S(2)}, u32[]{:S(2)}) collective-permute-start(bf16[8,32,768]{2,1,0:T(8,128)(2,1)S(1)} %broadcast_select_fusion), channel_id=1, source_target_pairs={{0,1},{1,0},{2,3},{3,2},{4,5},{5,4},{6,7},{7,6},{8,9},{9,8},{10,11... | collective-permute-start | bytes 1179656 | tf_op jit(solution)/shard_map/ppermute | solution.py:367
  107.2 13.0 %collective-permute-start.9 = (bf16[72,3072]{1,0:T(8,128)(2,1)S(1)}, bf16[72,3072]{1,0:T(8,128)(2,1)S(1)}, u32[]{:S(2)}, u32[]{:S(2)}) collective-permute-start(bf16[72,3072]{1,0:T(8,128)(2,1)S(1)} %pad_maximum_fusion), channel_id=1, source_target_pairs={{0,4},{4,8},{8,12},{12,14},{14,10},{10,6},{6,2},{2,0},{1,5},{5,9},... | collective-permute-start | bytes 1327112 | tf_op jit(solution)/shard_map/ppermute | solution.py:331
  110.1 14.4 %collective-permute-start.13 = (bf16[72,3072]{1,0:T(8,128)(2,1)S(1)}, bf16[72,3072]{1,0:T(8,128)(2,1)S(1)}, u32[]{:S(2)}, u32[]{:S(2)}) collective-permute-start(bf16[72,3072]{1,0:T(8,128)(2,1)S(1)} %pad_maximum_fusion.1), channel_id=1, source_target_pairs={{0,2},{4,0},{8,4},{12,8},{14,12},{10,14},{6,10},{2,6},{1,3},{5,1},... | collective-permute-start | bytes 1327112 | tf_op jit(solution)/shard_map/ppermute | solution.py:332
  110.6 13.8 %collective-permute-start.20 = (bf16[4,32,768]{2,1,0:T(8,128)(2,1)S(1)}, bf16[4,32,768]{2,1,0:T(8,128)(2,1)S(1)}, u32[]{:S(2)}, u32[]{:S(2)}) collective-permute-start(bf16[4,32,768]{2,1,0:T(8,128)(2,1)S(1)} %slice_bitcast_fusion), channel_id=1, source_target_pairs={{0,2},{2,0},{4,6},{6,4},{8,10},{10,8},{12,14},{14,12},{1,3},{3,1},... | collective-permute-start | bytes 589832 | tf_op jit(solution)/shard_map/ppermute | solution.py:372
  120.3 15.2 %collective-permute-start.10 = (bf16[72,3072]{1,0:T(8,128)(2,1)S(1)}, bf16[72,3072]{1,0:T(8,128)(2,1)S(1)}, u32[]{:S(2)}, u32[]{:S(2)}) collective-permute-start(bf16[72,3072]{1,0:T(8,128)(2,1)S(1)} %add_convert_fusion.3), channel_id=1, source_target_pairs={{0,4},{4,8},{8,12},{12,14},{14,10},{10,6},{6,2},{2,0},{1,5},{5,9},... | collective-permute-start | bytes 1327112 | tf_op jit(solution)/shard_map/ppermute | solution.py:331
  124.5 8.3 %collective-permute-start.21 = (bf16[2,32,768]{2,1,0:T(8,128)(2,1)S(1)}, bf16[2,32,768]{2,1,0:T(8,128)(2,1)S(1)}, u32[]{:S(2)}, u32[]{:S(2)}) collective-permute-start(bf16[2,32,768]{2,1,0:T(8,128)(2,1)S(1)} %slice_bitcast_fusion.2), channel_id=1, source_target_pairs={{0,4},{2,6},{4,0},{6,2},{8,12},{10,14},{12,8},{14,10},{1,5},{3,7},... | collective-permute-start | bytes 294920 | tf_op jit(solution)/shard_map/ppermute | solution.py:372
  124.7 13.5 %collective-permute-start.14 = (bf16[72,3072]{1,0:T(8,128)(2,1)S(1)}, bf16[72,3072]{1,0:T(8,128)(2,1)S(1)}, u32[]{:S(2)}, u32[]{:S(2)}) collective-permute-start(bf16[72,3072]{1,0:T(8,128)(2,1)S(1)} %add_convert_fusion.1), channel_id=1, source_target_pairs={{0,2},{4,0},{8,4},{12,8},{14,12},{10,14},{6,10},{2,6},{1,3},{5,1},... | collective-permute-start | bytes 1327112 | tf_op jit(solution)/shard_map/ppermute | solution.py:332
  132.8 8.6 %collective-permute-start.22 = (bf16[1,32,768]{2,1,0:T(8,128)(2,1)S(1)}, bf16[1,32,768]{2,1,0:T(8,128)(2,1)S(1)}, u32[]{:S(2)}, u32[]{:S(2)}) collective-permute-start(bf16[1,32,768]{2,1,0:T(8,128)(2,1)S(1)} %slice_bitcast_fusion.6), channel_id=1, source_target_pairs={{0,8},{2,10},{4,12},{6,14},{8,0},{10,2},{12,4},{14,6},{1,9},{3,11}... | collective-permute-start | bytes 147464 | tf_op jit(solution)/shard_map/ppermute | solution.py:372
  135.6 11.0 %collective-permute-start.11 = (bf16[72,3072]{1,0:T(8,128)(2,1)S(1)}, bf16[72,3072]{1,0:T(8,128)(2,1)S(1)}, u32[]{:S(2)}, u32[]{:S(2)}) collective-permute-start(bf16[72,3072]{1,0:T(8,128)(2,1)S(1)} %add_convert_fusion.2), channel_id=1, source_target_pairs={{0,4},{4,8},{8,12},{12,14},{14,10},{10,6},{6,2},{2,0},{1,5},{5,9},... | collective-permute-start | bytes 1327112 | tf_op jit(solution)/shard_map/ppermute | solution.py:331
  138.3 11.7 %collective-permute-start.15 = (bf16[72,3072]{1,0:T(8,128)(2,1)S(1)}, bf16[72,3072]{1,0:T(8,128)(2,1)S(1)}, u32[]{:S(2)}, u32[]{:S(2)}) collective-permute-start(bf16[72,3072]{1,0:T(8,128)(2,1)S(1)} %add_convert_fusion), channel_id=1, source_target_pairs={{0,2},{4,0},{8,4},{12,8},{14,12},{10,14},{6,10},{2,6},{1,3},{5,1},... | collective-permute-start | bytes 1327112 | tf_op jit(solution)/shard_map/ppermute | solution.py:332
  (30 other events, 443.7 us)

commit v2 on v1

--- a/solution.py
+++ b/solution.py
@@ -12,7 +12,8 @@
 TN = (((0,), (0,)), ((), ()))
 BF = jnp.bfloat16
 F32 = jnp.float32
-VMEM_LIMIT = 48 * 1024 * 1024
+VMEM_LIMIT = 20 * 1024 * 1024
+TILE = 256
 
 
 def ring_order(mesh):
@@ -50,82 +51,112 @@
     return (row == slot).astype(BF), (row - capacity == slot).astype(BF)
 
 
-def prepare_kernel(capacity, choice_ref, weight_ref, grad_ref, tokens_ref, down_ref, block_ref):
+def prepare_kernel(capacity, choice_hbm, weight_hbm, grad_hbm, tokens_hbm, down_hbm, block_ref,
+                   choice_ref, weight_ref, grad_ref, tokens_ref, down_ref, sems):
     half = grad_ref.shape[1] // 2
     rank = down_ref.shape[0]
+    pairs = [
+        (choice_hbm, choice_ref),
+        (grad_hbm.at[:, :half], grad_ref.at[:, :half]),
+        (grad_hbm.at[:, half:], grad_ref.at[:, half:]),
+        (weight_hbm, weight_ref),
+        (down_hbm, down_ref),
+        (tokens_hbm, tokens_ref),
+    ]
+    copies = [pltpu.make_async_copy(a, b, sems.at[i]) for i, (a, b) in enumerate(pairs)]
+    for copy in copies:
+        copy.start()
+    copies[0].wait()
     choice = choice_ref[...]
     upper, lower = pick_rows(choice, capacity)
-    block_ref[:, :half] = (dot(upper, grad_ref[:, :half]) + dot(lower, grad_ref[:, half:])).astype(BF)
-    low = dot(tokens_ref[...], down_ref[...], NT).astype(BF)
+    copies[1].wait()
+    first = dot(upper, grad_ref[:, :half])
+    copies[2].wait()
+    block_ref[:, :half] = (first + dot(lower, grad_ref[:, half:])).astype(BF)
+    copies[3].wait()
     weight = jnp.sum(
         jnp.where(choice == 0, weight_ref[...].astype(F32), 0.0), axis=0, keepdims=True
     )
     column = jnp.sum(upper.astype(F32) * weight, axis=1, keepdims=True)
+    block_ref[:, half + rank :] = jnp.broadcast_to(column, (2 * capacity, rank)).astype(BF)
+    copies[4].wait()
+    copies[5].wait()
+    low = dot(tokens_ref[...], down_ref[...], NT).astype(BF)
     block_ref[:, half : half + rank] = dot(upper, low).astype(BF)
-    block_ref[:, half + rank :] = jnp.broadcast_to(column, (2 * capacity, rank)).astype(BF)
 
 
 def hidden_kernel(capacity, slot, count, *refs):
     blocks, (gate_ref, up_ref, down_ref, dgate_ref, dup_ref, rows) = refs[:count], refs[count:]
-    half = down_ref.shape[1] // 2
+    hidden, width = down_ref.shape
+    half = width // 2
     rank = (blocks[0].shape[1] - half) // 2
     tall = rows.shape[0] // count
-
-    @pl.when(pl.program_id(0) == 0)
-    def _():
+    for i, block in enumerate(blocks):
+        rows[i * tall : i * tall + 2 * capacity, :] = block[:, :half]
+    step = TILE if hidden % TILE == 0 else hidden
+    live = lax.broadcasted_iota(jnp.int32, (slot, step), 0) < capacity
+    for t in range(0, hidden, step):
+        first = dot(rows[...], down_ref[t : t + step, :half], NT)
+        second = dot(rows[...], down_ref[t : t + step, half:], NT)
         for i, block in enumerate(blocks):
-            rows[i * tall : i * tall + 2 * capacity, :] = block[:, :half]
-
-    first = dot(rows[...], down_ref[:, :half], NT)
-    second = dot(rows[...], down_ref[:, half:], NT)
-    live = lax.broadcasted_iota(jnp.int32, (slot, first.shape[1]), 0) < capacity
-    for i, block in enumerate(blocks):
-        at = i * tall
-        weight = block[:, half:].astype(F32)[:slot, rank : rank + 1]
-        grad = (first[at : at + slot] + second[at + capacity : at + capacity + slot]) * weight
-        grad = jnp.where(live, grad, 0.0)
-        gate = gate_ref[i].astype(F32)
-        up = up_ref[i].astype(F32)
-        sig = 1.0 / (1.0 + jnp.exp(-gate))
-        dgate_ref[i] = (grad * up * (sig * (1.0 + gate * (1.0 - sig)))).astype(BF)
-        dup_ref[i] = (grad * gate * sig).astype(BF)
+            at = i * tall
+            weight = block[:, half:].astype(F32)[:slot, rank : rank + 1]
+            grad = (first[at : at + slot] + second[at + capacity : at + capacity + slot]) * weight
+            grad = jnp.where(live, grad, 0.0)
+            gate = gate_ref[i, :, t : t + step].astype(F32)
+            up = up_ref[i, :, t : t + step].astype(F32)
+            sig = 1.0 / (1.0 + jnp.exp(-gate))
+            slope = sig * (1.0 + gate * (1.0 - sig))
+            dgate_ref[i, :, t : t + step] = (grad * up * slope).astype(BF)
+            dup_ref[i, :, t : t + step] = (grad * gate * sig).astype(BF)
+
+
+def stack(groups, slot, sources, target):
+    at = 0
+    for size, source in zip(groups, sources):
+        for i in range(size):
+            target[at : at + slot, :] = source[i]
+            at += slot
+
+
+def low_kernel(slot, groups, *refs):
+    members, pieces = sum(groups), len(groups)
+    dgates, dups, extras = refs[:pieces], refs[pieces : 2 * pieces], refs[2 * pieces : 2 * pieces + members]
+    lora_gate, lora_up, low_out, lora_out, dgate, dup, low = refs[2 * pieces + members :]
+    rank = lora_gate.shape[0]
+    stack(groups, slot, dgates, dgate)
+    stack(groups, slot, dups, dup)
+    for i, extra in enumerate(extras):
+        low[i * slot : (i + 1) * slot, :] = extra[:slot, :rank]
+    low_out[...] = SCALE * (dot(dgate[...], lora_gate[...], NT) + dot(dup[...], lora_up[...], NT))
+    lora_out[:rank, :] = (SCALE * dot(low[...], dgate[...], TN)).astype(BF)
+    lora_out[rank:, :] = (SCALE * dot(low[...], dup[...], TN)).astype(BF)
 
 
 def partial_kernel(capacity, slot, groups, cut, *refs):
-    members = sum(groups)
-    pieces = len(groups)
-    dgates, refs = refs[:pieces], refs[pieces:]
-    dups, refs = refs[:pieces], refs[pieces:]
-    extras, refs = refs[:members], refs[members:]
-    (gate_a, gate_b, up_a, up_b, lora_gate, lora_up), refs = refs[:6], refs[6:]
-    outs, refs = refs[: members + 1], refs[members + 1 :]
-    low_out, lora_out, dgate, dup, low, tile = refs
-    rank = lora_gate.shape[0]
-
-    @pl.when(pl.program_id(0) == 0)
-    def _():
-        at = 0
-        for size, dgate_ref, dup_ref in zip(groups, dgates, dups):
-            for i in range(size):
-                dgate[at : at + slot, :] = dgate_ref[i]
-                dup[at : at + slot, :] = dup_ref[i]
-                low[at : at + slot, :] = extras[at // slot][:slot, :rank]
-                at += slot
-        low_out[...] = SCALE * (dot(dgate[...], lora_gate[...], NT) + dot(dup[...], lora_up[...], NT))
-        lora_out[:rank, :] = (SCALE * dot(low[...], dgate[...], TN)).astype(BF)
-        lora_out[rank:, :] = (SCALE * dot(low[...], dup[...], TN)).astype(BF)
-
-    first = dot(dgate[...], gate_a[...], NT) + dot(dup[...], up_a[...], NT)
-    second = dot(dgate[...], gate_b[...], NT) + dot(dup[...], up_b[...], NT)
-    for i in range(members):
-        at = i * slot
-        tile[:capacity, :] = first[at : at + capacity]
-        tile[capacity:, :] = second[at : at + capacity]
-        if i < members - 1:
-            outs[i][...] = tile[...].astype(BF)
-        else:
-            outs[i][...] = tile[:cut, :].astype(BF)
-            outs[i + 1][...] = tile[cut:, :].astype(BF)
+    members, pieces = sum(groups), len(groups)
+    dgates, dups, refs = refs[:pieces], refs[pieces : 2 * pieces], refs[2 * pieces :]
+    gate_ref, up_ref, outs, (dgate, dup, tile) = refs[0], refs[1], refs[2:-3], refs[-3:]
+    half = gate_ref.shape[0] // 2
+    stack(groups, slot, dgates, dgate)
+    stack(groups, slot, dups, dup)
+
+    for t in range(0, half, TILE):
+        sums = []
+        for at in (t, t + half):
+            sums.append(
+                dot(dgate[...], gate_ref[at : at + TILE, :], NT)
+                + dot(dup[...], up_ref[at : at + TILE, :], NT)
+            )
+        for i in range(members):
+            at = i * slot
+            tile[:capacity, :] = sums[0][at : at + capacity]
+            tile[capacity:, :] = sums[1][at : at + capacity]
+            if cut:
+                outs[0][:, t : t + TILE] = tile[:cut, :].astype(BF)
+                outs[1][:, t : t + TILE] = tile[cut:, :].astype(BF)
+            else:
+                outs[i][:, t : t + TILE] = tile[...].astype(BF)
 
 
 def adapter_kernel(capacity, owner_ref, choice_ref, low_ref, tokens_ref, out_ref):
@@ -150,6 +181,14 @@
     total = total.astype(BF)
     out_ref[:, :half] = dot(upper, total, TN).astype(BF)
     out_ref[:, half:] = dot(lower, total, TN).astype(BF)
+
+
+def in_hbm(x):
+    return pltpu.with_memory_space_constraint(x, pltpu.HBM)
+
+
+def in_vmem(x):
+    return pltpu.with_memory_space_constraint(x, pltpu.VMEM)
 
 
 def params():
@@ -209,11 +248,20 @@
 
     block = pl.pallas_call(
         functools.partial(prepare_kernel, capacity),
+        in_specs=[pl.BlockSpec(memory_space=pl.ANY)] * 5,
         out_shape=jax.ShapeDtypeStruct((2 * capacity, wide), BF),
+        scratch_shapes=[
+            pltpu.VMEM(choice.shape, choice.dtype),
+            pltpu.VMEM(weights.shape, BF),
+            pltpu.VMEM(output_gradient.shape, BF),
+            pltpu.VMEM(tokens.shape, BF),
+            pltpu.VMEM(adapter_down_factor.shape, BF),
+            pltpu.SemaphoreType.DMA((6,)),
+        ],
         compiler_params=params(),
         cost_estimate=cost(4e8, 4.5e6),
         name="prepare",
-    )(choice, weights, output_gradient, tokens, adapter_down_factor)
+    )(*[in_hbm(x) for x in (choice, weights, output_gradient, tokens, adapter_down_factor)])
 
     def in_order(stored):
         rows = stored[0].reshape(n, capacity, hidden)[owners]
@@ -235,19 +283,14 @@
         axis=0,
     )
 
-    columns = 256
+    down_here, gate_here, up_here = in_vmem(down_weight), in_vmem(gate_weight), in_vmem(up_weight)
     dgates, dups = [], []
     start = 0
     for group in passes:
         size = len(group)
         grads = jax.ShapeDtypeStruct((size, slot, hidden), BF)
-        row_spec = pl.BlockSpec((size, slot, columns), lambda i: (0, 0, i))
         dgate, dup = pl.pallas_call(
             functools.partial(hidden_kernel, capacity, slot, size),
-            grid=(hidden // columns,),
-            in_specs=[pl.BlockSpec((2 * capacity, wide), lambda i: (0, 0))] * size
-            + [row_spec, row_spec, pl.BlockSpec((columns, width), lambda i: (i, 0))],
-            out_specs=[row_spec, row_spec],
             out_shape=[grads, grads],
             scratch_shapes=[pltpu.VMEM((size * tall, half), BF)],
             compiler_params=params(),
@@ -257,29 +300,16 @@
             *[got[r] for r in group],
             gate_rows[start : start + size],
             up_rows[start : start + size],
-            down_weight,
+            down_here,
         )
         dgates.append(dgate)
         dups.append(dup)
         start += size
 
-    steps = half // columns
     sizes = [len(group) for group in passes]
-    whole = lambda shape: pl.BlockSpec(shape, lambda i: (0,) * len(shape))
-    part_a = pl.BlockSpec((columns, hidden), lambda i: (i, 0))
-    part_b = pl.BlockSpec((columns, hidden), lambda i: (i + steps, 0))
-    heights = [2 * capacity] * (n - 1) + [cut, 2 * capacity - cut]
-    results = pl.pallas_call(
-        functools.partial(partial_kernel, capacity, slot, sizes, cut),
-        grid=(steps,),
-        in_specs=[whole((s, slot, hidden)) for s in sizes] * 2
-        + [pl.BlockSpec((2 * capacity, 2 * rank), lambda i: (0, half // (2 * rank)))] * n
-        + [part_a, part_b, part_a, part_b]
-        + [whole((rank, hidden))] * 2,
-        out_specs=[pl.BlockSpec((h, columns), lambda i: (0, i)) for h in heights]
-        + [whole((n * slot, rank)), whole((2 * rank, hidden))],
-        out_shape=[jax.ShapeDtypeStruct((h, half), BF) for h in heights]
-        + [
+    low_part, lora_local = pl.pallas_call(
+        functools.partial(low_kernel, slot, sizes),
+        out_shape=[
             jax.ShapeDtypeStruct((n * slot, rank), F32),
             jax.ShapeDtypeStruct((2 * rank, hidden), BF),
         ],
@@ -287,24 +317,32 @@
             pltpu.VMEM((n * slot, hidden), BF),
             pltpu.VMEM((n * slot, hidden), BF),
             pltpu.VMEM((n * slot, rank), BF),
-            pltpu.VMEM((2 * capacity, columns), F32),
         ],
         compiler_params=params(),
-        cost_estimate=cost(4 * n * slot * width * hidden, 4 * hidden * width),
-        name="partials",
-    )(
-        *dgates,
-        *dups,
-        *[got[r] for r in order],
-        gate_weight,
-        gate_weight,
-        up_weight,
-        up_weight,
-        adapter_gate_factor,
-        adapter_up_factor,
-    )
-    own = dict(zip(order[:-1], results))
-    last_a, last_b, low_part, lora_local = results[n - 1 :]
+        cost_estimate=cost(8 * n * slot * rank * hidden, 4 * n * slot * hidden),
+        name="low_rows",
+    )(*dgates, *dups, *[got[r][:, half:] for r in order], adapter_gate_factor, adapter_up_factor)
+
+    def partials(some, heights):
+        count = sum(sizes[i] for i in some)
+        return pl.pallas_call(
+            functools.partial(
+                partial_kernel, capacity, slot, [sizes[i] for i in some], cut if len(heights) > count else 0
+            ),
+            out_shape=[jax.ShapeDtypeStruct((h, half), BF) for h in heights],
+            scratch_shapes=[
+                pltpu.VMEM((count * slot, hidden), BF),
+                pltpu.VMEM((count * slot, hidden), BF),
+                pltpu.VMEM((2 * capacity, TILE), F32),
+            ],
+            compiler_params=params(),
+            cost_estimate=cost(4 * count * slot * width * hidden, 4 * hidden * width),
+            name="partials",
+        )(*[dgates[i] for i in some], *[dups[i] for i in some], gate_here, up_here)
+
+    last_a, last_b = partials([len(passes) - 1], [cut, 2 * capacity - cut])
+    rest = list(range(len(passes) - 1))
+    own = dict(zip(order[:-1], partials(rest, [2 * capacity] * (n - 1))))
 
     def add(a, b):
         return (a.astype(F32) + b.astype(F32)).astype(BF)
@@ -312,6 +350,7 @@
     going_right = lax.ppermute(last_a, "expert", to_right)
     going_left = lax.ppermute(last_b, "expert", to_left)
 
+    low_part, going_right, going_left = lax.optimization_barrier((low_part, going_right, going_left))
     low = low_part.reshape(n, slot, rank)[paired]
     bit = 1
     while bit < n:

time: 153 us -> 140 us (0.915)
  Pallas kernels: 48 us -> 35.3 us
  other arithmetic: 4.86 us -> 8.03 us
  local copies, waits for them, and re-layouts: 17.8 us -> 16.2 us
    pallas_call x6 -> x8, Pallas kernels: 41 us -> 28.4 us  [the longest x4 12.6 us: on_device(): pl.pallas_call(functools.partial(hidden_kernel, capacity, slot, size), ou...]
    unnamed x59 -> x57, local copies, waits for them, and re-layouts: 11.3 us -> 4.69 us
    ppermute x3, waiting for transfers between devices: 17.1 us -> 14.7 us  [on_device(): rightward = lax.ppermute(rightward, 'expert', to_right)]
    ppermute x1, waiting for transfers between devices: 0.01 us -> 2.13 us  [on_device(): lax.ppermute(leftward[cut:], 'expert', to_left)]
    ppermute x3, waiting for transfers between devices: 11.3 us -> 13.2 us  [on_device(): going_right = lax.ppermute(going_right, 'expert', to_right)]
    convert_element_type x8, other arithmetic: 0.73 us -> 2.63 us  [add(): return (a.astype(F32) + b.astype(F32)).astype(BF)]
    slice x3, local copies, waits for them, and re-layouts: 0.04 us -> 1.84 us  [on_device(): gate_rows[start:start + size]]
  transfers between devices with their start and end apart: 25 -> 25, of which waited for: 15 -> 15; matrix products, arithmetic and copies ran while one was open for 5% -> 13% of each run, Pallas kernels for 16% -> 12%
where the time goes in v2:
time: 140 us; the launch traced here: 139 us
  waiting for transfers between devices  48.9 us (35%)
  Pallas kernels  35.3 us (25%)
  starting transfers between devices  29.3 us (21%)
  local copies, waits for them, and re-layouts  16.2 us (12%)
  other arithmetic  8.03 us (6%)
    ppermute x6, waiting for transfers between devices, on_device(): lax.ppermute(pairs[:, 1], 'expert', [(e, e ^ bit) for e in range(n)])  15.6 us
    ppermute x3, waiting for transfers between devices, on_device(): rightward = lax.ppermute(rightward, 'expert', to_right)  14.7 us
    ppermute x3, waiting for transfers between devices, on_device(): going_right = lax.ppermute(going_right, 'expert', to_right)  13.2 us
    pallas_call x4, Pallas kernels, on_device(): pl.pallas_call(functools.partial(hidden_kernel, capacity, slot, size), ou...  12.6 us
    pallas_call x2, Pallas kernels, partials(): pl.pallas_call(functools.partial(partial_kernel, capacity, slot, [sizes[i...  11.6 us
    ppermute x6, starting transfers between devices, on_device(): lax.ppermute(pairs[:, 1], 'expert', [(e, e ^ bit) for e in range(n)])  8.67 us
    ppermute x3, starting transfers between devices, on_device(): rightward = lax.ppermute(rightward, 'expert', to_right)  6.36 us
    ppermute x3, starting transfers between devices, on_device(): going_right = lax.ppermute(going_right, 'expert', to_right)  5.41 us
  transfers between devices with their start and end apart: 25, of which 15 were waited for; matrix products, arithmetic and copies ran while one was open for 13% of the time, Pallas kernels for 12%

profile of v2, /device:TPU:0, one launch (start us, length us, event | category | flops | bytes accessed | tf_op | source)
XLA Modules:
  0.0 139.0 jit_solution(2539615592345852403)
XLA Ops:
  0.6 2.9 %prepare.1.refs_0_ = bf16[72,3200]{1,0:T(8,128)(2,1)S(1)} custom-call(s32[4,128]{1,0:T(4,128)} %bitcast.94, bf16[4,128]{1,0:T(4,128)(2,1)} %bitcast.107, bf16[128,6144]{1,0:T(8,128)(2,1)} %bitcast.98, bf16[128,6144]{1,0:T(8,128)(2,1)} %bitcast.91, bf16[64,6144]{1,0:T(8,128)(2,1)} %down_ref.1), custom_call_target="tpu_custom_call" | custom-call | flops 400000000 | bytes 4500000 | tf_op jit(solution)/shard_map/prepare/pallas_call | solution.py:249
  3.6 3.1 %collective-permute-start = (bf16[72,3200]{1,0:T(8,128)(2,1)S(1)}, bf16[72,3200]{1,0:T(8,128)(2,1)S(1)}, u32[]{:S(2)}, u32[]{:S(2)}) collective-permute-start(bf16[72,3200]{1,0:T(8,128)(2,1)S(1)} %prepare.1.refs_0_), channel_id=1, source_target_pairs={{0,4},{4,8},{8,12},{12,14},{14,10},{10,6},{6,2},{2,0},{1,5},{5,9},... | collective-permute-start | bytes 1382408 | tf_op jit(solution)/shard_map/ppermute | solution.py:275
  10.9 6.2 %collective-permute-done.refs_1_ = bf16[72,3200]{1,0:T(8,128)(2,1)S(1)} collective-permute-done((bf16[72,3200]{1,0:T(8,128)(2,1)S(1)}, bf16[72,3200]{1,0:T(8,128)(2,1)S(1)}, u32[]{:S(2)}, u32[]{:S(2)}) %collective-permute-start) | collective-permute-done | bytes 460832 | tf_op jit(solution)/shard_map/ppermute | solution.py:275
  21.1 7.8 %collective-permute-done.2.refs_0_ = bf16[72,3200]{1,0:T(8,128)(2,1)S(1)} collective-permute-done((bf16[72,3200]{1,0:T(8,128)(2,1)S(1)}, bf16[72,3200]{1,0:T(8,128)(2,1)S(1)}, u32[]{:S(2)}, u32[]{:S(2)}) %collective-permute-start.2) | collective-permute-done | bytes 460832 | tf_op jit(solution)/shard_map/ppermute | solution.py:275
  32.6 3.7 %copy-done = bf16[768,6144]{1,0:T(8,128)(2,1)S(1)} copy-done((bf16[768,6144]{1,0:T(8,128)(2,1)S(1)}, bf16[768,6144]{1,0:T(8,128)(2,1)}, u32[]{:S(2)}) %copy-start) | copy-done | bytes 9437208
  36.3 2.7 %hidden_rows.4 = (bf16[3,40,768]{2,1,0:T(8,128)(2,1)S(1)}, bf16[3,40,768]{2,1,0:T(8,128)(2,1)S(1)}) custom-call(bf16[72,3200]{1,0:T(8,128)(2,1)S(1)} %prepare.1.refs_0_, bf16[72,3200]{1,0:T(8,128)(2,1)S(1)} %collective-permute-done.refs_1_, bf16[72,3200]{1,0:T(8,128)(2,1)S(1)} %collective-permute-done.1.refs_2_, ...), custom_call_target="tpu_custom_call" | custom-call | flops 2264924160 | bytes 9437184 | tf_op jit(solution)/shard_map/hidden_rows/pallas_call | solution.py:292
  41.1 3.4 %hidden_rows.5 = (bf16[2,40,768]{2,1,0:T(8,128)(2,1)S(1)}, bf16[2,40,768]{2,1,0:T(8,128)(2,1)S(1)}) custom-call(bf16[72,3200]{1,0:T(8,128)(2,1)S(1)} %collective-permute-done.2.refs_0_, bf16[72,3200]{1,0:T(8,128)(2,1)S(1)} %collective-permute-done.3.refs_1_, bf16[2,40,768]{2,1,0:T(8,128)(2,1)S(1)} %get-tuple-element.51.refs_2_, ...), custom_call_target="tpu_custom_call" | custom-call | flops 1509949440 | bytes 9437184 | tf_op jit(solution)/shard_map/hidden_rows/pallas_call | solution.py:292
  45.5 3.4 %hidden_rows.6 = (bf16[2,40,768]{2,1,0:T(8,128)(2,1)S(1)}, bf16[2,40,768]{2,1,0:T(8,128)(2,1)S(1)}) custom-call(bf16[72,3200]{1,0:T(8,128)(2,1)S(1)} %collective-permute-done.4.refs_0_, bf16[72,3200]{1,0:T(8,128)(2,1)S(1)} %collective-permute-done.5.refs_1_, bf16[2,40,768]{2,1,0:T(8,128)(2,1)S(1)} %get-tuple-element.50.refs_2_, ...), custom_call_target="tpu_custom_call" | custom-call | flops 1509949440 | bytes 9437184 | tf_op jit(solution)/shard_map/hidden_rows/pallas_call | solution.py:292
  49.0 2.1 %collective-permute-done.7 = bf16[40,3200]{1,0:T(8,128)(2,1)S(1)} collective-permute-done((bf16[40,3200]{1,0:T(8,128)(2,1)S(1)}, bf16[40,3200]{1,0:T(8,128)(2,1)S(1)}, u32[]{:S(2)}, u32[]{:S(2)}) %collective-permute-start.7) | collective-permute-done | bytes 256032 | tf_op jit(solution)/shard_map/ppermute | solution.py:281
  51.1 3.0 %hidden_rows.7 = (bf16[1,40,768]{2,1,0:T(8,128)(2,1)S(1)}, bf16[1,40,768]{2,1,0:T(8,128)(2,1)S(1)}) custom-call(bf16[72,3200]{1,0:T(8,128)(2,1)S(1)} %constant_dynamic-update-slice_fusion.refs_0_, bf16[1,40,768]{2,1,0:T(8,128)(2,1)S(1)} %pad_slice_fusion.4.refs_1_, bf16[1,40,768]{2,1,0:T(8,128)(2,1)S(1)} %pad_slice_fusion.refs_2_, ...), custom_call_target="tpu_custom_call" | custom-call | flops 754974720 | bytes 9437184 | tf_op jit(solution)/shard_map/hidden_rows/pallas_call | solution.py:292
  54.2 5.8 %partials.3 = (bf16[32,3072]{1,0:T(8,128)(2,1)S(1)}, bf16[40,3072]{1,0:T(8,128)(2,1)S(1)}) custom-call(bf16[1,40,768]{2,1,0:T(8,128)(2,1)S(1)} %get-tuple-element.33.refs_3_.refs_0_, bf16[1,40,768]{2,1,0:T(8,128)(2,1)S(1)} %get-tuple-element.34.refs_7_.refs_1_, bf16[6144,768]{1,0:T(8,128)(2,1)S(1)} %bitcast.88, bf16[6144,768]{1,0:T(8,128)(2,1)S(1)} %bitcast.90), custom_call_target="tpu_custom_call" | custom-call | flops 754974720 | bytes 18874368 | tf_op jit(solution)/shard_map/partials/pallas_call | solution.py:328
  62.1 5.9 %partials.2 = (bf16[72,3072]{1,0:T(8,128)(2,1)S(1)}, bf16[72,3072]{1,0:T(8,128)(2,1)S(1)}, bf16[72,3072]{1,0:T(8,128)(2,1)S(1)}, bf16[72,3072]{1,0:T(8,128)(2,1)...) custom-call(bf16[3,40,768]{2,1,0:T(8,128)(2,1)S(1)} %get-tuple-element.26.refs_0_, ...), custom_call_target="tpu_custom_call" | custom-call | flops 5284823040 | bytes 18874368 | tf_op jit(solution)/shard_map/partials/pallas_call | solution.py:328
  75.8 3.0 %collective-permute-done.16 = f32[4,40,64]{2,1,0:T(8,128)S(1)} collective-permute-done((f32[4,40,64]{2,1,0:T(8,128)S(1)}, f32[4,40,64]{2,1,0:T(8,128)S(1)}, u32[]{:S(2)}, u32[]{:S(2)}) %collective-permute-start.16) | collective-permute-done | bytes 40992 | tf_op jit(solution)/shard_map/ppermute | solution.py:358
  83.8 2.7 %collective-permute-start.18 = (f32[1,40,64]{2,1,0:T(8,128)S(1)}, f32[1,40,64]{2,1,0:T(8,128)S(1)}, u32[]{:S(2)}, u32[]{:S(2)}) collective-permute-start(f32[1,40,64]{2,1,0:T(8,128)S(1)} %slice_bitcast_fusion.10), channel_id=1, source_target_pairs={{0,8},{2,10},{4,12},{6,14},{8,0},{10,2},{12,4},{14,6},{1,9},{3,11}... | collective-permute-start | bytes 30728 | tf_op jit(solution)/shard_map/ppermute | solution.py:358
  88.6 4.9 %adapter_gradient.1 = bf16[8,64,768]{2,1,0:T(8,128)(2,1)S(1)} custom-call(s32[8]{0:T(128)S(1)} %iota_xor_fusion.owner_ref, s32[4,128]{1,0:T(4,128)S(1)} %bitcast.95, bf16[40,64]{1,0:T(8,128)(2,1)S(1)} %fusion.11.low_ref, bf16[128,6144]{1,0:T(8,128)(2,1)S(1)} %bitcast.92), custom_call_target="tpu_custom_call" | custom-call | flops 100663296 | bytes 1572864 | tf_op jit(solution)/shard_map/adapter_gradient/pallas_call | solution.py:379
  98.7 9.0 %collective-permute-done.10 = bf16[72,3072]{1,0:T(8,128)(2,1)S(1)} collective-permute-done((bf16[72,3072]{1,0:T(8,128)(2,1)S(1)}, bf16[72,3072]{1,0:T(8,128)(2,1)S(1)}, u32[]{:S(2)}, u32[]{:S(2)}) %collective-permute-start.10) | collective-permute-done | bytes 442400 | tf_op jit(solution)/shard_map/ppermute | solution.py:370
  109.0 2.9 %collective-permute-done.20 = bf16[4,32,768]{2,1,0:T(8,128)(2,1)S(1)} collective-permute-done((bf16[4,32,768]{2,1,0:T(8,128)(2,1)S(1)}, bf16[4,32,768]{2,1,0:T(8,128)(2,1)S(1)}, u32[]{:S(2)}, u32[]{:S(2)}) %collective-permute-start.20) | collective-permute-done | bytes 196640 | tf_op jit(solution)/shard_map/ppermute | solution.py:411
  112.2 2.4 %collective-permute-start.14 = (bf16[72,3072]{1,0:T(8,128)(2,1)S(1)}, bf16[72,3072]{1,0:T(8,128)(2,1)S(1)}, u32[]{:S(2)}, u32[]{:S(2)}) collective-permute-start(bf16[72,3072]{1,0:T(8,128)(2,1)S(1)} %add_convert_fusion.1), channel_id=1, source_target_pairs={{0,2},{4,0},{8,4},{12,8},{14,12},{10,14},{6,10},{2,6},{1,3},{5,1},... | collective-permute-start | bytes 1327112 | tf_op jit(solution)/shard_map/ppermute | solution.py:371
  114.6 5.9 %collective-permute-done.21 = bf16[2,32,768]{2,1,0:T(8,128)(2,1)S(1)} collective-permute-done((bf16[2,32,768]{2,1,0:T(8,128)(2,1)S(1)}, bf16[2,32,768]{2,1,0:T(8,128)(2,1)S(1)}, u32[]{:S(2)}, u32[]{:S(2)}) %collective-permute-start.21) | collective-permute-done | bytes 98336 | tf_op jit(solution)/shard_map/ppermute | solution.py:411
  120.5 2.8 %collective-permute-start.22 = (bf16[1,32,768]{2,1,0:T(8,128)(2,1)S(1)}, bf16[1,32,768]{2,1,0:T(8,128)(2,1)S(1)}, u32[]{:S(2)}, u32[]{:S(2)}) collective-permute-start(bf16[1,32,768]{2,1,0:T(8,128)(2,1)S(1)} %slice_bitcast_fusion.6), channel_id=1, source_target_pairs={{0,8},{2,10},{4,12},{6,14},{8,0},{10,2},{12,4},{14,6},{1,9},{3,11}... | collective-permute-start | bytes 147464 | tf_op jit(solution)/shard_map/ppermute | solution.py:411
  123.4 2.5 %collective-permute-start.12 = (bf16[72,3072]{1,0:T(8,128)(2,1)S(1)}, bf16[72,3072]{1,0:T(8,128)(2,1)S(1)}, u32[]{:S(2)}, u32[]{:S(2)}) collective-permute-start(bf16[72,3072]{1,0:T(8,128)(2,1)S(1)} %add_convert_fusion.2), channel_id=1, source_target_pairs={{0,4},{4,8},{8,12},{12,14},{14,10},{10,6},{6,2},{2,0},{1,5},{5,9},... | collective-permute-start | bytes 1327112 | tf_op jit(solution)/shard_map/ppermute | solution.py:370
  130.1 4.3 %collective-permute-done.12.left_ref = bf16[72,3072]{1,0:T(8,128)(2,1)S(1)} collective-permute-done((bf16[72,3072]{1,0:T(8,128)(2,1)S(1)}, bf16[72,3072]{1,0:T(8,128)(2,1)S(1)}, u32[]{:S(2)}, u32[]{:S(2)}) %collective-permute-start.12) | collective-permute-done | bytes 442400 | tf_op jit(solution)/shard_map/ppermute | solution.py:370
  134.4 2.6 %collective-permute-done.15.right_ref = bf16[72,3072]{1,0:T(8,128)(2,1)S(1)} collective-permute-done((bf16[72,3072]{1,0:T(8,128)(2,1)S(1)}, bf16[72,3072]{1,0:T(8,128)(2,1)S(1)}, u32[]{:S(2)}, u32[]{:S(2)}) %collective-permute-start.15) | collective-permute-done | bytes 442400 | tf_op jit(solution)/shard_map/ppermute | solution.py:371
  137.0 2.0 %finish.1 = bf16[128,6144]{1,0:T(8,128)(2,1)} custom-call(s32[4,128]{1,0:T(4,128)S(1)} %bitcast.96, bf16[72,3072]{1,0:T(8,128)(2,1)S(1)} %collective-permute-done.12.left_ref, bf16[72,3072]{1,0:T(8,128)(2,1)S(1)} %collective-permute-done.15.right_ref, bf16[72,3072]{1,0:T(8,128)(2,1)S(1)} %copy-done.13, bf16[40,64]{1,0:T(8,128)(2,1)S(1)} %fusion.11.low_ref, ...), custom_call_target="tpu_custom_call" | custom-call | flops 400000000 | bytes 4500000 | tf_op jit(solution)/shard_map/finish/pallas_call | solution.py:420
  (148 shorter events, 42.8 us)
Async XLA Ops:
  3.6 13.6 %collective-permute-start = (bf16[72,3200]{1,0:T(8,128)(2,1)S(1)}, bf16[72,3200]{1,0:T(8,128)(2,1)S(1)}, u32[]{:S(2)}, u32[]{:S(2)}) collective-permute-start(bf16[72,3200]{1,0:T(8,128)(2,1)S(1)} %prepare.1.refs_0_), channel_id=1, source_target_pairs={{0,4},{4,8},{8,12},{12,14},{14,10},{10,6},{6,2},{2,0},{1,5},{5,9},... | collective-permute-start | bytes 1382408 | tf_op jit(solution)/shard_map/ppermute | solution.py:275
  6.6 13.2 %collective-permute-start.1 = (bf16[72,3200]{1,0:T(8,128)(2,1)S(1)}, bf16[72,3200]{1,0:T(8,128)(2,1)S(1)}, u32[]{:S(2)}, u32[]{:S(2)}) collective-permute-start(bf16[72,3200]{1,0:T(8,128)(2,1)S(1)} %prepare.1.refs_0_), channel_id=1, source_target_pairs={{0,2},{4,0},{8,4},{12,8},{14,12},{10,14},{6,10},{2,6},{1,3},{5,1},... | collective-permute-start | bytes 1382408 | tf_op jit(solution)/shard_map/ppermute | solution.py:276
  17.1 11.7 %collective-permute-start.2 = (bf16[72,3200]{1,0:T(8,128)(2,1)S(1)}, bf16[72,3200]{1,0:T(8,128)(2,1)S(1)}, u32[]{:S(2)}, u32[]{:S(2)}) collective-permute-start(bf16[72,3200]{1,0:T(8,128)(2,1)S(1)} %collective-permute-done.refs_1_), channel_id=1, source_target_pairs={{0,4},{4,8},{8,12},{12,14},{14,10},{10,6},{6,2},{2,0},{1,5},{5,9},... | collective-permute-start | bytes 1382408 | tf_op jit(solution)/shard_map/ppermute | solution.py:275
  19.8 12.2 %collective-permute-start.3 = (bf16[72,3200]{1,0:T(8,128)(2,1)S(1)}, bf16[72,3200]{1,0:T(8,128)(2,1)S(1)}, u32[]{:S(2)}, u32[]{:S(2)}) collective-permute-start(bf16[72,3200]{1,0:T(8,128)(2,1)S(1)} %collective-permute-done.1.refs_2_), channel_id=1, source_target_pairs={{0,2},{4,0},{8,4},{12,8},{14,12},{10,14},{6,10},{2,6},{1,3},{5,1},... | collective-permute-start | bytes 1382408 | tf_op jit(solution)/shard_map/ppermute | solution.py:276
  28.9 10.8 %collective-permute-start.4 = (bf16[72,3200]{1,0:T(8,128)(2,1)S(1)}, bf16[72,3200]{1,0:T(8,128)(2,1)S(1)}, u32[]{:S(2)}, u32[]{:S(2)}) collective-permute-start(bf16[72,3200]{1,0:T(8,128)(2,1)S(1)} %collective-permute-done.2.refs_0_), channel_id=1, source_target_pairs={{0,4},{4,8},{8,12},{12,14},{14,10},{10,6},{6,2},{2,0},{1,5},{5,9},... | collective-permute-start | bytes 1382408 | tf_op jit(solution)/shard_map/ppermute | solution.py:275
  32.0 12.6 %collective-permute-start.5 = (bf16[72,3200]{1,0:T(8,128)(2,1)S(1)}, bf16[72,3200]{1,0:T(8,128)(2,1)S(1)}, u32[]{:S(2)}, u32[]{:S(2)}) collective-permute-start(bf16[72,3200]{1,0:T(8,128)(2,1)S(1)} %collective-permute-done.3.refs_1_), channel_id=1, source_target_pairs={{0,2},{4,0},{8,4},{12,8},{14,12},{10,14},{6,10},{2,6},{1,3},{5,1},... | collective-permute-start | bytes 1382408 | tf_op jit(solution)/shard_map/ppermute | solution.py:276
  39.7 9.2 %collective-permute-start.6 = (bf16[32,3200]{1,0:T(8,128)(2,1)S(1)}, bf16[32,3200]{1,0:T(8,128)(2,1)S(1)}, u32[]{:S(2)}, u32[]{:S(2)}) collective-permute-start(bf16[32,3200]{1,0:T(8,128)(2,1)S(1)} %slice.160), channel_id=1, source_target_pairs={{0,4},{4,8},{8,12},{12,14},{14,10},{10,6},{6,2},{2,0},{1,5},{5,9},... | collective-permute-start | bytes 614408 | tf_op jit(solution)/shard_map/ppermute | solution.py:280
  44.6 6.5 %collective-permute-start.7 = (bf16[40,3200]{1,0:T(8,128)(2,1)S(1)}, bf16[40,3200]{1,0:T(8,128)(2,1)S(1)}, u32[]{:S(2)}, u32[]{:S(2)}) collective-permute-start(bf16[40,3200]{1,0:T(8,128)(2,1)S(1)} %slice.161), channel_id=1, source_target_pairs={{0,2},{4,0},{8,4},{12,8},{14,12},{10,14},{6,10},{2,6},{1,3},{5,1},... | collective-permute-start | bytes 768008 | tf_op jit(solution)/shard_map/ppermute | solution.py:281
  60.0 10.9 %collective-permute-start.8 = (bf16[32,3072]{1,0:T(8,128)(2,1)S(1)}, bf16[32,3072]{1,0:T(8,128)(2,1)S(1)}, u32[]{:S(2)}, u32[]{:S(2)}) collective-permute-start(bf16[32,3072]{1,0:T(8,128)(2,1)S(1)} %get-tuple-element.36), channel_id=1, source_target_pairs={{0,4},{4,8},{8,12},{12,14},{14,10},{10,6},{6,2},{2,0},{1,5},{5,9},... | collective-permute-start | bytes 589832 | tf_op jit(solution)/shard_map/ppermute | solution.py:350
  61.7 9.3 %collective-permute-start.9 = (bf16[40,3072]{1,0:T(8,128)(2,1)S(1)}, bf16[40,3072]{1,0:T(8,128)(2,1)S(1)}, u32[]{:S(2)}, u32[]{:S(2)}) collective-permute-start(bf16[40,3072]{1,0:T(8,128)(2,1)S(1)} %get-tuple-element.37), channel_id=1, source_target_pairs={{0,2},{4,0},{8,4},{12,8},{14,12},{10,14},{6,10},{2,6},{1,3},{5,1},... | collective-permute-start | bytes 737288 | tf_op jit(solution)/shard_map/ppermute | solution.py:351
  70.9 3.8 %collective-permute-start.24 = (bf16[128,768]{1,0:T(8,128)(2,1)}, bf16[128,768]{1,0:T(8,128)(2,1)}, u32[]{:S(2)}, u32[]{:S(2)}) collective-permute-start(bf16[128,768]{1,0:T(8,128)(2,1)} %get-tuple-element.47), channel_id=1, source_target_pairs={{0,1},{1,0},{2,3},{3,2},{4,5},{5,4},{6,7},{7,6},{8,9},{9,8},{10,11... | collective-permute-start | bytes 589832 | tf_op jit(solution)/shard_map/ppermute | solution.py:407
  74.0 4.8 %collective-permute-start.16 = (f32[4,40,64]{2,1,0:T(8,128)S(1)}, f32[4,40,64]{2,1,0:T(8,128)S(1)}, u32[]{:S(2)}, u32[]{:S(2)}) collective-permute-start(f32[4,40,64]{2,1,0:T(8,128)S(1)} %slice_bitcast_fusion.4), channel_id=1, source_target_pairs={{0,2},{2,0},{4,6},{6,4},{8,10},{10,8},{12,14},{14,12},{1,3},{3,1},... | collective-permute-start | bytes 122888 | tf_op jit(solution)/shard_map/ppermute | solution.py:358
  79.8 4.1 %collective-permute-start.17 = (f32[2,40,64]{2,1,0:T(8,128)S(1)}, f32[2,40,64]{2,1,0:T(8,128)S(1)}, u32[]{:S(2)}, u32[]{:S(2)}) collective-permute-start(f32[2,40,64]{2,1,0:T(8,128)S(1)} %slice_bitcast_fusion.8), channel_id=1, source_target_pairs={{0,4},{2,6},{4,0},{6,2},{8,12},{10,14},{12,8},{14,10},{1,5},{3,7},... | collective-permute-start | bytes 61448 | tf_op jit(solution)/shard_map/ppermute | solution.py:358
  83.8 4.7 %collective-permute-start.18 = (f32[1,40,64]{2,1,0:T(8,128)S(1)}, f32[1,40,64]{2,1,0:T(8,128)S(1)}, u32[]{:S(2)}, u32[]{:S(2)}) collective-permute-start(f32[1,40,64]{2,1,0:T(8,128)S(1)} %slice_bitcast_fusion.10), channel_id=1, source_target_pairs={{0,8},{2,10},{4,12},{6,14},{8,0},{10,2},{12,4},{14,6},{1,9},{3,11}... | collective-permute-start | bytes 30728 | tf_op jit(solution)/shard_map/ppermute | solution.py:358
  93.6 4.1 %collective-permute-start.19 = (bf16[8,32,768]{2,1,0:T(8,128)(2,1)S(1)}, bf16[8,32,768]{2,1,0:T(8,128)(2,1)S(1)}, u32[]{:S(2)}, u32[]{:S(2)}) collective-permute-start(bf16[8,32,768]{2,1,0:T(8,128)(2,1)S(1)} %broadcast_select_fusion), channel_id=1, source_target_pairs={{0,1},{1,0},{2,3},{3,2},{4,5},{5,4},{6,7},{7,6},{8,9},{9,8},{10,11... | collective-permute-start | bytes 1179656 | tf_op jit(solution)/shard_map/ppermute | solution.py:406
  94.7 13.0 %collective-permute-start.10 = (bf16[72,3072]{1,0:T(8,128)(2,1)S(1)}, bf16[72,3072]{1,0:T(8,128)(2,1)S(1)}, u32[]{:S(2)}, u32[]{:S(2)}) collective-permute-start(bf16[72,3072]{1,0:T(8,128)(2,1)S(1)} %pad_maximum_fusion), channel_id=1, source_target_pairs={{0,4},{4,8},{8,12},{12,14},{14,10},{10,6},{6,2},{2,0},{1,5},{5,9},... | collective-permute-start | bytes 1327112 | tf_op jit(solution)/shard_map/ppermute | solution.py:370
  97.3 14.8 %collective-permute-start.13 = (bf16[72,3072]{1,0:T(8,128)(2,1)S(1)}, bf16[72,3072]{1,0:T(8,128)(2,1)S(1)}, u32[]{:S(2)}, u32[]{:S(2)}) collective-permute-start(bf16[72,3072]{1,0:T(8,128)(2,1)S(1)} %pad_maximum_fusion.1), channel_id=1, source_target_pairs={{0,2},{4,0},{8,4},{12,8},{14,12},{10,14},{6,10},{2,6},{1,3},{5,1},... | collective-permute-start | bytes 1327112 | tf_op jit(solution)/shard_map/ppermute | solution.py:371
  97.9 14.0 %collective-permute-start.20 = (bf16[4,32,768]{2,1,0:T(8,128)(2,1)S(1)}, bf16[4,32,768]{2,1,0:T(8,128)(2,1)S(1)}, u32[]{:S(2)}, u32[]{:S(2)}) collective-permute-start(bf16[4,32,768]{2,1,0:T(8,128)(2,1)S(1)} %slice_bitcast_fusion), channel_id=1, source_target_pairs={{0,2},{2,0},{4,6},{6,4},{8,10},{10,8},{12,14},{14,12},{1,3},{3,1},... | collective-permute-start | bytes 589832 | tf_op jit(solution)/shard_map/ppermute | solution.py:411
  107.8 15.5 %collective-permute-start.11 = (bf16[72,3072]{1,0:T(8,128)(2,1)S(1)}, bf16[72,3072]{1,0:T(8,128)(2,1)S(1)}, u32[]{:S(2)}, u32[]{:S(2)}) collective-permute-start(bf16[72,3072]{1,0:T(8,128)(2,1)S(1)} %add_convert_fusion.3), channel_id=1, source_target_pairs={{0,4},{4,8},{8,12},{12,14},{14,10},{10,6},{6,2},{2,0},{1,5},{5,9},... | collective-permute-start | bytes 1327112 | tf_op jit(solution)/shard_map/ppermute | solution.py:370
  112.0 8.5 %collective-permute-start.21 = (bf16[2,32,768]{2,1,0:T(8,128)(2,1)S(1)}, bf16[2,32,768]{2,1,0:T(8,128)(2,1)S(1)}, u32[]{:S(2)}, u32[]{:S(2)}) collective-permute-start(bf16[2,32,768]{2,1,0:T(8,128)(2,1)S(1)} %slice_bitcast_fusion.2), channel_id=1, source_target_pairs={{0,4},{2,6},{4,0},{6,2},{8,12},{10,14},{12,8},{14,10},{1,5},{3,7},... | collective-permute-start | bytes 294920 | tf_op jit(solution)/shard_map/ppermute | solution.py:411
  112.2 13.8 %collective-permute-start.14 = (bf16[72,3072]{1,0:T(8,128)(2,1)S(1)}, bf16[72,3072]{1,0:T(8,128)(2,1)S(1)}, u32[]{:S(2)}, u32[]{:S(2)}) collective-permute-start(bf16[72,3072]{1,0:T(8,128)(2,1)S(1)} %add_convert_fusion.1), channel_id=1, source_target_pairs={{0,2},{4,0},{8,4},{12,8},{14,12},{10,14},{6,10},{2,6},{1,3},{5,1},... | collective-permute-start | bytes 1327112 | tf_op jit(solution)/shard_map/ppermute | solution.py:371
  120.5 7.6 %collective-permute-start.22 = (bf16[1,32,768]{2,1,0:T(8,128)(2,1)S(1)}, bf16[1,32,768]{2,1,0:T(8,128)(2,1)S(1)}, u32[]{:S(2)}, u32[]{:S(2)}) collective-permute-start(bf16[1,32,768]{2,1,0:T(8,128)(2,1)S(1)} %slice_bitcast_fusion.6), channel_id=1, source_target_pairs={{0,8},{2,10},{4,12},{6,14},{8,0},{10,2},{12,4},{14,6},{1,9},{3,11}... | collective-permute-start | bytes 147464 | tf_op jit(solution)/shard_map/ppermute | solution.py:411
  123.4 11.0 %collective-permute-start.12 = (bf16[72,3072]{1,0:T(8,128)(2,1)S(1)}, bf16[72,3072]{1,0:T(8,128)(2,1)S(1)}, u32[]{:S(2)}, u32[]{:S(2)}) collective-permute-start(bf16[72,3072]{1,0:T(8,128)(2,1)S(1)} %add_convert_fusion.2), channel_id=1, source_target_pairs={{0,4},{4,8},{8,12},{12,14},{14,10},{10,6},{6,2},{2,0},{1,5},{5,9},... | collective-permute-start | bytes 1327112 | tf_op jit(solution)/shard_map/ppermute | solution.py:370
  126.1 10.8 %collective-permute-start.15 = (bf16[72,3072]{1,0:T(8,128)(2,1)S(1)}, bf16[72,3072]{1,0:T(8,128)(2,1)S(1)}, u32[]{:S(2)}, u32[]{:S(2)}) collective-permute-start(bf16[72,3072]{1,0:T(8,128)(2,1)S(1)} %add_convert_fusion), channel_id=1, source_target_pairs={{0,2},{4,0},{8,4},{12,8},{14,12},{10,14},{6,10},{2,6},{1,3},{5,1},... | collective-permute-start | bytes 1327112 | tf_op jit(solution)/shard_map/ppermute | solution.py:371
  (29 other events, 480.1 us)

commit v3 on v2

--- a/solution.py
+++ b/solution.py
@@ -86,10 +86,12 @@
 
 
 def hidden_kernel(capacity, slot, count, *refs):
-    blocks, (gate_ref, up_ref, down_ref, dgate_ref, dup_ref, rows) = refs[:count], refs[count:]
+    blocks, refs = refs[:count], refs[count:]
+    (gate_ref, up_ref, down_ref, lora_gate, lora_up, dgate_ref, dup_ref), refs = refs[:7], refs[7:]
+    lows, rows = refs[:count], refs[count]
     hidden, width = down_ref.shape
     half = width // 2
-    rank = (blocks[0].shape[1] - half) // 2
+    rank = lora_gate.shape[0]
     tall = rows.shape[0] // count
     for i, block in enumerate(blocks):
         rows[i * tall : i * tall + 2 * capacity, :] = block[:, :half]
@@ -109,6 +111,8 @@
             slope = sig * (1.0 + gate * (1.0 - sig))
             dgate_ref[i, :, t : t + step] = (grad * up * slope).astype(BF)
             dup_ref[i, :, t : t + step] = (grad * gate * sig).astype(BF)
+    for i in range(count):
+        lows[i][...] = SCALE * (dot(dgate_ref[i], lora_gate[...], NT) + dot(dup_ref[i], lora_up[...], NT))
 
 
 def stack(groups, slot, sources, target):
@@ -119,16 +123,15 @@
             at += slot
 
 
-def low_kernel(slot, groups, *refs):
+def lora_kernel(slot, groups, *refs):
     members, pieces = sum(groups), len(groups)
     dgates, dups, extras = refs[:pieces], refs[pieces : 2 * pieces], refs[2 * pieces : 2 * pieces + members]
-    lora_gate, lora_up, low_out, lora_out, dgate, dup, low = refs[2 * pieces + members :]
-    rank = lora_gate.shape[0]
+    lora_out, dgate, dup, low = refs[2 * pieces + members :]
+    rank = lora_out.shape[0] // 2
     stack(groups, slot, dgates, dgate)
     stack(groups, slot, dups, dup)
     for i, extra in enumerate(extras):
         low[i * slot : (i + 1) * slot, :] = extra[:slot, :rank]
-    low_out[...] = SCALE * (dot(dgate[...], lora_gate[...], NT) + dot(dup[...], lora_up[...], NT))
     lora_out[:rank, :] = (SCALE * dot(low[...], dgate[...], TN)).astype(BF)
     lora_out[rank:, :] = (SCALE * dot(low[...], dup[...], TN)).astype(BF)
 
@@ -159,10 +162,29 @@
                 outs[i][:, t : t + TILE] = tile[...].astype(BF)
 
 
-def adapter_kernel(capacity, owner_ref, choice_ref, low_ref, tokens_ref, out_ref):
+def merge_kernel(cut, upper, part_ref, own_ref, out_ref):
+    span, other = (slice(0, cut), slice(cut, None)) if upper else (slice(cut, None), slice(0, cut))
+    out_ref[span, :] = (part_ref[...].astype(F32) + own_ref[span, :].astype(F32)).astype(BF)
+    out_ref[other, :] = own_ref[other, :]
+
+
+def adapter_kernel(capacity, count, where_ref, choice_ref, tokens_ref, *refs):
+    lows, (low_ref, keep_ref, send_ref) = refs[:count], refs[count:]
+    share = keep_ref.shape[2]
+    part = keep_ref.shape[1]
+    low = lows[0][...]
+    for other in lows[1:]:
+        low = low + other[...]
+    low = low.astype(BF)
+    low_ref[...] = low
     upper, _ = pick_rows(choice_ref[...], capacity)
-    low = dot(upper[: low_ref.shape[0]], low_ref[...], TN).astype(BF)
-    out_ref[0] = dot(low, tokens_ref[...], TN).astype(BF)
+    low = dot(upper[: low.shape[0]], low, TN).astype(BF)
+    core = where_ref[count]
+    for i in range(count):
+        columns = pl.ds(pl.multiple_of(where_ref[i] * share, 128), share)
+        down = dot(low, tokens_ref[:, columns], TN)
+        keep_ref[i] = jnp.where(core == 0, down[:part], down[part:]).astype(BF)
+        send_ref[i] = jnp.where(core == 0, down[part:], down[:part]).astype(BF)
 
 
 def finish_kernel(capacity, choice_ref, left_ref, right_ref, own_ref, low_ref, down_ref, out_ref, low_tall):
@@ -236,16 +258,11 @@
         place[e] = i
     to_right = [(ring[i], ring[(i + 1) % n]) for i in range(n)]
     to_left = [(ring[i], ring[(i - 1) % n]) for i in range(n)]
-    passes = [[0, -1, 1]] + [[-s, s] for s in range(2, middle)] + [[middle]]
+    passes = [[0]] + [[-s, s] for s in range(1, middle)] + [[middle]]
     order = [r for group in passes for r in group]
     owners = jnp.array(
         [[ring[(place[e] + r) % n] for r in order] for e in range(n)], jnp.int32
     )[me]
-    paired = jnp.array(
-        [[[(place[e ^ x] - place[e] - r) % n for r in order].index(0) for x in range(n)] for e in range(n)],
-        jnp.int32,
-    )[me]
-
     block = pl.pallas_call(
         functools.partial(prepare_kernel, capacity),
         in_specs=[pl.BlockSpec(memory_space=pl.ANY)] * 5,
@@ -269,29 +286,16 @@
 
     gate_rows, up_rows = in_order(stored_gate_rows), in_order(stored_up_rows)
 
+    down_here, gate_here, up_here = in_vmem(down_weight), in_vmem(gate_weight), in_vmem(up_weight)
+    dgates, dups, lows = [], [], []
     got = {0: block}
-    rightward = leftward = block
-    for s in range(1, middle):
-        rightward = lax.ppermute(rightward, "expert", to_right)
-        leftward = lax.ppermute(leftward, "expert", to_left)
-        got[-s], got[s] = rightward, leftward
-    got[middle] = jnp.concatenate(
-        [
-            lax.ppermute(rightward[:cut], "expert", to_right),
-            lax.ppermute(leftward[cut:], "expert", to_left),
-        ],
-        axis=0,
-    )
-
-    down_here, gate_here, up_here = in_vmem(down_weight), in_vmem(gate_weight), in_vmem(up_weight)
-    dgates, dups = [], []
-    start = 0
-    for group in passes:
-        size = len(group)
+
+    def hidden_pass(group):
+        size, start = len(group), len(lows)
         grads = jax.ShapeDtypeStruct((size, slot, hidden), BF)
-        dgate, dup = pl.pallas_call(
+        results = pl.pallas_call(
             functools.partial(hidden_kernel, capacity, slot, size),
-            out_shape=[grads, grads],
+            out_shape=[grads, grads] + [jax.ShapeDtypeStruct((slot, rank), F32)] * size,
             scratch_shapes=[pltpu.VMEM((size * tall, half), BF)],
             compiler_params=params(),
             cost_estimate=cost(2 * size * tall * width * hidden, 2 * hidden * width),
@@ -301,28 +305,35 @@
             gate_rows[start : start + size],
             up_rows[start : start + size],
             down_here,
+            adapter_gate_factor,
+            adapter_up_factor,
         )
-        dgates.append(dgate)
-        dups.append(dup)
-        start += size
+        dgates.append(results[0])
+        dups.append(results[1])
+        for r, low in zip(group, results[2:]):
+            pairs = [(ring[i], ring[(i + r) % n]) for i in range(n)]
+            lows.append(lax.ppermute(low, "expert", pairs) if r else low)
+
+    rightward = leftward = block
+    for s in range(1, middle + 1):
+        if s < middle:
+            rightward = lax.ppermute(rightward, "expert", to_right)
+            leftward = lax.ppermute(leftward, "expert", to_left)
+        else:
+            rightward = lax.ppermute(rightward[:cut], "expert", to_right)
+            leftward = lax.ppermute(leftward[cut:], "expert", to_left)
+        arrived = list(lows)
+        hidden_pass(passes[s - 1])
+        rightward, leftward, dgates[-1], dups[-1], arrived = lax.optimization_barrier(
+            (rightward, leftward, dgates[-1], dups[-1], arrived)
+        )
+        lows[: len(arrived)] = arrived
+        if s < middle:
+            got[-s], got[s] = rightward, leftward
+    got[middle] = jnp.concatenate([rightward, leftward], axis=0)
+    hidden_pass(passes[-1])
 
     sizes = [len(group) for group in passes]
-    low_part, lora_local = pl.pallas_call(
-        functools.partial(low_kernel, slot, sizes),
-        out_shape=[
-            jax.ShapeDtypeStruct((n * slot, rank), F32),
-            jax.ShapeDtypeStruct((2 * rank, hidden), BF),
-        ],
-        scratch_shapes=[
-            pltpu.VMEM((n * slot, hidden), BF),
-            pltpu.VMEM((n * slot, hidden), BF),
-            pltpu.VMEM((n * slot, rank), BF),
-        ],
-        compiler_params=params(),
-        cost_estimate=cost(8 * n * slot * rank * hidden, 4 * n * slot * hidden),
-        name="low_rows",
-    )(*dgates, *dups, *[got[r][:, half:] for r in order], adapter_gate_factor, adapter_up_factor)
-
     def partials(some, heights):
         count = sum(sizes[i] for i in some)
         return pl.pallas_call(
@@ -342,7 +353,7 @@
 
     last_a, last_b = partials([len(passes) - 1], [cut, 2 * capacity - cut])
     rest = list(range(len(passes) - 1))
-    own = dict(zip(order[:-1], partials(rest, [2 * capacity] * (n - 1))))
+    own = partials(rest, [2 * capacity] * (n - 1))
 
     def add(a, b):
         return (a.astype(F32) + b.astype(F32)).astype(BF)
@@ -350,22 +361,21 @@
     going_right = lax.ppermute(last_a, "expert", to_right)
     going_left = lax.ppermute(last_b, "expert", to_left)
 
-    low_part, going_right, going_left = lax.optimization_barrier((low_part, going_right, going_left))
-    low = low_part.reshape(n, slot, rank)[paired]
-    bit = 1
-    while bit < n:
-        pairs = low.reshape(low.shape[0] // 2, 2, slot, rank)
-        other = lax.ppermute(pairs[:, 1], "expert", [(e, e ^ bit) for e in range(n)])
-        low = pairs[:, 0] + other
-        bit *= 2
-    low = low[0].astype(BF)
-
-    own_right = own[middle - 1]
-    own_left = own[-(middle - 1)]
-    going_right = jnp.concatenate(
-        [add(own_right[:cut], going_right), own_right[cut:]], axis=0
-    )
-    going_left = jnp.concatenate([own_left[:cut], add(own_left[cut:], going_left)], axis=0)
+
+    going_right, going_left, own = lax.optimization_barrier((going_right, going_left, own))
+    own = dict(zip(order[:-1], own))
+
+    def merge(upper, part, mine):
+        return pl.pallas_call(
+            functools.partial(merge_kernel, cut, upper),
+            out_shape=jax.ShapeDtypeStruct(mine.shape, BF),
+            compiler_params=params(),
+            cost_estimate=cost(mine.size, 6 * mine.size),
+            name="first_add",
+        )(part, mine)
+
+    going_right = merge(True, going_right, own[middle - 1])
+    going_left = merge(False, going_left, own[-(middle - 1)])
     for s in range(middle - 1, 0, -1):
         going_right = lax.ppermute(going_right, "expert", to_right)
         going_left = lax.ppermute(going_left, "expert", to_left)
@@ -374,36 +384,44 @@
             going_left = add(going_left, own[-(s - 1)])
 
     share = width // n
+    part = rank // 2
     columns_of = jnp.arange(n, dtype=jnp.int32) ^ me
     if share % 128 == 0:
-        down = pl.pallas_call(
-            functools.partial(adapter_kernel, capacity),
-            grid_spec=pltpu.PrefetchScalarGridSpec(
-                num_scalar_prefetch=1,
-                grid=(n,),
-                in_specs=[
-                    pl.BlockSpec(choice.shape, lambda i, o: (0, 0)),
-                    pl.BlockSpec((slot, rank), lambda i, o: (0, 0)),
-                    pl.BlockSpec((own_count, share), lambda i, o: (0, o[i])),
-                ],
-                out_specs=pl.BlockSpec((1, rank, share), lambda i, o: (i, 0, 0)),
-            ),
-            out_shape=jax.ShapeDtypeStruct((n, rank, share), BF),
+        split = jax.ShapeDtypeStruct((n, part, share), BF)
+        whole = pl.BlockSpec(memory_space=pltpu.VMEM)
+        low, keep, send = pl.pallas_call(
+            functools.partial(adapter_kernel, capacity, n),
+            in_specs=[pl.BlockSpec(memory_space=pltpu.SMEM)] + [whole] * (n + 2),
+            out_shape=[jax.ShapeDtypeStruct((slot, rank), BF), split, split],
             compiler_params=params(),
             cost_estimate=cost(2 * own_count * rank * width, 2 * own_count * width),
             name="adapter_gradient",
-        )(columns_of, choice, low, tokens)
+        )(jnp.append(columns_of, core), choice, tokens, *lows)
     else:
         upper, _ = pick_rows(choice, capacity)
+        low = sum(lows).astype(BF)
         low_tokens = dot(upper[:slot], low, TN).astype(BF)
         down = dot(low_tokens, tokens, TN).astype(BF).reshape(rank, n, share)
         down = down.transpose(1, 0, 2)[columns_of]
+        keep = jnp.where(core == 0, down[:, :part], down[:, part:])
+        send = jnp.where(core == 0, down[:, part:], down[:, :part])
 
     swap = [(0, 1), (1, 0)]
-    part = rank // 2
-    keep = jnp.where(core == 0, down[:, :part], down[:, part:])
-    send = jnp.where(core == 0, down[:, part:], down[:, :part])
     down = add(keep, lax.ppermute(send, "dp", swap))
+    extras, _ = lax.optimization_barrier(([got[r][:, half:] for r in order], down))
+    lora_local = pl.pallas_call(
+        functools.partial(lora_kernel, slot, sizes),
+        out_shape=jax.ShapeDtypeStruct((2 * rank, hidden), BF),
+        scratch_shapes=[
+            pltpu.VMEM((n * slot, hidden), BF),
+            pltpu.VMEM((n * slot, hidden), BF),
+            pltpu.VMEM((n * slot, rank), BF),
+        ],
+        compiler_params=params(),
+        cost_estimate=cost(4 * n * slot * rank * hidden, 4 * n * slot * hidden),
+        name="lora_rows",
+    )(*dgates, *dups, *extras)
+
     lora = lora_local.astype(F32) + lax.ppermute(lora_local, "dp", swap).astype(F32)
     bit = 1
     while bit < n:

time: 140 us -> 144 us (1.029)
  local copies, waits for them, and re-layouts: 16.2 us -> 32.6 us
  waiting for transfers between devices: 48.9 us -> 38.8 us
  other arithmetic: 8.03 us -> 3.11 us
  starting transfers between devices: 29.3 us -> 32.1 us
    ppermute x3, waiting for transfers between devices: 2.71 us -> 21.3 us  [on_device(): going_left = lax.ppermute(going_left, 'expert', to_left)]
    unnamed x57 -> x91, local copies, waits for them, and re-layouts: 4.69 us -> 21 us
    ppermute x6 -> x3, waiting for transfers between devices: 15.6 us -> 0.1 us  [on_device(): lax.ppermute(pairs[:, 1], 'expert', [(e, e ^ bit) for e in range(n)])]
    ppermute x2 -> x9, starting transfers between devices: 2.32 us -> 13.4 us  [the longest x7 11.4 us: hidden_pass(): lows.append(lax.ppermute(low, 'expert', pairs) if r else low)]
    ppermute x3, waiting for transfers between devices: 13.2 us -> 2.37 us  [on_device(): going_right = lax.ppermute(going_right, 'expert', to_right)]
    ppermute x3, waiting for transfers between devices: 14.7 us -> 4.81 us  [on_device(): rightward = lax.ppermute(rightward, 'expert', to_right)]
    ppermute x6 -> x3, starting transfers between devices: 8.67 us -> 2.63 us  [on_device(): lax.ppermute(pairs[:, 1], 'expert', [(e, e ^ bit) for e in range(n)])]
    ppermute x2 -> x9, waiting for transfers between devices: 2.14 us -> 7.42 us  [the longest x7 7.41 us: hidden_pass(): lows.append(lax.ppermute(low, 'expert', pairs) if r else low)]
  transfers between devices with their start and end apart: 25 -> 29, of which waited for: 15 -> 11; matrix products, arithmetic and copies ran while one was open for 13% -> 10% of each run, Pallas kernels for 12% -> 20%
where the time goes in v3:
time: 144 us; the launch traced here: 143 us
  waiting for transfers between devices  38.8 us (27%)
  Pallas kernels  35.7 us (25%)
  local copies, waits for them, and re-layouts  32.6 us (23%)
  starting transfers between devices  32.1 us (22%)
  other arithmetic  3.11 us (2%)
    ppermute x3, waiting for transfers between devices, on_device(): going_left = lax.ppermute(going_left, 'expert', to_left)  21.3 us
    unnamed x91, local copies, waits for them, and re-layouts  21 us
    pallas_call x5, Pallas kernels, hidden_pass(): pl.pallas_call(functools.partial(hidden_kernel, capacity, slot, size), ou...  16.7 us
    pallas_call x2, Pallas kernels, partials(): pl.pallas_call(functools.partial(partial_kernel, capacity, slot, [sizes[i...  11.5 us
    ppermute x7, starting transfers between devices, hidden_pass(): lows.append(lax.ppermute(low, 'expert', pairs) if r else low)  11.4 us
    ppermute x7, waiting for transfers between devices, hidden_pass(): lows.append(lax.ppermute(low, 'expert', pairs) if r else low)  7.41 us
    ppermute x3, waiting for transfers between devices, on_device(): rightward = lax.ppermute(rightward, 'expert', to_right)  4.81 us
    ppermute x3, starting transfers between devices, on_device(): going_left = lax.ppermute(going_left, 'expert', to_left)  4.59 us
  transfers between devices with their start and end apart: 29, of which 11 were waited for; matrix products, arithmetic and copies ran while one was open for 10% of the time, Pallas kernels for 20%

profile of v3, /device:TPU:0, one launch (start us, length us, event | category | flops | bytes accessed | tf_op | source)
XLA Modules:
  0.0 143.5 jit_solution(12989646498075771621)
XLA Ops:
  0.7 2.9 %prepare.1.refs_0_ = bf16[72,3200]{1,0:T(8,128)(2,1)S(1)} custom-call(s32[4,128]{1,0:T(4,128)} %bitcast.51, bf16[4,128]{1,0:T(4,128)(2,1)} %bitcast.60, bf16[128,6144]{1,0:T(8,128)(2,1)} %bitcast.55, bf16[128,6144]{1,0:T(8,128)(2,1)} %bitcast.49, bf16[64,6144]{1,0:T(8,128)(2,1)} %down_ref.1), custom_call_target="tpu_custom_call" | custom-call | flops 400000000 | bytes 4500000 | tf_op jit(solution)/shard_map/prepare/pallas_call | solution.py:266
  3.6 3.0 %collective-permute-start.1 = (bf16[72,3200]{1,0:T(8,128)(2,1)S(1)}, bf16[72,3200]{1,0:T(8,128)(2,1)S(1)}, u32[]{:S(2)}, u32[]{:S(2)}) collective-permute-start(bf16[72,3200]{1,0:T(8,128)(2,1)S(1)} %prepare.1.refs_0_), channel_id=1, source_target_pairs={{0,2},{4,0},{8,4},{12,8},{14,12},{10,14},{6,10},{2,6},{1,3},{5,1},... | collective-permute-start | bytes 1382408 | tf_op jit(solution)/shard_map/ppermute | solution.py:321
  13.4 3.7 %copy-done = bf16[768,6144]{1,0:T(8,128)(2,1)S(1)} copy-done((bf16[768,6144]{1,0:T(8,128)(2,1)S(1)}, bf16[768,6144]{1,0:T(8,128)(2,1)}, u32[]{:S(2)}) %copy-start) | copy-done | bytes 9437208
  17.1 3.2 %hidden_rows.5 = (bf16[1,40,768]{2,1,0:T(8,128)(2,1)S(1)}, bf16[1,40,768]{2,1,0:T(8,128)(2,1)S(1)}, f32[40,64]{1,0:T(8,128)S(1)}) custom-call(bf16[72,3200]{1,0:T(8,128)(2,1)S(1)} %prepare.1.refs_0_, bf16[1,40,768]{2,1,0:T(8,128)(2,1)S(1)} %get-tuple-element.160.refs_1_, bf16[1,40,768]{2,1,0:T(8,128)(2,1)S(1)} %get-tuple-element.149.refs_2_, ...), custom_call_target="tpu_custom_call" | custom-call | flops 754974720 | bytes 9437184 | tf_op jit(solution)/shard_map/hidden_rows/pallas_call | solution.py:296
  20.9 2.0 %collective-permute-start.2 = (bf16[72,3200]{1,0:T(8,128)(2,1)S(1)}, bf16[72,3200]{1,0:T(8,128)(2,1)S(1)}, u32[]{:S(2)}, u32[]{:S(2)}) collective-permute-start(bf16[72,3200]{1,0:T(8,128)(2,1)S(1)} %collective-permute-done.refs_0_), channel_id=1, source_target_pairs={{0,4},{4,8},{8,12},{12,14},{14,10},{10,6},{6,2},{2,0},{1,5},{5,9},... | collective-permute-start | bytes 1382408 | tf_op jit(solution)/shard_map/ppermute | solution.py:320
  24.1 3.4 %hidden_rows.6 = (bf16[2,40,768]{2,1,0:T(8,128)(2,1)S(1)}, bf16[2,40,768]{2,1,0:T(8,128)(2,1)S(1)}, f32[40,64]{1,0:T(8,128)S(1)}, f32[40,64]{1,0:T(8,128)S(1)}) custom-call(bf16[72,3200]{1,0:T(8,128)(2,1)S(1)} %collective-permute-done.refs_0_, bf16[72,3200]{1,0:T(8,128)(2,1)S(1)} %collective-permute-done.1.refs_1_, ...), custom_call_target="tpu_custom_call" | custom-call | flops 1509949440 | bytes 9437184 | tf_op jit(solution)/shard_map/hidden_rows/pallas_call | solution.py:296
  28.2 4.8 %collective-permute-done.2.refs_0_ = bf16[72,3200]{1,0:T(8,128)(2,1)S(1)} collective-permute-done((bf16[72,3200]{1,0:T(8,128)(2,1)S(1)}, bf16[72,3200]{1,0:T(8,128)(2,1)S(1)}, u32[]{:S(2)}, u32[]{:S(2)}) %collective-permute-start.2) | collective-permute-done | bytes 460832 | tf_op jit(solution)/shard_map/ppermute | solution.py:320
  38.5 3.4 %hidden_rows.7 = (bf16[2,40,768]{2,1,0:T(8,128)(2,1)S(1)}, bf16[2,40,768]{2,1,0:T(8,128)(2,1)S(1)}, f32[40,64]{1,0:T(8,128)S(1)}, f32[40,64]{1,0:T(8,128)S(1)}) custom-call(bf16[72,3200]{1,0:T(8,128)(2,1)S(1)} %collective-permute-done.2.refs_0_, bf16[72,3200]{1,0:T(8,128)(2,1)S(1)} %collective-permute-done.3.refs_1_, ...), custom_call_target="tpu_custom_call" | custom-call | flops 1509949440 | bytes 9437184 | tf_op jit(solution)/shard_map/hidden_rows/pallas_call | solution.py:296
  43.2 3.5 %collective-permute-done.6.refs_1_ = f32[40,64]{1,0:T(8,128)S(1)} collective-permute-done((f32[40,64]{1,0:T(8,128)S(1)}, f32[40,64]{1,0:T(8,128)S(1)}, u32[]{:S(2)}, u32[]{:S(2)}) %collective-permute-start.6) | collective-permute-done | bytes 10272 | tf_op jit(solution)/shard_map/ppermute | solution.py:315
  50.7 2.4 %collective-permute-start.11 = (f32[40,64]{1,0:T(8,128)S(1)}, f32[40,64]{1,0:T(8,128)S(1)}, u32[]{:S(2)}, u32[]{:S(2)}) collective-permute-start(f32[40,64]{1,0:T(8,128)S(1)} %get-tuple-element.98), channel_id=1, source_target_pairs={{0,8},{4,12},{8,14},{12,10},{14,6},{10,2},{6,0},{2,4},{1,9},{5,13}... | collective-permute-start | bytes 30728 | tf_op jit(solution)/shard_map/ppermute | solution.py:315
  53.1 3.7 %copy-done.2 = bf16[768,6144]{1,0:T(8,128)(2,1)S(1)} copy-done((bf16[768,6144]{1,0:T(8,128)(2,1)S(1)}, bf16[768,6144]{1,0:T(8,128)(2,1)}, u32[]{:S(2)}) %copy-start.2) | copy-done | bytes 9437208
  56.8 3.4 %hidden_rows.8 = (bf16[2,40,768]{2,1,0:T(8,128)(2,1)S(1)}, bf16[2,40,768]{2,1,0:T(8,128)(2,1)S(1)}, f32[40,64]{1,0:T(8,128)S(1)}, f32[40,64]{1,0:T(8,128)S(1)}) custom-call(bf16[72,3200]{1,0:T(8,128)(2,1)S(1)} %collective-permute-done.4.refs_0_, bf16[72,3200]{1,0:T(8,128)(2,1)S(1)} %collective-permute-done.5.refs_1_, ...), custom_call_target="tpu_custom_call" | custom-call | flops 1509949440 | bytes 9437184 | tf_op jit(solution)/shard_map/hidden_rows/pallas_call | solution.py:296
  61.7 2.4 %collective-permute-start.21 = (f32[40,64]{1,0:T(8,128)S(1)}, f32[40,64]{1,0:T(8,128)S(1)}, u32[]{:S(2)}, u32[]{:S(2)}) collective-permute-start(f32[40,64]{1,0:T(8,128)S(1)} %get-tuple-element.135), channel_id=1, source_target_pairs={{0,12},{4,14},{8,10},{12,6},{14,2},{10,0},{6,4},{2,8},{1,13},{5,15... | collective-permute-start | bytes 30728 | tf_op jit(solution)/shard_map/ppermute | solution.py:315
  65.2 3.2 %hidden_rows.9 = (bf16[1,40,768]{2,1,0:T(8,128)(2,1)S(1)}, bf16[1,40,768]{2,1,0:T(8,128)(2,1)S(1)}, f32[40,64]{1,0:T(8,128)S(1)}) custom-call(bf16[72,3200]{1,0:T(8,128)(2,1)S(1)} %constant_dynamic-update-slice_fusion.refs_0_, bf16[1,40,768]{2,1,0:T(8,128)(2,1)S(1)} %copy-done.27, bf16[1,40,768]{2,1,0:T(8,128)(2,1)S(1)} %copy-done.26, ...), custom_call_target="tpu_custom_call" | custom-call | flops 754974720 | bytes 9437184 | tf_op jit(solution)/shard_map/hidden_rows/pallas_call | solution.py:296
  68.4 2.5 %collective-permute-start.22 = (f32[40,64]{1,0:T(8,128)S(1)}, f32[40,64]{1,0:T(8,128)S(1)}, u32[]{:S(2)}, u32[]{:S(2)}) collective-permute-start(f32[40,64]{1,0:T(8,128)S(1)} %get-tuple-element.136), channel_id=1, source_target_pairs={{0,14},{4,10},{8,6},{12,2},{14,0},{10,4},{6,8},{2,12},{1,15},{5,11... | collective-permute-start | bytes 30728 | tf_op jit(solution)/shard_map/ppermute | solution.py:315
  71.0 3.9 %collective-permute-done.22.refs_7_ = f32[40,64]{1,0:T(8,128)S(1)} collective-permute-done((f32[40,64]{1,0:T(8,128)S(1)}, f32[40,64]{1,0:T(8,128)S(1)}, u32[]{:S(2)}, u32[]{:S(2)}) %collective-permute-start.22) | collective-permute-done | bytes 10272 | tf_op jit(solution)/shard_map/ppermute | solution.py:315
  81.3 3.7 %copy-done.3 = bf16[6144,768]{1,0:T(8,128)(2,1)S(1)} copy-done((bf16[6144,768]{1,0:T(8,128)(2,1)S(1)}, bf16[6144,768]{1,0:T(8,128)(2,1)}, u32[]{:S(2)}) %copy-start.3) | copy-done | bytes 9437208
  85.0 3.7 %copy-done.4 = bf16[6144,768]{1,0:T(8,128)(2,1)S(1)} copy-done((bf16[6144,768]{1,0:T(8,128)(2,1)S(1)}, bf16[6144,768]{1,0:T(8,128)(2,1)}, u32[]{:S(2)}) %copy-start.4) | copy-done | bytes 9437208
  89.6 5.7 %partials.2 = (bf16[32,3072]{1,0:T(8,128)(2,1)S(1)}, bf16[40,3072]{1,0:T(8,128)(2,1)S(1)}) custom-call(bf16[1,40,768]{2,1,0:T(8,128)(2,1)S(1)} %get-tuple-element.101.refs_0_.refs_4_, bf16[1,40,768]{2,1,0:T(8,128)(2,1)S(1)} %copy-done.25, bf16[6144,768]{1,0:T(8,128)(2,1)S(1)} %copy-done.3, bf16[6144,768]{1,0:T(8,128)(2,1)S(1)} %copy-done.4), custom_call_target="tpu_custom_call" | custom-call | flops 754974720 | bytes 18874368 | tf_op jit(solution)/shard_map/partials/pallas_call | solution.py:339
  99.1 5.9 %partials.3 = (bf16[72,3072]{1,0:T(8,128)(2,1)S(1)}, bf16[72,3072]{1,0:T(8,128)(2,1)S(1)}, bf16[72,3072]{1,0:T(8,128)(2,1)S(1)}, bf16[72,3072]{1,0:T(8,128)(2,1)...) custom-call(bf16[1,40,768]{2,1,0:T(8,128)(2,1)S(1)} %copy-done.29, ...), custom_call_target="tpu_custom_call" | custom-call | flops 5284823040 | bytes 18874368 | tf_op jit(solution)/shard_map/partials/pallas_call | solution.py:339
  109.1 8.7 %collective-permute-done.17 = bf16[72,3072]{1,0:T(8,128)(2,1)S(1)} collective-permute-done((bf16[72,3072]{1,0:T(8,128)(2,1)S(1)}, bf16[72,3072]{1,0:T(8,128)(2,1)S(1)}, u32[]{:S(2)}, u32[]{:S(2)}) %collective-permute-start.17) | collective-permute-done | bytes 442400 | tf_op jit(solution)/shard_map/ppermute | solution.py:381
  122.0 7.1 %collective-permute-done.18 = bf16[72,3072]{1,0:T(8,128)(2,1)S(1)} collective-permute-done((bf16[72,3072]{1,0:T(8,128)(2,1)S(1)}, bf16[72,3072]{1,0:T(8,128)(2,1)S(1)}, u32[]{:S(2)}, u32[]{:S(2)}) %collective-permute-start.18) | collective-permute-done | bytes 442400 | tf_op jit(solution)/shard_map/ppermute | solution.py:381
  133.7 5.4 %collective-permute-done.19.right_ref = bf16[72,3072]{1,0:T(8,128)(2,1)S(1)} collective-permute-done((bf16[72,3072]{1,0:T(8,128)(2,1)S(1)}, bf16[72,3072]{1,0:T(8,128)(2,1)S(1)}, u32[]{:S(2)}, u32[]{:S(2)}) %collective-permute-start.19) | collective-permute-done | bytes 442400 | tf_op jit(solution)/shard_map/ppermute | solution.py:381
  139.1 2.4 %collective-permute-done.16.left_ref = bf16[72,3072]{1,0:T(8,128)(2,1)S(1)} collective-permute-done((bf16[72,3072]{1,0:T(8,128)(2,1)S(1)}, bf16[72,3072]{1,0:T(8,128)(2,1)S(1)}, u32[]{:S(2)}, u32[]{:S(2)}) %collective-permute-start.16) | collective-permute-done | bytes 442400 | tf_op jit(solution)/shard_map/ppermute | solution.py:380
  (174 shorter events, 48.1 us)
Async XLA Ops:
  3.6 17.3 %collective-permute-start.1 = (bf16[72,3200]{1,0:T(8,128)(2,1)S(1)}, bf16[72,3200]{1,0:T(8,128)(2,1)S(1)}, u32[]{:S(2)}, u32[]{:S(2)}) collective-permute-start(bf16[72,3200]{1,0:T(8,128)(2,1)S(1)} %prepare.1.refs_0_), channel_id=1, source_target_pairs={{0,2},{4,0},{8,4},{12,8},{14,12},{10,14},{6,10},{2,6},{1,3},{5,1},... | collective-permute-start | bytes 1382408 | tf_op jit(solution)/shard_map/ppermute | solution.py:321
  6.6 14.3 %collective-permute-start = (bf16[72,3200]{1,0:T(8,128)(2,1)S(1)}, bf16[72,3200]{1,0:T(8,128)(2,1)S(1)}, u32[]{:S(2)}, u32[]{:S(2)}) collective-permute-start(bf16[72,3200]{1,0:T(8,128)(2,1)S(1)} %prepare.1.refs_0_), channel_id=1, source_target_pairs={{0,4},{4,8},{8,12},{12,14},{14,10},{10,6},{6,2},{2,0},{1,5},{5,9},... | collective-permute-start | bytes 1382408 | tf_op jit(solution)/shard_map/ppermute | solution.py:320
  20.9 12.1 %collective-permute-start.2 = (bf16[72,3200]{1,0:T(8,128)(2,1)S(1)}, bf16[72,3200]{1,0:T(8,128)(2,1)S(1)}, u32[]{:S(2)}, u32[]{:S(2)}) collective-permute-start(bf16[72,3200]{1,0:T(8,128)(2,1)S(1)} %collective-permute-done.refs_0_), channel_id=1, source_target_pairs={{0,4},{4,8},{8,12},{12,14},{14,10},{10,6},{6,2},{2,0},{1,5},{5,9},... | collective-permute-start | bytes 1382408 | tf_op jit(solution)/shard_map/ppermute | solution.py:320
  23.0 11.5 %collective-permute-start.3 = (bf16[72,3200]{1,0:T(8,128)(2,1)S(1)}, bf16[72,3200]{1,0:T(8,128)(2,1)S(1)}, u32[]{:S(2)}, u32[]{:S(2)}) collective-permute-start(bf16[72,3200]{1,0:T(8,128)(2,1)S(1)} %collective-permute-done.1.refs_1_), channel_id=1, source_target_pairs={{0,2},{4,0},{8,4},{12,8},{14,12},{10,14},{6,10},{2,6},{1,3},{5,1},... | collective-permute-start | bytes 1382408 | tf_op jit(solution)/shard_map/ppermute | solution.py:321
  34.4 12.9 %collective-permute-start.4 = (bf16[72,3200]{1,0:T(8,128)(2,1)S(1)}, bf16[72,3200]{1,0:T(8,128)(2,1)S(1)}, u32[]{:S(2)}, u32[]{:S(2)}) collective-permute-start(bf16[72,3200]{1,0:T(8,128)(2,1)S(1)} %collective-permute-done.2.refs_0_), channel_id=1, source_target_pairs={{0,4},{4,8},{8,12},{12,14},{14,10},{10,6},{6,2},{2,0},{1,5},{5,9},... | collective-permute-start | bytes 1382408 | tf_op jit(solution)/shard_map/ppermute | solution.py:320
  36.0 11.3 %collective-permute-start.5 = (bf16[72,3200]{1,0:T(8,128)(2,1)S(1)}, bf16[72,3200]{1,0:T(8,128)(2,1)S(1)}, u32[]{:S(2)}, u32[]{:S(2)}) collective-permute-start(bf16[72,3200]{1,0:T(8,128)(2,1)S(1)} %collective-permute-done.3.refs_1_), channel_id=1, source_target_pairs={{0,2},{4,0},{8,4},{12,8},{14,12},{10,14},{6,10},{2,6},{1,3},{5,1},... | collective-permute-start | bytes 1382408 | tf_op jit(solution)/shard_map/ppermute | solution.py:321
  36.4 10.3 %collective-permute-start.6 = (f32[40,64]{1,0:T(8,128)S(1)}, f32[40,64]{1,0:T(8,128)S(1)}, u32[]{:S(2)}, u32[]{:S(2)}) collective-permute-start(f32[40,64]{1,0:T(8,128)S(1)} %get-tuple-element.88), channel_id=1, source_target_pairs={{0,2},{4,0},{8,4},{12,8},{14,12},{10,14},{6,10},{2,6},{1,3},{5,1},... | collective-permute-start | bytes 30728 | tf_op jit(solution)/shard_map/ppermute | solution.py:315
  36.8 9.9 %collective-permute-start.7 = (f32[40,64]{1,0:T(8,128)S(1)}, f32[40,64]{1,0:T(8,128)S(1)}, u32[]{:S(2)}, u32[]{:S(2)}) collective-permute-start(f32[40,64]{1,0:T(8,128)S(1)} %get-tuple-element.89), channel_id=1, source_target_pairs={{0,4},{4,8},{8,12},{12,14},{14,10},{10,6},{6,2},{2,0},{1,5},{5,9},... | collective-permute-start | bytes 30728 | tf_op jit(solution)/shard_map/ppermute | solution.py:315
  48.0 16.1 %collective-permute-start.9 = (bf16[40,3200]{1,0:T(8,128)(2,1)}, bf16[40,3200]{1,0:T(8,128)(2,1)}, u32[]{:S(2)}, u32[]{:S(2)}) collective-permute-start(bf16[40,3200]{1,0:T(8,128)(2,1)} %slice.91), channel_id=1, source_target_pairs={{0,2},{4,0},{8,4},{12,8},{14,12},{10,14},{6,10},{2,6},{1,3},{5,1},... | collective-permute-start | bytes 768008 | tf_op jit(solution)/shard_map/ppermute | solution.py:324
  48.5 15.6 %collective-permute-start.8 = (bf16[32,3200]{1,0:T(8,128)(2,1)S(1)}, bf16[32,3200]{1,0:T(8,128)(2,1)S(1)}, u32[]{:S(2)}, u32[]{:S(2)}) collective-permute-start(bf16[32,3200]{1,0:T(8,128)(2,1)S(1)} %slice.90), channel_id=1, source_target_pairs={{0,4},{4,8},{8,12},{12,14},{14,10},{10,6},{6,2},{2,0},{1,5},{5,9},... | collective-permute-start | bytes 614408 | tf_op jit(solution)/shard_map/ppermute | solution.py:323
  50.1 11.6 %collective-permute-start.10 = (f32[40,64]{1,0:T(8,128)S(1)}, f32[40,64]{1,0:T(8,128)S(1)}, u32[]{:S(2)}, u32[]{:S(2)}) collective-permute-start(f32[40,64]{1,0:T(8,128)S(1)} %get-tuple-element.97), channel_id=1, source_target_pairs={{0,6},{4,2},{8,0},{12,4},{14,8},{10,12},{6,14},{2,10},{1,7},{5,3},... | collective-permute-start | bytes 30728 | tf_op jit(solution)/shard_map/ppermute | solution.py:315
  50.7 13.5 %collective-permute-start.11 = (f32[40,64]{1,0:T(8,128)S(1)}, f32[40,64]{1,0:T(8,128)S(1)}, u32[]{:S(2)}, u32[]{:S(2)}) collective-permute-start(f32[40,64]{1,0:T(8,128)S(1)} %get-tuple-element.98), channel_id=1, source_target_pairs={{0,8},{4,12},{8,14},{12,10},{14,6},{10,2},{6,0},{2,4},{1,9},{5,13}... | collective-permute-start | bytes 30728 | tf_op jit(solution)/shard_map/ppermute | solution.py:315
  60.2 10.8 %collective-permute-start.20 = (f32[40,64]{1,0:T(8,128)S(1)}, f32[40,64]{1,0:T(8,128)S(1)}, u32[]{:S(2)}, u32[]{:S(2)}) collective-permute-start(f32[40,64]{1,0:T(8,128)S(1)} %get-tuple-element.134), channel_id=1, source_target_pairs={{0,10},{4,6},{8,2},{12,0},{14,4},{10,8},{6,12},{2,14},{1,11},{5,7}... | collective-permute-start | bytes 30728 | tf_op jit(solution)/shard_map/ppermute | solution.py:315
  79.1 18.2 %collective-permute-start.23 = (bf16[8,32,768]{2,1,0:T(8,128)(2,1)}, bf16[8,32,768]{2,1,0:T(8,128)(2,1)}, u32[]{:S(2)}, u32[]{:S(2)}) collective-permute-start(bf16[8,32,768]{2,1,0:T(8,128)(2,1)} %get-tuple-element.139), channel_id=1, source_target_pairs={{0,1},{1,0},{2,3},{3,2},{4,5},{5,4},{6,7},{7,6},{8,9},{9,8},{10,11... | collective-permute-start | bytes 1179656 | tf_op jit(solution)/shard_map/ppermute | solution.py:410
  95.3 9.7 %collective-permute-start.12 = (bf16[32,3072]{1,0:T(8,128)(2,1)S(1)}, bf16[32,3072]{1,0:T(8,128)(2,1)S(1)}, u32[]{:S(2)}, u32[]{:S(2)}) collective-permute-start(bf16[32,3072]{1,0:T(8,128)(2,1)S(1)} %get-tuple-element.103), channel_id=1, source_target_pairs={{0,4},{4,8},{8,12},{12,14},{14,10},{10,6},{6,2},{2,0},{1,5},{5,9},... | collective-permute-start | bytes 589832 | tf_op jit(solution)/shard_map/ppermute | solution.py:361
  95.3 9.7 %collective-permute-start.13 = (bf16[40,3072]{1,0:T(8,128)(2,1)S(1)}, bf16[40,3072]{1,0:T(8,128)(2,1)S(1)}, u32[]{:S(2)}, u32[]{:S(2)}) collective-permute-start(bf16[40,3072]{1,0:T(8,128)(2,1)S(1)} %get-tuple-element.104), channel_id=1, source_target_pairs={{0,2},{4,0},{8,4},{12,8},{14,12},{10,14},{6,10},{2,6},{1,3},{5,1},... | collective-permute-start | bytes 737288 | tf_op jit(solution)/shard_map/ppermute | solution.py:362
  105.1 12.8 %collective-permute-start.17 = (bf16[72,3072]{1,0:T(8,128)(2,1)S(1)}, bf16[72,3072]{1,0:T(8,128)(2,1)S(1)}, u32[]{:S(2)}, u32[]{:S(2)}) collective-permute-start(bf16[72,3072]{1,0:T(8,128)(2,1)S(1)} %first_add.3), channel_id=1, source_target_pairs={{0,2},{4,0},{8,4},{12,8},{14,12},{10,14},{6,10},{2,6},{1,3},{5,1},... | collective-permute-start | bytes 1327112 | tf_op jit(solution)/shard_map/ppermute | solution.py:381
  106.7 12.5 %collective-permute-start.14 = (bf16[72,3072]{1,0:T(8,128)(2,1)S(1)}, bf16[72,3072]{1,0:T(8,128)(2,1)S(1)}, u32[]{:S(2)}, u32[]{:S(2)}) collective-permute-start(bf16[72,3072]{1,0:T(8,128)(2,1)S(1)} %first_add.2), channel_id=1, source_target_pairs={{0,4},{4,8},{8,12},{12,14},{14,10},{10,6},{6,2},{2,0},{1,5},{5,9},... | collective-permute-start | bytes 1327112 | tf_op jit(solution)/shard_map/ppermute | solution.py:380
  107.8 12.4 %collective-permute-start.25 = (bf16[2,32,768]{2,1,0:T(8,128)(2,1)S(1)}, bf16[2,32,768]{2,1,0:T(8,128)(2,1)S(1)}, u32[]{:S(2)}, u32[]{:S(2)}) collective-permute-start(bf16[2,32,768]{2,1,0:T(8,128)(2,1)S(1)} %slice_bitcast_fusion.2), channel_id=1, source_target_pairs={{0,4},{2,6},{4,0},{6,2},{8,12},{10,14},{12,8},{14,10},{1,5},{3,7},... | collective-permute-start | bytes 294920 | tf_op jit(solution)/shard_map/ppermute | solution.py:429
  118.0 11.2 %collective-permute-start.18 = (bf16[72,3072]{1,0:T(8,128)(2,1)S(1)}, bf16[72,3072]{1,0:T(8,128)(2,1)S(1)}, u32[]{:S(2)}, u32[]{:S(2)}) collective-permute-start(bf16[72,3072]{1,0:T(8,128)(2,1)S(1)} %add_convert_fusion.1), channel_id=1, source_target_pairs={{0,2},{4,0},{8,4},{12,8},{14,12},{10,14},{6,10},{2,6},{1,3},{5,1},... | collective-permute-start | bytes 1327112 | tf_op jit(solution)/shard_map/ppermute | solution.py:381
  119.4 11.6 %collective-permute-start.15 = (bf16[72,3072]{1,0:T(8,128)(2,1)S(1)}, bf16[72,3072]{1,0:T(8,128)(2,1)S(1)}, u32[]{:S(2)}, u32[]{:S(2)}) collective-permute-start(bf16[72,3072]{1,0:T(8,128)(2,1)S(1)} %add_convert_fusion.3), channel_id=1, source_target_pairs={{0,4},{4,8},{8,12},{12,14},{14,10},{10,6},{6,2},{2,0},{1,5},{5,9},... | collective-permute-start | bytes 1327112 | tf_op jit(solution)/shard_map/ppermute | solution.py:380
  120.3 11.4 %collective-permute-start.26 = (bf16[1,32,768]{2,1,0:T(8,128)(2,1)S(1)}, bf16[1,32,768]{2,1,0:T(8,128)(2,1)S(1)}, u32[]{:S(2)}, u32[]{:S(2)}) collective-permute-start(bf16[1,32,768]{2,1,0:T(8,128)(2,1)S(1)} %slice_bitcast_fusion.4), channel_id=1, source_target_pairs={{0,8},{2,10},{4,12},{6,14},{8,0},{10,2},{12,4},{14,6},{1,9},{3,11}... | collective-permute-start | bytes 147464 | tf_op jit(solution)/shard_map/ppermute | solution.py:429
  129.3 9.9 %collective-permute-start.19 = (bf16[72,3072]{1,0:T(8,128)(2,1)S(1)}, bf16[72,3072]{1,0:T(8,128)(2,1)S(1)}, u32[]{:S(2)}, u32[]{:S(2)}) collective-permute-start(bf16[72,3072]{1,0:T(8,128)(2,1)S(1)} %add_convert_fusion), channel_id=1, source_target_pairs={{0,2},{4,0},{8,4},{12,8},{14,12},{10,14},{6,10},{2,6},{1,3},{5,1},... | collective-permute-start | bytes 1327112 | tf_op jit(solution)/shard_map/ppermute | solution.py:381
  131.1 10.4 %collective-permute-start.16 = (bf16[72,3072]{1,0:T(8,128)(2,1)S(1)}, bf16[72,3072]{1,0:T(8,128)(2,1)S(1)}, u32[]{:S(2)}, u32[]{:S(2)}) collective-permute-start(bf16[72,3072]{1,0:T(8,128)(2,1)S(1)} %add_convert_fusion.2), channel_id=1, source_target_pairs={{0,4},{4,8},{8,12},{12,14},{14,10},{10,6},{6,2},{2,0},{1,5},{5,9},... | collective-permute-start | bytes 1327112 | tf_op jit(solution)/shard_map/ppermute | solution.py:380
  (50 other events, 600.7 us)

commit v4 on v3

--- a/solution.py
+++ b/solution.py
@@ -12,7 +12,7 @@
 TN = (((0,), (0,)), ((), ()))
 BF = jnp.bfloat16
 F32 = jnp.float32
-VMEM_LIMIT = 20 * 1024 * 1024
+VMEM_LIMIT = 10 * 1024 * 1024
 TILE = 256
 
 
@@ -87,7 +87,7 @@
 
 def hidden_kernel(capacity, slot, count, *refs):
     blocks, refs = refs[:count], refs[count:]
-    (gate_ref, up_ref, down_ref, lora_gate, lora_up, dgate_ref, dup_ref), refs = refs[:7], refs[7:]
+    (gate_ref, up_ref, down_ref, lora_gate, lora_up, dgate_ref, dup_ref, low_ref), refs = refs[:8], refs[8:]
     lows, rows = refs[:count], refs[count]
     hidden, width = down_ref.shape
     half = width // 2
@@ -95,24 +95,25 @@
     tall = rows.shape[0] // count
     for i, block in enumerate(blocks):
         rows[i * tall : i * tall + 2 * capacity, :] = block[:, :half]
-    step = TILE if hidden % TILE == 0 else hidden
-    live = lax.broadcasted_iota(jnp.int32, (slot, step), 0) < capacity
-    for t in range(0, hidden, step):
-        first = dot(rows[...], down_ref[t : t + step, :half], NT)
-        second = dot(rows[...], down_ref[t : t + step, half:], NT)
-        for i, block in enumerate(blocks):
-            at = i * tall
-            weight = block[:, half:].astype(F32)[:slot, rank : rank + 1]
-            grad = (first[at : at + slot] + second[at + capacity : at + capacity + slot]) * weight
-            grad = jnp.where(live, grad, 0.0)
-            gate = gate_ref[i, :, t : t + step].astype(F32)
-            up = up_ref[i, :, t : t + step].astype(F32)
-            sig = 1.0 / (1.0 + jnp.exp(-gate))
-            slope = sig * (1.0 + gate * (1.0 - sig))
-            dgate_ref[i, :, t : t + step] = (grad * up * slope).astype(BF)
-            dup_ref[i, :, t : t + step] = (grad * gate * sig).astype(BF)
-    for i in range(count):
-        lows[i][...] = SCALE * (dot(dgate_ref[i], lora_gate[...], NT) + dot(dup_ref[i], lora_up[...], NT))
+    first = dot(down_ref[:, :half], rows[...], NT).T
+    second = dot(down_ref[:, half:], rows[...], NT).T
+    live = lax.broadcasted_iota(jnp.int32, (slot, hidden), 0) < capacity
+    for i, block in enumerate(blocks):
+        at = i * tall
+        extra = block[:, half:]
+        low_ref[i] = extra[:slot, :rank]
+        weight = extra.astype(F32)[:slot, rank : rank + 1]
+        grad = (first[at : at + slot] + second[at + capacity : at + capacity + slot]) * weight
+        grad = jnp.where(live, grad, 0.0)
+        gate = gate_ref[i].astype(F32)
+        up = up_ref[i].astype(F32)
+        sig = 1.0 / (1.0 + jnp.exp(-gate))
+        slope = sig * (1.0 + gate * (1.0 - sig))
+        dgate = (grad * up * slope).astype(BF)
+        dup = (grad * gate * sig).astype(BF)
+        dgate_ref[i] = dgate
+        dup_ref[i] = dup
+        lows[i][...] = SCALE * (dot(dgate, lora_gate[...], NT) + dot(dup, lora_up[...], NT))
 
 
 def stack(groups, slot, sources, target):
@@ -124,19 +125,31 @@
 
 
 def lora_kernel(slot, groups, *refs):
-    members, pieces = sum(groups), len(groups)
-    dgates, dups, extras = refs[:pieces], refs[pieces : 2 * pieces], refs[2 * pieces : 2 * pieces + members]
-    lora_out, dgate, dup, low = refs[2 * pieces + members :]
+    pieces = len(groups)
+    dgates, dups, lows = refs[:pieces], refs[pieces : 2 * pieces], refs[2 * pieces : 3 * pieces]
+    lora_out, dgate, dup, low = refs[3 * pieces :]
     rank = lora_out.shape[0] // 2
     stack(groups, slot, dgates, dgate)
     stack(groups, slot, dups, dup)
-    for i, extra in enumerate(extras):
-        low[i * slot : (i + 1) * slot, :] = extra[:slot, :rank]
+    stack(groups, slot, lows, low)
     lora_out[:rank, :] = (SCALE * dot(low[...], dgate[...], TN)).astype(BF)
     lora_out[rank:, :] = (SCALE * dot(low[...], dup[...], TN)).astype(BF)
 
 
-def partial_kernel(capacity, slot, groups, cut, *refs):
+def first_partial_kernel(capacity, slot, cut, dgate_in, dup_in, gate_ref, up_ref, top, rest, dgate, dup, tile):
+    half = gate_ref.shape[0] // 2
+    dgate[:slot, :] = dgate_in[0]
+    dup[:slot, :] = dup_in[0]
+    step = tile.shape[1]
+    for t in range(0, half, step):
+        for at, place in ((t, 0), (t + half, capacity)):
+            total = dot(gate_ref[at : at + step, :], dgate[...], NT) + dot(up_ref[at : at + step, :], dup[...], NT)
+            tile[place : place + capacity, :] = total.T[:capacity]
+        top[:, t : t + step] = tile[:cut, :].astype(BF)
+        rest[:, t : t + step] = tile[cut:, :].astype(BF)
+
+
+def partial_kernel(capacity, slot, groups, *refs):
     members, pieces = sum(groups), len(groups)
     dgates, dups, refs = refs[:pieces], refs[pieces : 2 * pieces], refs[2 * pieces :]
     gate_ref, up_ref, outs, (dgate, dup, tile) = refs[0], refs[1], refs[2:-3], refs[-3:]
@@ -155,11 +168,7 @@
             at = i * slot
             tile[:capacity, :] = sums[0][at : at + capacity]
             tile[capacity:, :] = sums[1][at : at + capacity]
-            if cut:
-                outs[0][:, t : t + TILE] = tile[:cut, :].astype(BF)
-                outs[1][:, t : t + TILE] = tile[cut:, :].astype(BF)
-            else:
-                outs[i][:, t : t + TILE] = tile[...].astype(BF)
+            outs[i][:, t : t + TILE] = tile[...].astype(BF)
 
 
 def merge_kernel(cut, upper, part_ref, own_ref, out_ref):
@@ -243,7 +252,7 @@
     capacity = stored_gate_rows.shape[1] // n
     hidden = stored_gate_rows.shape[2]
     rank = adapter_down_factor.shape[0]
-    tall = -(-2 * capacity // 16) * 16
+    tall = -(-2 * capacity // 128) * 128
     slot = -(-capacity // 8) * 8
     cut = capacity // 16 * 16
     wide = half + 2 * rank
@@ -287,7 +296,7 @@
     gate_rows, up_rows = in_order(stored_gate_rows), in_order(stored_up_rows)
 
     down_here, gate_here, up_here = in_vmem(down_weight), in_vmem(gate_weight), in_vmem(up_weight)
-    dgates, dups, lows = [], [], []
+    dgates, dups, low_rows, lows = [], [], [], []
     got = {0: block}
 
     def hidden_pass(group):
@@ -295,7 +304,8 @@
         grads = jax.ShapeDtypeStruct((size, slot, hidden), BF)
         results = pl.pallas_call(
             functools.partial(hidden_kernel, capacity, slot, size),
-            out_shape=[grads, grads] + [jax.ShapeDtypeStruct((slot, rank), F32)] * size,
+            out_shape=[grads, grads, jax.ShapeDtypeStruct((size, slot, rank), BF)]
+            + [jax.ShapeDtypeStruct((slot, rank), F32)] * size,
             scratch_shapes=[pltpu.VMEM((size * tall, half), BF)],
             compiler_params=params(),
             cost_estimate=cost(2 * size * tall * width * hidden, 2 * hidden * width),
@@ -310,7 +320,8 @@
         )
         dgates.append(results[0])
         dups.append(results[1])
-        for r, low in zip(group, results[2:]):
+        low_rows.append(results[2])
+        for r, low in zip(group, results[3:]):
             pairs = [(ring[i], ring[(i + r) % n]) for i in range(n)]
             lows.append(lax.ppermute(low, "expert", pairs) if r else low)
 
@@ -334,26 +345,31 @@
     hidden_pass(passes[-1])
 
     sizes = [len(group) for group in passes]
-    def partials(some, heights):
-        count = sum(sizes[i] for i in some)
-        return pl.pallas_call(
-            functools.partial(
-                partial_kernel, capacity, slot, [sizes[i] for i in some], cut if len(heights) > count else 0
-            ),
-            out_shape=[jax.ShapeDtypeStruct((h, half), BF) for h in heights],
-            scratch_shapes=[
-                pltpu.VMEM((count * slot, hidden), BF),
-                pltpu.VMEM((count * slot, hidden), BF),
-                pltpu.VMEM((2 * capacity, TILE), F32),
-            ],
-            compiler_params=params(),
-            cost_estimate=cost(4 * count * slot * width * hidden, 4 * hidden * width),
-            name="partials",
-        )(*[dgates[i] for i in some], *[dups[i] for i in some], gate_here, up_here)
-
-    last_a, last_b = partials([len(passes) - 1], [cut, 2 * capacity - cut])
-    rest = list(range(len(passes) - 1))
-    own = partials(rest, [2 * capacity] * (n - 1))
+    last_a, last_b = pl.pallas_call(
+        functools.partial(first_partial_kernel, capacity, slot, cut),
+        out_shape=[jax.ShapeDtypeStruct((h, half), BF) for h in (cut, 2 * capacity - cut)],
+        scratch_shapes=[
+            pltpu.VMEM((128, hidden), BF),
+            pltpu.VMEM((128, hidden), BF),
+            pltpu.VMEM((2 * capacity, half // 2), F32),
+        ],
+        compiler_params=params(),
+        cost_estimate=cost(4 * slot * width * hidden, 4 * hidden * width),
+        name="first_partial",
+    )(dgates[-1], dups[-1], gate_here, up_here)
+    lows, last_a, last_b = lax.optimization_barrier((lows, last_a, last_b))
+    own = pl.pallas_call(
+        functools.partial(partial_kernel, capacity, slot, sizes[:-1]),
+        out_shape=[jax.ShapeDtypeStruct((2 * capacity, half), BF)] * (n - 1),
+        scratch_shapes=[
+            pltpu.VMEM(((n - 1) * slot, hidden), BF),
+            pltpu.VMEM(((n - 1) * slot, hidden), BF),
+            pltpu.VMEM((2 * capacity, TILE), F32),
+        ],
+        compiler_params=params(),
+        cost_estimate=cost(4 * (n - 1) * slot * width * hidden, 4 * hidden * width),
+        name="partials",
+    )(*dgates[:-1], *dups[:-1], gate_here, up_here)
 
     def add(a, b):
         return (a.astype(F32) + b.astype(F32)).astype(BF)
@@ -408,7 +424,7 @@
 
     swap = [(0, 1), (1, 0)]
     down = add(keep, lax.ppermute(send, "dp", swap))
-    extras, _ = lax.optimization_barrier(([got[r][:, half:] for r in order], down))
+    extras, _ = lax.optimization_barrier((low_rows, down))
     lora_local = pl.pallas_call(
         functools.partial(lora_kernel, slot, sizes),
         out_shape=jax.ShapeDtypeStruct((2 * rank, hidden), BF),

time: 144 us -> 133 us (0.924)
  local copies, waits for them, and re-layouts: 32.6 us -> 27.6 us
  waiting for transfers between devices: 38.8 us -> 35.5 us
  Pallas kernels: 35.7 us -> 34.2 us
    ppermute x3, waiting for transfers between devices: 0.1 us -> 9.74 us  [on_device(): lax.ppermute(pairs[:, 1], 'expert', [(e, e ^ bit) for e in range(n)])]
    ppermute x7, waiting for transfers between devices: 7.41 us -> 0.73 us  [hidden_pass(): lows.append(lax.ppermute(low, 'expert', pairs) if r else low)]
    ppermute x3, waiting for transfers between devices: 21.3 us -> 15.9 us  [on_device(): going_left = lax.ppermute(going_left, 'expert', to_left)]
    ppermute x3, waiting for transfers between devices: 2.37 us -> 0.01 us  [on_device(): going_right = lax.ppermute(going_right, 'expert', to_right)]
    ppermute x3, starting transfers between devices: 1.95 us -> 4.27 us  [on_device(): going_right = lax.ppermute(going_right, 'expert', to_right)]
    slice x8 -> x0, local copies, waits for them, and re-layouts: 2.2 us -> none  [on_device(): got[r][:, half:]]
    ppermute x3, starting transfers between devices: 4.59 us -> 2.44 us  [on_device(): going_left = lax.ppermute(going_left, 'expert', to_left)]
    unnamed x91 -> x38, local copies, waits for them, and re-layouts: 21 us -> 22.3 us
  transfers between devices with their start and end apart: 29 -> 29, of which waited for: 11 -> 9; matrix products, arithmetic and copies ran while one was open for 10% -> 6% of each run, Pallas kernels for 20% -> 21%
where the time goes in v4:
time: 133 us; the launch traced here: 132 us
  waiting for transfers between devices  35.5 us (27%)
  Pallas kernels  34.2 us (26%)
  starting transfers between devices  31.9 us (24%)
  local copies, waits for them, and re-layouts  27.6 us (21%)
  other arithmetic  2.16 us (2%)
    unnamed x38, local copies, waits for them, and re-layouts  22.3 us
    pallas_call x5, Pallas kernels, hidden_pass(): pl.pallas_call(functools.partial(hidden_kernel, capacity, slot, size), ou...  16.3 us
    ppermute x3, waiting for transfers between devices, on_device(): going_left = lax.ppermute(going_left, 'expert', to_left)  15.9 us
    ppermute x7, starting transfers between devices, hidden_pass(): lows.append(lax.ppermute(low, 'expert', pairs) if r else low)  11.6 us
    ppermute x3, waiting for transfers between devices, on_device(): lax.ppermute(pairs[:, 1], 'expert', [(e, e ^ bit) for e in range(n)])  9.74 us
    ppermute x3, waiting for transfers between devices, on_device(): rightward = lax.ppermute(rightward, 'expert', to_right)  5.98 us
    pallas_call x1, Pallas kernels, on_device(): pl.pallas_call(functools.partial(partial_kernel, capacity, slot, sizes[:-...  5.9 us
    pallas_call x1, Pallas kernels, on_device(): pl.pallas_call(functools.partial(first_partial_kernel, capacity, slot, cu...  5.29 us
  transfers between devices with their start and end apart: 29, of which 9 were waited for; matrix products, arithmetic and copies ran while one was open for 6% of the time, Pallas kernels for 21%

profile of v4, /device:TPU:0, one launch (start us, length us, event | category | flops | bytes accessed | tf_op | source)
XLA Modules:
  0.0 132.4 jit_solution(4951942688474473220)
XLA Ops:
  0.7 2.9 %prepare.1.refs_0_ = bf16[72,3200]{1,0:T(8,128)(2,1)S(1)} custom-call(s32[4,128]{1,0:T(4,128)} %bitcast.53, bf16[4,128]{1,0:T(4,128)(2,1)} %bitcast.62, bf16[128,6144]{1,0:T(8,128)(2,1)} %bitcast.57, bf16[128,6144]{1,0:T(8,128)(2,1)} %bitcast.51, bf16[64,6144]{1,0:T(8,128)(2,1)} %down_ref.1), custom_call_target="tpu_custom_call" | custom-call | flops 400000000 | bytes 4500000 | tf_op jit(solution)/shard_map/prepare/pallas_call | solution.py:275
  3.6 3.0 %collective-permute-start.1 = (bf16[72,3200]{1,0:T(8,128)(2,1)S(1)}, bf16[72,3200]{1,0:T(8,128)(2,1)S(1)}, u32[]{:S(2)}, u32[]{:S(2)}) collective-permute-start(bf16[72,3200]{1,0:T(8,128)(2,1)S(1)} %prepare.1.refs_0_), channel_id=1, source_target_pairs={{0,2},{4,0},{8,4},{12,8},{14,12},{10,14},{6,10},{2,6},{1,3},{5,1},... | collective-permute-start | bytes 1382408 | tf_op jit(solution)/shard_map/ppermute | solution.py:332
  10.9 3.8 %copy-done = bf16[768,6144]{1,0:T(8,128)(2,1)S(1)} copy-done((bf16[768,6144]{1,0:T(8,128)(2,1)S(1)}, bf16[768,6144]{1,0:T(8,128)(2,1)}, u32[]{:S(2)}) %copy-start) | copy-done | bytes 9437208
  14.7 2.9 %hidden_rows.5 = (bf16[1,40,768]{2,1,0:T(8,128)(2,1)S(1)}, bf16[1,40,768]{2,1,0:T(8,128)(2,1)S(1)}, bf16[1,40,64]{2,1,0:T(8,128)(2,1)S(1)}, f32[40,64]{1,0:T(8,128)S(1)}) custom-call(bf16[72,3200]{1,0:T(8,128)(2,1)S(1)} %prepare.1.refs_0_, bf16[1,40,768]{2,1,0:T(8,128)(2,1)S(1)} %get-tuple-element.184.refs_1_, ...), custom_call_target="tpu_custom_call" | custom-call | flops 1207959552 | bytes 9437184 | tf_op jit(solution)/shard_map/hidden_rows/pallas_call | solution.py:305
  21.8 3.1 %hidden_rows.6 = (bf16[2,40,768]{2,1,0:T(8,128)(2,1)S(1)}, bf16[2,40,768]{2,1,0:T(8,128)(2,1)S(1)}, bf16[2,40,64]{2,1,0:T(8,128)(2,1)S(1)}, f32[40,64]{1,0:T(8,128)S(1)}, f32[40,64]{1,0:T(8,128)S(1)}) custom-call(bf16[72,3200]{1,0:T(8,128)(2,1)S(1)} %collective-permute-done.refs_0_, bf16[72,3200]{1,0:T(8,128)(2,1)S(1)} %collective-permute-done.1.refs_1_, ...), custom_call_target="tpu_custom_call" | custom-call | flops 2415919104 | bytes 9437184 | tf_op jit(solution)/shard_map/hidden_rows/pallas_call | solution.py:305
  24.9 5.0 %collective-permute-done.2.refs_0_ = bf16[72,3200]{1,0:T(8,128)(2,1)} collective-permute-done((bf16[72,3200]{1,0:T(8,128)(2,1)S(1)}, bf16[72,3200]{1,0:T(8,128)(2,1)}, u32[]{:S(2)}, u32[]{:S(2)}) %collective-permute-start.2) | collective-permute-done | bytes 460832 | tf_op jit(solution)/shard_map/ppermute | solution.py:331
  35.3 3.7 %copy-done.2 = bf16[768,6144]{1,0:T(8,128)(2,1)S(1)} copy-done((bf16[768,6144]{1,0:T(8,128)(2,1)S(1)}, bf16[768,6144]{1,0:T(8,128)(2,1)}, u32[]{:S(2)}) %copy-start.2) | copy-done | bytes 9437208
  39.0 4.4 %hidden_rows.7 = (bf16[2,40,768]{2,1,0:T(8,128)(2,1)S(1)}, bf16[2,40,768]{2,1,0:T(8,128)(2,1)S(1)}, bf16[2,40,64]{2,1,0:T(8,128)(2,1)S(1)}, f32[40,64]{1,0:T(8,128)S(1)}, f32[40,64]{1,0:T(8,128)S(1)}) custom-call(bf16[72,3200]{1,0:T(8,128)(2,1)} %collective-permute-done.2.refs_0_, bf16[72,3200]{1,0:T(8,128)(2,1)} %collective-permute-done.3.refs_1_, ...), custom_call_target="tpu_custom_call" | custom-call | flops 2415919104 | bytes 9437184 | tf_op jit(solution)/shard_map/hidden_rows/pallas_call | solution.py:305
  49.3 3.7 %copy-done.3 = bf16[768,6144]{1,0:T(8,128)(2,1)S(1)} copy-done((bf16[768,6144]{1,0:T(8,128)(2,1)S(1)}, bf16[768,6144]{1,0:T(8,128)(2,1)}, u32[]{:S(2)}) %copy-start.3) | copy-done | bytes 9437208
  53.0 3.1 %hidden_rows.8 = (bf16[2,40,768]{2,1,0:T(8,128)(2,1)S(1)}, bf16[2,40,768]{2,1,0:T(8,128)(2,1)S(1)}, bf16[2,40,64]{2,1,0:T(8,128)(2,1)S(1)}, f32[40,64]{1,0:T(8,128)S(1)}, f32[40,64]{1,0:T(8,128)S(1)}) custom-call(bf16[72,3200]{1,0:T(8,128)(2,1)S(1)} %collective-permute-done.4.refs_0_, bf16[72,3200]{1,0:T(8,128)(2,1)S(1)} %collective-permute-done.5.refs_1_, ...), custom_call_target="tpu_custom_call" | custom-call | flops 2415919104 | bytes 9437184 | tf_op jit(solution)/shard_map/hidden_rows/pallas_call | solution.py:305
  57.8 2.1 %collective-permute-start.13 = (f32[40,64]{1,0:T(8,128)S(1)}, f32[40,64]{1,0:T(8,128)S(1)}, u32[]{:S(2)}, u32[]{:S(2)}) collective-permute-start(f32[40,64]{1,0:T(8,128)S(1)} %get-tuple-element.117), channel_id=1, source_target_pairs={{0,12},{4,14},{8,10},{12,6},{14,2},{10,0},{6,4},{2,8},{1,13},{5,15... | collective-permute-start | bytes 30728 | tf_op jit(solution)/shard_map/ppermute | solution.py:326
  60.0 2.9 %hidden_rows.9 = (bf16[1,40,768]{2,1,0:T(8,128)(2,1)S(1)}, bf16[1,40,768]{2,1,0:T(8,128)(2,1)S(1)}, bf16[1,40,64]{2,1,0:T(8,128)(2,1)S(1)}, f32[40,64]{1,0:T(8,128)S(1)}) custom-call(bf16[72,3200]{1,0:T(8,128)(2,1)S(1)} %pad_maximum_fusion.refs_0_, bf16[1,40,768]{2,1,0:T(8,128)(2,1)S(1)} %get-tuple-element.185.refs_1_, ...), custom_call_target="tpu_custom_call" | custom-call | flops 1207959552 | bytes 9437184 | tf_op jit(solution)/shard_map/hidden_rows/pallas_call | solution.py:305
  62.9 2.8 %collective-permute-start.14 = (f32[40,64]{1,0:T(8,128)S(1)}, f32[40,64]{1,0:T(8,128)S(1)}, u32[]{:S(2)}, u32[]{:S(2)}) collective-permute-start(f32[40,64]{1,0:T(8,128)S(1)} %get-tuple-element.120), channel_id=1, source_target_pairs={{0,14},{4,10},{8,6},{12,2},{14,0},{10,4},{6,8},{2,12},{1,15},{5,11... | collective-permute-start | bytes 30728 | tf_op jit(solution)/shard_map/ppermute | solution.py:326
  65.7 3.7 %copy-done.5 = bf16[6144,768]{1,0:T(8,128)(2,1)S(1)} copy-done((bf16[6144,768]{1,0:T(8,128)(2,1)S(1)}, bf16[6144,768]{1,0:T(8,128)(2,1)}, u32[]{:S(2)}) %copy-start.5) | copy-done | bytes 9437208
  69.4 5.3 %first_partial.1 = (bf16[32,3072]{1,0:T(8,128)(2,1)S(1)}, bf16[40,3072]{1,0:T(8,128)(2,1)S(1)}) custom-call(bf16[1,40,768]{2,1,0:T(8,128)(2,1)S(1)} %get-tuple-element.121.dgate_in.refs_4_, bf16[1,40,768]{2,1,0:T(8,128)(2,1)S(1)} %get-tuple-element.122.dup_in.refs_9_, bf16[6144,768]{1,0:T(8,128)(2,1)S(1)} %bitcast.50, bf16[6144,768]{1,0:T(8,128)(2,1)S(1)} %copy-done.5), custom_call_target="tpu_custom_call" | custom-call | flops 754974720 | bytes 18874368 | tf_op jit(solution)/shard_map/first_partial/pallas_call | solution.py:348
  76.2 2.0 %collective-permute-start.16 = (bf16[40,3072]{1,0:T(8,128)(2,1)S(1)}, bf16[40,3072]{1,0:T(8,128)(2,1)S(1)}, u32[]{:S(2)}, u32[]{:S(2)}) collective-permute-start(bf16[40,3072]{1,0:T(8,128)(2,1)S(1)} %get-tuple-element.126), channel_id=1, source_target_pairs={{0,2},{4,0},{8,4},{12,8},{14,12},{10,14},{6,10},{2,6},{1,3},{5,1},... | collective-permute-start | bytes 737288 | tf_op jit(solution)/shard_map/ppermute | solution.py:378
  79.9 3.7 %copy-done.4 = bf16[6144,768]{1,0:T(8,128)(2,1)S(1)} copy-done((bf16[6144,768]{1,0:T(8,128)(2,1)S(1)}, bf16[6144,768]{1,0:T(8,128)(2,1)}, u32[]{:S(2)}) %copy-start.4) | copy-done | bytes 9437208
  83.6 3.7 %copy-done.6 = bf16[6144,768]{1,0:T(8,128)(2,1)S(1)} copy-done((bf16[6144,768]{1,0:T(8,128)(2,1)S(1)}, bf16[6144,768]{1,0:T(8,128)(2,1)}, u32[]{:S(2)}) %copy-start.6) | copy-done | bytes 9437208
  87.3 5.9 %partials.1 = (bf16[72,3072]{1,0:T(8,128)(2,1)S(1)}, bf16[72,3072]{1,0:T(8,128)(2,1)S(1)}, bf16[72,3072]{1,0:T(8,128)(2,1)S(1)}, bf16[72,3072]{1,0:T(8,128)(2,1)...) custom-call(bf16[1,40,768]{2,1,0:T(8,128)(2,1)S(1)} %get-tuple-element.127.refs_0_, ...), custom_call_target="tpu_custom_call" | custom-call | flops 5284823040 | bytes 18874368 | tf_op jit(solution)/shard_map/partials/pallas_call | solution.py:361
  97.4 9.7 %collective-permute-done.25 = bf16[2,32,768]{2,1,0:T(8,128)(2,1)S(1)} collective-permute-done((bf16[2,32,768]{2,1,0:T(8,128)(2,1)S(1)}, bf16[2,32,768]{2,1,0:T(8,128)(2,1)S(1)}, u32[]{:S(2)}, u32[]{:S(2)}) %collective-permute-start.25) | collective-permute-done | bytes 98336 | tf_op jit(solution)/shard_map/ppermute | solution.py:445
  109.8 9.5 %collective-permute-done.21 = bf16[72,3072]{1,0:T(8,128)(2,1)S(1)} collective-permute-done((bf16[72,3072]{1,0:T(8,128)(2,1)S(1)}, bf16[72,3072]{1,0:T(8,128)(2,1)S(1)}, u32[]{:S(2)}, u32[]{:S(2)}) %collective-permute-start.21) | collective-permute-done | bytes 442400 | tf_op jit(solution)/shard_map/ppermute | solution.py:397
  119.7 2.2 %collective-permute-start.19 = (bf16[72,3072]{1,0:T(8,128)(2,1)S(1)}, bf16[72,3072]{1,0:T(8,128)(2,1)S(1)}, u32[]{:S(2)}, u32[]{:S(2)}) collective-permute-start(bf16[72,3072]{1,0:T(8,128)(2,1)S(1)} %add_convert_fusion.2), channel_id=1, source_target_pairs={{0,4},{4,8},{8,12},{12,14},{14,10},{10,6},{6,2},{2,0},{1,5},{5,9},... | collective-permute-start | bytes 1327112 | tf_op jit(solution)/shard_map/ppermute | solution.py:396
  123.9 6.4 %collective-permute-done.22.right_ref = bf16[72,3072]{1,0:T(8,128)(2,1)S(1)} collective-permute-done((bf16[72,3072]{1,0:T(8,128)(2,1)S(1)}, bf16[72,3072]{1,0:T(8,128)(2,1)S(1)}, u32[]{:S(2)}, u32[]{:S(2)}) %collective-permute-start.22) | collective-permute-done | bytes 442400 | tf_op jit(solution)/shard_map/ppermute | solution.py:397
  130.4 2.0 %finish.1 = bf16[128,6144]{1,0:T(8,128)(2,1)} custom-call(s32[4,128]{1,0:T(4,128)S(1)} %bitcast.55, bf16[72,3072]{1,0:T(8,128)(2,1)S(1)} %collective-permute-done.19.left_ref, bf16[72,3072]{1,0:T(8,128)(2,1)S(1)} %collective-permute-done.22.right_ref, bf16[72,3072]{1,0:T(8,128)(2,1)S(1)} %get-tuple-element.150.own_ref, ...), custom_call_target="tpu_custom_call" | custom-call | flops 400000000 | bytes 4500000 | tf_op jit(solution)/shard_map/finish/pallas_call | solution.py:454
  (114 shorter events, 33.9 us)
Async XLA Ops:
  3.6 14.0 %collective-permute-start.1 = (bf16[72,3200]{1,0:T(8,128)(2,1)S(1)}, bf16[72,3200]{1,0:T(8,128)(2,1)S(1)}, u32[]{:S(2)}, u32[]{:S(2)}) collective-permute-start(bf16[72,3200]{1,0:T(8,128)(2,1)S(1)} %prepare.1.refs_0_), channel_id=1, source_target_pairs={{0,2},{4,0},{8,4},{12,8},{14,12},{10,14},{6,10},{2,6},{1,3},{5,1},... | collective-permute-start | bytes 1382408 | tf_op jit(solution)/shard_map/ppermute | solution.py:332
  6.6 12.0 %collective-permute-start = (bf16[72,3200]{1,0:T(8,128)(2,1)S(1)}, bf16[72,3200]{1,0:T(8,128)(2,1)S(1)}, u32[]{:S(2)}, u32[]{:S(2)}) collective-permute-start(bf16[72,3200]{1,0:T(8,128)(2,1)S(1)} %prepare.1.refs_0_), channel_id=1, source_target_pairs={{0,4},{4,8},{8,12},{12,14},{14,10},{10,6},{6,2},{2,0},{1,5},{5,9},... | collective-permute-start | bytes 1382408 | tf_op jit(solution)/shard_map/ppermute | solution.py:331
  18.6 11.2 %collective-permute-start.2 = (bf16[72,3200]{1,0:T(8,128)(2,1)S(1)}, bf16[72,3200]{1,0:T(8,128)(2,1)}, u32[]{:S(2)}, u32[]{:S(2)}) collective-permute-start(bf16[72,3200]{1,0:T(8,128)(2,1)S(1)} %collective-permute-done.refs_0_), channel_id=1, source_target_pairs={{0,4},{4,8},{8,12},{12,14},{14,10},{10,6},{6,2},{2,0},{1,5},{5,9},... | collective-permute-start | bytes 1382408 | tf_op jit(solution)/shard_map/ppermute | solution.py:331
  19.7 11.6 %collective-permute-start.3 = (bf16[72,3200]{1,0:T(8,128)(2,1)S(1)}, bf16[72,3200]{1,0:T(8,128)(2,1)}, u32[]{:S(2)}, u32[]{:S(2)}) collective-permute-start(bf16[72,3200]{1,0:T(8,128)(2,1)S(1)} %collective-permute-done.1.refs_1_), channel_id=1, source_target_pairs={{0,2},{4,0},{8,4},{12,8},{14,12},{10,14},{6,10},{2,6},{1,3},{5,1},... | collective-permute-start | bytes 1382408 | tf_op jit(solution)/shard_map/ppermute | solution.py:332
  31.2 12.9 %collective-permute-start.4 = (bf16[72,3200]{1,0:T(8,128)(2,1)}, bf16[72,3200]{1,0:T(8,128)(2,1)S(1)}, u32[]{:S(2)}, u32[]{:S(2)}) collective-permute-start(bf16[72,3200]{1,0:T(8,128)(2,1)} %collective-permute-done.2.refs_0_), channel_id=1, source_target_pairs={{0,4},{4,8},{8,12},{12,14},{14,10},{10,6},{6,2},{2,0},{1,5},{5,9},... | collective-permute-start | bytes 1382408 | tf_op jit(solution)/shard_map/ppermute | solution.py:331
  32.8 11.3 %collective-permute-start.5 = (bf16[72,3200]{1,0:T(8,128)(2,1)}, bf16[72,3200]{1,0:T(8,128)(2,1)S(1)}, u32[]{:S(2)}, u32[]{:S(2)}) collective-permute-start(bf16[72,3200]{1,0:T(8,128)(2,1)} %collective-permute-done.3.refs_1_), channel_id=1, source_target_pairs={{0,2},{4,0},{8,4},{12,8},{14,12},{10,14},{6,10},{2,6},{1,3},{5,1},... | collective-permute-start | bytes 1382408 | tf_op jit(solution)/shard_map/ppermute | solution.py:332
  33.3 10.8 %collective-permute-start.6 = (f32[40,64]{1,0:T(8,128)S(1)}, f32[40,64]{1,0:T(8,128)S(1)}, u32[]{:S(2)}, u32[]{:S(2)}) collective-permute-start(f32[40,64]{1,0:T(8,128)S(1)} %get-tuple-element.100), channel_id=1, source_target_pairs={{0,2},{4,0},{8,4},{12,8},{14,12},{10,14},{6,10},{2,6},{1,3},{5,1},... | collective-permute-start | bytes 30728 | tf_op jit(solution)/shard_map/ppermute | solution.py:326
  44.1 15.8 %collective-permute-start.9 = (bf16[40,3200]{1,0:T(8,128)(2,1)S(1)}, bf16[40,3200]{1,0:T(8,128)(2,1)S(1)}, u32[]{:S(2)}, u32[]{:S(2)}) collective-permute-start(bf16[40,3200]{1,0:T(8,128)(2,1)S(1)} %slice.67), channel_id=1, source_target_pairs={{0,2},{4,0},{8,4},{12,8},{14,12},{10,14},{6,10},{2,6},{1,3},{5,1},... | collective-permute-start | bytes 768008 | tf_op jit(solution)/shard_map/ppermute | solution.py:335
  44.7 13.1 %collective-permute-start.10 = (f32[40,64]{1,0:T(8,128)S(1)}, f32[40,64]{1,0:T(8,128)S(1)}, u32[]{:S(2)}, u32[]{:S(2)}) collective-permute-start(f32[40,64]{1,0:T(8,128)S(1)} %get-tuple-element.109), channel_id=1, source_target_pairs={{0,6},{4,2},{8,0},{12,4},{14,8},{10,12},{6,14},{2,10},{1,7},{5,3},... | collective-permute-start | bytes 30728 | tf_op jit(solution)/shard_map/ppermute | solution.py:326
  46.5 13.4 %collective-permute-start.11 = (f32[40,64]{1,0:T(8,128)S(1)}, f32[40,64]{1,0:T(8,128)S(1)}, u32[]{:S(2)}, u32[]{:S(2)}) collective-permute-start(f32[40,64]{1,0:T(8,128)S(1)} %get-tuple-element.110), channel_id=1, source_target_pairs={{0,8},{4,12},{8,14},{12,10},{14,6},{10,2},{6,0},{2,4},{1,9},{5,13}... | collective-permute-start | bytes 30728 | tf_op jit(solution)/shard_map/ppermute | solution.py:326
  47.7 12.3 %collective-permute-start.8 = (bf16[32,3200]{1,0:T(8,128)(2,1)S(1)}, bf16[32,3200]{1,0:T(8,128)(2,1)S(1)}, u32[]{:S(2)}, u32[]{:S(2)}) collective-permute-start(bf16[32,3200]{1,0:T(8,128)(2,1)S(1)} %slice.66), channel_id=1, source_target_pairs={{0,4},{4,8},{8,12},{12,14},{14,10},{10,6},{6,2},{2,0},{1,5},{5,9},... | collective-permute-start | bytes 614408 | tf_op jit(solution)/shard_map/ppermute | solution.py:334
  56.0 18.6 %collective-permute-start.12 = (f32[40,64]{1,0:T(8,128)S(1)}, f32[40,64]{1,0:T(8,128)S(1)}, u32[]{:S(2)}, u32[]{:S(2)}) collective-permute-start(f32[40,64]{1,0:T(8,128)S(1)} %get-tuple-element.116), channel_id=1, source_target_pairs={{0,10},{4,6},{8,2},{12,0},{14,4},{10,8},{6,12},{2,14},{1,11},{5,7}... | collective-permute-start | bytes 30728 | tf_op jit(solution)/shard_map/ppermute | solution.py:326
  57.8 16.9 %collective-permute-start.13 = (f32[40,64]{1,0:T(8,128)S(1)}, f32[40,64]{1,0:T(8,128)S(1)}, u32[]{:S(2)}, u32[]{:S(2)}) collective-permute-start(f32[40,64]{1,0:T(8,128)S(1)} %get-tuple-element.117), channel_id=1, source_target_pairs={{0,12},{4,14},{8,10},{12,6},{14,2},{10,0},{6,4},{2,8},{1,13},{5,15... | collective-permute-start | bytes 30728 | tf_op jit(solution)/shard_map/ppermute | solution.py:326
  62.9 11.8 %collective-permute-start.14 = (f32[40,64]{1,0:T(8,128)S(1)}, f32[40,64]{1,0:T(8,128)S(1)}, u32[]{:S(2)}, u32[]{:S(2)}) collective-permute-start(f32[40,64]{1,0:T(8,128)S(1)} %get-tuple-element.120), channel_id=1, source_target_pairs={{0,14},{4,10},{8,6},{12,2},{14,0},{10,4},{6,8},{2,12},{1,15},{5,11... | collective-permute-start | bytes 30728 | tf_op jit(solution)/shard_map/ppermute | solution.py:326
  76.1 17.1 %collective-permute-start.15 = (bf16[32,3072]{1,0:T(8,128)(2,1)S(1)}, bf16[32,3072]{1,0:T(8,128)(2,1)S(1)}, u32[]{:S(2)}, u32[]{:S(2)}) collective-permute-start(bf16[32,3072]{1,0:T(8,128)(2,1)S(1)} %get-tuple-element.125), channel_id=1, source_target_pairs={{0,4},{4,8},{8,12},{12,14},{14,10},{10,6},{6,2},{2,0},{1,5},{5,9},... | collective-permute-start | bytes 589832 | tf_op jit(solution)/shard_map/ppermute | solution.py:377
  76.2 17.1 %collective-permute-start.16 = (bf16[40,3072]{1,0:T(8,128)(2,1)S(1)}, bf16[40,3072]{1,0:T(8,128)(2,1)S(1)}, u32[]{:S(2)}, u32[]{:S(2)}) collective-permute-start(bf16[40,3072]{1,0:T(8,128)(2,1)S(1)} %get-tuple-element.126), channel_id=1, source_target_pairs={{0,2},{4,0},{8,4},{12,8},{14,12},{10,14},{6,10},{2,6},{1,3},{5,1},... | collective-permute-start | bytes 737288 | tf_op jit(solution)/shard_map/ppermute | solution.py:378
  78.3 17.6 %collective-permute-start.24 = (bf16[4,32,768]{2,1,0:T(8,128)(2,1)S(1)}, bf16[4,32,768]{2,1,0:T(8,128)(2,1)S(1)}, u32[]{:S(2)}, u32[]{:S(2)}) collective-permute-start(bf16[4,32,768]{2,1,0:T(8,128)(2,1)S(1)} %slice_bitcast_fusion), channel_id=1, source_target_pairs={{0,2},{2,0},{4,6},{6,4},{8,10},{10,8},{12,14},{14,12},{1,3},{3,1},... | collective-permute-start | bytes 589832 | tf_op jit(solution)/shard_map/ppermute | solution.py:445
  93.3 14.1 %collective-permute-start.20 = (bf16[72,3072]{1,0:T(8,128)(2,1)S(1)}, bf16[72,3072]{1,0:T(8,128)(2,1)S(1)}, u32[]{:S(2)}, u32[]{:S(2)}) collective-permute-start(bf16[72,3072]{1,0:T(8,128)(2,1)S(1)} %first_add.3), channel_id=1, source_target_pairs={{0,2},{4,0},{8,4},{12,8},{14,12},{10,14},{6,10},{2,6},{1,3},{5,1},... | collective-permute-start | bytes 1327112 | tf_op jit(solution)/shard_map/ppermute | solution.py:397
  93.9 15.4 %collective-permute-start.17 = (bf16[72,3072]{1,0:T(8,128)(2,1)S(1)}, bf16[72,3072]{1,0:T(8,128)(2,1)S(1)}, u32[]{:S(2)}, u32[]{:S(2)}) collective-permute-start(bf16[72,3072]{1,0:T(8,128)(2,1)S(1)} %first_add.2), channel_id=1, source_target_pairs={{0,4},{4,8},{8,12},{12,14},{14,10},{10,6},{6,2},{2,0},{1,5},{5,9},... | collective-permute-start | bytes 1327112 | tf_op jit(solution)/shard_map/ppermute | solution.py:396
  96.0 11.1 %collective-permute-start.25 = (bf16[2,32,768]{2,1,0:T(8,128)(2,1)S(1)}, bf16[2,32,768]{2,1,0:T(8,128)(2,1)S(1)}, u32[]{:S(2)}, u32[]{:S(2)}) collective-permute-start(bf16[2,32,768]{2,1,0:T(8,128)(2,1)S(1)} %slice_bitcast_fusion.2), channel_id=1, source_target_pairs={{0,4},{2,6},{4,0},{6,2},{8,12},{10,14},{12,8},{14,10},{1,5},{3,7},... | collective-permute-start | bytes 294920 | tf_op jit(solution)/shard_map/ppermute | solution.py:445
  107.2 14.8 %collective-permute-start.26 = (bf16[1,32,768]{2,1,0:T(8,128)(2,1)S(1)}, bf16[1,32,768]{2,1,0:T(8,128)(2,1)S(1)}, u32[]{:S(2)}, u32[]{:S(2)}) collective-permute-start(bf16[1,32,768]{2,1,0:T(8,128)(2,1)S(1)} %slice_bitcast_fusion.4), channel_id=1, source_target_pairs={{0,8},{2,10},{4,12},{6,14},{8,0},{10,2},{12,4},{14,6},{1,9},{3,11}... | collective-permute-start | bytes 147464 | tf_op jit(solution)/shard_map/ppermute | solution.py:445
  107.6 11.7 %collective-permute-start.21 = (bf16[72,3072]{1,0:T(8,128)(2,1)S(1)}, bf16[72,3072]{1,0:T(8,128)(2,1)S(1)}, u32[]{:S(2)}, u32[]{:S(2)}) collective-permute-start(bf16[72,3072]{1,0:T(8,128)(2,1)S(1)} %add_convert_fusion.1), channel_id=1, source_target_pairs={{0,2},{4,0},{8,4},{12,8},{14,12},{10,14},{6,10},{2,6},{1,3},{5,1},... | collective-permute-start | bytes 1327112 | tf_op jit(solution)/shard_map/ppermute | solution.py:397
  119.4 11.0 %collective-permute-start.22 = (bf16[72,3072]{1,0:T(8,128)(2,1)S(1)}, bf16[72,3072]{1,0:T(8,128)(2,1)S(1)}, u32[]{:S(2)}, u32[]{:S(2)}) collective-permute-start(bf16[72,3072]{1,0:T(8,128)(2,1)S(1)} %add_convert_fusion), channel_id=1, source_target_pairs={{0,2},{4,0},{8,4},{12,8},{14,12},{10,14},{6,10},{2,6},{1,3},{5,1},... | collective-permute-start | bytes 1327112 | tf_op jit(solution)/shard_map/ppermute | solution.py:397
  119.7 10.7 %collective-permute-start.19 = (bf16[72,3072]{1,0:T(8,128)(2,1)S(1)}, bf16[72,3072]{1,0:T(8,128)(2,1)S(1)}, u32[]{:S(2)}, u32[]{:S(2)}) collective-permute-start(bf16[72,3072]{1,0:T(8,128)(2,1)S(1)} %add_convert_fusion.2), channel_id=1, source_target_pairs={{0,4},{4,8},{8,12},{12,14},{14,10},{10,6},{6,2},{2,0},{1,5},{5,9},... | collective-permute-start | bytes 1327112 | tf_op jit(solution)/shard_map/ppermute | solution.py:396
  (24 other events, 229.5 us)

commit v5 on v4

v5 whole, which is shorter than its diff:
```python
import functools

import jax
import jax.numpy as jnp
from jax import lax
from jax.experimental import pallas as pl
from jax.experimental.pallas import tpu as pltpu
from jax.sharding import PartitionSpec as P

SCALE = 0.25
NT = (((1,), (1,)), ((), ()))
TN = (((0,), (0,)), ((), ()))
BF = jnp.bfloat16
F32 = jnp.float32
VMEM_LIMIT = 10 * 1024 * 1024
TILE = 256


def ring_order(mesh):
    count = mesh.shape["expert"]
    plain = list(range(count))
    if count < 4 or count % 2:
        return plain
    snake = list(range(0, count, 2)) + list(range(count - 1, 0, -2))
    spots = [getattr(d, "coords", None) for d in mesh.devices[0, :, 0]]
    if any(s is None for s in spots):
        return snake if count == 8 else plain

    def length(order):
        hops = zip(order, order[1:] + order[:1])
        return sum(sum(abs(a - b) for a, b in zip(spots[i], spots[j])) for i, j in hops)

    return min((plain, snake), key=length)


def dot(a, b, dims=None):
    if dims is None:
        dims = (((1,), (0,)), ((), ()))
    return lax.dot_general(a, b, dims, preferred_element_type=F32)


def pick_rows(choice, capacity):
    tokens = choice.shape[1]
    named = jnp.max((choice == 0).astype(F32), axis=0, keepdims=True)
    before = lax.broadcasted_iota(jnp.int32, (tokens, tokens), 0)
    after = lax.broadcasted_iota(jnp.int32, (tokens, tokens), 1)
    upto = (before <= after).astype(BF)
    count = dot(jnp.broadcast_to(named, (8, tokens)).astype(BF), upto)[:1]
    slot = jnp.where(named > 0, count - 1.0, -1000.0).astype(jnp.int32)
    row = lax.broadcasted_iota(jnp.int32, (2 * capacity, tokens), 0)
    return (row == slot).astype(BF), (row - capacity == slot).astype(BF)


def prepare_kernel(capacity, choice_hbm, weight_hbm, grad_hbm, tokens_hbm, down_hbm, top, rest,
                   choice_ref, weight_ref, grad_ref, tokens_ref, down_ref, sems):
    half = grad_ref.shape[1] // 2
    rank = down_ref.shape[0]
    pairs = [
        (choice_hbm, choice_ref),
        (grad_hbm.at[:, :half], grad_ref.at[:, :half]),
        (grad_hbm.at[:, half:], grad_ref.at[:, half:]),
        (weight_hbm, weight_ref),
        (down_hbm, down_ref),
        (tokens_hbm, tokens_ref),
    ]
    copies = [pltpu.make_async_copy(a, b, sems.at[i]) for i, (a, b) in enumerate(pairs)]
    for copy in copies:
        copy.start()
    copies[0].wait()
    choice = choice_ref[...]
    upper, lower = pick_rows(choice, capacity)
    copies[1].wait()
    first = dot(upper, grad_ref[:, :half])
    copies[2].wait()
    rows = (first + dot(lower, grad_ref[:, half:])).astype(BF)
    cut = top.shape[0]
    top[:, :half] = rows[:cut]
    rest[:, :half] = rows[cut:]
    copies[3].wait()
    weight = jnp.sum(
        jnp.where(choice == 0, weight_ref[...].astype(F32), 0.0), axis=0, keepdims=True
    )
    column = jnp.sum(upper.astype(F32) * weight, axis=1, keepdims=True)
    column = jnp.broadcast_to(column, (2 * capacity, rank)).astype(BF)
    top[:, half + rank :] = column[:cut]
    rest[:, half + rank :] = column[cut:]
    copies[4].wait()
    copies[5].wait()
    low = dot(tokens_ref[...], down_ref[...], NT).astype(BF)
    low = dot(upper, low).astype(BF)
    top[:, half : half + rank] = low[:cut]
    rest[:, half : half + rank] = low[cut:]


def place_here(place):
    me = lax.axis_index("expert")
    return me, sum(jnp.where(me == e, p, 0) for e, p in enumerate(place))


def reorder_kernel(place, capacity, gate_in, up_in, gate_out, up_out, tall):
    count, slot, hidden = gate_out.shape
    _, here = place_here(place)
    live = lax.broadcasted_iota(jnp.int32, (slot, hidden), 0) < capacity
    for source, target in ((gate_in, gate_out), (up_in, up_out)):
        tall[: count * capacity, :] = source[...].astype(F32)
        tall[count * capacity :, :] = jnp.zeros((slot, hidden), F32)
        for e in range(count):
            away = lax.rem(place[e] - here + count, count)
            at = jnp.where(2 * away < count, 2 * away, 2 * (count - away) - 1)
            rows = tall[e * capacity : e * capacity + slot, :]
            target[at] = jnp.where(live, rows, 0.0).astype(BF)


def low_order_kernel(ring, place, order, *refs):
    lows, (keep, send) = refs[:-2], refs[-2:]
    count = len(ring)
    me, here = place_here(place)
    for low, r in zip(lows, order):
        spot = lax.rem(here + r + count, count)
        owner = sum(jnp.where(spot == i, e, 0) for i, e in enumerate(ring))
        key = owner ^ me

        @pl.when(key % 2 == 0)
        def _(low=low, key=key):
            keep[key // 2] = low[...]

        @pl.when(key % 2 == 1)
        def _(low=low, key=key):
            send[key // 2] = low[...]


def halve_kernel(ours, theirs, *outs):
    count = ours.shape[0]
    for i in range(count):
        total = ours[i].astype(F32) + theirs[i].astype(F32)
        out = outs[i % len(outs)]
        out[i // len(outs)] = total.astype(out.dtype)


def hidden_kernel(capacity, slot, start, count, *refs):
    tops, rests, refs = refs[:count], refs[count : 2 * count], refs[2 * count :]
    (gate_ref, up_ref, down_ref, lora_gate, lora_up, dgate_ref, dup_ref, low_ref), refs = refs[:8], refs[8:]
    lows, rows = refs[:count], refs[count]
    hidden, width = down_ref.shape
    half = width // 2
    rank = lora_gate.shape[0]
    cut = tops[0].shape[0]
    tall = rows.shape[0] // count
    for i in range(count):
        rows[i * tall : i * tall + cut, :] = tops[i][:, :half]
        rows[i * tall + cut : i * tall + 2 * capacity, :] = rests[i][:, :half]
    first = dot(down_ref[:, :half], rows[...], NT).T
    second = dot(down_ref[:, half:], rows[...], NT).T
    live = lax.broadcasted_iota(jnp.int32, (slot, hidden), 0) < capacity
    for i in range(count):
        at = i * tall
        extra = tops[i][:, half:], rests[i][: slot - cut, half:]
        low_ref[i, :cut, :] = extra[0][:, :rank]
        low_ref[i, cut:, :] = extra[1][:, :rank]
        weight = jnp.concatenate([x.astype(F32)[:, rank : rank + 1] for x in extra], axis=0)
        grad = (first[at : at + slot] + second[at + capacity : at + capacity + slot]) * weight
        grad = jnp.where(live, grad, 0.0)
        gate = gate_ref[start + i].astype(F32)
        up = up_ref[start + i].astype(F32)
        sig = 1.0 / (1.0 + jnp.exp(-gate))
        slope = sig * (1.0 + gate * (1.0 - sig))
        dgate = (grad * up * slope).astype(BF)
        dup = (grad * gate * sig).astype(BF)
        dgate_ref[i] = dgate
        dup_ref[i] = dup
        lows[i][...] = SCALE * (dot(dgate, lora_gate[...], NT) + dot(dup, lora_up[...], NT))


def stack(groups, slot, sources, target):
    at = 0
    for size, source in zip(groups, sources):
        for i in range(size):
            target[at : at + slot, :] = source[i]
            at += slot


def lora_kernel(slot, groups, *refs):
    pieces = len(groups)
    dgates, dups, lows = refs[:pieces], refs[pieces : 2 * pieces], refs[2 * pieces : 3 * pieces]
    lora_out, dgate, dup, low = refs[3 * pieces :]
    rank = lora_out.shape[0] // 2
    stack(groups, slot, dgates, dgate)
    stack(groups, slot, dups, dup)
    stack(groups, slot, lows, low)
    lora_out[:rank, :] = (SCALE * dot(low[...], dgate[...], TN)).astype(BF)
    lora_out[rank:, :] = (SCALE * dot(low[...], dup[...], TN)).astype(BF)


def first_partial_kernel(capacity, slot, cut, dgate_in, dup_in, gate_ref, up_ref, top, rest, dgate, dup, tile):
    half = gate_ref.shape[0] // 2
    dgate[:slot, :] = dgate_in[0]
    dup[:slot, :] = dup_in[0]
    step = tile.shape[1]
    for t in range(0, half, step):
        for at, place in ((t, 0), (t + half, capacity)):
            total = dot(gate_ref[at : at + step, :], dgate[...], NT) + dot(up_ref[at : at + step, :], dup[...], NT)
            tile[place : place + capacity, :] = total.T[:capacity]
        top[:, t : t + step] = tile[:cut, :].astype(BF)
        rest[:, t : t + step] = tile[cut:, :].astype(BF)


def partial_kernel(capacity, slot, groups, *refs):
    members, pieces = sum(groups), len(groups)
    dgates, dups, refs = refs[:pieces], refs[pieces : 2 * pieces], refs[2 * pieces :]
    gate_ref, up_ref, outs, (dgate, dup, tile) = refs[0], refs[1], refs[2:-3], refs[-3:]
    half = gate_ref.shape[0] // 2
    stack(groups, slot, dgates, dgate)
    stack(groups, slot, dups, dup)

    for t in range(0, half, TILE):
        sums = []
        for at in (t, t + half):
            sums.append(
                dot(dgate[...], gate_ref[at : at + TILE, :], NT)
                + dot(dup[...], up_ref[at : at + TILE, :], NT)
            )
        for i in range(members):
            at = i * slot
            tile[:capacity, :] = sums[0][at : at + capacity]
            tile[capacity:, :] = sums[1][at : at + capacity]
            cut = outs[2 * i].shape[0]
            outs[2 * i][:, t : t + TILE] = tile[:cut, :].astype(BF)
            outs[2 * i + 1][:, t : t + TILE] = tile[cut:, :].astype(BF)


def adapter_kernel(capacity, choice_ref, tokens_ref, low_in, low_ref, keep_ref, send_ref):
    count, part, share = keep_ref.shape
    low = low_in[0].astype(BF)
    low_ref[...] = low
    upper, _ = pick_rows(choice_ref[...], capacity)
    low = dot(upper[: low.shape[0]], low, TN).astype(BF)
    me, core = lax.axis_index("expert"), lax.axis_index("dp")
    for i in range(count):
        columns = pl.ds(pl.multiple_of((me ^ i) * share, 128), share)
        down = dot(low, tokens_ref[:, columns], TN)
        keep_ref[i] = jnp.where(core == 0, down[:part], down[part:]).astype(BF)
        send_ref[i] = jnp.where(core == 0, down[part:], down[:part]).astype(BF)


def join_kernel(down_ref, there_ref, lora_ref, lora_there, down_out, gate_out, up_out):
    part = down_ref.shape[0]
    core = lax.axis_index("dp")
    down, there = down_ref[...].astype(F32), there_ref[...].astype(F32)
    down_out[:part, :] = jnp.where(core == 0, down, there)
    down_out[part:, :] = jnp.where(core == 0, there, down)
    rank = gate_out.shape[0]
    gate_out[...] = lora_ref[:rank, :].astype(F32) + lora_there[:rank, :].astype(F32)
    up_out[...] = lora_ref[rank:, :].astype(F32) + lora_there[rank:, :].astype(F32)


def finish_kernel(capacity, choice_ref, *refs):
    tops, rests, (low_ref, down_ref, out_ref, low_tall) = refs[:3], refs[3:6], refs[6:]
    cut, half = tops[0].shape
    upper, lower = pick_rows(choice_ref[...], capacity)
    low = low_ref[...].astype(F32)[:capacity]
    zero = jnp.zeros_like(low)
    low_tall[:capacity, :] = low
    low_tall[capacity:, :] = zero
    low_upper = low_tall[...].astype(BF)
    low_tall[:capacity, :] = zero
    low_tall[capacity:, :] = low
    low_lower = low_tall[...].astype(BF)
    adapter = dot(low_upper, down_ref[:, :half]) + dot(low_lower, down_ref[:, half:])
    top = sum(x[...].astype(F32) for x in tops) + adapter[:cut]
    rest = sum(x[...].astype(F32) for x in rests) + adapter[cut:]
    top, rest = top.astype(BF), rest.astype(BF)
    for pick, at in ((upper, 0), (lower, half)):
        picked = dot(pick[:cut], top, TN) + dot(pick[cut:], rest, TN)
        out_ref[:, at : at + half] = picked.astype(BF)


def in_hbm(x):
    return pltpu.with_memory_space_constraint(x, pltpu.HBM)


def in_vmem(x):
    return pltpu.with_memory_space_constraint(x, pltpu.VMEM)


def on_device(
    ring,
    tokens,
    output_gradient,
    token_expert_choice,
    routing_weight_table,
    stored_gate_rows,
    stored_up_rows,
    gate_weight,
    up_weight,
    down_weight,
    adapter_down_factor,
    adapter_gate_factor,
    adapter_up_factor,
):
    n = len(ring)
    tokens, output_gradient = tokens[0], output_gradient[0]
    own_count, width = tokens.shape
    half = width // 2
    capacity = stored_gate_rows.shape[1] // n
    hidden = stored_gate_rows.shape[2]
    rank = adapter_down_factor.shape[0]
    tall = -(-2 * capacity // 128) * 128
    slot = -(-capacity // 8) * 8
    cut = capacity // 16 * 16
    wide = half + 2 * rank
    middle = n // 2
    choice = token_expert_choice[0].T
    weights = routing_weight_table[0].T

    place = [0] * n
    for i, e in enumerate(ring):
        place[e] = i
    to_right = [(ring[i], ring[(i + 1) % n]) for i in range(n)]
    to_left = [(ring[i], ring[(i - 1) % n]) for i in range(n)]
    passes = [[0]] + [[-s, s] for s in range(1, middle)] + [[middle]]
    sizes = [len(group) for group in passes]
    order = [r for group in passes for r in group]
    heights = [cut, 2 * capacity - cut]

    def call(kernel, name, shapes, args, scratch=(), work=(0, 0), **more):
        return pl.pallas_call(
            kernel,
            out_shape=[jax.ShapeDtypeStruct(shape, dtype) for shape, dtype in shapes],
            scratch_shapes=list(scratch),
            compiler_params=pltpu.CompilerParams(vmem_limit_bytes=VMEM_LIMIT),
            cost_estimate=pl.CostEstimate(
                flops=int(work[0]), bytes_accessed=int(work[1]), transcendentals=0
            ),
            name=name,
            **more,
        )(*args)

    def right(x):
        return lax.ppermute(x, "expert", to_right)

    def left(x):
        return lax.ppermute(x, "expert", to_left)

    block = call(
        functools.partial(prepare_kernel, capacity),
        "prepare",
        [((h, wide), BF) for h in heights],
        [in_hbm(x) for x in (choice, weights, output_gradient, tokens, adapter_down_factor)],
        [
            pltpu.VMEM(choice.shape, choice.dtype),
            pltpu.VMEM(weights.shape, BF),
            pltpu.VMEM(output_gradient.shape, BF),
            pltpu.VMEM(tokens.shape, BF),
            pltpu.VMEM(adapter_down_factor.shape, BF),
            pltpu.SemaphoreType.DMA((6,)),
        ],
        (4e8, 4.5e6),
        in_specs=[pl.BlockSpec(memory_space=pl.ANY)] * 5,
    )
    gate_rows, up_rows = call(
        functools.partial(reorder_kernel, place, capacity),
        "reorder",
        [((n, slot, hidden), BF)] * 2,
        [stored_gate_rows[0], stored_up_rows[0]],
        [pltpu.VMEM((n * capacity + slot, hidden), F32)],
        (0, 8 * n * slot * hidden),
    )

    down_here, gate_here, up_here = in_vmem(down_weight), in_vmem(gate_weight), in_vmem(up_weight)
    dgates, dups, low_rows, lows = [], [], [], []
    got = {0: tuple(block)}

    def hidden_pass(group):
        size, start = len(group), len(lows)
        results = call(
            functools.partial(hidden_kernel, capacity, slot, start, size),
            "hidden_rows",
            [((size, slot, hidden), BF)] * 2
            + [((size, slot, rank), BF)]
            + [((slot, rank), F32)] * size,
            [got[r][0] for r in group]
            + [got[r][1] for r in group]
            + [gate_rows, up_rows, down_here, adapter_gate_factor, adapter_up_factor],
            [pltpu.VMEM((size * tall, half), BF)],
            (2 * size * tall * width * hidden, 2 * hidden * width),
        )
        dgates.append(results[0])
        dups.append(results[1])
        low_rows.append(results[2])
        lows.extend(results[3:])

    right_top, right_rest = left_top, left_rest = block
    for s in range(1, middle + 1):
        right_top, left_rest = right(right_top), left(left_rest)
        if s < middle:
            right_rest, left_top = right(right_rest), left(left_top)
        hidden_pass(passes[s - 1])
        if s < middle:
            right_rest, left_top, dgates[-1], dups[-1] = lax.optimization_barrier(
                (right_rest, left_top, dgates[-1], dups[-1])
            )
            got[-s], got[s] = (right_top, right_rest), (left_top, left_rest)
        else:
            right_top, left_rest, dgates[-1], dups[-1] = lax.optimization_barrier(
                (right_top, left_rest, dgates[-1], dups[-1])
            )
    got[middle] = (right_top, left_rest)
    hidden_pass(passes[-1])

    low_keep, low_send = call(
        functools.partial(low_order_kernel, ring, place, order),
        "low_order",
        [((n // 2, slot, rank), F32)] * 2,
        lows,
    )

    right_top, left_rest = call(
        functools.partial(first_partial_kernel, capacity, slot, cut),
        "first_partial",
        [((h, half), BF) for h in heights],
        [dgates[-1], dups[-1], gate_here, up_here],
        [
            pltpu.VMEM((128, hidden), BF),
            pltpu.VMEM((128, hidden), BF),
            pltpu.VMEM((2 * capacity, half // 2), F32),
        ],
        (4 * slot * width * hidden, 4 * hidden * width),
    )
    own = call(
        functools.partial(partial_kernel, capacity, slot, sizes[:-1]),
        "partials",
        [((h, half), BF) for h in heights] * (n - 1),
        [*dgates[:-1], *dups[:-1], gate_here, up_here],
        [
            pltpu.VMEM(((n - 1) * slot, hidden), BF),
            pltpu.VMEM(((n - 1) * slot, hidden), BF),
            pltpu.VMEM((2 * capacity, TILE), F32),
        ],
        (4 * (n - 1) * slot * width * hidden, 4 * hidden * width),
    )

    def add(a, b):
        return (a.astype(F32) + b.astype(F32)).astype(BF)

    def exchange(keep, send, bit):
        other = lax.ppermute(send, "expert", [(e, e ^ bit) for e in range(n)])
        count = keep.shape[0]
        parts = 2 if count > 1 else 1
        shape = (count // parts,) + keep.shape[1:]
        return list(call(halve_kernel, "halve", [(shape, keep.dtype)] * parts, [keep, other]))

    low_keep, right_top, left_rest = lax.optimization_barrier((low_keep, right_top, left_rest))
    right_top, left_rest = right(right_top), left(left_rest)
    low_keep, low_send = exchange(low_keep, low_send, 1)
    right_top, left_rest, low_keep, own = lax.optimization_barrier((right_top, left_rest, low_keep, own))
    own = {r: (own[2 * i], own[2 * i + 1]) for i, r in enumerate(order[:-1])}
    pair = exchange(low_keep, low_send, 2)
    for s in range(middle - 1, 0, -1):
        right_top, left_rest = add(right_top, own[s][0]), add(left_rest, own[-s][1])
        if s == middle - 1:
            right_rest, left_top = own[s][1], own[-s][0]
            pair[0], right_top, left_rest = lax.optimization_barrier((pair[0], right_top, left_rest))
        else:
            right_rest, left_top = add(right_rest, own[s][1]), add(left_top, own[-s][0])
        right_top, left_rest = right(right_top), left(left_rest)
        right_rest, left_top = right(right_rest), left(left_top)
    bit = 4
    while bit < n:
        pair = exchange(*pair, bit)
        bit *= 2
    low_total = pair[0]

    share = width // n
    part = rank // 2
    swap = [(0, 1), (1, 0)]
    if share % 128 == 0:
        low, keep, send = call(
            functools.partial(adapter_kernel, capacity),
            "adapter_gradient",
            [((slot, rank), BF)] + [((n, part, share), BF)] * 2,
            [choice, tokens, low_total],
            work=(2 * own_count * rank * width, 2 * own_count * width),
        )
    else:
        me, core = lax.axis_index("expert"), lax.axis_index("dp")
        upper, _ = pick_rows(choice, capacity)
        low = low_total[0].astype(BF)
        low_tokens = dot(upper[:slot], low, TN).astype(BF)
        down = dot(low_tokens, tokens, TN).astype(BF).reshape(rank, n, share)
        down = down.transpose(1, 0, 2)[jnp.arange(n, dtype=jnp.int32) ^ me]
        keep = jnp.where(core == 0, down[:, :part], down[:, part:])
        send = jnp.where(core == 0, down[:, part:], down[:, :part])
    other = lax.ppermute(send, "dp", swap)
    pair = call(halve_kernel, "halve", [((n // 2, part, share), BF)] * 2, [keep, other])
    low_rows, _ = lax.optimization_barrier((low_rows, pair))
    (lora,) = call(
        functools.partial(lora_kernel, slot, sizes),
        "lora_rows",
        [((2 * rank, hidden), BF)],
        [*dgates, *dups, *low_rows],
        [
            pltpu.VMEM((n * slot, hidden), BF),
            pltpu.VMEM((n * slot, hidden), BF),
            pltpu.VMEM((n * slot, rank), BF),
        ],
        (4 * n * slot * rank * hidden, 4 * n * slot * hidden),
    )
    lora_there = lax.ppermute(lora, "dp", swap)
    bit = 1
    while bit < n:
        pair = exchange(*pair, bit)
        bit *= 2
    down = pair[0][0]
    there = lax.ppermute(down, "dp", swap)
    grad_down, grad_gate, grad_up = call(
        join_kernel,
        "join",
        [((rank, hidden), F32)] * 3,
        [down, there, lora, lora_there],
    )

    (input_gradient,) = call(
        functools.partial(finish_kernel, capacity),
        "finish",
        [((own_count, width), BF)],
        [choice, right_top, left_top, own[0][0], right_rest, left_rest, own[0][1], low, adapter_down_factor],
        [pltpu.VMEM((2 * capacity, rank), F32)],
        (4e8, 4.5e6),
    )
    return (input_gradient[None], grad_down, grad_gate, grad_up)


def solution(mesh):
    placed = (
        P(("groups", "dp"), "expert", None),
        P(("groups", "dp"), "expert", None),
        P(("groups", "dp"), "expert", None),
        P(("groups", "dp"), "expert", None),
        P(("groups", "dp"), None, "expert"),
        P(("groups", "dp"), None, "expert"),
        P(None, "expert"),
        P(None, "expert"),
        P("expert", None),
        P("groups", None),
        P("groups", "expert"),
        P("groups", "expert"),
    )
    return jax.shard_map(
        functools.partial(on_device, ring_order(mesh)),
        mesh=mesh,
        in_specs=placed,
        out_specs=(
            P(("groups", "dp"), "expert", None),
            P("groups", "expert"),
            P("groups", "expert"),
            P("groups", "expert"),
        ),
        check_vma=False,
    )
```

time: 133 us -> 118 us (0.89)
  local copies, waits for them, and re-layouts: 27.6 us -> 7.55 us
  starting transfers between devices: 31.9 us -> 42.5 us
  waiting for transfers between devices: 35.5 us -> 30.9 us
  other arithmetic: 2.16 us -> 0.56 us
    unnamed x38 -> x34, local copies, waits for them, and re-layouts: 22.3 us -> 7.55 us
    ppermute x28 -> x36, starting transfers between devices: 31.8 us -> 41.9 us  [the longest x14 18.1 us: left(): return lax.ppermute(x, 'expert', to_left)]
    ppermute x28 -> x36, waiting for transfers between devices: 35 us -> 30.8 us  [the longest x14 15.5 us: left(): return lax.ppermute(x, 'expert', to_left)]
    another operation x2 -> x0, local copies, waits for them, and re-layouts: 2.2 us -> none  [in_order(): rows = stored[0].reshape(n, capacity, hidden)[owners]]
    slice x5 -> x0, local copies, waits for them, and re-layouts: 1.91 us -> none  [the longest x2 1.11 us: hidden_pass(): up_rows[start:start + size]]
    pallas_call x13 -> x21, Pallas kernels: 34.2 us -> 34.4 us  [call(): pl.pallas_call(kernel, out_shape=[jax.ShapeDtypeStruct(shape, dtype) for...]
  transfers between devices with their start and end apart: 29 -> 37, of which waited for: 9 -> 15; matrix products, arithmetic and copies ran while one was open for 6% -> 0% of each run, Pallas kernels for 21% -> 23%
where the time goes in v5:
time: 118 us; the launch traced here: 117 us
  starting transfers between devices  42.5 us (36%)
  Pallas kernels  34.4 us (29%)
  waiting for transfers between devices  30.9 us (26%)
  local copies, waits for them, and re-layouts  7.55 us (6%)
    pallas_call x21, Pallas kernels, call(): pl.pallas_call(kernel, out_shape=[jax.ShapeDtypeStruct(shape, dtype) for...  34.4 us
    ppermute x14, starting transfers between devices, left(): return lax.ppermute(x, 'expert', to_left)  18.1 us
    ppermute x14, starting transfers between devices, right(): return lax.ppermute(x, 'expert', to_right)  16.1 us
    ppermute x14, waiting for transfers between devices, left(): return lax.ppermute(x, 'expert', to_left)  15.5 us
    ppermute x6, waiting for transfers between devices, exchange(): other = lax.ppermute(send, 'expert', [(e, e ^ bit) for e in range(n)])  8.41 us
    ppermute x6, starting transfers between devices, exchange(): other = lax.ppermute(send, 'expert', [(e, e ^ bit) for e in range(n)])  7.58 us
    unnamed x34, local copies, waits for them, and re-layouts  7.55 us
    ppermute x14, waiting for transfers between devices, right(): return lax.ppermute(x, 'expert', to_right)  6.96 us
  transfers between devices with their start and end apart: 37, of which 15 were waited for; matrix products, arithmetic and copies ran while one was open for 0% of the time, Pallas kernels for 23%

profile of v5, /device:TPU:0, one launch (start us, length us, event | category | flops | bytes accessed | tf_op | source)
XLA Modules:
  0.0 116.8 jit_solution(2179497342427391983)
XLA Ops:
  0.7 2.9 %prepare.1 = (bf16[32,3200]{1,0:T(8,128)(2,1)S(1)}, bf16[40,3200]{1,0:T(8,128)(2,1)S(1)}) custom-call(s32[4,128]{1,0:T(4,128)} %bitcast.22, bf16[4,128]{1,0:T(4,128)(2,1)} %bitcast.27, bf16[128,6144]{1,0:T(8,128)(2,1)} %bitcast.26, bf16[128,6144]{1,0:T(8,128)(2,1)} %bitcast.16, bf16[64,6144]{1,0:T(8,128)(2,1)} %refs_7_.7), custom_call_target="tpu_custom_call" | custom-call | flops 400000000 | bytes 4500000 | tf_op jit(solution)/shard_map/prepare/pallas_call | solution.py:326
  3.6 3.0 %collective-permute-start.3 = (bf16[40,3200]{1,0:T(8,128)(2,1)S(1)}, bf16[40,3200]{1,0:T(8,128)(2,1)S(1)}, u32[]{:S(2)}, u32[]{:S(2)}) collective-permute-start(bf16[40,3200]{1,0:T(8,128)(2,1)S(1)} %get-tuple-element.110.refs_1_), channel_id=1, source_target_pairs={{0,2},{4,0},{8,4},{12,8},{14,12},{10,14},{6,10},{2,6},{1,3},{5,1},... | collective-permute-start | bytes 768008 | tf_op jit(solution)/shard_map/ppermute | solution.py:342
  6.8 6.1 %collective-permute-done.3.refs_3_ = bf16[40,3200]{1,0:T(8,128)(2,1)S(1)} collective-permute-done((bf16[40,3200]{1,0:T(8,128)(2,1)S(1)}, bf16[40,3200]{1,0:T(8,128)(2,1)S(1)}, u32[]{:S(2)}, u32[]{:S(2)}) %collective-permute-start.3) | collective-permute-done | bytes 256032 | tf_op jit(solution)/shard_map/ppermute | solution.py:342
  18.8 3.7 %copy-done = bf16[768,6144]{1,0:T(8,128)(2,1)S(1)} copy-done((bf16[768,6144]{1,0:T(8,128)(2,1)S(1)}, bf16[768,6144]{1,0:T(8,128)(2,1)}, u32[]{:S(2)}) %copy-start) | copy-done | bytes 9437208
  24.3 2.9 %hidden_rows.5 = (bf16[1,40,768]{2,1,0:T(8,128)(2,1)S(1)}, bf16[1,40,768]{2,1,0:T(8,128)(2,1)S(1)}, bf16[1,40,64]{2,1,0:T(8,128)(2,1)S(1)}, f32[40,64]{1,0:T(8,128)S(1)}) custom-call(bf16[32,3200]{1,0:T(8,128)(2,1)S(1)} %get-tuple-element.109.refs_0_, bf16[40,3200]{1,0:T(8,128)(2,1)S(1)} %get-tuple-element.110.refs_1_, ...), custom_call_target="tpu_custom_call" | custom-call | flops 1207959552 | bytes 9437184 | tf_op jit(solution)/shard_map/hidden_rows/pallas_call | solution.py:326
  27.6 1.7 %collective-permute-start.4 = (bf16[32,3200]{1,0:T(8,128)(2,1)S(1)}, bf16[32,3200]{1,0:T(8,128)(2,1)S(1)}, u32[]{:S(2)}, u32[]{:S(2)}) collective-permute-start(bf16[32,3200]{1,0:T(8,128)(2,1)S(1)} %collective-permute-done.refs_0_), channel_id=1, source_target_pairs={{0,4},{4,8},{8,12},{12,14},{14,10},{10,6},{6,2},{2,0},{1,5},{5,9},... | collective-permute-start | bytes 614408 | tf_op jit(solution)/shard_map/ppermute | solution.py:339
  31.3 3.1 %hidden_rows.6 = (bf16[2,40,768]{2,1,0:T(8,128)(2,1)S(1)}, bf16[2,40,768]{2,1,0:T(8,128)(2,1)S(1)}, bf16[2,40,64]{2,1,0:T(8,128)(2,1)S(1)}, f32[40,64]{1,0:T(8,128)S(1)}, f32[40,64]{1,0:T(8,128)S(1)}) custom-call(bf16[32,3200]{1,0:T(8,128)(2,1)S(1)} %collective-permute-done.refs_0_, bf16[32,3200]{1,0:T(8,128)(2,1)S(1)} %collective-permute-done.2.refs_1_, ...), custom_call_target="tpu_custom_call" | custom-call | flops 2415919104 | bytes 9437184 | tf_op jit(solution)/shard_map/hidden_rows/pallas_call | solution.py:326
  34.4 2.2 %collective-permute-done.6.refs_1_ = bf16[32,3200]{1,0:T(8,128)(2,1)S(1)} collective-permute-done((bf16[32,3200]{1,0:T(8,128)(2,1)S(1)}, bf16[32,3200]{1,0:T(8,128)(2,1)S(1)}, u32[]{:S(2)}, u32[]{:S(2)}) %collective-permute-start.6) | collective-permute-done | bytes 204832 | tf_op jit(solution)/shard_map/ppermute | solution.py:342
  38.2 2.6 %collective-permute-done.4.refs_0_ = bf16[32,3200]{1,0:T(8,128)(2,1)S(1)} collective-permute-done((bf16[32,3200]{1,0:T(8,128)(2,1)S(1)}, bf16[32,3200]{1,0:T(8,128)(2,1)S(1)}, u32[]{:S(2)}, u32[]{:S(2)}) %collective-permute-start.4) | collective-permute-done | bytes 204832 | tf_op jit(solution)/shard_map/ppermute | solution.py:339
  41.0 1.8 %collective-permute-start.10 = (bf16[32,3200]{1,0:T(8,128)(2,1)S(1)}, bf16[32,3200]{1,0:T(8,128)(2,1)S(1)}, u32[]{:S(2)}, u32[]{:S(2)}) collective-permute-start(bf16[32,3200]{1,0:T(8,128)(2,1)S(1)} %collective-permute-done.6.refs_1_), channel_id=1, source_target_pairs={{0,2},{4,0},{8,4},{12,8},{14,12},{10,14},{6,10},{2,6},{1,3},{5,1},... | collective-permute-start | bytes 614408 | tf_op jit(solution)/shard_map/ppermute | solution.py:342
  44.4 3.1 %hidden_rows.7 = (bf16[2,40,768]{2,1,0:T(8,128)(2,1)S(1)}, bf16[2,40,768]{2,1,0:T(8,128)(2,1)S(1)}, bf16[2,40,64]{2,1,0:T(8,128)(2,1)S(1)}, f32[40,64]{1,0:T(8,128)S(1)}, f32[40,64]{1,0:T(8,128)S(1)}) custom-call(bf16[32,3200]{1,0:T(8,128)(2,1)S(1)} %collective-permute-done.4.refs_0_, bf16[32,3200]{1,0:T(8,128)(2,1)S(1)} %collective-permute-done.6.refs_1_, ...), custom_call_target="tpu_custom_call" | custom-call | flops 2415919104 | bytes 9437184 | tf_op jit(solution)/shard_map/hidden_rows/pallas_call | solution.py:326
  48.9 3.1 %hidden_rows.8 = (bf16[2,40,768]{2,1,0:T(8,128)(2,1)S(1)}, bf16[2,40,768]{2,1,0:T(8,128)(2,1)S(1)}, bf16[2,40,64]{2,1,0:T(8,128)(2,1)S(1)}, f32[40,64]{1,0:T(8,128)S(1)}, f32[40,64]{1,0:T(8,128)S(1)}) custom-call(bf16[32,3200]{1,0:T(8,128)(2,1)S(1)} %collective-permute-done.8.refs_0_, bf16[32,3200]{1,0:T(8,128)(2,1)S(1)} %collective-permute-done.10.refs_1_, ...), custom_call_target="tpu_custom_call" | custom-call | flops 2415919104 | bytes 9437184 | tf_op jit(solution)/shard_map/hidden_rows/pallas_call | solution.py:326
  53.6 2.9 %hidden_rows.9 = (bf16[1,40,768]{2,1,0:T(8,128)(2,1)S(1)}, bf16[1,40,768]{2,1,0:T(8,128)(2,1)S(1)}, bf16[1,40,64]{2,1,0:T(8,128)(2,1)S(1)}, f32[40,64]{1,0:T(8,128)S(1)}) custom-call(bf16[32,3200]{1,0:T(8,128)(2,1)S(1)} %collective-permute-done.12.refs_0_, bf16[40,3200]{1,0:T(8,128)(2,1)S(1)} %collective-permute-done.13.refs_1_, ...), custom_call_target="tpu_custom_call" | custom-call | flops 1207959552 | bytes 9437184 | tf_op jit(solution)/shard_map/hidden_rows/pallas_call | solution.py:326
  58.6 5.3 %first_partial.1 = (bf16[32,3072]{1,0:T(8,128)(2,1)S(1)}, bf16[40,3072]{1,0:T(8,128)(2,1)S(1)}) custom-call(bf16[1,40,768]{2,1,0:T(8,128)(2,1)S(1)} %get-tuple-element.138.dgate_in.refs_4_, bf16[1,40,768]{2,1,0:T(8,128)(2,1)S(1)} %get-tuple-element.139.dup_in.refs_9_, bf16[6144,768]{1,0:T(8,128)(2,1)S(1)} %bitcast.13, bf16[6144,768]{1,0:T(8,128)(2,1)S(1)} %bitcast.15), custom_call_target="tpu_custom_call" | custom-call | flops 754974720 | bytes 18874368 | tf_op jit(solution)/shard_map/first_partial/pallas_call | solution.py:326
  67.7 5.9 %partials.1 = (bf16[32,3072]{1,0:T(8,128)(2,1)S(1)}, bf16[40,3072]{1,0:T(8,128)(2,1)S(1)}, bf16[32,3072]{1,0:T(8,128)(2,1)S(1)}, bf16[40,3072]{1,0:T(8,128)(2,1)...) custom-call(bf16[1,40,768]{2,1,0:T(8,128)(2,1)S(1)} %get-tuple-eleme, ...), custom_call_target="tpu_custom_call" | custom-call | flops 5284823040 | bytes 18874368 | tf_op jit(solution)/shard_map/partials/pallas_call | solution.py:326
  86.2 2.6 %collective-permute-done.22 = bf16[32,3072]{1,0:T(8,128)(2,1)S(1)} collective-permute-done((bf16[32,3072]{1,0:T(8,128)(2,1)S(1)}, bf16[32,3072]{1,0:T(8,128)(2,1)S(1)}, u32[]{:S(2)}, u32[]{:S(2)}) %collective-permute-start.22) | collective-permute-done | bytes 196640 | tf_op jit(solution)/shard_map/ppermute | solution.py:342
  90.6 3.5 %collective-permute-done.28 = bf16[40,3072]{1,0:T(8,128)(2,1)S(1)} collective-permute-done((bf16[40,3072]{1,0:T(8,128)(2,1)S(1)}, bf16[40,3072]{1,0:T(8,128)(2,1)S(1)}, u32[]{:S(2)}, u32[]{:S(2)}) %collective-permute-start.28) | collective-permute-done | bytes 245792 | tf_op jit(solution)/shard_map/ppermute | solution.py:342
  95.2 5.8 %collective-permute-done.32.theirs = bf16[4,32,768]{2,1,0:T(8,128)(2,1)S(1)} collective-permute-done((bf16[4,32,768]{2,1,0:T(8,128)(2,1)S(1)}, bf16[4,32,768]{2,1,0:T(8,128)(2,1)S(1)}, u32[]{:S(2)}, u32[]{:S(2)}) %collective-permute-start.32) | collective-permute-done | bytes 196640 | tf_op jit(solution)/shard_map/ppermute | solution.py:446
  101.2 2.1 %collective-permute-start.26 = (bf16[40,3072]{1,0:T(8,128)(2,1)S(1)}, bf16[40,3072]{1,0:T(8,128)(2,1)S(1)}, u32[]{:S(2)}, u32[]{:S(2)}) collective-permute-start(bf16[40,3072]{1,0:T(8,128)(2,1)S(1)} %add_convert_fusion.2), channel_id=1, source_target_pairs={{0,4},{4,8},{8,12},{12,14},{14,10},{10,6},{6,2},{2,0},{1,5},{5,9},... | collective-permute-start | bytes 737288 | tf_op jit(solution)/shard_map/ppermute | solution.py:339
  103.2 2.5 %collective-permute-done.33.theirs = bf16[2,32,768]{2,1,0:T(8,128)(2,1)S(1)} collective-permute-done((bf16[2,32,768]{2,1,0:T(8,128)(2,1)S(1)}, bf16[2,32,768]{2,1,0:T(8,128)(2,1)S(1)}, u32[]{:S(2)}, u32[]{:S(2)}) %collective-permute-start.33) | collective-permute-done | bytes 98336 | tf_op jit(solution)/shard_map/ppermute | solution.py:446
  105.8 2.0 %collective-permute-start.34 = (bf16[1,32,768]{2,1,0:T(8,128)(2,1)S(1)}, bf16[1,32,768]{2,1,0:T(8,128)(2,1)S(1)}, u32[]{:S(2)}, u32[]{:S(2)}) collective-permute-start(bf16[1,32,768]{2,1,0:T(8,128)(2,1)S(1)} %get-tuple-element.200), channel_id=1, source_target_pairs={{0,8},{2,10},{4,12},{6,14},{8,0},{10,2},{12,4},{14,6},{1,9},{3,11}... | collective-permute-start | bytes 147464 | tf_op jit(solution)/shard_map/ppermute | solution.py:446
  107.8 2.5 %collective-permute-start.20 = (bf16[32,3072]{1,0:T(8,128)(2,1)S(1)}, bf16[32,3072]{1,0:T(8,128)(2,1)S(1)}, u32[]{:S(2)}, u32[]{:S(2)}) collective-permute-start(bf16[32,3072]{1,0:T(8,128)(2,1)S(1)} %add_convert_fusion.7), channel_id=1, source_target_pairs={{0,4},{4,8},{8,12},{12,14},{14,10},{10,6},{6,2},{2,0},{1,5},{5,9},... | collective-permute-start | bytes 589832 | tf_op jit(solution)/shard_map/ppermute | solution.py:339
  111.4 2.1 %collective-permute-done.20.refs_0_ = bf16[32,3072]{1,0:T(8,128)(2,1)S(1)} collective-permute-done((bf16[32,3072]{1,0:T(8,128)(2,1)S(1)}, bf16[32,3072]{1,0:T(8,128)(2,1)S(1)}, u32[]{:S(2)}, u32[]{:S(2)}) %collective-permute-start.20) | collective-permute-done | bytes 196640 | tf_op jit(solution)/shard_map/ppermute | solution.py:339
  113.6 2.4 %finish.1 = bf16[128,6144]{1,0:T(8,128)(2,1)} custom-call(s32[4,128]{1,0:T(4,128)S(1)} %bitcast.24, bf16[32,3072]{1,0:T(8,128)(2,1)S(1)} %collective-permute-done.20.refs_0_, bf16[32,3072]{1,0:T(8,128)(2,1)S(1)} %collective-permute-done.23.refs_1_, bf16[32,3072]{1,0:T(8,128)(2,1)S(1)} %get-tuple-element.182.refs_2_, ...), custom_call_target="tpu_custom_call" | custom-call | flops 400000000 | bytes 4500000 | tf_op jit(solution)/shard_map/finish/pallas_call | solution.py:326
  (117 shorter events, 40.0 us)
Async XLA Ops:
  3.6 9.2 %collective-permute-start.3 = (bf16[40,3200]{1,0:T(8,128)(2,1)S(1)}, bf16[40,3200]{1,0:T(8,128)(2,1)S(1)}, u32[]{:S(2)}, u32[]{:S(2)}) collective-permute-start(bf16[40,3200]{1,0:T(8,128)(2,1)S(1)} %get-tuple-element.110.refs_1_), channel_id=1, source_target_pairs={{0,2},{4,0},{8,4},{12,8},{14,12},{10,14},{6,10},{2,6},{1,3},{5,1},... | collective-permute-start | bytes 768008 | tf_op jit(solution)/shard_map/ppermute | solution.py:342
  6.6 20.6 %collective-permute-start.1 = (bf16[40,3200]{1,0:T(8,128)(2,1)S(1)}, bf16[40,3200]{1,0:T(8,128)(2,1)S(1)}, u32[]{:S(2)}, u32[]{:S(2)}) collective-permute-start(bf16[40,3200]{1,0:T(8,128)(2,1)S(1)} %get-tuple-element.110.refs_1_), channel_id=1, source_target_pairs={{0,4},{4,8},{8,12},{12,14},{14,10},{10,6},{6,2},{2,0},{1,5},{5,9},... | collective-permute-start | bytes 768008 | tf_op jit(solution)/shard_map/ppermute | solution.py:339
  12.9 16.8 %collective-permute-start.7 = (bf16[40,3200]{1,0:T(8,128)(2,1)S(1)}, bf16[40,3200]{1,0:T(8,128)(2,1)S(1)}, u32[]{:S(2)}, u32[]{:S(2)}) collective-permute-start(bf16[40,3200]{1,0:T(8,128)(2,1)S(1)} %collective-permute-done.3.refs_3_), channel_id=1, source_target_pairs={{0,2},{4,0},{8,4},{12,8},{14,12},{10,14},{6,10},{2,6},{1,3},{5,1},... | collective-permute-start | bytes 768008 | tf_op jit(solution)/shard_map/ppermute | solution.py:342
  14.5 12.6 %collective-permute-start.2 = (bf16[32,3200]{1,0:T(8,128)(2,1)S(1)}, bf16[32,3200]{1,0:T(8,128)(2,1)S(1)}, u32[]{:S(2)}, u32[]{:S(2)}) collective-permute-start(bf16[32,3200]{1,0:T(8,128)(2,1)S(1)} %get-tuple-element.109.refs_0_), channel_id=1, source_target_pairs={{0,2},{4,0},{8,4},{12,8},{14,12},{10,14},{6,10},{2,6},{1,3},{5,1},... | collective-permute-start | bytes 614408 | tf_op jit(solution)/shard_map/ppermute | solution.py:342
  16.1 11.5 %collective-permute-start = (bf16[32,3200]{1,0:T(8,128)(2,1)S(1)}, bf16[32,3200]{1,0:T(8,128)(2,1)S(1)}, u32[]{:S(2)}, u32[]{:S(2)}) collective-permute-start(bf16[32,3200]{1,0:T(8,128)(2,1)S(1)} %get-tuple-element.109.refs_0_), channel_id=1, source_target_pairs={{0,4},{4,8},{8,12},{12,14},{14,10},{10,6},{6,2},{2,0},{1,5},{5,9},... | collective-permute-start | bytes 614408 | tf_op jit(solution)/shard_map/ppermute | solution.py:339
  27.2 9.4 %collective-permute-start.5 = (bf16[40,3200]{1,0:T(8,128)(2,1)S(1)}, bf16[40,3200]{1,0:T(8,128)(2,1)S(1)}, u32[]{:S(2)}, u32[]{:S(2)}) collective-permute-start(bf16[40,3200]{1,0:T(8,128)(2,1)S(1)} %collective-permute-done.1.refs_2_), channel_id=1, source_target_pairs={{0,4},{4,8},{8,12},{12,14},{14,10},{10,6},{6,2},{2,0},{1,5},{5,9},... | collective-permute-start | bytes 768008 | tf_op jit(solution)/shard_map/ppermute | solution.py:339
  27.6 13.1 %collective-permute-start.4 = (bf16[32,3200]{1,0:T(8,128)(2,1)S(1)}, bf16[32,3200]{1,0:T(8,128)(2,1)S(1)}, u32[]{:S(2)}, u32[]{:S(2)}) collective-permute-start(bf16[32,3200]{1,0:T(8,128)(2,1)S(1)} %collective-permute-done.refs_0_), channel_id=1, source_target_pairs={{0,4},{4,8},{8,12},{12,14},{14,10},{10,6},{6,2},{2,0},{1,5},{5,9},... | collective-permute-start | bytes 614408 | tf_op jit(solution)/shard_map/ppermute | solution.py:339
  29.6 13.1 %collective-permute-start.11 = (bf16[40,3200]{1,0:T(8,128)(2,1)S(1)}, bf16[40,3200]{1,0:T(8,128)(2,1)S(1)}, u32[]{:S(2)}, u32[]{:S(2)}) collective-permute-start(bf16[40,3200]{1,0:T(8,128)(2,1)S(1)} %collective-permute-done.7.refs_3_), channel_id=1, source_target_pairs={{0,2},{4,0},{8,4},{12,8},{14,12},{10,14},{6,10},{2,6},{1,3},{5,1},... | collective-permute-start | bytes 768008 | tf_op jit(solution)/shard_map/ppermute | solution.py:342
  36.6 12.3 %collective-permute-start.9 = (bf16[40,3200]{1,0:T(8,128)(2,1)S(1)}, bf16[40,3200]{1,0:T(8,128)(2,1)S(1)}, u32[]{:S(2)}, u32[]{:S(2)}) collective-permute-start(bf16[40,3200]{1,0:T(8,128)(2,1)S(1)} %collective-permute-done.5.refs_2_), channel_id=1, source_target_pairs={{0,4},{4,8},{8,12},{12,14},{14,10},{10,6},{6,2},{2,0},{1,5},{5,9},... | collective-permute-start | bytes 768008 | tf_op jit(solution)/shard_map/ppermute | solution.py:339
  41.0 7.9 %collective-permute-start.10 = (bf16[32,3200]{1,0:T(8,128)(2,1)S(1)}, bf16[32,3200]{1,0:T(8,128)(2,1)S(1)}, u32[]{:S(2)}, u32[]{:S(2)}) collective-permute-start(bf16[32,3200]{1,0:T(8,128)(2,1)S(1)} %collective-permute-done.6.refs_1_), channel_id=1, source_target_pairs={{0,2},{4,0},{8,4},{12,8},{14,12},{10,14},{6,10},{2,6},{1,3},{5,1},... | collective-permute-start | bytes 614408 | tf_op jit(solution)/shard_map/ppermute | solution.py:342
  42.8 10.8 %collective-permute-start.13 = (bf16[40,3200]{1,0:T(8,128)(2,1)S(1)}, bf16[40,3200]{1,0:T(8,128)(2,1)S(1)}, u32[]{:S(2)}, u32[]{:S(2)}) collective-permute-start(bf16[40,3200]{1,0:T(8,128)(2,1)S(1)} %collective-permute-done.11.refs_3_), channel_id=1, source_target_pairs={{0,2},{4,0},{8,4},{12,8},{14,12},{10,14},{6,10},{2,6},{1,3},{5,1},... | collective-permute-start | bytes 768008 | tf_op jit(solution)/shard_map/ppermute | solution.py:342
  56.9 9.1 %collective-permute-start.16 = (f32[4,40,64]{2,1,0:T(8,128)S(1)}, f32[4,40,64]{2,1,0:T(8,128)S(1)}, u32[]{:S(2)}, u32[]{:S(2)}) collective-permute-start(f32[4,40,64]{2,1,0:T(8,128)S(1)} %get-tuple-element.145), channel_id=1, source_target_pairs={{0,2},{2,0},{4,6},{6,4},{8,10},{10,8},{12,14},{14,12},{1,3},{3,1},... | collective-permute-start | bytes 122888 | tf_op jit(solution)/shard_map/ppermute | solution.py:446
  64.0 9.7 %collective-permute-start.14 = (bf16[32,3072]{1,0:T(8,128)(2,1)S(1)}, bf16[32,3072]{1,0:T(8,128)(2,1)S(1)}, u32[]{:S(2)}, u32[]{:S(2)}) collective-permute-start(bf16[32,3072]{1,0:T(8,128)(2,1)S(1)} %get-tuple-element.142), channel_id=1, source_target_pairs={{0,4},{4,8},{8,12},{12,14},{14,10},{10,6},{6,2},{2,0},{1,5},{5,9},... | collective-permute-start | bytes 589832 | tf_op jit(solution)/shard_map/ppermute | solution.py:339
  65.6 8.1 %collective-permute-start.15 = (bf16[40,3072]{1,0:T(8,128)(2,1)S(1)}, bf16[40,3072]{1,0:T(8,128)(2,1)S(1)}, u32[]{:S(2)}, u32[]{:S(2)}) collective-permute-start(bf16[40,3072]{1,0:T(8,128)(2,1)S(1)} %get-tuple-element.143), channel_id=1, source_target_pairs={{0,2},{4,0},{8,4},{12,8},{14,12},{10,14},{6,10},{2,6},{1,3},{5,1},... | collective-permute-start | bytes 737288 | tf_op jit(solution)/shard_map/ppermute | solution.py:342
  66.1 7.6 %collective-permute-start.17 = (f32[2,40,64]{2,1,0:T(8,128)S(1)}, f32[2,40,64]{2,1,0:T(8,128)S(1)}, u32[]{:S(2)}, u32[]{:S(2)}) collective-permute-start(f32[2,40,64]{2,1,0:T(8,128)S(1)} %get-tuple-element.170), channel_id=1, source_target_pairs={{0,4},{2,6},{4,0},{6,2},{8,12},{10,14},{12,8},{14,10},{1,5},{3,7},... | collective-permute-start | bytes 61448 | tf_op jit(solution)/shard_map/ppermute | solution.py:446
  80.2 9.6 %collective-permute-start.31 = (bf16[8,32,768]{2,1,0:T(8,128)(2,1)S(1)}, bf16[8,32,768]{2,1,0:T(8,128)(2,1)S(1)}, u32[]{:S(2)}, u32[]{:S(2)}) collective-permute-start(bf16[8,32,768]{2,1,0:T(8,128)(2,1)S(1)} %get-tuple-element.194), channel_id=1, source_target_pairs={{0,1},{1,0},{2,3},{3,2},{4,5},{5,4},{6,7},{7,6},{8,9},{9,8},{10,11... | collective-permute-start | bytes 1179656 | tf_op jit(solution)/shard_map/ppermute | solution.py:493
  81.0 7.8 %collective-permute-start.22 = (bf16[32,3072]{1,0:T(8,128)(2,1)S(1)}, bf16[32,3072]{1,0:T(8,128)(2,1)S(1)}, u32[]{:S(2)}, u32[]{:S(2)}) collective-permute-start(bf16[32,3072]{1,0:T(8,128)(2,1)S(1)} %add_convert_fusion.6), channel_id=1, source_target_pairs={{0,2},{4,0},{8,4},{12,8},{14,12},{10,14},{6,10},{2,6},{1,3},{5,1},... | collective-permute-start | bytes 589832 | tf_op jit(solution)/shard_map/ppermute | solution.py:342
  82.1 25.6 %collective-permute-start.19 = (bf16[32,3072]{1,0:T(8,128)(2,1)S(1)}, bf16[32,3072]{1,0:T(8,128)(2,1)S(1)}, u32[]{:S(2)}, u32[]{:S(2)}) collective-permute-start(bf16[32,3072]{1,0:T(8,128)(2,1)S(1)} %add_convert_fusion.8), channel_id=1, source_target_pairs={{0,4},{4,8},{8,12},{12,14},{14,10},{10,6},{6,2},{2,0},{1,5},{5,9},... | collective-permute-start | bytes 589832 | tf_op jit(solution)/shard_map/ppermute | solution.py:339
  83.8 10.3 %collective-permute-start.28 = (bf16[40,3072]{1,0:T(8,128)(2,1)S(1)}, bf16[40,3072]{1,0:T(8,128)(2,1)S(1)}, u32[]{:S(2)}, u32[]{:S(2)}) collective-permute-start(bf16[40,3072]{1,0:T(8,128)(2,1)S(1)} %add_convert_fusion.1), channel_id=1, source_target_pairs={{0,2},{4,0},{8,4},{12,8},{14,12},{10,14},{6,10},{2,6},{1,3},{5,1},... | collective-permute-start | bytes 737288 | tf_op jit(solution)/shard_map/ppermute | solution.py:342
  85.1 16.0 %collective-permute-start.25 = (bf16[40,3072]{1,0:T(8,128)(2,1)S(1)}, bf16[40,3072]{1,0:T(8,128)(2,1)S(1)}, u32[]{:S(2)}, u32[]{:S(2)}) collective-permute-start(bf16[40,3072]{1,0:T(8,128)(2,1)S(1)} %add_convert_fusion.3), channel_id=1, source_target_pairs={{0,4},{4,8},{8,12},{12,14},{14,10},{10,6},{6,2},{2,0},{1,5},{5,9},... | collective-permute-start | bytes 737288 | tf_op jit(solution)/shard_map/ppermute | solution.py:339
  88.9 22.0 %collective-permute-start.23 = (bf16[32,3072]{1,0:T(8,128)(2,1)S(1)}, bf16[32,3072]{1,0:T(8,128)(2,1)S(1)}, u32[]{:S(2)}, u32[]{:S(2)}) collective-permute-start(bf16[32,3072]{1,0:T(8,128)(2,1)S(1)} %add_convert_fusion.5), channel_id=1, source_target_pairs={{0,2},{4,0},{8,4},{12,8},{14,12},{10,14},{6,10},{2,6},{1,3},{5,1},... | collective-permute-start | bytes 589832 | tf_op jit(solution)/shard_map/ppermute | solution.py:342
  90.0 11.0 %collective-permute-start.32 = (bf16[4,32,768]{2,1,0:T(8,128)(2,1)S(1)}, bf16[4,32,768]{2,1,0:T(8,128)(2,1)S(1)}, u32[]{:S(2)}, u32[]{:S(2)}) collective-permute-start(bf16[4,32,768]{2,1,0:T(8,128)(2,1)S(1)} %get-tuple-element.196), channel_id=1, source_target_pairs={{0,2},{2,0},{4,6},{6,4},{8,10},{10,8},{12,14},{14,12},{1,3},{3,1},... | collective-permute-start | bytes 589832 | tf_op jit(solution)/shard_map/ppermute | solution.py:446
  94.1 19.4 %collective-permute-start.29 = (bf16[40,3072]{1,0:T(8,128)(2,1)S(1)}, bf16[40,3072]{1,0:T(8,128)(2,1)S(1)}, u32[]{:S(2)}, u32[]{:S(2)}) collective-permute-start(bf16[40,3072]{1,0:T(8,128)(2,1)S(1)} %add_convert_fusion), channel_id=1, source_target_pairs={{0,2},{4,0},{8,4},{12,8},{14,12},{10,14},{6,10},{2,6},{1,3},{5,1},... | collective-permute-start | bytes 737288 | tf_op jit(solution)/shard_map/ppermute | solution.py:342
  101.2 12.4 %collective-permute-start.26 = (bf16[40,3072]{1,0:T(8,128)(2,1)S(1)}, bf16[40,3072]{1,0:T(8,128)(2,1)S(1)}, u32[]{:S(2)}, u32[]{:S(2)}) collective-permute-start(bf16[40,3072]{1,0:T(8,128)(2,1)S(1)} %add_convert_fusion.2), channel_id=1, source_target_pairs={{0,4},{4,8},{8,12},{12,14},{14,10},{10,6},{6,2},{2,0},{1,5},{5,9},... | collective-permute-start | bytes 737288 | tf_op jit(solution)/shard_map/ppermute | solution.py:339
  (30 other events, 281.1 us)

commit v6 on v5

--- a/solution.py
+++ b/solution.py
@@ -51,7 +51,7 @@
     return (row == slot).astype(BF), (row - capacity == slot).astype(BF)
 
 
-def prepare_kernel(capacity, choice_hbm, weight_hbm, grad_hbm, tokens_hbm, down_hbm, top, rest,
+def prepare_kernel(capacity, choice_hbm, weight_hbm, grad_hbm, tokens_hbm, down_hbm, block_ref,
                    choice_ref, weight_ref, grad_ref, tokens_ref, down_ref, sems):
     half = grad_ref.shape[1] // 2
     rank = down_ref.shape[0]
@@ -72,24 +72,31 @@
     copies[1].wait()
     first = dot(upper, grad_ref[:, :half])
     copies[2].wait()
-    rows = (first + dot(lower, grad_ref[:, half:])).astype(BF)
-    cut = top.shape[0]
-    top[:, :half] = rows[:cut]
-    rest[:, :half] = rows[cut:]
+    block_ref[:, :half] = (first + dot(lower, grad_ref[:, half:])).astype(BF)
     copies[3].wait()
     weight = jnp.sum(
         jnp.where(choice == 0, weight_ref[...].astype(F32), 0.0), axis=0, keepdims=True
     )
     column = jnp.sum(upper.astype(F32) * weight, axis=1, keepdims=True)
-    column = jnp.broadcast_to(column, (2 * capacity, rank)).astype(BF)
-    top[:, half + rank :] = column[:cut]
-    rest[:, half + rank :] = column[cut:]
+    block_ref[:, half + rank :] = jnp.broadcast_to(column, (2 * capacity, rank)).astype(BF)
     copies[4].wait()
     copies[5].wait()
     low = dot(tokens_ref[...], down_ref[...], NT).astype(BF)
-    low = dot(upper, low).astype(BF)
-    top[:, half : half + rank] = low[:cut]
-    rest[:, half : half + rank] = low[cut:]
+    block_ref[:, half : half + rank] = dot(upper, low).astype(BF)
+
+
+def cut_kernel(right_in, left_in, top, rest):
+    cut = top.shape[0]
+    top[...] = right_in[:cut, :]
+    rest[...] = left_in[cut:, :]
+
+
+def merge_kernel(top_in, rest_in, own_right, own_left, right_out, left_out):
+    cut = top_in.shape[0]
+    right_out[:cut, :] = (top_in[...].astype(F32) + own_right[:cut, :].astype(F32)).astype(BF)
+    right_out[cut:, :] = own_right[cut:, :]
+    left_out[:cut, :] = own_left[:cut, :]
+    left_out[cut:, :] = (rest_in[...].astype(F32) + own_left[cut:, :].astype(F32)).astype(BF)
 
 
 def place_here(place):
@@ -111,24 +118,6 @@
             target[at] = jnp.where(live, rows, 0.0).astype(BF)
 
 
-def low_order_kernel(ring, place, order, *refs):
-    lows, (keep, send) = refs[:-2], refs[-2:]
-    count = len(ring)
-    me, here = place_here(place)
-    for low, r in zip(lows, order):
-        spot = lax.rem(here + r + count, count)
-        owner = sum(jnp.where(spot == i, e, 0) for i, e in enumerate(ring))
-        key = owner ^ me
-
-        @pl.when(key % 2 == 0)
-        def _(low=low, key=key):
-            keep[key // 2] = low[...]
-
-        @pl.when(key % 2 == 1)
-        def _(low=low, key=key):
-            send[key // 2] = low[...]
-
-
 def halve_kernel(ours, theirs, *outs):
     count = ours.shape[0]
     for i in range(count):
@@ -137,27 +126,35 @@
         out[i // len(outs)] = total.astype(out.dtype)
 
 
-def hidden_kernel(capacity, slot, start, count, *refs):
-    tops, rests, refs = refs[:count], refs[count : 2 * count], refs[2 * count :]
+def hidden_kernel(capacity, slot, start, count, pieces, *refs):
+    blocks, refs = [refs[i * pieces : (i + 1) * pieces] for i in range(count)], refs[count * pieces :]
     (gate_ref, up_ref, down_ref, lora_gate, lora_up, dgate_ref, dup_ref, low_ref), refs = refs[:8], refs[8:]
     lows, rows = refs[:count], refs[count]
     hidden, width = down_ref.shape
     half = width // 2
     rank = lora_gate.shape[0]
-    cut = tops[0].shape[0]
     tall = rows.shape[0] // count
-    for i in range(count):
-        rows[i * tall : i * tall + cut, :] = tops[i][:, :half]
-        rows[i * tall + cut : i * tall + 2 * capacity, :] = rests[i][:, :half]
-    first = dot(down_ref[:, :half], rows[...], NT).T
-    second = dot(down_ref[:, half:], rows[...], NT).T
+    for i, block in enumerate(blocks):
+        at = i * tall
+        for piece in block:
+            rows[at : at + piece.shape[0], :] = piece[:, :half]
+            at += piece.shape[0]
+    if tall % 128 == 0:
+        first = dot(down_ref[:, :half], rows[...], NT).T
+        second = dot(down_ref[:, half:], rows[...], NT).T
+    else:
+        first = dot(rows[...], down_ref[:, :half], NT)
+        second = dot(rows[...], down_ref[:, half:], NT)
     live = lax.broadcasted_iota(jnp.int32, (slot, hidden), 0) < capacity
     for i in range(count):
         at = i * tall
-        extra = tops[i][:, half:], rests[i][: slot - cut, half:]
-        low_ref[i, :cut, :] = extra[0][:, :rank]
-        low_ref[i, cut:, :] = extra[1][:, :rank]
-        weight = jnp.concatenate([x.astype(F32)[:, rank : rank + 1] for x in extra], axis=0)
+        extras, seen = [], 0
+        for piece in blocks[i]:
+            height = min(piece.shape[0], slot - seen)
+            extras.append(piece[:height, half:])
+            low_ref[i, seen : seen + height, :] = extras[-1][:, :rank]
+            seen += height
+        weight = jnp.concatenate([x.astype(F32)[:, rank : rank + 1] for x in extras], axis=0)
         grad = (first[at : at + slot] + second[at + capacity : at + capacity + slot]) * weight
         grad = jnp.where(live, grad, 0.0)
         gate = gate_ref[start + i].astype(F32)
@@ -223,14 +220,13 @@
             at = i * slot
             tile[:capacity, :] = sums[0][at : at + capacity]
             tile[capacity:, :] = sums[1][at : at + capacity]
-            cut = outs[2 * i].shape[0]
-            outs[2 * i][:, t : t + TILE] = tile[:cut, :].astype(BF)
-            outs[2 * i + 1][:, t : t + TILE] = tile[cut:, :].astype(BF)
-
-
-def adapter_kernel(capacity, choice_ref, tokens_ref, low_in, low_ref, keep_ref, send_ref):
+            outs[i][:, t : t + TILE] = tile[...].astype(BF)
+
+
+def adapter_kernel(capacity, choice_ref, tokens_ref, *refs):
+    lows, (low_ref, keep_ref, send_ref) = refs[:-3], refs[-3:]
     count, part, share = keep_ref.shape
-    low = low_in[0].astype(BF)
+    low = sum(x[...] for x in lows).astype(BF)
     low_ref[...] = low
     upper, _ = pick_rows(choice_ref[...], capacity)
     low = dot(upper[: low.shape[0]], low, TN).astype(BF)
@@ -254,8 +250,8 @@
 
 
 def finish_kernel(capacity, choice_ref, *refs):
-    tops, rests, (low_ref, down_ref, out_ref, low_tall) = refs[:3], refs[3:6], refs[6:]
-    cut, half = tops[0].shape
+    parts, (low_ref, down_ref, out_ref, low_tall) = refs[:3], refs[3:]
+    half = parts[0].shape[1]
     upper, lower = pick_rows(choice_ref[...], capacity)
     low = low_ref[...].astype(F32)[:capacity]
     zero = jnp.zeros_like(low)
@@ -265,13 +261,11 @@
     low_tall[:capacity, :] = zero
     low_tall[capacity:, :] = low
     low_lower = low_tall[...].astype(BF)
-    adapter = dot(low_upper, down_ref[:, :half]) + dot(low_lower, down_ref[:, half:])
-    top = sum(x[...].astype(F32) for x in tops) + adapter[:cut]
-    rest = sum(x[...].astype(F32) for x in rests) + adapter[cut:]
-    top, rest = top.astype(BF), rest.astype(BF)
-    for pick, at in ((upper, 0), (lower, half)):
-        picked = dot(pick[:cut], top, TN) + dot(pick[cut:], rest, TN)
-        out_ref[:, at : at + half] = picked.astype(BF)
+    total = sum(x[...].astype(F32) for x in parts)
+    total += dot(low_upper, down_ref[:, :half]) + dot(low_lower, down_ref[:, half:])
+    total = total.astype(BF)
+    out_ref[:, :half] = dot(upper, total, TN).astype(BF)
+    out_ref[:, half:] = dot(lower, total, TN).astype(BF)
 
 
 def in_hbm(x):
@@ -317,7 +311,7 @@
         place[e] = i
     to_right = [(ring[i], ring[(i + 1) % n]) for i in range(n)]
     to_left = [(ring[i], ring[(i - 1) % n]) for i in range(n)]
-    passes = [[0]] + [[-s, s] for s in range(1, middle)] + [[middle]]
+    passes = [[0, -1, 1]] + [[-s, s] for s in range(2, middle)] + [[middle]]
     sizes = [len(group) for group in passes]
     order = [r for group in passes for r in group]
     heights = [cut, 2 * capacity - cut]
@@ -341,10 +335,10 @@
     def left(x):
         return lax.ppermute(x, "expert", to_left)
 
-    block = call(
+    (block,) = call(
         functools.partial(prepare_kernel, capacity),
         "prepare",
-        [((h, wide), BF) for h in heights],
+        [((2 * capacity, wide), BF)],
         [in_hbm(x) for x in (choice, weights, output_gradient, tokens, adapter_down_factor)],
         [
             pltpu.VMEM(choice.shape, choice.dtype),
@@ -368,18 +362,18 @@
 
     down_here, gate_here, up_here = in_vmem(down_weight), in_vmem(gate_weight), in_vmem(up_weight)
     dgates, dups, low_rows, lows = [], [], [], []
-    got = {0: tuple(block)}
+    got = {0: (block,)}
 
     def hidden_pass(group):
-        size, start = len(group), len(lows)
+        size, start, pieces = len(group), len(lows), len(got[group[0]])
+        tall = -(-2 * capacity // 128) * 128 if size < 3 else -(-2 * capacity // 16) * 16
         results = call(
-            functools.partial(hidden_kernel, capacity, slot, start, size),
+            functools.partial(hidden_kernel, capacity, slot, start, size, pieces),
             "hidden_rows",
             [((size, slot, hidden), BF)] * 2
             + [((size, slot, rank), BF)]
             + [((slot, rank), F32)] * size,
-            [got[r][0] for r in group]
-            + [got[r][1] for r in group]
+            [piece for r in group for piece in got[r]]
             + [gate_rows, up_rows, down_here, adapter_gate_factor, adapter_up_factor],
             [pltpu.VMEM((size * tall, half), BF)],
             (2 * size * tall * width * hidden, 2 * hidden * width),
@@ -389,30 +383,39 @@
         low_rows.append(results[2])
         lows.extend(results[3:])
 
-    right_top, right_rest = left_top, left_rest = block
-    for s in range(1, middle + 1):
-        right_top, left_rest = right(right_top), left(left_rest)
-        if s < middle:
-            right_rest, left_top = right(right_rest), left(left_top)
-        hidden_pass(passes[s - 1])
-        if s < middle:
-            right_rest, left_top, dgates[-1], dups[-1] = lax.optimization_barrier(
-                (right_rest, left_top, dgates[-1], dups[-1])
+    def to_owner(at):
+        r = order[at]
+        lows[at] = lax.ppermute(lows[at], "expert", [(ring[i], ring[(i + r) % n]) for i in range(n)])
+
+    going_right = going_left = block
+    sent = [0, 0]
+    for s in range(1, middle):
+        going_right, going_left = right(going_right), left(going_left)
+        if s == 1:
+            going_right, going_left, gate_rows, up_rows = lax.optimization_barrier(
+                (going_right, going_left, gate_rows, up_rows)
             )
-            got[-s], got[s] = (right_top, right_rest), (left_top, left_rest)
         else:
-            right_top, left_rest, dgates[-1], dups[-1] = lax.optimization_barrier(
-                (right_top, left_rest, dgates[-1], dups[-1])
+            hidden_pass(passes[s - 2])
+            going_right, going_left, dgates[-1], dups[-1], lows[: sent[1]] = lax.optimization_barrier(
+                (going_right, going_left, dgates[-1], dups[-1], lows[: sent[1]])
             )
+            sent = [sent[1], len(lows)]
+            for at in range(max(sent[0], 1), sent[1]):
+                to_owner(at)
+        got[-s], got[s] = (going_right,), (going_left,)
+    right_top, left_rest = call(
+        cut_kernel, "cut", [((h, wide), BF) for h in heights], [going_right, going_left]
+    )
+    right_top, left_rest = right(right_top), left(left_rest)
+    hidden_pass(passes[-2])
+    right_top, left_rest, dgates[-1], dups[-1], lows[: sent[1]] = lax.optimization_barrier(
+        (right_top, left_rest, dgates[-1], dups[-1], lows[: sent[1]])
+    )
+    for at in range(max(sent[1], 1), len(lows)):
+        to_owner(at)
     got[middle] = (right_top, left_rest)
     hidden_pass(passes[-1])
-
-    low_keep, low_send = call(
-        functools.partial(low_order_kernel, ring, place, order),
-        "low_order",
-        [((n // 2, slot, rank), F32)] * 2,
-        lows,
-    )
 
     right_top, left_rest = call(
         functools.partial(first_partial_kernel, capacity, slot, cut),
@@ -426,10 +429,11 @@
         ],
         (4 * slot * width * hidden, 4 * hidden * width),
     )
+    right_top, left_rest, lows[-1] = lax.optimization_barrier((right_top, left_rest, lows[-1]))
     own = call(
         functools.partial(partial_kernel, capacity, slot, sizes[:-1]),
         "partials",
-        [((h, half), BF) for h in heights] * (n - 1),
+        [((2 * capacity, half), BF)] * (n - 1),
         [*dgates[:-1], *dups[:-1], gate_here, up_here],
         [
             pltpu.VMEM(((n - 1) * slot, hidden), BF),
@@ -447,69 +451,74 @@
         count = keep.shape[0]
         parts = 2 if count > 1 else 1
         shape = (count // parts,) + keep.shape[1:]
-        return list(call(halve_kernel, "halve", [(shape, keep.dtype)] * parts, [keep, other]))
-
-    low_keep, right_top, left_rest = lax.optimization_barrier((low_keep, right_top, left_rest))
+        return call(halve_kernel, "halve", [(shape, keep.dtype)] * parts, [keep, other])
+
     right_top, left_rest = right(right_top), left(left_rest)
-    low_keep, low_send = exchange(low_keep, low_send, 1)
-    right_top, left_rest, low_keep, own = lax.optimization_barrier((right_top, left_rest, low_keep, own))
-    own = {r: (own[2 * i], own[2 * i + 1]) for i, r in enumerate(order[:-1])}
-    pair = exchange(low_keep, low_send, 2)
-    for s in range(middle - 1, 0, -1):
-        right_top, left_rest = add(right_top, own[s][0]), add(left_rest, own[-s][1])
-        if s == middle - 1:
-            right_rest, left_top = own[s][1], own[-s][0]
-            pair[0], right_top, left_rest = lax.optimization_barrier((pair[0], right_top, left_rest))
-        else:
-            right_rest, left_top = add(right_rest, own[s][1]), add(left_top, own[-s][0])
-        right_top, left_rest = right(right_top), left(left_rest)
-        right_rest, left_top = right(right_rest), left(left_top)
-    bit = 4
-    while bit < n:
-        pair = exchange(*pair, bit)
-        bit *= 2
-    low_total = pair[0]
+    to_owner(n - 1)
+    right_top, left_rest, own, lows = lax.optimization_barrier((right_top, left_rest, own, lows))
+    own = dict(zip(order[:-1], own))
+    going_right, going_left = call(
+        merge_kernel,
+        "first_add",
+        [((2 * capacity, half), BF)] * 2,
+        [right_top, left_rest, own[middle - 1], own[1 - middle]],
+    )
 
     share = width // n
     part = rank // 2
     swap = [(0, 1), (1, 0)]
-    if share % 128 == 0:
-        low, keep, send = call(
-            functools.partial(adapter_kernel, capacity),
-            "adapter_gradient",
-            [((slot, rank), BF)] + [((n, part, share), BF)] * 2,
-            [choice, tokens, low_total],
-            work=(2 * own_count * rank * width, 2 * own_count * width),
+
+    def adapter_gradient():
+        if share % 128 == 0:
+            low, keep, send = call(
+                functools.partial(adapter_kernel, capacity),
+                "adapter_gradient",
+                [((slot, rank), BF)] + [((n, part, share), BF)] * 2,
+                [choice, tokens, *lows],
+                work=(2 * own_count * rank * width, 2 * own_count * width),
+            )
+        else:
+            me, core = lax.axis_index("expert"), lax.axis_index("dp")
+            upper, _ = pick_rows(choice, capacity)
+            low = sum(lows).astype(BF)
+            low_tokens = dot(upper[:slot], low, TN).astype(BF)
+            down = dot(low_tokens, tokens, TN).astype(BF).reshape(rank, n, share)
+            down = down.transpose(1, 0, 2)[jnp.arange(n, dtype=jnp.int32) ^ me]
+            keep = jnp.where(core == 0, down[:, :part], down[:, part:])
+            send = jnp.where(core == 0, down[:, part:], down[:, :part])
+        other = lax.ppermute(send, "dp", swap)
+        return low, call(halve_kernel, "halve", [((n // 2, part, share), BF)] * 2, [keep, other])
+
+    def lora_gradients():
+        (local,) = call(
+            functools.partial(lora_kernel, slot, sizes),
+            "lora_rows",
+            [((2 * rank, hidden), BF)],
+            [*dgates, *dups, *low_rows],
+            [
+                pltpu.VMEM((n * slot, hidden), BF),
+                pltpu.VMEM((n * slot, hidden), BF),
+                pltpu.VMEM((n * slot, rank), BF),
+            ],
+            (4 * n * slot * rank * hidden, 4 * n * slot * hidden),
         )
-    else:
-        me, core = lax.axis_index("expert"), lax.axis_index("dp")
-        upper, _ = pick_rows(choice, capacity)
-        low = low_total[0].astype(BF)
-        low_tokens = dot(upper[:slot], low, TN).astype(BF)
-        down = dot(low_tokens, tokens, TN).astype(BF).reshape(rank, n, share)
-        down = down.transpose(1, 0, 2)[jnp.arange(n, dtype=jnp.int32) ^ me]
-        keep = jnp.where(core == 0, down[:, :part], down[:, part:])
-        send = jnp.where(core == 0, down[:, part:], down[:, :part])
-    other = lax.ppermute(send, "dp", swap)
-    pair = call(halve_kernel, "halve", [((n // 2, part, share), BF)] * 2, [keep, other])
-    low_rows, _ = lax.optimization_barrier((low_rows, pair))
-    (lora,) = call(
-        functools.partial(lora_kernel, slot, sizes),
-        "lora_rows",
-        [((2 * rank, hidden), BF)],
-        [*dgates, *dups, *low_rows],
-        [
-            pltpu.VMEM((n * slot, hidden), BF),
-            pltpu.VMEM((n * slot, hidden), BF),
-            pltpu.VMEM((n * slot, rank), BF),
-        ],
-        (4 * n * slot * rank * hidden, 4 * n * slot * hidden),
-    )
-    lora_there = lax.ppermute(lora, "dp", swap)
-    bit = 1
-    while bit < n:
+        return local, lax.ppermute(local, "dp", swap)
+
+    bits = [1 << i for i in range(n.bit_length() - 1)]
+    for hop, s in enumerate(range(middle - 1, 0, -1)):
+        going_right, going_left = right(going_right), left(going_left)
+        if hop == 0:
+            low, pair = adapter_gradient()
+        elif hop == 1:
+            for bit in bits[:2]:
+                pair = exchange(*pair, bit)
+            low_rows, pair = lax.optimization_barrier((low_rows, pair))
+        if s > 1:
+            going_right, going_left, pair = lax.optimization_barrier((going_right, going_left, pair))
+            going_right, going_left = add(going_right, own[s - 1]), add(going_left, own[1 - s])
+    lora, lora_there = lora_gradients()
+    for bit in bits[2:]:
         pair = exchange(*pair, bit)
-        bit *= 2
     down = pair[0][0]
     there = lax.ppermute(down, "dp", swap)
     grad_down, grad_gate, grad_up = call(
@@ -523,7 +532,7 @@
         functools.partial(finish_kernel, capacity),
         "finish",
         [((own_count, width), BF)],
-        [choice, right_top, left_top, own[0][0], right_rest, left_rest, own[0][1], low, adapter_down_factor],
+        [choice, going_right, going_left, own[0], low, adapter_down_factor],
         [pltpu.VMEM((2 * capacity, rank), F32)],
         (4e8, 4.5e6),
     )

time: 118 us -> 119 us (level)
  waiting for transfers between devices: 30.9 us -> 44.9 us
  starting transfers between devices: 42.5 us -> 33.9 us
  Pallas kernels: 34.4 us -> 30.7 us
    ppermute x6 -> x3, waiting for transfers between devices: 8.41 us -> 21.3 us  [exchange(): other = lax.ppermute(send, 'expert', [(e, e ^ bit) for e in range(n)])]
    ppermute x2 -> x9, starting transfers between devices: 0.07 us -> 12.3 us  [the longest x7 12.2 us: to_owner(): lax.ppermute(lows[at], 'expert', [(ring[i], ring[(i + r) % n]) for i in r...]
    ppermute x14 -> x8, starting transfers between devices: 16.1 us -> 5.61 us  [right(): return lax.ppermute(x, 'expert', to_right)]
    ppermute x2 -> x9, waiting for transfers between devices: 0.01 us -> 7.14 us  [the longest x7 5.43 us: to_owner(): lax.ppermute(lows[at], 'expert', [(ring[i], ring[(i + r) % n]) for i in r...]
    ppermute x14 -> x8, waiting for transfers between devices: 15.5 us -> 9.68 us  [left(): return lax.ppermute(x, 'expert', to_left)]
    ppermute x6 -> x3, starting transfers between devices: 7.58 us -> 2.46 us  [exchange(): other = lax.ppermute(send, 'expert', [(e, e ^ bit) for e in range(n)])]
    ppermute x14 -> x8, starting transfers between devices: 18.1 us -> 13.4 us  [left(): return lax.ppermute(x, 'expert', to_left)]
    pallas_call x21 -> x18, Pallas kernels: 34.4 us -> 30.7 us  [call(): pl.pallas_call(kernel, out_shape=[jax.ShapeDtypeStruct(shape, dtype) for...]
  transfers between devices with their start and end apart: 37 -> 29, of which waited for: 15 -> 13; matrix products, arithmetic and copies ran while one was open for 0% -> 0% of each run, Pallas kernels for 23% -> 22%
where the time goes in v6:
time: 119 us
  waiting for transfers between devices  44.9 us (38%)
  starting transfers between devices  33.9 us (28%)
  Pallas kernels  30.7 us (26%)
  local copies, waits for them, and re-layouts  7.57 us (6%)
    pallas_call x18, Pallas kernels, call(): pl.pallas_call(kernel, out_shape=[jax.ShapeDtypeStruct(shape, dtype) for...  30.7 us
    ppermute x3, waiting for transfers between devices, exchange(): other = lax.ppermute(send, 'expert', [(e, e ^ bit) for e in range(n)])  21.3 us
    ppermute x8, starting transfers between devices, left(): return lax.ppermute(x, 'expert', to_left)  13.4 us
    ppermute x7, starting transfers between devices, to_owner(): lax.ppermute(lows[at], 'expert', [(ring[i], ring[(i + r) % n]) for i in r...  12.2 us
    ppermute x8, waiting for transfers between devices, left(): return lax.ppermute(x, 'expert', to_left)  9.68 us
    unnamed x34, local copies, waits for them, and re-layouts  7.57 us
    ppermute x8, starting transfers between devices, right(): return lax.ppermute(x, 'expert', to_right)  5.61 us
    ppermute x8, waiting for transfers between devices, right(): return lax.ppermute(x, 'expert', to_right)  5.56 us
  transfers between devices with their start and end apart: 29, of which 13 were waited for; matrix products, arithmetic and copies ran while one was open for 0% of the time, Pallas kernels for 22%

profile of v6, /device:TPU:0, one launch (start us, length us, event | category | flops | bytes accessed | tf_op | source)
XLA Modules:
  0.0 118.5 jit_solution(14265888074884923679)
XLA Ops:
  0.6 2.9 %prepare.1.refs_0_ = bf16[72,3200]{1,0:T(8,128)(2,1)S(1)} custom-call(s32[4,128]{1,0:T(4,128)} %bitcast.22, bf16[4,128]{1,0:T(4,128)(2,1)} %bitcast.27, bf16[128,6144]{1,0:T(8,128)(2,1)} %bitcast.26, bf16[128,6144]{1,0:T(8,128)(2,1)} %bitcast.16, bf16[64,6144]{1,0:T(8,128)(2,1)} %refs_4_.7), custom_call_target="tpu_custom_call" | custom-call | flops 400000000 | bytes 4500000 | tf_op jit(solution)/shard_map/prepare/pallas_call | solution.py:320
  3.6 3.0 %collective-permute-start.1 = (bf16[72,3200]{1,0:T(8,128)(2,1)S(1)}, bf16[72,3200]{1,0:T(8,128)(2,1)S(1)}, u32[]{:S(2)}, u32[]{:S(2)}) collective-permute-start(bf16[72,3200]{1,0:T(8,128)(2,1)S(1)} %prepare.1.refs_0_), channel_id=1, source_target_pairs={{0,2},{4,0},{8,4},{12,8},{14,12},{10,14},{6,10},{2,6},{1,3},{5,1},... | collective-permute-start | bytes 1382408 | tf_op jit(solution)/shard_map/ppermute | solution.py:336
  9.0 8.3 %collective-permute-done.1.refs_2_ = bf16[72,3200]{1,0:T(8,128)(2,1)S(1)} collective-permute-done((bf16[72,3200]{1,0:T(8,128)(2,1)S(1)}, bf16[72,3200]{1,0:T(8,128)(2,1)S(1)}, u32[]{:S(2)}, u32[]{:S(2)}) %collective-permute-start.1) | collective-permute-done | bytes 460832 | tf_op jit(solution)/shard_map/ppermute | solution.py:336
  20.7 3.7 %copy-done = bf16[768,6144]{1,0:T(8,128)(2,1)S(1)} copy-done((bf16[768,6144]{1,0:T(8,128)(2,1)S(1)}, bf16[768,6144]{1,0:T(8,128)(2,1)}, u32[]{:S(2)}) %copy-start) | copy-done | bytes 9437208
  26.1 3.1 %hidden_rows.4 = (bf16[3,40,768]{2,1,0:T(8,128)(2,1)S(1)}, bf16[3,40,768]{2,1,0:T(8,128)(2,1)S(1)}, bf16[3,40,64]{2,1,0:T(8,128)(2,1)S(1)}, f32[40,64]{1,0:T(8,1...) custom-call(bf16[72,3200]{1,0:T(8,128)(2,1)S(1)} %prepare.1.refs_0_, ...), custom_call_target="tpu_custom_call" | custom-call | flops 2264924160 | bytes 9437184 | tf_op jit(solution)/shard_map/hidden_rows/pallas_call | solution.py:320
  34.2 3.1 %hidden_rows.5 = (bf16[2,40,768]{2,1,0:T(8,128)(2,1)S(1)}, bf16[2,40,768]{2,1,0:T(8,128)(2,1)S(1)}, bf16[2,40,64]{2,1,0:T(8,128)(2,1)S(1)}, f32[40,64]{1,0:T(8,128)S(1)}, f32[40,64]{1,0:T(8,128)S(1)}) custom-call(bf16[72,3200]{1,0:T(8,128)(2,1)S(1)} %collective-permute-done.2.refs_0_, bf16[72,3200]{1,0:T(8,128)(2,1)S(1)} %collective-permute-done.3.refs_1_, ...), custom_call_target="tpu_custom_call" | custom-call | flops 2415919104 | bytes 9437184 | tf_op jit(solution)/shard_map/hidden_rows/pallas_call | solution.py:320
  37.3 5.4 %collective-permute-done.6.refs_1_ = f32[40,64]{1,0:T(8,128)S(1)} collective-permute-done((f32[40,64]{1,0:T(8,128)S(1)}, f32[40,64]{1,0:T(8,128)S(1)}, u32[]{:S(2)}, u32[]{:S(2)}) %collective-permute-start.6) | collective-permute-done | bytes 10272 | tf_op jit(solution)/shard_map/ppermute | solution.py:388
  43.4 2.2 %collective-permute-start.10 = (f32[40,64]{1,0:T(8,128)S(1)}, f32[40,64]{1,0:T(8,128)S(1)}, u32[]{:S(2)}, u32[]{:S(2)}) collective-permute-start(f32[40,64]{1,0:T(8,128)S(1)} %get-tuple-element.133), channel_id=1, source_target_pairs={{0,6},{4,2},{8,0},{12,4},{14,8},{10,12},{6,14},{2,10},{1,7},{5,3},... | collective-permute-start | bytes 30728 | tf_op jit(solution)/shard_map/ppermute | solution.py:388
  47.8 3.1 %hidden_rows.6 = (bf16[2,40,768]{2,1,0:T(8,128)(2,1)S(1)}, bf16[2,40,768]{2,1,0:T(8,128)(2,1)S(1)}, bf16[2,40,64]{2,1,0:T(8,128)(2,1)S(1)}, f32[40,64]{1,0:T(8,128)S(1)}, f32[40,64]{1,0:T(8,128)S(1)}) custom-call(bf16[72,3200]{1,0:T(8,128)(2,1)S(1)} %collective-permute-done.4.right_in.refs_0_, bf16[72,3200]{1,0:T(8,128)(2,1)S(1)} %collective-permute-done.5.left_in.refs_1_, ...), custom_call_target="tpu_custom_call" | custom-call | flops 2415919104 | bytes 9437184 | tf_op jit(solution)/shard_map/hidden_rows/pallas_call | solution.py:320
  50.9 2.2 %collective-permute-start.14 = (f32[40,64]{1,0:T(8,128)S(1)}, f32[40,64]{1,0:T(8,128)S(1)}, u32[]{:S(2)}, u32[]{:S(2)}) collective-permute-start(f32[40,64]{1,0:T(8,128)S(1)} %get-tuple-element.162), channel_id=1, source_target_pairs={{0,10},{4,6},{8,2},{12,0},{14,4},{10,8},{6,12},{2,14},{1,11},{5,7}... | collective-permute-start | bytes 30728 | tf_op jit(solution)/shard_map/ppermute | solution.py:388
  54.8 2.9 %hidden_rows.7 = (bf16[1,40,768]{2,1,0:T(8,128)(2,1)S(1)}, bf16[1,40,768]{2,1,0:T(8,128)(2,1)S(1)}, bf16[1,40,64]{2,1,0:T(8,128)(2,1)S(1)}, f32[40,64]{1,0:T(8,128)S(1)}) custom-call(bf16[32,3200]{1,0:T(8,128)(2,1)S(1)} %collective-permute-done.8.refs_0_, bf16[40,3200]{1,0:T(8,128)(2,1)S(1)} %collective-permute-done.9.refs_1_, ...), custom_call_target="tpu_custom_call" | custom-call | flops 1207959552 | bytes 9437184 | tf_op jit(solution)/shard_map/hidden_rows/pallas_call | solution.py:320
  57.8 5.3 %first_partial.1 = (bf16[32,3072]{1,0:T(8,128)(2,1)S(1)}, bf16[40,3072]{1,0:T(8,128)(2,1)S(1)}) custom-call(bf16[1,40,768]{2,1,0:T(8,128)(2,1)S(1)} %get-tuple-element.137.dgate_in.refs_3_, bf16[1,40,768]{2,1,0:T(8,128)(2,1)S(1)} %get-tuple-element.138.dup_in.refs_7_, bf16[6144,768]{1,0:T(8,128)(2,1)S(1)} %bitcast.13, bf16[6144,768]{1,0:T(8,128)(2,1)S(1)} %bitcast.15), custom_call_target="tpu_custom_call" | custom-call | flops 754974720 | bytes 18874368 | tf_op jit(solution)/shard_map/first_partial/pallas_call | solution.py:320
  63.1 3.3 %collective-permute-start.16 = (f32[40,64]{1,0:T(8,128)S(1)}, f32[40,64]{1,0:T(8,128)S(1)}, u32[]{:S(2)}, u32[]{:S(2)}) collective-permute-start(f32[40,64]{1,0:T(8,128)S(1)} %get-tuple-element.164), channel_id=1, source_target_pairs={{0,14},{4,10},{8,6},{12,2},{14,0},{10,4},{6,8},{2,12},{1,15},{5,11... | collective-permute-start | bytes 30728 | tf_op jit(solution)/shard_map/ppermute | solution.py:388
  66.5 2.0 %collective-permute-start.13 = (bf16[40,3072]{1,0:T(8,128)(2,1)S(1)}, bf16[40,3072]{1,0:T(8,128)(2,1)S(1)}, u32[]{:S(2)}, u32[]{:S(2)}) collective-permute-start(bf16[40,3072]{1,0:T(8,128)(2,1)S(1)} %get-tuple-element.143), channel_id=1, source_target_pairs={{0,2},{4,0},{8,4},{12,8},{14,12},{10,14},{6,10},{2,6},{1,3},{5,1},... | collective-permute-start | bytes 737288 | tf_op jit(solution)/shard_map/ppermute | solution.py:336
  68.5 5.9 %partials.1 = (bf16[72,3072]{1,0:T(8,128)(2,1)S(1)}, bf16[72,3072]{1,0:T(8,128)(2,1)S(1)}, bf16[72,3072]{1,0:T(8,128)(2,1)S(1)}, bf16[72,3072]{1,0:T(8,128)(2,1)...) custom-call(bf16[3,40,768]{2,1,0:T(8,128)(2,1)S(1)} %get-tuple-element.144.refs_0_, ...), custom_call_target="tpu_custom_call" | custom-call | flops 5284823040 | bytes 18874368 | tf_op jit(solution)/shard_map/partials/pallas_call | solution.py:320
  75.3 2.3 %collective-permute-start.18 = (bf16[72,3072]{1,0:T(8,128)(2,1)S(1)}, bf16[72,3072]{1,0:T(8,128)(2,1)S(1)}, u32[]{:S(2)}, u32[]{:S(2)}) collective-permute-start(bf16[72,3072]{1,0:T(8,128)(2,1)S(1)} %get-tuple-element.170), channel_id=1, source_target_pairs={{0,2},{4,0},{8,4},{12,8},{14,12},{10,14},{6,10},{2,6},{1,3},{5,1},... | collective-permute-start | bytes 1327112 | tf_op jit(solution)/shard_map/ppermute | solution.py:336
  78.4 1.7 %collective-permute-done.19.theirs = bf16[8,32,768]{2,1,0:T(8,128)(2,1)S(1)} collective-permute-done((bf16[8,32,768]{2,1,0:T(8,128)(2,1)S(1)}, bf16[8,32,768]{2,1,0:T(8,128)(2,1)S(1)}, u32[]{:S(2)}, u32[]{:S(2)}) %collective-permute-start.19) | collective-permute-done | bytes 393248 | tf_op jit(solution)/shard_map/ppermute | solution.py:489
  80.2 3.6 %collective-permute-done.17 = bf16[72,3072]{1,0:T(8,128)(2,1)S(1)} collective-permute-done((bf16[72,3072]{1,0:T(8,128)(2,1)S(1)}, bf16[72,3072]{1,0:T(8,128)(2,1)S(1)}, u32[]{:S(2)}, u32[]{:S(2)}) %collective-permute-start.17) | collective-permute-done | bytes 442400 | tf_op jit(solution)/shard_map/ppermute | solution.py:333
  84.2 2.5 %collective-permute-start.21 = (bf16[72,3072]{1,0:T(8,128)(2,1)S(1)}, bf16[72,3072]{1,0:T(8,128)(2,1)S(1)}, u32[]{:S(2)}, u32[]{:S(2)}) collective-permute-start(bf16[72,3072]{1,0:T(8,128)(2,1)S(1)} %add_convert_fusion.2), channel_id=1, source_target_pairs={{0,2},{4,0},{8,4},{12,8},{14,12},{10,14},{6,10},{2,6},{1,3},{5,1},... | collective-permute-start | bytes 1327112 | tf_op jit(solution)/shard_map/ppermute | solution.py:336
  87.6 2.0 %collective-permute-start.22 = (bf16[4,32,768]{2,1,0:T(8,128)(2,1)S(1)}, bf16[4,32,768]{2,1,0:T(8,128)(2,1)S(1)}, u32[]{:S(2)}, u32[]{:S(2)}) collective-permute-start(bf16[4,32,768]{2,1,0:T(8,128)(2,1)S(1)} %get-tuple-element.192), channel_id=1, source_target_pairs={{0,2},{2,0},{4,6},{6,4},{8,10},{10,8},{12,14},{14,12},{1,3},{3,1},... | collective-permute-start | bytes 589832 | tf_op jit(solution)/shard_map/ppermute | solution.py:450
  89.7 9.0 %collective-permute-done.22.theirs = bf16[4,32,768]{2,1,0:T(8,128)(2,1)S(1)} collective-permute-done((bf16[4,32,768]{2,1,0:T(8,128)(2,1)S(1)}, bf16[4,32,768]{2,1,0:T(8,128)(2,1)S(1)}, u32[]{:S(2)}, u32[]{:S(2)}) %collective-permute-start.22) | collective-permute-done | bytes 196640 | tf_op jit(solution)/shard_map/ppermute | solution.py:450
  98.8 5.7 %collective-permute-done.23.theirs = bf16[2,32,768]{2,1,0:T(8,128)(2,1)S(1)} collective-permute-done((bf16[2,32,768]{2,1,0:T(8,128)(2,1)S(1)}, bf16[2,32,768]{2,1,0:T(8,128)(2,1)S(1)}, u32[]{:S(2)}, u32[]{:S(2)}) %collective-permute-start.23) | collective-permute-done | bytes 98336 | tf_op jit(solution)/shard_map/ppermute | solution.py:450
  107.7 6.6 %collective-permute-done.26.theirs = bf16[1,32,768]{2,1,0:T(8,128)(2,1)S(1)} collective-permute-done((bf16[1,32,768]{2,1,0:T(8,128)(2,1)S(1)}, bf16[1,32,768]{2,1,0:T(8,128)(2,1)S(1)}, u32[]{:S(2)}, u32[]{:S(2)}) %collective-permute-start.26) | collective-permute-done | bytes 49184 | tf_op jit(solution)/shard_map/ppermute | solution.py:450
  116.5 2.0 %finish.1 = bf16[128,6144]{1,0:T(8,128)(2,1)} custom-call(s32[4,128]{1,0:T(4,128)S(1)} %bitcast.24, bf16[72,3072]{1,0:T(8,128)(2,1)S(1)} %collective-permute-done.24.refs_0_, bf16[72,3072]{1,0:T(8,128)(2,1)S(1)} %collective-permute-done.25.refs_1_, bf16[72,3072]{1,0:T(8,128)(2,1)S(1)} %get-tuple-element.203.refs_2_, ...), custom_call_target="tpu_custom_call" | custom-call | flops 400000000 | bytes 4500000 | tf_op jit(solution)/shard_map/finish/pallas_call | solution.py:320
  (92 shorter events, 25.5 us)
Async XLA Ops:
  3.6 13.6 %collective-permute-start.1 = (bf16[72,3200]{1,0:T(8,128)(2,1)S(1)}, bf16[72,3200]{1,0:T(8,128)(2,1)S(1)}, u32[]{:S(2)}, u32[]{:S(2)}) collective-permute-start(bf16[72,3200]{1,0:T(8,128)(2,1)S(1)} %prepare.1.refs_0_), channel_id=1, source_target_pairs={{0,2},{4,0},{8,4},{12,8},{14,12},{10,14},{6,10},{2,6},{1,3},{5,1},... | collective-permute-start | bytes 1382408 | tf_op jit(solution)/shard_map/ppermute | solution.py:336
  6.6 12.0 %collective-permute-start = (bf16[72,3200]{1,0:T(8,128)(2,1)S(1)}, bf16[72,3200]{1,0:T(8,128)(2,1)S(1)}, u32[]{:S(2)}, u32[]{:S(2)}) collective-permute-start(bf16[72,3200]{1,0:T(8,128)(2,1)S(1)} %prepare.1.refs_0_), channel_id=1, source_target_pairs={{0,4},{4,8},{8,12},{12,14},{14,10},{10,6},{6,2},{2,0},{1,5},{5,9},... | collective-permute-start | bytes 1382408 | tf_op jit(solution)/shard_map/ppermute | solution.py:333
  18.6 11.1 %collective-permute-start.2 = (bf16[72,3200]{1,0:T(8,128)(2,1)S(1)}, bf16[72,3200]{1,0:T(8,128)(2,1)S(1)}, u32[]{:S(2)}, u32[]{:S(2)}) collective-permute-start(bf16[72,3200]{1,0:T(8,128)(2,1)S(1)} %collective-permute-done.refs_1_), channel_id=1, source_target_pairs={{0,4},{4,8},{8,12},{12,14},{14,10},{10,6},{6,2},{2,0},{1,5},{5,9},... | collective-permute-start | bytes 1382408 | tf_op jit(solution)/shard_map/ppermute | solution.py:333
  19.0 11.1 %collective-permute-start.3 = (bf16[72,3200]{1,0:T(8,128)(2,1)S(1)}, bf16[72,3200]{1,0:T(8,128)(2,1)S(1)}, u32[]{:S(2)}, u32[]{:S(2)}) collective-permute-start(bf16[72,3200]{1,0:T(8,128)(2,1)S(1)} %collective-permute-done.1.refs_2_), channel_id=1, source_target_pairs={{0,2},{4,0},{8,4},{12,8},{14,12},{10,14},{6,10},{2,6},{1,3},{5,1},... | collective-permute-start | bytes 1382408 | tf_op jit(solution)/shard_map/ppermute | solution.py:336
  30.2 12.6 %collective-permute-start.4 = (bf16[72,3200]{1,0:T(8,128)(2,1)S(1)}, bf16[72,3200]{1,0:T(8,128)(2,1)S(1)}, u32[]{:S(2)}, u32[]{:S(2)}) collective-permute-start(bf16[72,3200]{1,0:T(8,128)(2,1)S(1)} %collective-permute-done.2.refs_0_), channel_id=1, source_target_pairs={{0,4},{4,8},{8,12},{12,14},{14,10},{10,6},{6,2},{2,0},{1,5},{5,9},... | collective-permute-start | bytes 1382408 | tf_op jit(solution)/shard_map/ppermute | solution.py:333
  31.7 11.1 %collective-permute-start.5 = (bf16[72,3200]{1,0:T(8,128)(2,1)S(1)}, bf16[72,3200]{1,0:T(8,128)(2,1)S(1)}, u32[]{:S(2)}, u32[]{:S(2)}) collective-permute-start(bf16[72,3200]{1,0:T(8,128)(2,1)S(1)} %collective-permute-done.3.refs_1_), channel_id=1, source_target_pairs={{0,2},{4,0},{8,4},{12,8},{14,12},{10,14},{6,10},{2,6},{1,3},{5,1},... | collective-permute-start | bytes 1382408 | tf_op jit(solution)/shard_map/ppermute | solution.py:336
  32.2 10.5 %collective-permute-start.6 = (f32[40,64]{1,0:T(8,128)S(1)}, f32[40,64]{1,0:T(8,128)S(1)}, u32[]{:S(2)}, u32[]{:S(2)}) collective-permute-start(f32[40,64]{1,0:T(8,128)S(1)} %get-tuple-element.122), channel_id=1, source_target_pairs={{0,2},{4,0},{8,4},{12,8},{14,12},{10,14},{6,10},{2,6},{1,3},{5,1},... | collective-permute-start | bytes 30728 | tf_op jit(solution)/shard_map/ppermute | solution.py:388
  33.5 9.2 %collective-permute-start.7 = (f32[40,64]{1,0:T(8,128)S(1)}, f32[40,64]{1,0:T(8,128)S(1)}, u32[]{:S(2)}, u32[]{:S(2)}) collective-permute-start(f32[40,64]{1,0:T(8,128)S(1)} %get-tuple-element.123), channel_id=1, source_target_pairs={{0,4},{4,8},{8,12},{12,14},{14,10},{10,6},{6,2},{2,0},{1,5},{5,9},... | collective-permute-start | bytes 30728 | tf_op jit(solution)/shard_map/ppermute | solution.py:388
  42.8 12.0 %collective-permute-start.9 = (bf16[40,3200]{1,0:T(8,128)(2,1)S(1)}, bf16[40,3200]{1,0:T(8,128)(2,1)S(1)}, u32[]{:S(2)}, u32[]{:S(2)}) collective-permute-start(bf16[40,3200]{1,0:T(8,128)(2,1)S(1)} %get-tuple-element.127), channel_id=1, source_target_pairs={{0,2},{4,0},{8,4},{12,8},{14,12},{10,14},{6,10},{2,6},{1,3},{5,1},... | collective-permute-start | bytes 768008 | tf_op jit(solution)/shard_map/ppermute | solution.py:336
  43.4 9.8 %collective-permute-start.10 = (f32[40,64]{1,0:T(8,128)S(1)}, f32[40,64]{1,0:T(8,128)S(1)}, u32[]{:S(2)}, u32[]{:S(2)}) collective-permute-start(f32[40,64]{1,0:T(8,128)S(1)} %get-tuple-element.133), channel_id=1, source_target_pairs={{0,6},{4,2},{8,0},{12,4},{14,8},{10,12},{6,14},{2,10},{1,7},{5,3},... | collective-permute-start | bytes 30728 | tf_op jit(solution)/shard_map/ppermute | solution.py:388
  45.6 9.2 %collective-permute-start.11 = (f32[40,64]{1,0:T(8,128)S(1)}, f32[40,64]{1,0:T(8,128)S(1)}, u32[]{:S(2)}, u32[]{:S(2)}) collective-permute-start(f32[40,64]{1,0:T(8,128)S(1)} %get-tuple-element.134), channel_id=1, source_target_pairs={{0,8},{4,12},{8,14},{12,10},{14,6},{10,2},{6,0},{2,4},{1,9},{5,13}... | collective-permute-start | bytes 30728 | tf_op jit(solution)/shard_map/ppermute | solution.py:388
  46.3 8.5 %collective-permute-start.8 = (bf16[32,3200]{1,0:T(8,128)(2,1)S(1)}, bf16[32,3200]{1,0:T(8,128)(2,1)S(1)}, u32[]{:S(2)}, u32[]{:S(2)}) collective-permute-start(bf16[32,3200]{1,0:T(8,128)(2,1)S(1)} %get-tuple-element.126), channel_id=1, source_target_pairs={{0,4},{4,8},{8,12},{12,14},{14,10},{10,6},{6,2},{2,0},{1,5},{5,9},... | collective-permute-start | bytes 614408 | tf_op jit(solution)/shard_map/ppermute | solution.py:333
  50.9 23.5 %collective-permute-start.14 = (f32[40,64]{1,0:T(8,128)S(1)}, f32[40,64]{1,0:T(8,128)S(1)}, u32[]{:S(2)}, u32[]{:S(2)}) collective-permute-start(f32[40,64]{1,0:T(8,128)S(1)} %get-tuple-element.162), channel_id=1, source_target_pairs={{0,10},{4,6},{8,2},{12,0},{14,4},{10,8},{6,12},{2,14},{1,11},{5,7}... | collective-permute-start | bytes 30728 | tf_op jit(solution)/shard_map/ppermute | solution.py:388
  53.1 21.3 %collective-permute-start.15 = (f32[40,64]{1,0:T(8,128)S(1)}, f32[40,64]{1,0:T(8,128)S(1)}, u32[]{:S(2)}, u32[]{:S(2)}) collective-permute-start(f32[40,64]{1,0:T(8,128)S(1)} %get-tuple-element.163), channel_id=1, source_target_pairs={{0,12},{4,14},{8,10},{12,6},{14,2},{10,0},{6,4},{2,8},{1,13},{5,15... | collective-permute-start | bytes 30728 | tf_op jit(solution)/shard_map/ppermute | solution.py:388
  63.1 11.3 %collective-permute-start.16 = (f32[40,64]{1,0:T(8,128)S(1)}, f32[40,64]{1,0:T(8,128)S(1)}, u32[]{:S(2)}, u32[]{:S(2)}) collective-permute-start(f32[40,64]{1,0:T(8,128)S(1)} %get-tuple-element.164), channel_id=1, source_target_pairs={{0,14},{4,10},{8,6},{12,2},{14,0},{10,4},{6,8},{2,12},{1,15},{5,11... | collective-permute-start | bytes 30728 | tf_op jit(solution)/shard_map/ppermute | solution.py:388
  66.5 8.0 %collective-permute-start.12 = (bf16[32,3072]{1,0:T(8,128)(2,1)S(1)}, bf16[32,3072]{1,0:T(8,128)(2,1)S(1)}, u32[]{:S(2)}, u32[]{:S(2)}) collective-permute-start(bf16[32,3072]{1,0:T(8,128)(2,1)S(1)} %get-tuple-element.142), channel_id=1, source_target_pairs={{0,4},{4,8},{8,12},{12,14},{14,10},{10,6},{6,2},{2,0},{1,5},{5,9},... | collective-permute-start | bytes 589832 | tf_op jit(solution)/shard_map/ppermute | solution.py:333
  66.5 8.6 %collective-permute-start.13 = (bf16[40,3072]{1,0:T(8,128)(2,1)S(1)}, bf16[40,3072]{1,0:T(8,128)(2,1)S(1)}, u32[]{:S(2)}, u32[]{:S(2)}) collective-permute-start(bf16[40,3072]{1,0:T(8,128)(2,1)S(1)} %get-tuple-element.143), channel_id=1, source_target_pairs={{0,2},{4,0},{8,4},{12,8},{14,12},{10,14},{6,10},{2,6},{1,3},{5,1},... | collective-permute-start | bytes 737288 | tf_op jit(solution)/shard_map/ppermute | solution.py:336
  75.2 8.6 %collective-permute-start.17 = (bf16[72,3072]{1,0:T(8,128)(2,1)S(1)}, bf16[72,3072]{1,0:T(8,128)(2,1)S(1)}, u32[]{:S(2)}, u32[]{:S(2)}) collective-permute-start(bf16[72,3072]{1,0:T(8,128)(2,1)S(1)} %get-tuple-element.169), channel_id=1, source_target_pairs={{0,4},{4,8},{8,12},{12,14},{14,10},{10,6},{6,2},{2,0},{1,5},{5,9},... | collective-permute-start | bytes 1327112 | tf_op jit(solution)/shard_map/ppermute | solution.py:333
  75.3 8.8 %collective-permute-start.18 = (bf16[72,3072]{1,0:T(8,128)(2,1)S(1)}, bf16[72,3072]{1,0:T(8,128)(2,1)S(1)}, u32[]{:S(2)}, u32[]{:S(2)}) collective-permute-start(bf16[72,3072]{1,0:T(8,128)(2,1)S(1)} %get-tuple-element.170), channel_id=1, source_target_pairs={{0,2},{4,0},{8,4},{12,8},{14,12},{10,14},{6,10},{2,6},{1,3},{5,1},... | collective-permute-start | bytes 1327112 | tf_op jit(solution)/shard_map/ppermute | solution.py:336
  84.2 20.3 %collective-permute-start.21 = (bf16[72,3072]{1,0:T(8,128)(2,1)S(1)}, bf16[72,3072]{1,0:T(8,128)(2,1)S(1)}, u32[]{:S(2)}, u32[]{:S(2)}) collective-permute-start(bf16[72,3072]{1,0:T(8,128)(2,1)S(1)} %add_convert_fusion.2), channel_id=1, source_target_pairs={{0,2},{4,0},{8,4},{12,8},{14,12},{10,14},{6,10},{2,6},{1,3},{5,1},... | collective-permute-start | bytes 1327112 | tf_op jit(solution)/shard_map/ppermute | solution.py:336
  86.9 17.7 %collective-permute-start.20 = (bf16[72,3072]{1,0:T(8,128)(2,1)S(1)}, bf16[72,3072]{1,0:T(8,128)(2,1)S(1)}, u32[]{:S(2)}, u32[]{:S(2)}) collective-permute-start(bf16[72,3072]{1,0:T(8,128)(2,1)S(1)} %add_convert_fusion.3), channel_id=1, source_target_pairs={{0,4},{4,8},{8,12},{12,14},{14,10},{10,6},{6,2},{2,0},{1,5},{5,9},... | collective-permute-start | bytes 1327112 | tf_op jit(solution)/shard_map/ppermute | solution.py:333
  87.6 11.0 %collective-permute-start.22 = (bf16[4,32,768]{2,1,0:T(8,128)(2,1)S(1)}, bf16[4,32,768]{2,1,0:T(8,128)(2,1)S(1)}, u32[]{:S(2)}, u32[]{:S(2)}) collective-permute-start(bf16[4,32,768]{2,1,0:T(8,128)(2,1)S(1)} %get-tuple-element.192), channel_id=1, source_target_pairs={{0,2},{2,0},{4,6},{6,4},{8,10},{10,8},{12,14},{14,12},{1,3},{3,1},... | collective-permute-start | bytes 589832 | tf_op jit(solution)/shard_map/ppermute | solution.py:450
  104.7 11.8 %collective-permute-start.25 = (bf16[72,3072]{1,0:T(8,128)(2,1)S(1)}, bf16[72,3072]{1,0:T(8,128)(2,1)S(1)}, u32[]{:S(2)}, u32[]{:S(2)}) collective-permute-start(bf16[72,3072]{1,0:T(8,128)(2,1)S(1)} %add_convert_fusion), channel_id=1, source_target_pairs={{0,2},{4,0},{8,4},{12,8},{14,12},{10,14},{6,10},{2,6},{1,3},{5,1},... | collective-permute-start | bytes 1327112 | tf_op jit(solution)/shard_map/ppermute | solution.py:336
  105.7 10.8 %collective-permute-start.24 = (bf16[72,3072]{1,0:T(8,128)(2,1)S(1)}, bf16[72,3072]{1,0:T(8,128)(2,1)S(1)}, u32[]{:S(2)}, u32[]{:S(2)}) collective-permute-start(bf16[72,3072]{1,0:T(8,128)(2,1)S(1)} %add_convert_fusion.1), channel_id=1, source_target_pairs={{0,4},{4,8},{8,12},{12,14},{14,10},{10,6},{6,2},{2,0},{1,5},{5,9},... | collective-permute-start | bytes 1327112 | tf_op jit(solution)/shard_map/ppermute | solution.py:333
  (22 other events, 258.1 us)

commit v7 on v6

--- a/solution.py
+++ b/solution.py
@@ -118,12 +118,22 @@
             target[at] = jnp.where(live, rows, 0.0).astype(BF)
 
 
-def halve_kernel(ours, theirs, *outs):
-    count = ours.shape[0]
-    for i in range(count):
-        total = ours[i].astype(F32) + theirs[i].astype(F32)
-        out = outs[i % len(outs)]
-        out[i // len(outs)] = total.astype(out.dtype)
+def low_order_kernel(ring, place, order, *refs):
+    lows, out = refs[:-1], refs[-1]
+    count = len(ring)
+    _, here = place_here(place)
+    for low, r in zip(lows, order):
+        spot = lax.rem(here + r + count, count)
+        owner = sum(jnp.where(spot == i, e, 0) for i, e in enumerate(ring))
+        out[owner] = low[...]
+
+
+def add_kernel(ours, theirs, out):
+    out[...] = (ours[...].astype(F32) + theirs[...].astype(F32)).astype(out.dtype)
+
+
+def sum_kernel(parts, out):
+    out[...] = sum(parts[i].astype(F32) for i in range(parts.shape[0])).astype(out.dtype)
 
 
 def hidden_kernel(capacity, slot, start, count, pieces, *refs):
@@ -223,17 +233,15 @@
             outs[i][:, t : t + TILE] = tile[...].astype(BF)
 
 
-def adapter_kernel(capacity, choice_ref, tokens_ref, *refs):
-    lows, (low_ref, keep_ref, send_ref) = refs[:-3], refs[-3:]
+def adapter_kernel(capacity, choice_ref, tokens_ref, lows, low_ref, keep_ref, send_ref):
     count, part, share = keep_ref.shape
-    low = sum(x[...] for x in lows).astype(BF)
+    low = sum(lows[i] for i in range(count)).astype(BF)
     low_ref[...] = low
     upper, _ = pick_rows(choice_ref[...], capacity)
     low = dot(upper[: low.shape[0]], low, TN).astype(BF)
-    me, core = lax.axis_index("expert"), lax.axis_index("dp")
+    core = lax.axis_index("dp")
     for i in range(count):
-        columns = pl.ds(pl.multiple_of((me ^ i) * share, 128), share)
-        down = dot(low, tokens_ref[:, columns], TN)
+        down = dot(low, tokens_ref[:, i * share : (i + 1) * share], TN)
         keep_ref[i] = jnp.where(core == 0, down[:part], down[part:]).astype(BF)
         send_ref[i] = jnp.where(core == 0, down[part:], down[:part]).astype(BF)
 
@@ -383,12 +391,7 @@
         low_rows.append(results[2])
         lows.extend(results[3:])
 
-    def to_owner(at):
-        r = order[at]
-        lows[at] = lax.ppermute(lows[at], "expert", [(ring[i], ring[(i + r) % n]) for i in range(n)])
-
     going_right = going_left = block
-    sent = [0, 0]
     for s in range(1, middle):
         going_right, going_left = right(going_right), left(going_left)
         if s == 1:
@@ -397,25 +400,24 @@
             )
         else:
             hidden_pass(passes[s - 2])
-            going_right, going_left, dgates[-1], dups[-1], lows[: sent[1]] = lax.optimization_barrier(
-                (going_right, going_left, dgates[-1], dups[-1], lows[: sent[1]])
+            going_right, going_left, dgates[-1], dups[-1] = lax.optimization_barrier(
+                (going_right, going_left, dgates[-1], dups[-1])
             )
-            sent = [sent[1], len(lows)]
-            for at in range(max(sent[0], 1), sent[1]):
-                to_owner(at)
         got[-s], got[s] = (going_right,), (going_left,)
     right_top, left_rest = call(
         cut_kernel, "cut", [((h, wide), BF) for h in heights], [going_right, going_left]
     )
     right_top, left_rest = right(right_top), left(left_rest)
     hidden_pass(passes[-2])
-    right_top, left_rest, dgates[-1], dups[-1], lows[: sent[1]] = lax.optimization_barrier(
-        (right_top, left_rest, dgates[-1], dups[-1], lows[: sent[1]])
-    )
-    for at in range(max(sent[1], 1), len(lows)):
-        to_owner(at)
+    right_top, left_rest, dgates[-1], dups[-1] = lax.optimization_barrier(
+        (right_top, left_rest, dgates[-1], dups[-1])
+    )
     got[middle] = (right_top, left_rest)
     hidden_pass(passes[-1])
+    (low_parts,) = call(
+        functools.partial(low_order_kernel, ring, place, order), "low_order", [((n, slot, rank), F32)], lows
+    )
+    low_parts = lax.all_to_all(low_parts, "expert", 0, 0)
 
     right_top, left_rest = call(
         functools.partial(first_partial_kernel, capacity, slot, cut),
@@ -429,7 +431,6 @@
         ],
         (4 * slot * width * hidden, 4 * hidden * width),
     )
-    right_top, left_rest, lows[-1] = lax.optimization_barrier((right_top, left_rest, lows[-1]))
     own = call(
         functools.partial(partial_kernel, capacity, slot, sizes[:-1]),
         "partials",
@@ -446,16 +447,8 @@
     def add(a, b):
         return (a.astype(F32) + b.astype(F32)).astype(BF)
 
-    def exchange(keep, send, bit):
-        other = lax.ppermute(send, "expert", [(e, e ^ bit) for e in range(n)])
-        count = keep.shape[0]
-        parts = 2 if count > 1 else 1
-        shape = (count // parts,) + keep.shape[1:]
-        return call(halve_kernel, "halve", [(shape, keep.dtype)] * parts, [keep, other])
-
     right_top, left_rest = right(right_top), left(left_rest)
-    to_owner(n - 1)
-    right_top, left_rest, own, lows = lax.optimization_barrier((right_top, left_rest, own, lows))
+    right_top, left_rest, low_parts, own = lax.optimization_barrier((right_top, left_rest, low_parts, own))
     own = dict(zip(order[:-1], own))
     going_right, going_left = call(
         merge_kernel,
@@ -474,20 +467,20 @@
                 functools.partial(adapter_kernel, capacity),
                 "adapter_gradient",
                 [((slot, rank), BF)] + [((n, part, share), BF)] * 2,
-                [choice, tokens, *lows],
+                [choice, tokens, low_parts],
                 work=(2 * own_count * rank * width, 2 * own_count * width),
             )
         else:
-            me, core = lax.axis_index("expert"), lax.axis_index("dp")
+            core = lax.axis_index("dp")
             upper, _ = pick_rows(choice, capacity)
-            low = sum(lows).astype(BF)
+            low = jnp.sum(low_parts, axis=0).astype(BF)
             low_tokens = dot(upper[:slot], low, TN).astype(BF)
             down = dot(low_tokens, tokens, TN).astype(BF).reshape(rank, n, share)
-            down = down.transpose(1, 0, 2)[jnp.arange(n, dtype=jnp.int32) ^ me]
+            down = down.transpose(1, 0, 2)
             keep = jnp.where(core == 0, down[:, :part], down[:, part:])
             send = jnp.where(core == 0, down[:, part:], down[:, :part])
         other = lax.ppermute(send, "dp", swap)
-        return low, call(halve_kernel, "halve", [((n // 2, part, share), BF)] * 2, [keep, other])
+        return low, call(add_kernel, "add_dp", [((n, part, share), BF)], [keep, other])[0]
 
     def lora_gradients():
         (local,) = call(
@@ -504,22 +497,17 @@
         )
         return local, lax.ppermute(local, "dp", swap)
 
-    bits = [1 << i for i in range(n.bit_length() - 1)]
     for hop, s in enumerate(range(middle - 1, 0, -1)):
         going_right, going_left = right(going_right), left(going_left)
         if hop == 0:
-            low, pair = adapter_gradient()
-        elif hop == 1:
-            for bit in bits[:2]:
-                pair = exchange(*pair, bit)
-            low_rows, pair = lax.optimization_barrier((low_rows, pair))
+            low, parts = adapter_gradient()
+            going_right, going_left, parts = lax.optimization_barrier((going_right, going_left, parts))
+            parts = lax.all_to_all(parts, "expert", 0, 0)
         if s > 1:
-            going_right, going_left, pair = lax.optimization_barrier((going_right, going_left, pair))
             going_right, going_left = add(going_right, own[s - 1]), add(going_left, own[1 - s])
+    low_rows, parts = lax.optimization_barrier((low_rows, parts))
     lora, lora_there = lora_gradients()
-    for bit in bits[2:]:
-        pair = exchange(*pair, bit)
-    down = pair[0][0]
+    (down,) = call(sum_kernel, "sum_expert", [((part, share), BF)], [parts])
     there = lax.ppermute(down, "dp", swap)
     grad_down, grad_gate, grad_up = call(
         join_kernel,

time: 119 us -> 150 us (1.26)
  local copies, waits for them, and re-layouts: 7.57 us -> 36.2 us
  other arithmetic: 0.42 us -> 7.8 us
  waiting for transfers between devices: 44.9 us -> 39.7 us
  starting transfers between devices: 33.9 us -> 30.1 us
  Pallas kernels: 30.7 us -> 34.4 us
    unnamed x34 -> x77, local copies, waits for them, and re-layouts: 7.57 us -> 34.7 us
    ppermute x10 -> x0, waiting for transfers between devices: 26.8 us -> none  [the longest x3 21.3 us: exchange(): other = lax.ppermute(send, 'expert', [(e, e ^ bit) for e in range(n)])]
    ppermute x8, waiting for transfers between devices: 9.68 us -> 25.4 us  [left(): return lax.ppermute(x, 'expert', to_left)]
    ppermute x10 -> x0, starting transfers between devices: 14.6 us -> none  [the longest x7 12.2 us: to_owner(): lax.ppermute(lows[at], 'expert', [(ring[i], ring[(i + r) % n]) for i in r...]
    all_to_all x0 -> x2, starting transfers between devices: none -> 10.2 us  [the longest x1 5.59 us: on_device(): low_parts = lax.all_to_all(low_parts, 'expert', 0, 0)]
    ppermute x8, waiting for transfers between devices: 5.56 us -> 11.8 us  [right(): return lax.ppermute(x, 'expert', to_right)]
    convert_element_type x4, other arithmetic: 0.42 us -> 6.35 us  [add(): return (a.astype(F32) + b.astype(F32)).astype(BF)]
    ppermute x8, starting transfers between devices: 5.61 us -> 11.2 us  [right(): return lax.ppermute(x, 'expert', to_right)]
  transfers between devices with their start and end apart: 29 -> 21, of which waited for: 13 -> 14; matrix products, arithmetic and copies ran while one was open for 0% -> 6% of each run, Pallas kernels for 22% -> 16%
where the time goes in v7:
time: 150 us; the launch traced here: 149 us
  waiting for transfers between devices  39.7 us (26%)
  local copies, waits for them, and re-layouts  36.2 us (24%)
  Pallas kernels  34.4 us (23%)
  starting transfers between devices  30.1 us (20%)
  other arithmetic  7.8 us (5%)
    unnamed x77, local copies, waits for them, and re-layouts  34.7 us
    pallas_call x17, Pallas kernels, call(): pl.pallas_call(kernel, out_shape=[jax.ShapeDtypeStruct(shape, dtype) for...  34.4 us
    ppermute x8, waiting for transfers between devices, left(): return lax.ppermute(x, 'expert', to_left)  25.4 us
    ppermute x8, waiting for transfers between devices, right(): return lax.ppermute(x, 'expert', to_right)  11.8 us
    ppermute x8, starting transfers between devices, right(): return lax.ppermute(x, 'expert', to_right)  11.2 us
    ppermute x8, starting transfers between devices, left(): return lax.ppermute(x, 'expert', to_left)  7.92 us
    convert_element_type x4, other arithmetic, add(): return (a.astype(F32) + b.astype(F32)).astype(BF)  6.35 us
    all_to_all x1, starting transfers between devices, on_device(): low_parts = lax.all_to_all(low_parts, 'expert', 0, 0)  5.59 us
  transfers between devices with their start and end apart: 21, of which 14 were waited for; matrix products, arithmetic and copies ran while one was open for 6% of the time, Pallas kernels for 16%

profile of v7, /device:TPU:0, one launch (start us, length us, event | category | flops | bytes accessed | tf_op | source)
XLA Modules:
  0.0 149.1 jit_solution(7195844743927208263)
XLA Ops:
  0.6 2.9 %prepare.1.refs_0_ = bf16[72,3200]{1,0:T(8,128)(2,1)S(1)} custom-call(s32[4,128]{1,0:T(4,128)} %bitcast.15, bf16[4,128]{1,0:T(4,128)(2,1)} %bitcast.20, bf16[128,6144]{1,0:T(8,128)(2,1)} %bitcast.19, bf16[128,6144]{1,0:T(8,128)(2,1)} %bitcast.11, bf16[64,6144]{1,0:T(8,128)(2,1)} %refs_4_.7), custom_call_target="tpu_custom_call" | custom-call | flops 400000000 | bytes 4500000 | tf_op jit(solution)/shard_map/prepare/pallas_call | solution.py:328
  3.6 3.0 %collective-permute-start.1 = (bf16[72,3200]{1,0:T(8,128)(2,1)S(1)}, bf16[72,3200]{1,0:T(8,128)(2,1)S(1)}, u32[]{:S(2)}, u32[]{:S(2)}) collective-permute-start(bf16[72,3200]{1,0:T(8,128)(2,1)S(1)} %prepare.1.refs_0_), channel_id=1, source_target_pairs={{0,2},{4,0},{8,4},{12,8},{14,12},{10,14},{6,10},{2,6},{1,3},{5,1},... | collective-permute-start | bytes 1382408 | tf_op jit(solution)/shard_map/ppermute | solution.py:344
  9.0 8.3 %collective-permute-done.1.refs_2_ = bf16[72,3200]{1,0:T(8,128)(2,1)S(1)} collective-permute-done((bf16[72,3200]{1,0:T(8,128)(2,1)S(1)}, bf16[72,3200]{1,0:T(8,128)(2,1)S(1)}, u32[]{:S(2)}, u32[]{:S(2)}) %collective-permute-start.1) | collective-permute-done | bytes 460832 | tf_op jit(solution)/shard_map/ppermute | solution.py:344
  20.7 3.7 %copy-done = bf16[768,6144]{1,0:T(8,128)(2,1)S(1)} copy-done((bf16[768,6144]{1,0:T(8,128)(2,1)S(1)}, bf16[768,6144]{1,0:T(8,128)(2,1)}, u32[]{:S(2)}) %copy-start) | copy-done | bytes 9437208
  26.1 3.1 %hidden_rows.4 = (bf16[3,40,768]{2,1,0:T(8,128)(2,1)S(1)}, bf16[3,40,768]{2,1,0:T(8,128)(2,1)S(1)}, bf16[3,40,64]{2,1,0:T(8,128)(2,1)S(1)}, f32[40,64]{1,0:T(8,1...) custom-call(bf16[72,3200]{1,0:T(8,128)(2,1)S(1)} %prepare.1.refs_0_, ...), custom_call_target="tpu_custom_call" | custom-call | flops 2264924160 | bytes 9437184 | tf_op jit(solution)/shard_map/hidden_rows/pallas_call | solution.py:328
  32.2 3.1 %hidden_rows.5 = (bf16[2,40,768]{2,1,0:T(8,128)(2,1)S(1)}, bf16[2,40,768]{2,1,0:T(8,128)(2,1)S(1)}, bf16[2,40,64]{2,1,0:T(8,128)(2,1)S(1)}, f32[40,64]{1,0:T(8,128)S(1)}, f32[40,64]{1,0:T(8,128)S(1)}) custom-call(bf16[72,3200]{1,0:T(8,128)(2,1)S(1)} %collective-permute-done.2.refs_0_, bf16[72,3200]{1,0:T(8,128)(2,1)S(1)} %collective-permute-done.3.refs_1_, ...), custom_call_target="tpu_custom_call" | custom-call | flops 2415919104 | bytes 9437184 | tf_op jit(solution)/shard_map/hidden_rows/pallas_call | solution.py:328
  35.9 4.5 %collective-permute-done.4.right_in.refs_0_ = bf16[72,3200]{1,0:T(8,128)(2,1)S(1)} collective-permute-done((bf16[72,3200]{1,0:T(8,128)(2,1)S(1)}, bf16[72,3200]{1,0:T(8,128)(2,1)S(1)}, u32[]{:S(2)}, u32[]{:S(2)}) %collective-permute-start.4) | collective-permute-done | bytes 460832 | tf_op jit(solution)/shard_map/ppermute | solution.py:341
  44.5 3.1 %hidden_rows.6 = (bf16[2,40,768]{2,1,0:T(8,128)(2,1)S(1)}, bf16[2,40,768]{2,1,0:T(8,128)(2,1)S(1)}, bf16[2,40,64]{2,1,0:T(8,128)(2,1)S(1)}, f32[40,64]{1,0:T(8,128)S(1)}, f32[40,64]{1,0:T(8,128)S(1)}) custom-call(bf16[72,3200]{1,0:T(8,128)(2,1)S(1)} %collective-permute-done.4.right_in.refs_0_, bf16[72,3200]{1,0:T(8,128)(2,1)S(1)} %collective-permute-done.5.left_in.refs_1_, ...), custom_call_target="tpu_custom_call" | custom-call | flops 2415919104 | bytes 9437184 | tf_op jit(solution)/shard_map/hidden_rows/pallas_call | solution.py:328
  48.7 2.9 %hidden_rows.7 = (bf16[1,40,768]{2,1,0:T(8,128)(2,1)S(1)}, bf16[1,40,768]{2,1,0:T(8,128)(2,1)S(1)}, bf16[1,40,64]{2,1,0:T(8,128)(2,1)S(1)}, f32[40,64]{1,0:T(8,128)S(1)}) custom-call(bf16[32,3200]{1,0:T(8,128)(2,1)S(1)} %collective-permute-done.6.refs_0_, bf16[40,3200]{1,0:T(8,128)(2,1)S(1)} %collective-permute-done.7.refs_1_, ...), custom_call_target="tpu_custom_call" | custom-call | flops 1207959552 | bytes 9437184 | tf_op jit(solution)/shard_map/hidden_rows/pallas_call | solution.py:328
  53.1 5.6 %all-to-all-start = ((f32[8,1,2560]{2,1,0:T(1,128)}), f32[8,1,2560]{2,1,0:T(1,128)S(1)}, u32[]{:S(2)}, u32[]{:S(2)}) async-start(f32[8,1,2560]{2,1,0:T(1,128)} %reshape.8), calls=%async_computation | async-start | bytes 163840 | tf_op jit(solution)/shard_map/all_to_all | solution.py:420
  58.7 3.7 %copy-done.2 = bf16[6144,768]{1,0:T(8,128)(2,1)S(1)} copy-done((bf16[6144,768]{1,0:T(8,128)(2,1)S(1)}, bf16[6144,768]{1,0:T(8,128)(2,1)}, u32[]{:S(2)}) %copy-start.2) | copy-done | bytes 9437208
  62.4 3.7 %copy-done.4 = bf16[6144,768]{1,0:T(8,128)(2,1)S(1)} copy-done((bf16[6144,768]{1,0:T(8,128)(2,1)S(1)}, bf16[6144,768]{1,0:T(8,128)(2,1)}, u32[]{:S(2)}) %copy-start.4) | copy-done | bytes 9437208
  66.1 6.0 %first_partial.1 = (bf16[32,3072]{1,0:T(8,128)(2,1)}, bf16[40,3072]{1,0:T(8,128)(2,1)}) custom-call(bf16[1,40,768]{2,1,0:T(8,128)(2,1)S(1)} %get-tuple-element.99.dgate_in.refs_3_, bf16[1,40,768]{2,1,0:T(8,128)(2,1)S(1)} %get-tuple-element.100.dup_in.refs_7_, bf16[6144,768]{1,0:T(8,128)(2,1)S(1)} %copy-done.2, bf16[6144,768]{1,0:T(8,128)(2,1)S(1)} %copy-done.4), custom_call_target="tpu_custom_call" | custom-call | flops 754974720 | bytes 18874368 | tf_op jit(solution)/shard_map/first_partial/pallas_call | solution.py:328
  72.1 2.0 %collective-permute-start.8 = (bf16[32,3072]{1,0:T(8,128)(2,1)}, bf16[32,3072]{1,0:T(8,128)(2,1)}, u32[]{:S(2)}, u32[]{:S(2)}) collective-permute-start(bf16[32,3072]{1,0:T(8,128)(2,1)} %get-tuple-element.101), channel_id=1, source_target_pairs={{0,4},{4,8},{8,12},{12,14},{14,10},{10,6},{6,2},{2,0},{1,5},{5,9},... | collective-permute-start | bytes 589832 | tf_op jit(solution)/shard_map/ppermute | solution.py:341
  74.2 3.7 %copy-done.3 = bf16[6144,768]{1,0:T(8,128)(2,1)S(1)} copy-done((bf16[6144,768]{1,0:T(8,128)(2,1)S(1)}, bf16[6144,768]{1,0:T(8,128)(2,1)}, u32[]{:S(2)}) %copy-start.3) | copy-done | bytes 9437208
  77.9 3.7 %copy-done.5 = bf16[6144,768]{1,0:T(8,128)(2,1)S(1)} copy-done((bf16[6144,768]{1,0:T(8,128)(2,1)S(1)}, bf16[6144,768]{1,0:T(8,128)(2,1)}, u32[]{:S(2)}) %copy-start.5) | copy-done | bytes 9437208
  81.6 5.9 %partials.1 = (bf16[72,3072]{1,0:T(8,128)(2,1)S(1)}, bf16[72,3072]{1,0:T(8,128)(2,1)S(1)}, bf16[72,3072]{1,0:T(8,128)(2,1)S(1)}, bf16[72,3072]{1,0:T(8,128)(2,1)...) custom-call(bf16[3,40,768]{2,1,0:T(8,128)(2,1)S(1)} %get-tuple-element.111.refs_0_, ...), custom_call_target="tpu_custom_call" | custom-call | flops 5284823040 | bytes 18874368 | tf_op jit(solution)/shard_map/partials/pallas_call | solution.py:328
  104.6 2.9 %collective-permute-done.10 = bf16[72,3072]{1,0:T(8,128)(2,1)S(1)} collective-permute-done((bf16[72,3072]{1,0:T(8,128)(2,1)S(1)}, bf16[72,3072]{1,0:T(8,128)(2,1)S(1)}, u32[]{:S(2)}, u32[]{:S(2)}) %collective-permute-start.10) | collective-permute-done | bytes 442400 | tf_op jit(solution)/shard_map/ppermute | solution.py:341
  109.6 4.6 %all-to-all-start.1 = ((bf16[8,32,768]{2,1,0:T(8,128)(2,1)}), bf16[8,32,768]{2,1,0:T(8,128)(2,1)S(1)}, u32[]{:S(2)}, u32[]{:S(2)}) async-start(bf16[8,32,768]{2,1,0:T(8,128)(2,1)} %add_dp.1), calls=%async_computation.1 | async-start | bytes 786432 | tf_op jit(solution)/shard_map/all_to_all | solution.py:505
  115.5 2.1 %collective-permute-start.15 = (bf16[72,3072]{1,0:T(8,128)(2,1)S(1)}, bf16[72,3072]{1,0:T(8,128)(2,1)S(1)}, u32[]{:S(2)}, u32[]{:S(2)}) collective-permute-start(bf16[72,3072]{1,0:T(8,128)(2,1)S(1)} %add_convert_fusion.1), channel_id=1, source_target_pairs={{0,2},{4,0},{8,4},{12,8},{14,12},{10,14},{6,10},{2,6},{1,3},{5,1},... | collective-permute-start | bytes 1327112 | tf_op jit(solution)/shard_map/ppermute | solution.py:344
  118.9 11.0 %collective-permute-done.15 = bf16[72,3072]{1,0:T(8,128)(2,1)S(1)} collective-permute-done((bf16[72,3072]{1,0:T(8,128)(2,1)S(1)}, bf16[72,3072]{1,0:T(8,128)(2,1)S(1)}, u32[]{:S(2)}, u32[]{:S(2)}) %collective-permute-start.15) | collective-permute-done | bytes 442400 | tf_op jit(solution)/shard_map/ppermute | solution.py:344
  133.7 3.6 %collective-permute-start.14 = (bf16[72,3072]{1,0:T(8,128)(2,1)}, bf16[72,3072]{1,0:T(8,128)(2,1)}, u32[]{:S(2)}, u32[]{:S(2)}) collective-permute-start(bf16[72,3072]{1,0:T(8,128)(2,1)} %add_convert_fusion.2), channel_id=1, source_target_pairs={{0,4},{4,8},{8,12},{12,14},{14,10},{10,6},{6,2},{2,0},{1,5},{5,9},... | collective-permute-start | bytes 1327112 | tf_op jit(solution)/shard_map/ppermute | solution.py:341
  141.6 2.4 %collective-permute-done.16.refs_1_ = bf16[72,3072]{1,0:T(8,128)(2,1)S(1)} collective-permute-done((bf16[72,3072]{1,0:T(8,128)(2,1)}, bf16[72,3072]{1,0:T(8,128)(2,1)S(1)}, u32[]{:S(2)}, u32[]{:S(2)}) %collective-permute-start.16) | collective-permute-done | bytes 442400 | tf_op jit(solution)/shard_map/ppermute | solution.py:344
  146.1 3.0 %finish.1 = bf16[128,6144]{1,0:T(8,128)(2,1)} custom-call(s32[4,128]{1,0:T(4,128)S(1)} %bitcast.17, bf16[72,3072]{1,0:T(8,128)(2,1)} %collective-permute-done.14.refs_0_, bf16[72,3072]{1,0:T(8,128)(2,1)S(1)} %collective-permute-done.16.refs_1_, bf16[72,3072]{1,0:T(8,128)(2,1)S(1)} %copy-done.23, bf16[40,64]{1,0:T(8,128)(2,1)S(1)} %copy-done.36, ...), custom_call_target="tpu_custom_call" | custom-call | flops 400000000 | bytes 4500000 | tf_op jit(solution)/shard_map/finish/pallas_call | solution.py:328
  (119 shorter events, 49.9 us)
Async XLA Ops:
  3.6 13.6 %collective-permute-start.1 = (bf16[72,3200]{1,0:T(8,128)(2,1)S(1)}, bf16[72,3200]{1,0:T(8,128)(2,1)S(1)}, u32[]{:S(2)}, u32[]{:S(2)}) collective-permute-start(bf16[72,3200]{1,0:T(8,128)(2,1)S(1)} %prepare.1.refs_0_), channel_id=1, source_target_pairs={{0,2},{4,0},{8,4},{12,8},{14,12},{10,14},{6,10},{2,6},{1,3},{5,1},... | collective-permute-start | bytes 1382408 | tf_op jit(solution)/shard_map/ppermute | solution.py:344
  6.6 12.0 %collective-permute-start = (bf16[72,3200]{1,0:T(8,128)(2,1)S(1)}, bf16[72,3200]{1,0:T(8,128)(2,1)S(1)}, u32[]{:S(2)}, u32[]{:S(2)}) collective-permute-start(bf16[72,3200]{1,0:T(8,128)(2,1)S(1)} %prepare.1.refs_0_), channel_id=1, source_target_pairs={{0,4},{4,8},{8,12},{12,14},{14,10},{10,6},{6,2},{2,0},{1,5},{5,9},... | collective-permute-start | bytes 1382408 | tf_op jit(solution)/shard_map/ppermute | solution.py:341
  18.6 11.1 %collective-permute-start.2 = (bf16[72,3200]{1,0:T(8,128)(2,1)S(1)}, bf16[72,3200]{1,0:T(8,128)(2,1)S(1)}, u32[]{:S(2)}, u32[]{:S(2)}) collective-permute-start(bf16[72,3200]{1,0:T(8,128)(2,1)S(1)} %collective-permute-done.refs_1_), channel_id=1, source_target_pairs={{0,4},{4,8},{8,12},{12,14},{14,10},{10,6},{6,2},{2,0},{1,5},{5,9},... | collective-permute-start | bytes 1382408 | tf_op jit(solution)/shard_map/ppermute | solution.py:341
  19.0 11.1 %collective-permute-start.3 = (bf16[72,3200]{1,0:T(8,128)(2,1)S(1)}, bf16[72,3200]{1,0:T(8,128)(2,1)S(1)}, u32[]{:S(2)}, u32[]{:S(2)}) collective-permute-start(bf16[72,3200]{1,0:T(8,128)(2,1)S(1)} %collective-permute-done.1.refs_2_), channel_id=1, source_target_pairs={{0,2},{4,0},{8,4},{12,8},{14,12},{10,14},{6,10},{2,6},{1,3},{5,1},... | collective-permute-start | bytes 1382408 | tf_op jit(solution)/shard_map/ppermute | solution.py:344
  30.2 10.2 %collective-permute-start.4 = (bf16[72,3200]{1,0:T(8,128)(2,1)S(1)}, bf16[72,3200]{1,0:T(8,128)(2,1)S(1)}, u32[]{:S(2)}, u32[]{:S(2)}) collective-permute-start(bf16[72,3200]{1,0:T(8,128)(2,1)S(1)} %collective-permute-done.2.refs_0_), channel_id=1, source_target_pairs={{0,4},{4,8},{8,12},{12,14},{14,10},{10,6},{6,2},{2,0},{1,5},{5,9},... | collective-permute-start | bytes 1382408 | tf_op jit(solution)/shard_map/ppermute | solution.py:341
  31.7 10.6 %collective-permute-start.5 = (bf16[72,3200]{1,0:T(8,128)(2,1)S(1)}, bf16[72,3200]{1,0:T(8,128)(2,1)S(1)}, u32[]{:S(2)}, u32[]{:S(2)}) collective-permute-start(bf16[72,3200]{1,0:T(8,128)(2,1)S(1)} %collective-permute-done.3.refs_1_), channel_id=1, source_target_pairs={{0,2},{4,0},{8,4},{12,8},{14,12},{10,14},{6,10},{2,6},{1,3},{5,1},... | collective-permute-start | bytes 1382408 | tf_op jit(solution)/shard_map/ppermute | solution.py:344
  42.4 6.4 %collective-permute-start.7 = (bf16[40,3200]{1,0:T(8,128)(2,1)S(1)}, bf16[40,3200]{1,0:T(8,128)(2,1)S(1)}, u32[]{:S(2)}, u32[]{:S(2)}) collective-permute-start(bf16[40,3200]{1,0:T(8,128)(2,1)S(1)} %get-tuple-element.94), channel_id=1, source_target_pairs={{0,2},{4,0},{8,4},{12,8},{14,12},{10,14},{6,10},{2,6},{1,3},{5,1},... | collective-permute-start | bytes 768008 | tf_op jit(solution)/shard_map/ppermute | solution.py:344
  42.9 5.8 %collective-permute-start.6 = (bf16[32,3200]{1,0:T(8,128)(2,1)S(1)}, bf16[32,3200]{1,0:T(8,128)(2,1)S(1)}, u32[]{:S(2)}, u32[]{:S(2)}) collective-permute-start(bf16[32,3200]{1,0:T(8,128)(2,1)S(1)} %get-tuple-element.93), channel_id=1, source_target_pairs={{0,4},{4,8},{8,12},{12,14},{14,10},{10,6},{6,2},{2,0},{1,5},{5,9},... | collective-permute-start | bytes 614408 | tf_op jit(solution)/shard_map/ppermute | solution.py:341
  53.1 39.8 %all-to-all-start = ((f32[8,1,2560]{2,1,0:T(1,128)}), f32[8,1,2560]{2,1,0:T(1,128)S(1)}, u32[]{:S(2)}, u32[]{:S(2)}) async-start(f32[8,1,2560]{2,1,0:T(1,128)} %reshape.8), calls=%async_computation | async-start | bytes 163840 | tf_op jit(solution)/shard_map/all_to_all | solution.py:420
  72.1 23.8 %collective-permute-start.8 = (bf16[32,3072]{1,0:T(8,128)(2,1)}, bf16[32,3072]{1,0:T(8,128)(2,1)}, u32[]{:S(2)}, u32[]{:S(2)}) collective-permute-start(bf16[32,3072]{1,0:T(8,128)(2,1)} %get-tuple-element.101), channel_id=1, source_target_pairs={{0,4},{4,8},{8,12},{12,14},{14,10},{10,6},{6,2},{2,0},{1,5},{5,9},... | collective-permute-start | bytes 589832 | tf_op jit(solution)/shard_map/ppermute | solution.py:341
  74.1 21.8 %collective-permute-start.9 = (bf16[40,3072]{1,0:T(8,128)(2,1)}, bf16[40,3072]{1,0:T(8,128)(2,1)}, u32[]{:S(2)}, u32[]{:S(2)}) collective-permute-start(bf16[40,3072]{1,0:T(8,128)(2,1)} %get-tuple-element.102), channel_id=1, source_target_pairs={{0,2},{4,0},{8,4},{12,8},{14,12},{10,14},{6,10},{2,6},{1,3},{5,1},... | collective-permute-start | bytes 737288 | tf_op jit(solution)/shard_map/ppermute | solution.py:344
  81.6 55.7 %copy-start.25 = (bf16[1,40,768]{2,1,0:T(8,128)(2,1)S(1)}, bf16[1,40,768]{2,1,0:T(8,128)(2,1)}, u32[]{:S(2)}) copy-start(bf16[1,40,768]{2,1,0:T(8,128)(2,1)} %copy-done.24) | copy-start | bytes 184324
  81.6 55.7 %copy-start.29 = (bf16[2,40,64]{2,1,0:T(8,128)(2,1)S(1)}, bf16[2,40,64]{2,1,0:T(8,128)(2,1)}, u32[]{:S(2)}) copy-start(bf16[2,40,64]{2,1,0:T(8,128)(2,1)} %copy-done.28) | copy-start | bytes 30724
  81.6 55.7 %copy-start.34 = (bf16[1,40,64]{2,1,0:T(8,128)(2,1)S(1)}, bf16[1,40,64]{2,1,0:T(8,128)(2,1)}, u32[]{:S(2)}) copy-start(bf16[1,40,64]{2,1,0:T(8,128)(2,1)} %copy-done.33) | copy-start | bytes 15364
  99.2 8.4 %collective-permute-start.10 = (bf16[72,3072]{1,0:T(8,128)(2,1)S(1)}, bf16[72,3072]{1,0:T(8,128)(2,1)S(1)}, u32[]{:S(2)}, u32[]{:S(2)}) collective-permute-start(bf16[72,3072]{1,0:T(8,128)(2,1)S(1)} %get-tuple-element.128), channel_id=1, source_target_pairs={{0,4},{4,8},{8,12},{12,14},{14,10},{10,6},{6,2},{2,0},{1,5},{5,9},... | collective-permute-start | bytes 1327112 | tf_op jit(solution)/shard_map/ppermute | solution.py:341
  101.2 8.4 %collective-permute-start.11 = (bf16[72,3072]{1,0:T(8,128)(2,1)S(1)}, bf16[72,3072]{1,0:T(8,128)(2,1)}, u32[]{:S(2)}, u32[]{:S(2)}) collective-permute-start(bf16[72,3072]{1,0:T(8,128)(2,1)S(1)} %get-tuple-element.129), channel_id=1, source_target_pairs={{0,2},{4,0},{8,4},{12,8},{14,12},{10,14},{6,10},{2,6},{1,3},{5,1},... | collective-permute-start | bytes 1327112 | tf_op jit(solution)/shard_map/ppermute | solution.py:344
  102.0 1.8 %collective-permute-start.12 = (bf16[8,32,768]{2,1,0:T(8,128)(2,1)S(1)}, bf16[8,32,768]{2,1,0:T(8,128)(2,1)S(1)}, u32[]{:S(2)}, u32[]{:S(2)}) collective-permute-start(bf16[8,32,768]{2,1,0:T(8,128)(2,1)S(1)} %get-tuple-element.132), channel_id=1, source_target_pairs={{0,1},{1,0},{2,3},{3,2},{4,5},{5,4},{6,7},{7,6},{8,9},{9,8},{10,11... | collective-permute-start | bytes 1179656 | tf_op jit(solution)/shard_map/ppermute | solution.py:482
  109.6 27.7 %all-to-all-start.1 = ((bf16[8,32,768]{2,1,0:T(8,128)(2,1)}), bf16[8,32,768]{2,1,0:T(8,128)(2,1)S(1)}, u32[]{:S(2)}, u32[]{:S(2)}) async-start(bf16[8,32,768]{2,1,0:T(8,128)(2,1)} %add_dp.1), calls=%async_computation.1 | async-start | bytes 786432 | tf_op jit(solution)/shard_map/all_to_all | solution.py:505
  115.5 14.4 %collective-permute-start.15 = (bf16[72,3072]{1,0:T(8,128)(2,1)S(1)}, bf16[72,3072]{1,0:T(8,128)(2,1)S(1)}, u32[]{:S(2)}, u32[]{:S(2)}) collective-permute-start(bf16[72,3072]{1,0:T(8,128)(2,1)S(1)} %add_convert_fusion.1), channel_id=1, source_target_pairs={{0,2},{4,0},{8,4},{12,8},{14,12},{10,14},{6,10},{2,6},{1,3},{5,1},... | collective-permute-start | bytes 1327112 | tf_op jit(solution)/shard_map/ppermute | solution.py:344
  118.8 13.0 %collective-permute-start.13 = (bf16[72,3072]{1,0:T(8,128)(2,1)S(1)}, bf16[72,3072]{1,0:T(8,128)(2,1)S(1)}, u32[]{:S(2)}, u32[]{:S(2)}) collective-permute-start(bf16[72,3072]{1,0:T(8,128)(2,1)S(1)} %add_convert_fusion.3), channel_id=1, source_target_pairs={{0,4},{4,8},{8,12},{12,14},{14,10},{10,6},{6,2},{2,0},{1,5},{5,9},... | collective-permute-start | bytes 1327112 | tf_op jit(solution)/shard_map/ppermute | solution.py:341
  131.8 12.2 %collective-permute-start.16 = (bf16[72,3072]{1,0:T(8,128)(2,1)}, bf16[72,3072]{1,0:T(8,128)(2,1)S(1)}, u32[]{:S(2)}, u32[]{:S(2)}) collective-permute-start(bf16[72,3072]{1,0:T(8,128)(2,1)} %add_convert_fusion), channel_id=1, source_target_pairs={{0,2},{4,0},{8,4},{12,8},{14,12},{10,14},{6,10},{2,6},{1,3},{5,1},... | collective-permute-start | bytes 1327112 | tf_op jit(solution)/shard_map/ppermute | solution.py:344
  133.7 11.7 %collective-permute-start.14 = (bf16[72,3072]{1,0:T(8,128)(2,1)}, bf16[72,3072]{1,0:T(8,128)(2,1)}, u32[]{:S(2)}, u32[]{:S(2)}) collective-permute-start(bf16[72,3072]{1,0:T(8,128)(2,1)} %add_convert_fusion.2), channel_id=1, source_target_pairs={{0,4},{4,8},{8,12},{12,14},{14,10},{10,6},{6,2},{2,0},{1,5},{5,9},... | collective-permute-start | bytes 1327112 | tf_op jit(solution)/shard_map/ppermute | solution.py:341
  139.2 1.6 %collective-permute-start.18 = (bf16[128,768]{1,0:T(8,128)(2,1)S(1)}, bf16[128,768]{1,0:T(8,128)(2,1)S(1)}, u32[]{:S(2)}, u32[]{:S(2)}) collective-permute-start(bf16[128,768]{1,0:T(8,128)(2,1)S(1)} %lora_rows.1.lora_ref), channel_id=1, source_target_pairs={{0,1},{1,0},{2,3},{3,2},{4,5},{5,4},{6,7},{7,6},{8,9},{9,8},{10,11... | collective-permute-start | bytes 589832 | tf_op jit(solution)/shard_map/ppermute | solution.py:498
  139.4 1.4 collective-permute-start.17
  (35 other events, 304.9 us)

commit v8 on v6

--- a/solution.py
+++ b/solution.py
@@ -116,6 +116,24 @@
             at = jnp.where(2 * away < count, 2 * away, 2 * (count - away) - 1)
             rows = tall[e * capacity : e * capacity + slot, :]
             target[at] = jnp.where(live, rows, 0.0).astype(BF)
+
+
+def low_order_kernel(ring, place, order, *refs):
+    lows, (keep, send) = refs[:-2], refs[-2:]
+    count = len(ring)
+    me, here = place_here(place)
+    for low, r in zip(lows, order):
+        spot = lax.rem(here + r + count, count)
+        owner = sum(jnp.where(spot == i, e, 0) for i, e in enumerate(ring))
+        key = owner ^ me
+
+        @pl.when(key % 2 == 0)
+        def _(low=low, key=key):
+            keep[key // 2] = low[...]
+
+        @pl.when(key % 2 == 1)
+        def _(low=low, key=key):
+            send[key // 2] = low[...]
 
 
 def halve_kernel(ours, theirs, *outs):
@@ -188,20 +206,7 @@
     lora_out[rank:, :] = (SCALE * dot(low[...], dup[...], TN)).astype(BF)
 
 
-def first_partial_kernel(capacity, slot, cut, dgate_in, dup_in, gate_ref, up_ref, top, rest, dgate, dup, tile):
-    half = gate_ref.shape[0] // 2
-    dgate[:slot, :] = dgate_in[0]
-    dup[:slot, :] = dup_in[0]
-    step = tile.shape[1]
-    for t in range(0, half, step):
-        for at, place in ((t, 0), (t + half, capacity)):
-            total = dot(gate_ref[at : at + step, :], dgate[...], NT) + dot(up_ref[at : at + step, :], dup[...], NT)
-            tile[place : place + capacity, :] = total.T[:capacity]
-        top[:, t : t + step] = tile[:cut, :].astype(BF)
-        rest[:, t : t + step] = tile[cut:, :].astype(BF)
-
-
-def partial_kernel(capacity, slot, groups, *refs):
+def partial_kernel(capacity, slot, groups, cut, *refs):
     members, pieces = sum(groups), len(groups)
     dgates, dups, refs = refs[:pieces], refs[pieces : 2 * pieces], refs[2 * pieces :]
     gate_ref, up_ref, outs, (dgate, dup, tile) = refs[0], refs[1], refs[2:-3], refs[-3:]
@@ -220,13 +225,16 @@
             at = i * slot
             tile[:capacity, :] = sums[0][at : at + capacity]
             tile[capacity:, :] = sums[1][at : at + capacity]
-            outs[i][:, t : t + TILE] = tile[...].astype(BF)
-
-
-def adapter_kernel(capacity, choice_ref, tokens_ref, *refs):
-    lows, (low_ref, keep_ref, send_ref) = refs[:-3], refs[-3:]
+            if i < members - 1:
+                outs[i][:, t : t + TILE] = tile[...].astype(BF)
+            else:
+                outs[i][:, t : t + TILE] = tile[:cut, :].astype(BF)
+                outs[i + 1][:, t : t + TILE] = tile[cut:, :].astype(BF)
+
+
+def adapter_kernel(capacity, choice_ref, tokens_ref, low_in, low_ref, keep_ref, send_ref):
     count, part, share = keep_ref.shape
-    low = sum(x[...] for x in lows).astype(BF)
+    low = low_in[0].astype(BF)
     low_ref[...] = low
     upper, _ = pick_rows(choice_ref[...], capacity)
     low = dot(upper[: low.shape[0]], low, TN).astype(BF)
@@ -383,12 +391,7 @@
         low_rows.append(results[2])
         lows.extend(results[3:])
 
-    def to_owner(at):
-        r = order[at]
-        lows[at] = lax.ppermute(lows[at], "expert", [(ring[i], ring[(i + r) % n]) for i in range(n)])
-
     going_right = going_left = block
-    sent = [0, 0]
     for s in range(1, middle):
         going_right, going_left = right(going_right), left(going_left)
         if s == 1:
@@ -397,51 +400,40 @@
             )
         else:
             hidden_pass(passes[s - 2])
-            going_right, going_left, dgates[-1], dups[-1], lows[: sent[1]] = lax.optimization_barrier(
-                (going_right, going_left, dgates[-1], dups[-1], lows[: sent[1]])
+            going_right, going_left, dgates[-1], dups[-1] = lax.optimization_barrier(
+                (going_right, going_left, dgates[-1], dups[-1])
             )
-            sent = [sent[1], len(lows)]
-            for at in range(max(sent[0], 1), sent[1]):
-                to_owner(at)
         got[-s], got[s] = (going_right,), (going_left,)
     right_top, left_rest = call(
         cut_kernel, "cut", [((h, wide), BF) for h in heights], [going_right, going_left]
     )
     right_top, left_rest = right(right_top), left(left_rest)
     hidden_pass(passes[-2])
-    right_top, left_rest, dgates[-1], dups[-1], lows[: sent[1]] = lax.optimization_barrier(
-        (right_top, left_rest, dgates[-1], dups[-1], lows[: sent[1]])
-    )
-    for at in range(max(sent[1], 1), len(lows)):
-        to_owner(at)
+    right_top, left_rest, dgates[-1], dups[-1] = lax.optimization_barrier(
+        (right_top, left_rest, dgates[-1], dups[-1])
+    )
     got[middle] = (right_top, left_rest)
     hidden_pass(passes[-1])
 
-    right_top, left_rest = call(
-        functools.partial(first_partial_kernel, capacity, slot, cut),
-        "first_partial",
-        [((h, half), BF) for h in heights],
-        [dgates[-1], dups[-1], gate_here, up_here],
+    low_keep, low_send = call(
+        functools.partial(low_order_kernel, ring, place, order),
+        "low_order",
+        [((n // 2, slot, rank), F32)] * 2,
+        lows,
+    )
+    *own, right_top, left_rest = call(
+        functools.partial(partial_kernel, capacity, slot, sizes, cut),
+        "partials",
+        [((2 * capacity, half), BF)] * (n - 1) + [((h, half), BF) for h in heights],
+        [*dgates, *dups, gate_here, up_here],
         [
-            pltpu.VMEM((128, hidden), BF),
-            pltpu.VMEM((128, hidden), BF),
-            pltpu.VMEM((2 * capacity, half // 2), F32),
-        ],
-        (4 * slot * width * hidden, 4 * hidden * width),
-    )
-    right_top, left_rest, lows[-1] = lax.optimization_barrier((right_top, left_rest, lows[-1]))
-    own = call(
-        functools.partial(partial_kernel, capacity, slot, sizes[:-1]),
-        "partials",
-        [((2 * capacity, half), BF)] * (n - 1),
-        [*dgates[:-1], *dups[:-1], gate_here, up_here],
-        [
-            pltpu.VMEM(((n - 1) * slot, hidden), BF),
-            pltpu.VMEM(((n - 1) * slot, hidden), BF),
+            pltpu.VMEM((n * slot, hidden), BF),
+            pltpu.VMEM((n * slot, hidden), BF),
             pltpu.VMEM((2 * capacity, TILE), F32),
         ],
-        (4 * (n - 1) * slot * width * hidden, 4 * hidden * width),
-    )
+        (4 * n * slot * width * hidden, 4 * hidden * width),
+    )
+    own = dict(zip(order[:-1], own))
 
     def add(a, b):
         return (a.astype(F32) + b.astype(F32)).astype(BF)
@@ -453,10 +445,12 @@
         shape = (count // parts,) + keep.shape[1:]
         return call(halve_kernel, "halve", [(shape, keep.dtype)] * parts, [keep, other])
 
+    low_keep, right_top, left_rest = lax.optimization_barrier((low_keep, right_top, left_rest))
     right_top, left_rest = right(right_top), left(left_rest)
-    to_owner(n - 1)
-    right_top, left_rest, own, lows = lax.optimization_barrier((right_top, left_rest, own, lows))
-    own = dict(zip(order[:-1], own))
+    bits = [1 << i for i in range(n.bit_length() - 1)]
+    pair = [low_keep, low_send]
+    pair = exchange(*pair, bits[0])
+    right_top, left_rest, pair = lax.optimization_barrier((right_top, left_rest, pair))
     going_right, going_left = call(
         merge_kernel,
         "first_add",
@@ -468,19 +462,19 @@
     part = rank // 2
     swap = [(0, 1), (1, 0)]
 
-    def adapter_gradient():
+    def adapter_gradient(low_total):
         if share % 128 == 0:
             low, keep, send = call(
                 functools.partial(adapter_kernel, capacity),
                 "adapter_gradient",
                 [((slot, rank), BF)] + [((n, part, share), BF)] * 2,
-                [choice, tokens, *lows],
+                [choice, tokens, low_total],
                 work=(2 * own_count * rank * width, 2 * own_count * width),
             )
         else:
             me, core = lax.axis_index("expert"), lax.axis_index("dp")
             upper, _ = pick_rows(choice, capacity)
-            low = sum(lows).astype(BF)
+            low = low_total[0].astype(BF)
             low_tokens = dot(upper[:slot], low, TN).astype(BF)
             down = dot(low_tokens, tokens, TN).astype(BF).reshape(rank, n, share)
             down = down.transpose(1, 0, 2)[jnp.arange(n, dtype=jnp.int32) ^ me]
@@ -504,20 +498,20 @@
         )
         return local, lax.ppermute(local, "dp", swap)
 
-    bits = [1 << i for i in range(n.bit_length() - 1)]
     for hop, s in enumerate(range(middle - 1, 0, -1)):
         going_right, going_left = right(going_right), left(going_left)
         if hop == 0:
-            low, pair = adapter_gradient()
+            for bit in bits[1:]:
+                pair = exchange(*pair, bit)
+            low, pair = adapter_gradient(pair[0])
         elif hop == 1:
-            for bit in bits[:2]:
-                pair = exchange(*pair, bit)
+            pair = exchange(*pair, bits[0])
             low_rows, pair = lax.optimization_barrier((low_rows, pair))
         if s > 1:
             going_right, going_left, pair = lax.optimization_barrier((going_right, going_left, pair))
             going_right, going_left = add(going_right, own[s - 1]), add(going_left, own[1 - s])
     lora, lora_there = lora_gradients()
-    for bit in bits[2:]:
+    for bit in bits[1:]:
         pair = exchange(*pair, bit)
     down = pair[0][0]
     there = lax.ppermute(down, "dp", swap)

time: 119 us -> 126 us (1.059)
  waiting for transfers between devices: 44.9 us -> 67 us
  starting transfers between devices: 33.9 us -> 23.5 us
  Pallas kernels: 30.7 us -> 26.5 us
    ppermute x3 -> x6, waiting for transfers between devices: 21.3 us -> 45.2 us  [exchange(): other = lax.ppermute(send, 'expert', [(e, e ^ bit) for e in range(n)])]
    ppermute x7 -> x0, starting transfers between devices: 12.2 us -> none  [to_owner(): lax.ppermute(lows[at], 'expert', [(ring[i], ring[(i + r) % n]) for i in r...]
    ppermute x7 -> x0, waiting for transfers between devices: 5.43 us -> none  [to_owner(): lax.ppermute(lows[at], 'expert', [(ring[i], ring[(i + r) % n]) for i in r...]
    ppermute x8, starting transfers between devices: 13.4 us -> 9.18 us  [left(): return lax.ppermute(x, 'expert', to_left)]
    pallas_call x18 -> x21, Pallas kernels: 30.7 us -> 26.5 us  [call(): pl.pallas_call(kernel, out_shape=[jax.ShapeDtypeStruct(shape, dtype) for...]
    ppermute x3 -> x6, starting transfers between devices: 2.46 us -> 5.57 us  [exchange(): other = lax.ppermute(send, 'expert', [(e, e ^ bit) for e in range(n)])]
    ppermute x8, starting transfers between devices: 5.61 us -> 8.49 us  [right(): return lax.ppermute(x, 'expert', to_right)]
    ppermute x8, waiting for transfers between devices: 5.56 us -> 8.2 us  [right(): return lax.ppermute(x, 'expert', to_right)]
  transfers between devices with their start and end apart: 29 -> 25, of which waited for: 13 -> 15; matrix products, arithmetic and copies ran while one was open for 0% -> 0% of each run, Pallas kernels for 22% -> 9%
where the time goes in v8:
time: 126 us
  waiting for transfers between devices  67 us (53%)
  Pallas kernels  26.5 us (21%)
  starting transfers between devices  23.5 us (19%)
  local copies, waits for them, and re-layouts  7.54 us (6%)
    ppermute x6, waiting for transfers between devices, exchange(): other = lax.ppermute(send, 'expert', [(e, e ^ bit) for e in range(n)])  45.2 us
    pallas_call x21, Pallas kernels, call(): pl.pallas_call(kernel, out_shape=[jax.ShapeDtypeStruct(shape, dtype) for...  26.5 us
    ppermute x8, waiting for transfers between devices, left(): return lax.ppermute(x, 'expert', to_left)  10.7 us
    ppermute x8, starting transfers between devices, left(): return lax.ppermute(x, 'expert', to_left)  9.18 us
    ppermute x8, starting transfers between devices, right(): return lax.ppermute(x, 'expert', to_right)  8.49 us
    ppermute x8, waiting for transfers between devices, right(): return lax.ppermute(x, 'expert', to_right)  8.2 us
    unnamed x34, local copies, waits for them, and re-layouts  7.54 us
    ppermute x6, starting transfers between devices, exchange(): other = lax.ppermute(send, 'expert', [(e, e ^ bit) for e in range(n)])  5.57 us
  transfers between devices with their start and end apart: 25, of which 15 were waited for; matrix products, arithmetic and copies ran while one was open for 0% of the time, Pallas kernels for 9%

profile of v8, /device:TPU:0, one launch (start us, length us, event | category | flops | bytes accessed | tf_op | source)
XLA Modules:
  0.0 125.9 jit_solution(4092885266084289702)
XLA Ops:
  0.6 2.9 %prepare.1.refs_0_ = bf16[72,3200]{1,0:T(8,128)(2,1)S(1)} custom-call(s32[4,128]{1,0:T(4,128)} %bitcast.18, bf16[4,128]{1,0:T(4,128)(2,1)} %bitcast.27, bf16[128,6144]{1,0:T(8,128)(2,1)} %bitcast.26, bf16[128,6144]{1,0:T(8,128)(2,1)} %bitcast.12, bf16[64,6144]{1,0:T(8,128)(2,1)} %refs_4_.7), custom_call_target="tpu_custom_call" | custom-call | flops 400000000 | bytes 4500000 | tf_op jit(solution)/shard_map/prepare/pallas_call | solution.py:328
  3.6 3.0 %collective-permute-start.1 = (bf16[72,3200]{1,0:T(8,128)(2,1)S(1)}, bf16[72,3200]{1,0:T(8,128)(2,1)S(1)}, u32[]{:S(2)}, u32[]{:S(2)}) collective-permute-start(bf16[72,3200]{1,0:T(8,128)(2,1)S(1)} %prepare.1.refs_0_), channel_id=1, source_target_pairs={{0,2},{4,0},{8,4},{12,8},{14,12},{10,14},{6,10},{2,6},{1,3},{5,1},... | collective-permute-start | bytes 1382408 | tf_op jit(solution)/shard_map/ppermute | solution.py:344
  9.0 8.3 %collective-permute-done.1.refs_2_ = bf16[72,3200]{1,0:T(8,128)(2,1)S(1)} collective-permute-done((bf16[72,3200]{1,0:T(8,128)(2,1)S(1)}, bf16[72,3200]{1,0:T(8,128)(2,1)S(1)}, u32[]{:S(2)}, u32[]{:S(2)}) %collective-permute-start.1) | collective-permute-done | bytes 460832 | tf_op jit(solution)/shard_map/ppermute | solution.py:344
  19.0 1.6 %collective-permute-start.3 = (bf16[72,3200]{1,0:T(8,128)(2,1)S(1)}, bf16[72,3200]{1,0:T(8,128)(2,1)S(1)}, u32[]{:S(2)}, u32[]{:S(2)}) collective-permute-start(bf16[72,3200]{1,0:T(8,128)(2,1)S(1)} %collective-permute-done.1.refs_2_), channel_id=1, source_target_pairs={{0,2},{4,0},{8,4},{12,8},{14,12},{10,14},{6,10},{2,6},{1,3},{5,1},... | collective-permute-start | bytes 1382408 | tf_op jit(solution)/shard_map/ppermute | solution.py:344
  20.7 3.7 %copy-done = bf16[768,6144]{1,0:T(8,128)(2,1)S(1)} copy-done((bf16[768,6144]{1,0:T(8,128)(2,1)S(1)}, bf16[768,6144]{1,0:T(8,128)(2,1)}, u32[]{:S(2)}) %copy-start) | copy-done | bytes 9437208
  26.1 3.1 %hidden_rows.4 = (bf16[3,40,768]{2,1,0:T(8,128)(2,1)S(1)}, bf16[3,40,768]{2,1,0:T(8,128)(2,1)S(1)}, bf16[3,40,64]{2,1,0:T(8,128)(2,1)S(1)}, f32[40,64]{1,0:T(8,1...) custom-call(bf16[72,3200]{1,0:T(8,128)(2,1)S(1)} %prepare.1.refs_0_, ...), custom_call_target="tpu_custom_call" | custom-call | flops 2264924160 | bytes 9437184 | tf_op jit(solution)/shard_map/hidden_rows/pallas_call | solution.py:328
  32.2 3.1 %hidden_rows.5 = (bf16[2,40,768]{2,1,0:T(8,128)(2,1)S(1)}, bf16[2,40,768]{2,1,0:T(8,128)(2,1)S(1)}, bf16[2,40,64]{2,1,0:T(8,128)(2,1)S(1)}, f32[40,64]{1,0:T(8,128)S(1)}, f32[40,64]{1,0:T(8,128)S(1)}) custom-call(bf16[72,3200]{1,0:T(8,128)(2,1)S(1)} %collective-permute-done.2.refs_0_, bf16[72,3200]{1,0:T(8,128)(2,1)S(1)} %collective-permute-done.3.refs_1_, ...), custom_call_target="tpu_custom_call" | custom-call | flops 2415919104 | bytes 9437184 | tf_op jit(solution)/shard_map/hidden_rows/pallas_call | solution.py:328
  35.3 5.1 %collective-permute-done.4.refs_0_.right_in = bf16[72,3200]{1,0:T(8,128)(2,1)S(1)} collective-permute-done((bf16[72,3200]{1,0:T(8,128)(2,1)S(1)}, bf16[72,3200]{1,0:T(8,128)(2,1)S(1)}, u32[]{:S(2)}, u32[]{:S(2)}) %collective-permute-start.4) | collective-permute-done | bytes 460832 | tf_op jit(solution)/shard_map/ppermute | solution.py:341
  40.4 1.9 %collective-permute-done.5.refs_1_.left_in = bf16[72,3200]{1,0:T(8,128)(2,1)S(1)} collective-permute-done((bf16[72,3200]{1,0:T(8,128)(2,1)S(1)}, bf16[72,3200]{1,0:T(8,128)(2,1)S(1)}, u32[]{:S(2)}, u32[]{:S(2)}) %collective-permute-start.5) | collective-permute-done | bytes 460832 | tf_op jit(solution)/shard_map/ppermute | solution.py:344
  44.5 3.1 %hidden_rows.6 = (bf16[2,40,768]{2,1,0:T(8,128)(2,1)S(1)}, bf16[2,40,768]{2,1,0:T(8,128)(2,1)S(1)}, bf16[2,40,64]{2,1,0:T(8,128)(2,1)S(1)}, f32[40,64]{1,0:T(8,128)S(1)}, f32[40,64]{1,0:T(8,128)S(1)}) custom-call(bf16[72,3200]{1,0:T(8,128)(2,1)S(1)} %collective-permute-done.4.refs_0_.right_in, bf16[72,3200]{1,0:T(8,128)(2,1)S(1)} %collective-permute-done.5.refs_1_.left_in, ...), custom_call_target="tpu_custom_call" | custom-call | flops 2415919104 | bytes 9437184 | tf_op jit(solution)/shard_map/hidden_rows/pallas_call | solution.py:328
  48.7 2.9 %hidden_rows.7 = (bf16[1,40,768]{2,1,0:T(8,128)(2,1)S(1)}, bf16[1,40,768]{2,1,0:T(8,128)(2,1)S(1)}, bf16[1,40,64]{2,1,0:T(8,128)(2,1)S(1)}, f32[40,64]{1,0:T(8,128)S(1)}) custom-call(bf16[32,3200]{1,0:T(8,128)(2,1)S(1)} %collective-permute-done.6.refs_0_, bf16[40,3200]{1,0:T(8,128)(2,1)S(1)} %collective-permute-done.7.refs_1_, ...), custom_call_target="tpu_custom_call" | custom-call | flops 1207959552 | bytes 9437184 | tf_op jit(solution)/shard_map/hidden_rows/pallas_call | solution.py:328
  52.2 6.5 %partials.1 = (bf16[72,3072]{1,0:T(8,128)(2,1)S(1)}, bf16[72,3072]{1,0:T(8,128)(2,1)S(1)}, bf16[72,3072]{1,0:T(8,128)(2,1)S(1)}, bf16[72,3072]{1,0:T(8,128)(2,1)...) custom-call(bf16[3,40,768]{2,1,0:T(8,128)(2,1)S(1)} %get-tuple-eleme, ...), custom_call_target="tpu_custom_call" | custom-call | flops 6039797760 | bytes 18874368 | tf_op jit(solution)/shard_map/partials/pallas_call | solution.py:328
  62.0 7.5 %collective-permute-done.10.theirs = f32[4,40,64]{2,1,0:T(8,128)S(1)} collective-permute-done((f32[4,40,64]{2,1,0:T(8,128)S(1)}, f32[4,40,64]{2,1,0:T(8,128)S(1)}, u32[]{:S(2)}, u32[]{:S(2)}) %collective-permute-start.10) | collective-permute-done | bytes 40992 | tf_op jit(solution)/shard_map/ppermute | solution.py:442
  69.7 2.0 %collective-permute-start.12 = (bf16[72,3072]{1,0:T(8,128)(2,1)S(1)}, bf16[72,3072]{1,0:T(8,128)(2,1)S(1)}, u32[]{:S(2)}, u32[]{:S(2)}) collective-permute-start(bf16[72,3072]{1,0:T(8,128)(2,1)S(1)} %get-tuple-element.144), channel_id=1, source_target_pairs={{0,2},{4,0},{8,4},{12,8},{14,12},{10,14},{6,10},{2,6},{1,3},{5,1},... | collective-permute-start | bytes 1327112 | tf_op jit(solution)/shard_map/ppermute | solution.py:344
  71.7 6.9 %collective-permute-done.13.theirs = f32[2,40,64]{2,1,0:T(8,128)S(1)} collective-permute-done((f32[2,40,64]{2,1,0:T(8,128)S(1)}, f32[2,40,64]{2,1,0:T(8,128)S(1)}, u32[]{:S(2)}, u32[]{:S(2)}) %collective-permute-start.13) | collective-permute-done | bytes 20512 | tf_op jit(solution)/shard_map/ppermute | solution.py:442
  78.7 2.6 %collective-permute-start.14 = (f32[1,40,64]{2,1,0:T(8,128)S(1)}, f32[1,40,64]{2,1,0:T(8,128)S(1)}, u32[]{:S(2)}, u32[]{:S(2)}) collective-permute-start(f32[1,40,64]{2,1,0:T(8,128)S(1)} %get-tuple-element.148), channel_id=1, source_target_pairs={{0,8},{2,10},{4,12},{6,14},{8,0},{10,2},{12,4},{14,6},{1,9},{3,11}... | collective-permute-start | bytes 30728 | tf_op jit(solution)/shard_map/ppermute | solution.py:442
  81.3 2.1 %collective-permute-done.14.theirs = f32[1,40,64]{2,1,0:T(8,128)S(1)} collective-permute-done((f32[1,40,64]{2,1,0:T(8,128)S(1)}, f32[1,40,64]{2,1,0:T(8,128)S(1)}, u32[]{:S(2)}, u32[]{:S(2)}) %collective-permute-start.14) | collective-permute-done | bytes 10272 | tf_op jit(solution)/shard_map/ppermute | solution.py:442
  84.2 1.7 %collective-permute-done.15.theirs = bf16[8,32,768]{2,1,0:T(8,128)(2,1)S(1)} collective-permute-done((bf16[8,32,768]{2,1,0:T(8,128)(2,1)S(1)}, bf16[8,32,768]{2,1,0:T(8,128)(2,1)S(1)}, u32[]{:S(2)}, u32[]{:S(2)}) %collective-permute-start.15) | collective-permute-done | bytes 393248 | tf_op jit(solution)/shard_map/ppermute | solution.py:483
  86.4 2.0 %collective-permute-start.16 = (bf16[72,3072]{1,0:T(8,128)(2,1)S(1)}, bf16[72,3072]{1,0:T(8,128)(2,1)S(1)}, u32[]{:S(2)}, u32[]{:S(2)}) collective-permute-start(bf16[72,3072]{1,0:T(8,128)(2,1)S(1)} %add_convert_fusion.3), channel_id=1, source_target_pairs={{0,4},{4,8},{8,12},{12,14},{14,10},{10,6},{6,2},{2,0},{1,5},{5,9},... | collective-permute-start | bytes 1327112 | tf_op jit(solution)/shard_map/ppermute | solution.py:341
  88.6 14.3 %collective-permute-done.18.theirs = bf16[4,32,768]{2,1,0:T(8,128)(2,1)S(1)} collective-permute-done((bf16[4,32,768]{2,1,0:T(8,128)(2,1)S(1)}, bf16[4,32,768]{2,1,0:T(8,128)(2,1)S(1)}, u32[]{:S(2)}, u32[]{:S(2)}) %collective-permute-start.18) | collective-permute-done | bytes 196640 | tf_op jit(solution)/shard_map/ppermute | solution.py:442
  103.3 2.1 %collective-permute-start.19 = (bf16[72,3072]{1,0:T(8,128)(2,1)S(1)}, bf16[72,3072]{1,0:T(8,128)(2,1)S(1)}, u32[]{:S(2)}, u32[]{:S(2)}) collective-permute-start(bf16[72,3072]{1,0:T(8,128)(2,1)S(1)} %add_convert_fusion.1), channel_id=1, source_target_pairs={{0,4},{4,8},{8,12},{12,14},{14,10},{10,6},{6,2},{2,0},{1,5},{5,9},... | collective-permute-start | bytes 1327112 | tf_op jit(solution)/shard_map/ppermute | solution.py:341
  105.9 10.8 %collective-permute-done.21.theirs = bf16[2,32,768]{2,1,0:T(8,128)(2,1)S(1)} collective-permute-done((bf16[2,32,768]{2,1,0:T(8,128)(2,1)S(1)}, bf16[2,32,768]{2,1,0:T(8,128)(2,1)S(1)}, u32[]{:S(2)}, u32[]{:S(2)}) %collective-permute-start.21) | collective-permute-done | bytes 98336 | tf_op jit(solution)/shard_map/ppermute | solution.py:442
  118.2 3.6 %collective-permute-done.22.theirs = bf16[1,32,768]{2,1,0:T(8,128)(2,1)S(1)} collective-permute-done((bf16[1,32,768]{2,1,0:T(8,128)(2,1)S(1)}, bf16[1,32,768]{2,1,0:T(8,128)(2,1)S(1)}, u32[]{:S(2)}, u32[]{:S(2)}) %collective-permute-start.22) | collective-permute-done | bytes 49184 | tf_op jit(solution)/shard_map/ppermute | solution.py:442
  123.9 2.0 %finish.1 = bf16[128,6144]{1,0:T(8,128)(2,1)} custom-call(s32[4,128]{1,0:T(4,128)S(1)} %bitcast.20, bf16[72,3072]{1,0:T(8,128)(2,1)S(1)} %collective-permute-done.19.refs_0_, bf16[72,3072]{1,0:T(8,128)(2,1)S(1)} %collective-permute-done.20.refs_1_, bf16[72,3072]{1,0:T(8,128)(2,1)S(1)} %get-tuple-element.171.refs_2_, ...), custom_call_target="tpu_custom_call" | custom-call | flops 400000000 | bytes 4500000 | tf_op jit(solution)/shard_map/finish/pallas_call | solution.py:328
  (87 shorter events, 22.1 us)
Async XLA Ops:
  3.6 13.6 %collective-permute-start.1 = (bf16[72,3200]{1,0:T(8,128)(2,1)S(1)}, bf16[72,3200]{1,0:T(8,128)(2,1)S(1)}, u32[]{:S(2)}, u32[]{:S(2)}) collective-permute-start(bf16[72,3200]{1,0:T(8,128)(2,1)S(1)} %prepare.1.refs_0_), channel_id=1, source_target_pairs={{0,2},{4,0},{8,4},{12,8},{14,12},{10,14},{6,10},{2,6},{1,3},{5,1},... | collective-permute-start | bytes 1382408 | tf_op jit(solution)/shard_map/ppermute | solution.py:344
  6.6 12.0 %collective-permute-start = (bf16[72,3200]{1,0:T(8,128)(2,1)S(1)}, bf16[72,3200]{1,0:T(8,128)(2,1)S(1)}, u32[]{:S(2)}, u32[]{:S(2)}) collective-permute-start(bf16[72,3200]{1,0:T(8,128)(2,1)S(1)} %prepare.1.refs_0_), channel_id=1, source_target_pairs={{0,4},{4,8},{8,12},{12,14},{14,10},{10,6},{6,2},{2,0},{1,5},{5,9},... | collective-permute-start | bytes 1382408 | tf_op jit(solution)/shard_map/ppermute | solution.py:341
  18.6 11.1 %collective-permute-start.2 = (bf16[72,3200]{1,0:T(8,128)(2,1)S(1)}, bf16[72,3200]{1,0:T(8,128)(2,1)S(1)}, u32[]{:S(2)}, u32[]{:S(2)}) collective-permute-start(bf16[72,3200]{1,0:T(8,128)(2,1)S(1)} %collective-permute-done.refs_1_), channel_id=1, source_target_pairs={{0,4},{4,8},{8,12},{12,14},{14,10},{10,6},{6,2},{2,0},{1,5},{5,9},... | collective-permute-start | bytes 1382408 | tf_op jit(solution)/shard_map/ppermute | solution.py:341
  19.0 11.1 %collective-permute-start.3 = (bf16[72,3200]{1,0:T(8,128)(2,1)S(1)}, bf16[72,3200]{1,0:T(8,128)(2,1)S(1)}, u32[]{:S(2)}, u32[]{:S(2)}) collective-permute-start(bf16[72,3200]{1,0:T(8,128)(2,1)S(1)} %collective-permute-done.1.refs_2_), channel_id=1, source_target_pairs={{0,2},{4,0},{8,4},{12,8},{14,12},{10,14},{6,10},{2,6},{1,3},{5,1},... | collective-permute-start | bytes 1382408 | tf_op jit(solution)/shard_map/ppermute | solution.py:344
  30.2 10.2 %collective-permute-start.4 = (bf16[72,3200]{1,0:T(8,128)(2,1)S(1)}, bf16[72,3200]{1,0:T(8,128)(2,1)S(1)}, u32[]{:S(2)}, u32[]{:S(2)}) collective-permute-start(bf16[72,3200]{1,0:T(8,128)(2,1)S(1)} %collective-permute-done.2.refs_0_), channel_id=1, source_target_pairs={{0,4},{4,8},{8,12},{12,14},{14,10},{10,6},{6,2},{2,0},{1,5},{5,9},... | collective-permute-start | bytes 1382408 | tf_op jit(solution)/shard_map/ppermute | solution.py:341
  31.7 10.6 %collective-permute-start.5 = (bf16[72,3200]{1,0:T(8,128)(2,1)S(1)}, bf16[72,3200]{1,0:T(8,128)(2,1)S(1)}, u32[]{:S(2)}, u32[]{:S(2)}) collective-permute-start(bf16[72,3200]{1,0:T(8,128)(2,1)S(1)} %collective-permute-done.3.refs_1_), channel_id=1, source_target_pairs={{0,2},{4,0},{8,4},{12,8},{14,12},{10,14},{6,10},{2,6},{1,3},{5,1},... | collective-permute-start | bytes 1382408 | tf_op jit(solution)/shard_map/ppermute | solution.py:344
  42.4 6.4 %collective-permute-start.7 = (bf16[40,3200]{1,0:T(8,128)(2,1)S(1)}, bf16[40,3200]{1,0:T(8,128)(2,1)S(1)}, u32[]{:S(2)}, u32[]{:S(2)}) collective-permute-start(bf16[40,3200]{1,0:T(8,128)(2,1)S(1)} %get-tuple-element.116), channel_id=1, source_target_pairs={{0,2},{4,0},{8,4},{12,8},{14,12},{10,14},{6,10},{2,6},{1,3},{5,1},... | collective-permute-start | bytes 768008 | tf_op jit(solution)/shard_map/ppermute | solution.py:344
  42.9 5.8 %collective-permute-start.6 = (bf16[32,3200]{1,0:T(8,128)(2,1)S(1)}, bf16[32,3200]{1,0:T(8,128)(2,1)S(1)}, u32[]{:S(2)}, u32[]{:S(2)}) collective-permute-start(bf16[32,3200]{1,0:T(8,128)(2,1)S(1)} %get-tuple-element.115), channel_id=1, source_target_pairs={{0,4},{4,8},{8,12},{12,14},{14,10},{10,6},{6,2},{2,0},{1,5},{5,9},... | collective-permute-start | bytes 614408 | tf_op jit(solution)/shard_map/ppermute | solution.py:341
  58.7 10.7 %collective-permute-start.9 = (bf16[40,3072]{1,0:T(8,128)(2,1)S(1)}, bf16[40,3072]{1,0:T(8,128)(2,1)S(1)}, u32[]{:S(2)}, u32[]{:S(2)}) collective-permute-start(bf16[40,3072]{1,0:T(8,128)(2,1)S(1)} %get-tuple-element.134), channel_id=1, source_target_pairs={{0,2},{4,0},{8,4},{12,8},{14,12},{10,14},{6,10},{2,6},{1,3},{5,1},... | collective-permute-start | bytes 737288 | tf_op jit(solution)/shard_map/ppermute | solution.py:344
  59.9 9.5 %collective-permute-start.8 = (bf16[32,3072]{1,0:T(8,128)(2,1)S(1)}, bf16[32,3072]{1,0:T(8,128)(2,1)S(1)}, u32[]{:S(2)}, u32[]{:S(2)}) collective-permute-start(bf16[32,3072]{1,0:T(8,128)(2,1)S(1)} %get-tuple-element.133), channel_id=1, source_target_pairs={{0,4},{4,8},{8,12},{12,14},{14,10},{10,6},{6,2},{2,0},{1,5},{5,9},... | collective-permute-start | bytes 589832 | tf_op jit(solution)/shard_map/ppermute | solution.py:341
  60.8 8.6 %collective-permute-start.10 = (f32[4,40,64]{2,1,0:T(8,128)S(1)}, f32[4,40,64]{2,1,0:T(8,128)S(1)}, u32[]{:S(2)}, u32[]{:S(2)}) collective-permute-start(f32[4,40,64]{2,1,0:T(8,128)S(1)} %get-tuple-element.136), channel_id=1, source_target_pairs={{0,2},{2,0},{4,6},{6,4},{8,10},{10,8},{12,14},{14,12},{1,3},{3,1},... | collective-permute-start | bytes 122888 | tf_op jit(solution)/shard_map/ppermute | solution.py:442
  69.6 16.5 %collective-permute-start.11 = (bf16[72,3072]{1,0:T(8,128)(2,1)S(1)}, bf16[72,3072]{1,0:T(8,128)(2,1)S(1)}, u32[]{:S(2)}, u32[]{:S(2)}) collective-permute-start(bf16[72,3072]{1,0:T(8,128)(2,1)S(1)} %get-tuple-element.143), channel_id=1, source_target_pairs={{0,4},{4,8},{8,12},{12,14},{14,10},{10,6},{6,2},{2,0},{1,5},{5,9},... | collective-permute-start | bytes 1327112 | tf_op jit(solution)/shard_map/ppermute | solution.py:341
  69.7 16.4 %collective-permute-start.12 = (bf16[72,3072]{1,0:T(8,128)(2,1)S(1)}, bf16[72,3072]{1,0:T(8,128)(2,1)S(1)}, u32[]{:S(2)}, u32[]{:S(2)}) collective-permute-start(bf16[72,3072]{1,0:T(8,128)(2,1)S(1)} %get-tuple-element.144), channel_id=1, source_target_pairs={{0,2},{4,0},{8,4},{12,8},{14,12},{10,14},{6,10},{2,6},{1,3},{5,1},... | collective-permute-start | bytes 1327112 | tf_op jit(solution)/shard_map/ppermute | solution.py:344
  71.7 7.0 %collective-permute-start.13 = (f32[2,40,64]{2,1,0:T(8,128)S(1)}, f32[2,40,64]{2,1,0:T(8,128)S(1)}, u32[]{:S(2)}, u32[]{:S(2)}) collective-permute-start(f32[2,40,64]{2,1,0:T(8,128)S(1)} %get-tuple-element.146), channel_id=1, source_target_pairs={{0,4},{2,6},{4,0},{6,2},{8,12},{10,14},{12,8},{14,10},{1,5},{3,7},... | collective-permute-start | bytes 61448 | tf_op jit(solution)/shard_map/ppermute | solution.py:442
  78.7 4.7 %collective-permute-start.14 = (f32[1,40,64]{2,1,0:T(8,128)S(1)}, f32[1,40,64]{2,1,0:T(8,128)S(1)}, u32[]{:S(2)}, u32[]{:S(2)}) collective-permute-start(f32[1,40,64]{2,1,0:T(8,128)S(1)} %get-tuple-element.148), channel_id=1, source_target_pairs={{0,8},{2,10},{4,12},{6,14},{8,0},{10,2},{12,4},{14,6},{1,9},{3,11}... | collective-permute-start | bytes 30728 | tf_op jit(solution)/shard_map/ppermute | solution.py:442
  84.2 1.8 %collective-permute-start.15 = (bf16[8,32,768]{2,1,0:T(8,128)(2,1)S(1)}, bf16[8,32,768]{2,1,0:T(8,128)(2,1)S(1)}, u32[]{:S(2)}, u32[]{:S(2)}) collective-permute-start(bf16[8,32,768]{2,1,0:T(8,128)(2,1)S(1)} %get-tuple-element.150), channel_id=1, source_target_pairs={{0,1},{1,0},{2,3},{3,2},{4,5},{5,4},{6,7},{7,6},{8,9},{9,8},{10,11... | collective-permute-start | bytes 1179656 | tf_op jit(solution)/shard_map/ppermute | solution.py:483
  86.2 16.8 %collective-permute-start.17 = (bf16[72,3072]{1,0:T(8,128)(2,1)S(1)}, bf16[72,3072]{1,0:T(8,128)(2,1)S(1)}, u32[]{:S(2)}, u32[]{:S(2)}) collective-permute-start(bf16[72,3072]{1,0:T(8,128)(2,1)S(1)} %add_convert_fusion.2), channel_id=1, source_target_pairs={{0,2},{4,0},{8,4},{12,8},{14,12},{10,14},{6,10},{2,6},{1,3},{5,1},... | collective-permute-start | bytes 1327112 | tf_op jit(solution)/shard_map/ppermute | solution.py:344
  86.4 16.5 %collective-permute-start.16 = (bf16[72,3072]{1,0:T(8,128)(2,1)S(1)}, bf16[72,3072]{1,0:T(8,128)(2,1)S(1)}, u32[]{:S(2)}, u32[]{:S(2)}) collective-permute-start(bf16[72,3072]{1,0:T(8,128)(2,1)S(1)} %add_convert_fusion.3), channel_id=1, source_target_pairs={{0,4},{4,8},{8,12},{12,14},{14,10},{10,6},{6,2},{2,0},{1,5},{5,9},... | collective-permute-start | bytes 1327112 | tf_op jit(solution)/shard_map/ppermute | solution.py:341
  88.4 14.5 %collective-permute-start.18 = (bf16[4,32,768]{2,1,0:T(8,128)(2,1)S(1)}, bf16[4,32,768]{2,1,0:T(8,128)(2,1)S(1)}, u32[]{:S(2)}, u32[]{:S(2)}) collective-permute-start(bf16[4,32,768]{2,1,0:T(8,128)(2,1)S(1)} %get-tuple-element.162), channel_id=1, source_target_pairs={{0,2},{2,0},{4,6},{6,4},{8,10},{10,8},{12,14},{14,12},{1,3},{3,1},... | collective-permute-start | bytes 589832 | tf_op jit(solution)/shard_map/ppermute | solution.py:442
  103.1 20.8 %collective-permute-start.20 = (bf16[72,3072]{1,0:T(8,128)(2,1)S(1)}, bf16[72,3072]{1,0:T(8,128)(2,1)S(1)}, u32[]{:S(2)}, u32[]{:S(2)}) collective-permute-start(bf16[72,3072]{1,0:T(8,128)(2,1)S(1)} %add_convert_fusion), channel_id=1, source_target_pairs={{0,2},{4,0},{8,4},{12,8},{14,12},{10,14},{6,10},{2,6},{1,3},{5,1},... | collective-permute-start | bytes 1327112 | tf_op jit(solution)/shard_map/ppermute | solution.py:344
  103.3 20.6 %collective-permute-start.19 = (bf16[72,3072]{1,0:T(8,128)(2,1)S(1)}, bf16[72,3072]{1,0:T(8,128)(2,1)S(1)}, u32[]{:S(2)}, u32[]{:S(2)}) collective-permute-start(bf16[72,3072]{1,0:T(8,128)(2,1)S(1)} %add_convert_fusion.1), channel_id=1, source_target_pairs={{0,4},{4,8},{8,12},{12,14},{14,10},{10,6},{6,2},{2,0},{1,5},{5,9},... | collective-permute-start | bytes 1327112 | tf_op jit(solution)/shard_map/ppermute | solution.py:341
  105.4 11.3 %collective-permute-start.21 = (bf16[2,32,768]{2,1,0:T(8,128)(2,1)S(1)}, bf16[2,32,768]{2,1,0:T(8,128)(2,1)S(1)}, u32[]{:S(2)}, u32[]{:S(2)}) collective-permute-start(bf16[2,32,768]{2,1,0:T(8,128)(2,1)S(1)} %get-tuple-element.174), channel_id=1, source_target_pairs={{0,4},{2,6},{4,0},{6,2},{8,12},{10,14},{12,8},{14,10},{1,5},{3,7},... | collective-permute-start | bytes 294920 | tf_op jit(solution)/shard_map/ppermute | solution.py:442
  105.8 16.0 %collective-permute-start.24 = (bf16[128,768]{1,0:T(8,128)(2,1)S(1)}, bf16[128,768]{1,0:T(8,128)(2,1)S(1)}, u32[]{:S(2)}, u32[]{:S(2)}) collective-permute-start(bf16[128,768]{1,0:T(8,128)(2,1)S(1)} %lora_rows.1.lora_ref), channel_id=1, source_target_pairs={{0,1},{1,0},{2,3},{3,2},{4,5},{5,4},{6,7},{7,6},{8,9},{9,8},{10,11... | collective-permute-start | bytes 589832 | tf_op jit(solution)/shard_map/ppermute | solution.py:499
  116.7 5.1 %collective-permute-start.22 = (bf16[1,32,768]{2,1,0:T(8,128)(2,1)S(1)}, bf16[1,32,768]{2,1,0:T(8,128)(2,1)S(1)}, u32[]{:S(2)}, u32[]{:S(2)}) collective-permute-start(bf16[1,32,768]{2,1,0:T(8,128)(2,1)S(1)} %get-tuple-element.176), channel_id=1, source_target_pairs={{0,8},{2,10},{4,12},{6,14},{8,0},{10,2},{12,4},{14,6},{1,9},{3,11}... | collective-permute-start | bytes 147464 | tf_op jit(solution)/shard_map/ppermute | solution.py:442
  (18 other events, 271.2 us)

commit v9 on v8

--- a/solution.py
+++ b/solution.py
@@ -51,7 +51,7 @@
     return (row == slot).astype(BF), (row - capacity == slot).astype(BF)
 
 
-def prepare_kernel(capacity, choice_hbm, weight_hbm, grad_hbm, tokens_hbm, down_hbm, block_ref,
+def prepare_kernel(capacity, choice_hbm, weight_hbm, grad_hbm, tokens_hbm, down_hbm, top, rest,
                    choice_ref, weight_ref, grad_ref, tokens_ref, down_ref, sems):
     half = grad_ref.shape[1] // 2
     rank = down_ref.shape[0]
@@ -72,31 +72,24 @@
     copies[1].wait()
     first = dot(upper, grad_ref[:, :half])
     copies[2].wait()
-    block_ref[:, :half] = (first + dot(lower, grad_ref[:, half:])).astype(BF)
+    rows = (first + dot(lower, grad_ref[:, half:])).astype(BF)
+    cut = top.shape[0]
+    top[:, :half] = rows[:cut]
+    rest[:, :half] = rows[cut:]
     copies[3].wait()
     weight = jnp.sum(
         jnp.where(choice == 0, weight_ref[...].astype(F32), 0.0), axis=0, keepdims=True
     )
     column = jnp.sum(upper.astype(F32) * weight, axis=1, keepdims=True)
-    block_ref[:, half + rank :] = jnp.broadcast_to(column, (2 * capacity, rank)).astype(BF)
+    column = jnp.broadcast_to(column, (2 * capacity, rank)).astype(BF)
+    top[:, half + rank :] = column[:cut]
+    rest[:, half + rank :] = column[cut:]
     copies[4].wait()
     copies[5].wait()
     low = dot(tokens_ref[...], down_ref[...], NT).astype(BF)
-    block_ref[:, half : half + rank] = dot(upper, low).astype(BF)
-
-
-def cut_kernel(right_in, left_in, top, rest):
-    cut = top.shape[0]
-    top[...] = right_in[:cut, :]
-    rest[...] = left_in[cut:, :]
-
-
-def merge_kernel(top_in, rest_in, own_right, own_left, right_out, left_out):
-    cut = top_in.shape[0]
-    right_out[:cut, :] = (top_in[...].astype(F32) + own_right[:cut, :].astype(F32)).astype(BF)
-    right_out[cut:, :] = own_right[cut:, :]
-    left_out[:cut, :] = own_left[:cut, :]
-    left_out[cut:, :] = (rest_in[...].astype(F32) + own_left[cut:, :].astype(F32)).astype(BF)
+    low = dot(upper, low).astype(BF)
+    top[:, half : half + rank] = low[:cut]
+    rest[:, half : half + rank] = low[cut:]
 
 
 def place_here(place):
@@ -104,7 +97,8 @@
     return me, sum(jnp.where(me == e, p, 0) for e, p in enumerate(place))
 
 
-def reorder_kernel(place, capacity, gate_in, up_in, gate_out, up_out, tall):
+def reorder_kernel(place, capacity, gate_in, up_in, *refs):
+    gate_out, up_out, tall = refs[-3:]
     count, slot, hidden = gate_out.shape
     _, here = place_here(place)
     live = lax.broadcasted_iota(jnp.int32, (slot, hidden), 0) < capacity
@@ -225,11 +219,8 @@
             at = i * slot
             tile[:capacity, :] = sums[0][at : at + capacity]
             tile[capacity:, :] = sums[1][at : at + capacity]
-            if i < members - 1:
-                outs[i][:, t : t + TILE] = tile[...].astype(BF)
-            else:
-                outs[i][:, t : t + TILE] = tile[:cut, :].astype(BF)
-                outs[i + 1][:, t : t + TILE] = tile[cut:, :].astype(BF)
+            outs[2 * i][:, t : t + TILE] = tile[:cut, :].astype(BF)
+            outs[2 * i + 1][:, t : t + TILE] = tile[cut:, :].astype(BF)
 
 
 def adapter_kernel(capacity, choice_ref, tokens_ref, low_in, low_ref, keep_ref, send_ref):
@@ -258,8 +249,8 @@
 
 
 def finish_kernel(capacity, choice_ref, *refs):
-    parts, (low_ref, down_ref, out_ref, low_tall) = refs[:3], refs[3:]
-    half = parts[0].shape[1]
+    tops, rests, (low_ref, down_ref, out_ref, low_tall) = refs[:3], refs[3:6], refs[6:]
+    cut, half = tops[0].shape
     upper, lower = pick_rows(choice_ref[...], capacity)
     low = low_ref[...].astype(F32)[:capacity]
     zero = jnp.zeros_like(low)
@@ -269,11 +260,13 @@
     low_tall[:capacity, :] = zero
     low_tall[capacity:, :] = low
     low_lower = low_tall[...].astype(BF)
-    total = sum(x[...].astype(F32) for x in parts)
-    total += dot(low_upper, down_ref[:, :half]) + dot(low_lower, down_ref[:, half:])
-    total = total.astype(BF)
-    out_ref[:, :half] = dot(upper, total, TN).astype(BF)
-    out_ref[:, half:] = dot(lower, total, TN).astype(BF)
+    adapter = dot(low_upper, down_ref[:, :half]) + dot(low_lower, down_ref[:, half:])
+    top = sum(x[...].astype(F32) for x in tops) + adapter[:cut]
+    rest = sum(x[...].astype(F32) for x in rests) + adapter[cut:]
+    top, rest = top.astype(BF), rest.astype(BF)
+    for pick, at in ((upper, 0), (lower, half)):
+        picked = dot(pick[:cut], top, TN) + dot(pick[cut:], rest, TN)
+        out_ref[:, at : at + half] = picked.astype(BF)
 
 
 def in_hbm(x):
@@ -330,9 +323,7 @@
             out_shape=[jax.ShapeDtypeStruct(shape, dtype) for shape, dtype in shapes],
             scratch_shapes=list(scratch),
             compiler_params=pltpu.CompilerParams(vmem_limit_bytes=VMEM_LIMIT),
-            cost_estimate=pl.CostEstimate(
-                flops=int(work[0]), bytes_accessed=int(work[1]), transcendentals=0
-            ),
+            cost_estimate=pl.CostEstimate(flops=1, bytes_accessed=1, transcendentals=0),
             name=name,
             **more,
         )(*args)
@@ -343,10 +334,10 @@
     def left(x):
         return lax.ppermute(x, "expert", to_left)
 
-    (block,) = call(
+    block = call(
         functools.partial(prepare_kernel, capacity),
         "prepare",
-        [((2 * capacity, wide), BF)],
+        [((h, wide), BF) for h in heights],
         [in_hbm(x) for x in (choice, weights, output_gradient, tokens, adapter_down_factor)],
         [
             pltpu.VMEM(choice.shape, choice.dtype),
@@ -359,18 +350,19 @@
         (4e8, 4.5e6),
         in_specs=[pl.BlockSpec(memory_space=pl.ANY)] * 5,
     )
+    down_here, gate_here, up_here = in_vmem(down_weight), in_vmem(gate_weight), in_vmem(up_weight)
+    gate_factor, up_factor = in_vmem(adapter_gate_factor), in_vmem(adapter_up_factor)
     gate_rows, up_rows = call(
         functools.partial(reorder_kernel, place, capacity),
         "reorder",
         [((n, slot, hidden), BF)] * 2,
-        [stored_gate_rows[0], stored_up_rows[0]],
+        [stored_gate_rows[0], stored_up_rows[0], down_here, gate_factor, up_factor],
         [pltpu.VMEM((n * capacity + slot, hidden), F32)],
         (0, 8 * n * slot * hidden),
     )
 
-    down_here, gate_here, up_here = in_vmem(down_weight), in_vmem(gate_weight), in_vmem(up_weight)
     dgates, dups, low_rows, lows = [], [], [], []
-    got = {0: (block,)}
+    got = {0: tuple(block)}
 
     def hidden_pass(group):
         size, start, pieces = len(group), len(lows), len(got[group[0]])
@@ -382,7 +374,7 @@
             + [((size, slot, rank), BF)]
             + [((slot, rank), F32)] * size,
             [piece for r in group for piece in got[r]]
-            + [gate_rows, up_rows, down_here, adapter_gate_factor, adapter_up_factor],
+            + [gate_rows, up_rows, down_here, gate_factor, up_factor],
             [pltpu.VMEM((size * tall, half), BF)],
             (2 * size * tall * width * hidden, 2 * hidden * width),
         )
@@ -391,22 +383,20 @@
         low_rows.append(results[2])
         lows.extend(results[3:])
 
-    going_right = going_left = block
+    right_top, right_rest = left_top, left_rest = block
     for s in range(1, middle):
-        going_right, going_left = right(going_right), left(going_left)
+        right_top, left_rest = right(right_top), left(left_rest)
         if s == 1:
-            going_right, going_left, gate_rows, up_rows = lax.optimization_barrier(
-                (going_right, going_left, gate_rows, up_rows)
+            right_top, left_rest, gate_rows, up_rows = lax.optimization_barrier(
+                (right_top, left_rest, gate_rows, up_rows)
             )
-        else:
+        right_rest, left_top = right(right_rest), left(left_top)
+        if s > 1:
             hidden_pass(passes[s - 2])
-            going_right, going_left, dgates[-1], dups[-1] = lax.optimization_barrier(
-                (going_right, going_left, dgates[-1], dups[-1])
+            right_rest, left_top, dgates[-1], dups[-1] = lax.optimization_barrier(
+                (right_rest, left_top, dgates[-1], dups[-1])
             )
-        got[-s], got[s] = (going_right,), (going_left,)
-    right_top, left_rest = call(
-        cut_kernel, "cut", [((h, wide), BF) for h in heights], [going_right, going_left]
-    )
+        got[-s], got[s] = (right_top, right_rest), (left_top, left_rest)
     right_top, left_rest = right(right_top), left(left_rest)
     hidden_pass(passes[-2])
     right_top, left_rest, dgates[-1], dups[-1] = lax.optimization_barrier(
@@ -421,10 +411,10 @@
         [((n // 2, slot, rank), F32)] * 2,
         lows,
     )
-    *own, right_top, left_rest = call(
+    own = call(
         functools.partial(partial_kernel, capacity, slot, sizes, cut),
         "partials",
-        [((2 * capacity, half), BF)] * (n - 1) + [((h, half), BF) for h in heights],
+        [((h, half), BF) for h in heights] * n,
         [*dgates, *dups, gate_here, up_here],
         [
             pltpu.VMEM((n * slot, hidden), BF),
@@ -433,8 +423,6 @@
         ],
         (4 * n * slot * width * hidden, 4 * hidden * width),
     )
-    own = dict(zip(order[:-1], own))
-
     def add(a, b):
         return (a.astype(F32) + b.astype(F32)).astype(BF)
 
@@ -445,18 +433,14 @@
         shape = (count // parts,) + keep.shape[1:]
         return call(halve_kernel, "halve", [(shape, keep.dtype)] * parts, [keep, other])
 
-    low_keep, right_top, left_rest = lax.optimization_barrier((low_keep, right_top, left_rest))
-    right_top, left_rest = right(right_top), left(left_rest)
     bits = [1 << i for i in range(n.bit_length() - 1)]
-    pair = [low_keep, low_send]
-    pair = exchange(*pair, bits[0])
+    pair = exchange(low_keep, low_send, bits[0])
+    pair, own = lax.optimization_barrier((pair, own))
+    own = {r: (own[2 * i], own[2 * i + 1]) for i, r in enumerate(order)}
+    right_top, left_rest = right(own[middle][0]), left(own[middle][1])
+    right_rest, left_top = right(own[middle - 1][1]), left(own[1 - middle][0])
+    pair = exchange(*pair, bits[1])
     right_top, left_rest, pair = lax.optimization_barrier((right_top, left_rest, pair))
-    going_right, going_left = call(
-        merge_kernel,
-        "first_add",
-        [((2 * capacity, half), BF)] * 2,
-        [right_top, left_rest, own[middle - 1], own[1 - middle]],
-    )
 
     share = width // n
     part = rank // 2
@@ -499,19 +483,25 @@
         return local, lax.ppermute(local, "dp", swap)
 
     for hop, s in enumerate(range(middle - 1, 0, -1)):
-        going_right, going_left = right(going_right), left(going_left)
+        right_top, left_rest = add(right_top, own[s][0]), add(left_rest, own[-s][1])
+        right_top, left_rest = right(right_top), left(left_rest)
         if hop == 0:
-            for bit in bits[1:]:
+            for bit in bits[2:]:
                 pair = exchange(*pair, bit)
-            low, pair = adapter_gradient(pair[0])
-        elif hop == 1:
-            pair = exchange(*pair, bits[0])
-            low_rows, pair = lax.optimization_barrier((low_rows, pair))
+        if hop == 2:
+            pair = exchange(*pair, bits[1])
         if s > 1:
-            going_right, going_left, pair = lax.optimization_barrier((going_right, going_left, pair))
-            going_right, going_left = add(going_right, own[s - 1]), add(going_left, own[1 - s])
+            right_rest, left_top, pair = lax.optimization_barrier((right_rest, left_top, pair))
+            right_rest, left_top = add(right_rest, own[s - 1][1]), add(left_top, own[1 - s][0])
+            right_rest, left_top = right(right_rest), left(left_top)
+            if hop == 0:
+                low, pair = adapter_gradient(pair[0])
+            if hop == 1:
+                pair = exchange(*pair, bits[0])
+                low_rows, pair = lax.optimization_barrier((low_rows, pair))
+            right_top, left_rest, pair = lax.optimization_barrier((right_top, left_rest, pair))
     lora, lora_there = lora_gradients()
-    for bit in bits[1:]:
+    for bit in bits[2 if middle > 3 else 1 :]:
         pair = exchange(*pair, bit)
     down = pair[0][0]
     there = lax.ppermute(down, "dp", swap)
@@ -526,7 +516,7 @@
         functools.partial(finish_kernel, capacity),
         "finish",
         [((own_count, width), BF)],
-        [choice, going_right, going_left, own[0], low, adapter_down_factor],
+        [choice, right_top, left_top, own[0][0], right_rest, left_rest, own[0][1], low, adapter_down_factor],
         [pltpu.VMEM((2 * capacity, rank), F32)],
         (4e8, 4.5e6),
     )

time: 126 us -> 122 us (0.968)
  waiting for transfers between devices: 67 us -> 44.5 us
  starting transfers between devices: 23.5 us -> 41.9 us
    ppermute x6, waiting for transfers between devices: 45.2 us -> 10.3 us  [exchange(): other = lax.ppermute(send, 'expert', [(e, e ^ bit) for e in range(n)])]
    ppermute x8 -> x14, waiting for transfers between devices: 10.7 us -> 25.5 us  [left(): return lax.ppermute(x, 'expert', to_left)]
    ppermute x8 -> x14, starting transfers between devices: 8.49 us -> 19 us  [right(): return lax.ppermute(x, 'expert', to_right)]
    ppermute x8 -> x14, starting transfers between devices: 9.18 us -> 14.6 us  [left(): return lax.ppermute(x, 'expert', to_left)]
    ppermute x6, starting transfers between devices: 5.57 us -> 8.13 us  [exchange(): other = lax.ppermute(send, 'expert', [(e, e ^ bit) for e in range(n)])]
    ppermute x1, waiting for transfers between devices: 1.71 us -> 0.01 us  [adapter_gradient(): other = lax.ppermute(send, 'dp', swap)]
    ppermute x8 -> x14, waiting for transfers between devices: 8.2 us -> 7.47 us  [right(): return lax.ppermute(x, 'expert', to_right)]
    pallas_call x21 -> x19, Pallas kernels: 26.5 us -> 26.6 us  [call(): pl.pallas_call(kernel, out_shape=[jax.ShapeDtypeStruct(shape, dtype) for...]
  transfers between devices with their start and end apart: 25 -> 37, of which waited for: 15 -> 17; matrix products, arithmetic and copies ran while one was open for 0% -> 0% of each run, Pallas kernels for 9% -> 15%
where the time goes in v9:
time: 122 us
  waiting for transfers between devices  44.5 us (36%)
  starting transfers between devices  41.9 us (34%)
  Pallas kernels  26.6 us (22%)
  local copies, waits for them, and re-layouts  7.54 us (6%)
    pallas_call x19, Pallas kernels, call(): pl.pallas_call(kernel, out_shape=[jax.ShapeDtypeStruct(shape, dtype) for...  26.6 us
    ppermute x14, waiting for transfers between devices, left(): return lax.ppermute(x, 'expert', to_left)  25.5 us
    ppermute x14, starting transfers between devices, right(): return lax.ppermute(x, 'expert', to_right)  19 us
    ppermute x14, starting transfers between devices, left(): return lax.ppermute(x, 'expert', to_left)  14.6 us
    ppermute x6, waiting for transfers between devices, exchange(): other = lax.ppermute(send, 'expert', [(e, e ^ bit) for e in range(n)])  10.3 us
    ppermute x6, starting transfers between devices, exchange(): other = lax.ppermute(send, 'expert', [(e, e ^ bit) for e in range(n)])  8.13 us
    unnamed x30, local copies, waits for them, and re-layouts  7.54 us
    ppermute x14, waiting for transfers between devices, right(): return lax.ppermute(x, 'expert', to_right)  7.47 us
  transfers between devices with their start and end apart: 37, of which 17 were waited for; matrix products, arithmetic and copies ran while one was open for 0% of the time, Pallas kernels for 15%

profile of v9, /device:TPU:0, one launch (start us, length us, event | category | flops | bytes accessed | tf_op | source)
XLA Modules:
  0.0 122.1 jit_solution(13364524120235901074)
XLA Ops:
  0.6 2.9 %prepare.1 = (bf16[32,3200]{1,0:T(8,128)(2,1)S(1)}, bf16[40,3200]{1,0:T(8,128)(2,1)S(1)}) custom-call(s32[4,128]{1,0:T(4,128)} %bitcast.22, bf16[4,128]{1,0:T(4,128)(2,1)} %bitcast.27, bf16[128,6144]{1,0:T(8,128)(2,1)} %bitcast.26, bf16[128,6144]{1,0:T(8,128)(2,1)} %bitcast.16, bf16[64,6144]{1,0:T(8,128)(2,1)} %refs_7_.5), custom_call_target="tpu_custom_call" | custom-call | flops 1 | bytes 1 | tf_op jit(solution)/shard_map/prepare/pallas_call | solution.py:321
  3.6 3.0 %collective-permute-start.1 = (bf16[40,3200]{1,0:T(8,128)(2,1)S(1)}, bf16[40,3200]{1,0:T(8,128)(2,1)S(1)}, u32[]{:S(2)}, u32[]{:S(2)}) collective-permute-start(bf16[40,3200]{1,0:T(8,128)(2,1)S(1)} %get-tuple-element.122.refs_1_), channel_id=1, source_target_pairs={{0,2},{4,0},{8,4},{12,8},{14,12},{10,14},{6,10},{2,6},{1,3},{5,1},... | collective-permute-start | bytes 768008 | tf_op jit(solution)/shard_map/ppermute | solution.py:335
  8.7 3.7 %copy-done = bf16[768,6144]{1,0:T(8,128)(2,1)S(1)} copy-done((bf16[768,6144]{1,0:T(8,128)(2,1)S(1)}, bf16[768,6144]{1,0:T(8,128)(2,1)}, u32[]{:S(2)}) %copy-start) | copy-done | bytes 9437208
  20.5 5.1 %collective-permute-done.7.refs_3_ = bf16[40,3200]{1,0:T(8,128)(2,1)S(1)} collective-permute-done((bf16[40,3200]{1,0:T(8,128)(2,1)S(1)}, bf16[40,3200]{1,0:T(8,128)(2,1)S(1)}, u32[]{:S(2)}, u32[]{:S(2)}) %collective-permute-start.7) | collective-permute-done | bytes 256032 | tf_op jit(solution)/shard_map/ppermute | solution.py:335
  25.6 4.3 %collective-permute-done.3.refs_4_ = bf16[32,3200]{1,0:T(8,128)(2,1)S(1)} collective-permute-done((bf16[32,3200]{1,0:T(8,128)(2,1)S(1)}, bf16[32,3200]{1,0:T(8,128)(2,1)S(1)}, u32[]{:S(2)}, u32[]{:S(2)}) %collective-permute-start.3) | collective-permute-done | bytes 204832 | tf_op jit(solution)/shard_map/ppermute | solution.py:335
  32.0 3.0 %hidden_rows.4 = (bf16[3,40,768]{2,1,0:T(8,128)(2,1)S(1)}, bf16[3,40,768]{2,1,0:T(8,128)(2,1)S(1)}, bf16[3,40,64]{2,1,0:T(8,128)(2,1)S(1)}, f32[40,64]{1,0:T(8,1...) custom-call(bf16[32,3200]{1,0:T(8,128)(2,1)S(1)} %get-tuple-element.121.refs_0_, ...), custom_call_target="tpu_custom_call" | custom-call | flops 1 | bytes 1 | tf_op jit(solution)/shard_map/hidden_rows/pallas_call | solution.py:321
  35.0 2.8 %collective-permute-done.6.refs_2_ = bf16[32,3200]{1,0:T(8,128)(2,1)S(1)} collective-permute-done((bf16[32,3200]{1,0:T(8,128)(2,1)S(1)}, bf16[32,3200]{1,0:T(8,128)(2,1)S(1)}, u32[]{:S(2)}, u32[]{:S(2)}) %collective-permute-start.6) | collective-permute-done | bytes 204832 | tf_op jit(solution)/shard_map/ppermute | solution.py:335
  41.8 3.1 %hidden_rows.5 = (bf16[2,40,768]{2,1,0:T(8,128)(2,1)S(1)}, bf16[2,40,768]{2,1,0:T(8,128)(2,1)S(1)}, bf16[2,40,64]{2,1,0:T(8,128)(2,1)S(1)}, f32[40,64]{1,0:T(8,128)S(1)}, f32[40,64]{1,0:T(8,128)S(1)}) custom-call(bf16[32,3200]{1,0:T(8,128)(2,1)S(1)} %collective-permute-done.4.refs_0_, bf16[40,3200]{1,0:T(8,128)(2,1)S(1)} %collective-permute-done.5.refs_1_, ...), custom_call_target="tpu_custom_call" | custom-call | flops 1 | bytes 1 | tf_op jit(solution)/shard_map/hidden_rows/pallas_call | solution.py:321
  44.9 4.7 %collective-permute-done.10.refs_2_ = bf16[32,3200]{1,0:T(8,128)(2,1)S(1)} collective-permute-done((bf16[32,3200]{1,0:T(8,128)(2,1)S(1)}, bf16[32,3200]{1,0:T(8,128)(2,1)S(1)}, u32[]{:S(2)}, u32[]{:S(2)}) %collective-permute-start.10) | collective-permute-done | bytes 204832 | tf_op jit(solution)/shard_map/ppermute | solution.py:335
  49.6 3.1 %hidden_rows.6 = (bf16[2,40,768]{2,1,0:T(8,128)(2,1)S(1)}, bf16[2,40,768]{2,1,0:T(8,128)(2,1)S(1)}, bf16[2,40,64]{2,1,0:T(8,128)(2,1)S(1)}, f32[40,64]{1,0:T(8,128)S(1)}, f32[40,64]{1,0:T(8,128)S(1)}) custom-call(bf16[32,3200]{1,0:T(8,128)(2,1)S(1)} %collective-permute-done.8.refs_0_, bf16[40,3200]{1,0:T(8,128)(2,1)S(1)} %collective-permute-done.9.refs_1_, ...), custom_call_target="tpu_custom_call" | custom-call | flops 1 | bytes 1 | tf_op jit(solution)/shard_map/hidden_rows/pallas_call | solution.py:321
  52.8 2.9 %hidden_rows.7 = (bf16[1,40,768]{2,1,0:T(8,128)(2,1)S(1)}, bf16[1,40,768]{2,1,0:T(8,128)(2,1)S(1)}, bf16[1,40,64]{2,1,0:T(8,128)(2,1)S(1)}, f32[40,64]{1,0:T(8,128)S(1)}) custom-call(bf16[32,3200]{1,0:T(8,128)(2,1)S(1)} %collective-permute-done.12.refs_0_, bf16[40,3200]{1,0:T(8,128)(2,1)S(1)} %collective-permute-done.13.refs_1_, ...), custom_call_target="tpu_custom_call" | custom-call | flops 1 | bytes 1 | tf_op jit(solution)/shard_map/hidden_rows/pallas_call | solution.py:321
  56.7 6.5 %partials.1 = (bf16[32,3072]{1,0:T(8,128)(2,1)S(1)}, bf16[40,3072]{1,0:T(8,128)(2,1)S(1)}, bf16[32,3072]{1,0:T(8,128)(2,1)S(1)}, bf16[40,3072]{1,0:T(8,128)(2,1)...) custom-call(bf16[3,40,768]{2,1,0:T(8,128)(2,1)S(1)} %get-tuple-eleme, ...), custom_call_target="tpu_custom_call" | custom-call | flops 1 | bytes 1 | tf_op jit(solution)/shard_map/partials/pallas_call | solution.py:321
  68.5 2.4 %collective-permute-done.17.theirs = f32[2,40,64]{2,1,0:T(8,128)S(1)} collective-permute-done((f32[2,40,64]{2,1,0:T(8,128)S(1)}, f32[2,40,64]{2,1,0:T(8,128)S(1)}, u32[]{:S(2)}, u32[]{:S(2)}) %collective-permute-start.17) | collective-permute-done | bytes 20512 | tf_op jit(solution)/shard_map/ppermute | solution.py:430
  72.2 2.3 %collective-permute-start.22 = (f32[1,40,64]{2,1,0:T(8,128)S(1)}, f32[1,40,64]{2,1,0:T(8,128)S(1)}, u32[]{:S(2)}, u32[]{:S(2)}) collective-permute-start(f32[1,40,64]{2,1,0:T(8,128)S(1)} %get-tuple-element.190), channel_id=1, source_target_pairs={{0,8},{2,10},{4,12},{6,14},{8,0},{10,2},{12,4},{14,6},{1,9},{3,11}... | collective-permute-start | bytes 30728 | tf_op jit(solution)/shard_map/ppermute | solution.py:430
  79.7 2.2 %collective-permute-start.27 = (bf16[32,3072]{1,0:T(8,128)(2,1)S(1)}, bf16[32,3072]{1,0:T(8,128)(2,1)S(1)}, u32[]{:S(2)}, u32[]{:S(2)}) collective-permute-start(bf16[32,3072]{1,0:T(8,128)(2,1)S(1)} %add_convert_fusion.7), channel_id=1, source_target_pairs={{0,2},{4,0},{8,4},{12,8},{14,12},{10,14},{6,10},{2,6},{1,3},{5,1},... | collective-permute-start | bytes 589832 | tf_op jit(solution)/shard_map/ppermute | solution.py:335
  82.9 4.2 %collective-permute-done.27 = bf16[32,3072]{1,0:T(8,128)(2,1)S(1)} collective-permute-done((bf16[32,3072]{1,0:T(8,128)(2,1)S(1)}, bf16[32,3072]{1,0:T(8,128)(2,1)S(1)}, u32[]{:S(2)}, u32[]{:S(2)}) %collective-permute-start.27) | collective-permute-done | bytes 196640 | tf_op jit(solution)/shard_map/ppermute | solution.py:335
  87.1 2.1 %collective-permute-start.28 = (bf16[4,32,768]{2,1,0:T(8,128)(2,1)S(1)}, bf16[4,32,768]{2,1,0:T(8,128)(2,1)S(1)}, u32[]{:S(2)}, u32[]{:S(2)}) collective-permute-start(bf16[4,32,768]{2,1,0:T(8,128)(2,1)S(1)} %get-tuple-element.211), channel_id=1, source_target_pairs={{0,2},{2,0},{4,6},{6,4},{8,10},{10,8},{12,14},{14,12},{1,3},{3,1},... | collective-permute-start | bytes 589832 | tf_op jit(solution)/shard_map/ppermute | solution.py:430
  89.4 2.1 %collective-permute-start.24 = (bf16[32,3072]{1,0:T(8,128)(2,1)S(1)}, bf16[32,3072]{1,0:T(8,128)(2,1)S(1)}, u32[]{:S(2)}, u32[]{:S(2)}) collective-permute-start(bf16[32,3072]{1,0:T(8,128)(2,1)S(1)} %add_convert_fusion.8), channel_id=1, source_target_pairs={{0,4},{4,8},{8,12},{12,14},{14,10},{10,6},{6,2},{2,0},{1,5},{5,9},... | collective-permute-start | bytes 589832 | tf_op jit(solution)/shard_map/ppermute | solution.py:332
  95.4 3.7 %collective-permute-done.24 = bf16[32,3072]{1,0:T(8,128)(2,1)S(1)} collective-permute-done((bf16[32,3072]{1,0:T(8,128)(2,1)S(1)}, bf16[32,3072]{1,0:T(8,128)(2,1)S(1)}, u32[]{:S(2)}, u32[]{:S(2)}) %collective-permute-start.24) | collective-permute-done | bytes 196640 | tf_op jit(solution)/shard_map/ppermute | solution.py:332
  99.1 3.6 %collective-permute-done.25 = bf16[40,3072]{1,0:T(8,128)(2,1)S(1)} collective-permute-done((bf16[40,3072]{1,0:T(8,128)(2,1)S(1)}, bf16[40,3072]{1,0:T(8,128)(2,1)S(1)}, u32[]{:S(2)}, u32[]{:S(2)}) %collective-permute-start.25) | collective-permute-done | bytes 245792 | tf_op jit(solution)/shard_map/ppermute | solution.py:335
  102.9 2.4 %collective-permute-start.32 = (bf16[40,3072]{1,0:T(8,128)(2,1)S(1)}, bf16[40,3072]{1,0:T(8,128)(2,1)S(1)}, u32[]{:S(2)}, u32[]{:S(2)}) collective-permute-start(bf16[40,3072]{1,0:T(8,128)(2,1)S(1)} %add_convert_fusion), channel_id=1, source_target_pairs={{0,2},{4,0},{8,4},{12,8},{14,12},{10,14},{6,10},{2,6},{1,3},{5,1},... | collective-permute-start | bytes 737288 | tf_op jit(solution)/shard_map/ppermute | solution.py:335
  105.3 3.1 %collective-permute-done.33.theirs = bf16[2,32,768]{2,1,0:T(8,128)(2,1)S(1)} collective-permute-done((bf16[2,32,768]{2,1,0:T(8,128)(2,1)S(1)}, bf16[2,32,768]{2,1,0:T(8,128)(2,1)S(1)}, u32[]{:S(2)}, u32[]{:S(2)}) %collective-permute-start.33) | collective-permute-done | bytes 98336 | tf_op jit(solution)/shard_map/ppermute | solution.py:430
  110.5 3.5 %collective-permute-done.34.theirs = bf16[1,32,768]{2,1,0:T(8,128)(2,1)S(1)} collective-permute-done((bf16[1,32,768]{2,1,0:T(8,128)(2,1)S(1)}, bf16[1,32,768]{2,1,0:T(8,128)(2,1)S(1)}, u32[]{:S(2)}, u32[]{:S(2)}) %collective-permute-start.34) | collective-permute-done | bytes 49184 | tf_op jit(solution)/shard_map/ppermute | solution.py:430
  119.7 2.4 %finish.1 = bf16[128,6144]{1,0:T(8,128)(2,1)} custom-call(s32[4,128]{1,0:T(4,128)S(1)} %bitcast.24, bf16[32,3072]{1,0:T(8,128)(2,1)S(1)} %collective-permute-done.29.refs_0_, bf16[32,3072]{1,0:T(8,128)(2,1)S(1)} %collective-permute-done.30.refs_1_, bf16[32,3072]{1,0:T(8,128)(2,1)S(1)} %get-tuple-element.220.refs_2_, ...), custom_call_target="tpu_custom_call" | custom-call | flops 1 | bytes 1 | tf_op jit(solution)/shard_map/finish/pallas_call | solution.py:321
  (111 shorter events, 42.1 us)
Async XLA Ops:
  3.6 12.8 %collective-permute-start.1 = (bf16[40,3200]{1,0:T(8,128)(2,1)S(1)}, bf16[40,3200]{1,0:T(8,128)(2,1)S(1)}, u32[]{:S(2)}, u32[]{:S(2)}) collective-permute-start(bf16[40,3200]{1,0:T(8,128)(2,1)S(1)} %get-tuple-element.122.refs_1_), channel_id=1, source_target_pairs={{0,2},{4,0},{8,4},{12,8},{14,12},{10,14},{6,10},{2,6},{1,3},{5,1},... | collective-permute-start | bytes 768008 | tf_op jit(solution)/shard_map/ppermute | solution.py:335
  6.6 9.8 %collective-permute-start = (bf16[32,3200]{1,0:T(8,128)(2,1)S(1)}, bf16[32,3200]{1,0:T(8,128)(2,1)S(1)}, u32[]{:S(2)}, u32[]{:S(2)}) collective-permute-start(bf16[32,3200]{1,0:T(8,128)(2,1)S(1)} %get-tuple-element.121.refs_0_), channel_id=1, source_target_pairs={{0,4},{4,8},{8,12},{12,14},{14,10},{10,6},{6,2},{2,0},{1,5},{5,9},... | collective-permute-start | bytes 614408 | tf_op jit(solution)/shard_map/ppermute | solution.py:332
  6.7 11.9 %collective-permute-start.2 = (bf16[40,3200]{1,0:T(8,128)(2,1)S(1)}, bf16[40,3200]{1,0:T(8,128)(2,1)S(1)}, u32[]{:S(2)}, u32[]{:S(2)}) collective-permute-start(bf16[40,3200]{1,0:T(8,128)(2,1)S(1)} %get-tuple-element.122.refs_1_), channel_id=1, source_target_pairs={{0,4},{4,8},{8,12},{12,14},{14,10},{10,6},{6,2},{2,0},{1,5},{5,9},... | collective-permute-start | bytes 768008 | tf_op jit(solution)/shard_map/ppermute | solution.py:332
  16.4 9.2 %collective-permute-start.7 = (bf16[40,3200]{1,0:T(8,128)(2,1)S(1)}, bf16[40,3200]{1,0:T(8,128)(2,1)S(1)}, u32[]{:S(2)}, u32[]{:S(2)}) collective-permute-start(bf16[40,3200]{1,0:T(8,128)(2,1)S(1)} %collective-permute-done.1.refs_5_), channel_id=1, source_target_pairs={{0,2},{4,0},{8,4},{12,8},{14,12},{10,14},{6,10},{2,6},{1,3},{5,1},... | collective-permute-start | bytes 768008 | tf_op jit(solution)/shard_map/ppermute | solution.py:335
  16.5 13.4 %collective-permute-start.3 = (bf16[32,3200]{1,0:T(8,128)(2,1)S(1)}, bf16[32,3200]{1,0:T(8,128)(2,1)S(1)}, u32[]{:S(2)}, u32[]{:S(2)}) collective-permute-start(bf16[32,3200]{1,0:T(8,128)(2,1)S(1)} %get-tuple-element.121.refs_0_), channel_id=1, source_target_pairs={{0,2},{4,0},{8,4},{12,8},{14,12},{10,14},{6,10},{2,6},{1,3},{5,1},... | collective-permute-start | bytes 614408 | tf_op jit(solution)/shard_map/ppermute | solution.py:335
  18.4 11.6 %collective-permute-start.4 = (bf16[32,3200]{1,0:T(8,128)(2,1)S(1)}, bf16[32,3200]{1,0:T(8,128)(2,1)S(1)}, u32[]{:S(2)}, u32[]{:S(2)}) collective-permute-start(bf16[32,3200]{1,0:T(8,128)(2,1)S(1)} %collective-permute-done.refs_2_), channel_id=1, source_target_pairs={{0,4},{4,8},{8,12},{12,14},{14,10},{10,6},{6,2},{2,0},{1,5},{5,9},... | collective-permute-start | bytes 614408 | tf_op jit(solution)/shard_map/ppermute | solution.py:332
  18.6 19.2 %collective-permute-start.5 = (bf16[40,3200]{1,0:T(8,128)(2,1)S(1)}, bf16[40,3200]{1,0:T(8,128)(2,1)S(1)}, u32[]{:S(2)}, u32[]{:S(2)}) collective-permute-start(bf16[40,3200]{1,0:T(8,128)(2,1)S(1)} %collective-permute-done.2.refs_3_), channel_id=1, source_target_pairs={{0,4},{4,8},{8,12},{12,14},{14,10},{10,6},{6,2},{2,0},{1,5},{5,9},... | collective-permute-start | bytes 768008 | tf_op jit(solution)/shard_map/ppermute | solution.py:332
  25.5 13.8 %collective-permute-start.11 = (bf16[40,3200]{1,0:T(8,128)(2,1)S(1)}, bf16[40,3200]{1,0:T(8,128)(2,1)S(1)}, u32[]{:S(2)}, u32[]{:S(2)}) collective-permute-start(bf16[40,3200]{1,0:T(8,128)(2,1)S(1)} %collective-permute-done.7.refs_3_), channel_id=1, source_target_pairs={{0,2},{4,0},{8,4},{12,8},{14,12},{10,14},{6,10},{2,6},{1,3},{5,1},... | collective-permute-start | bytes 768008 | tf_op jit(solution)/shard_map/ppermute | solution.py:335
  30.0 10.2 %collective-permute-start.8 = (bf16[32,3200]{1,0:T(8,128)(2,1)S(1)}, bf16[32,3200]{1,0:T(8,128)(2,1)S(1)}, u32[]{:S(2)}, u32[]{:S(2)}) collective-permute-start(bf16[32,3200]{1,0:T(8,128)(2,1)S(1)} %collective-permute-done.4.refs_0_), channel_id=1, source_target_pairs={{0,4},{4,8},{8,12},{12,14},{14,10},{10,6},{6,2},{2,0},{1,5},{5,9},... | collective-permute-start | bytes 614408 | tf_op jit(solution)/shard_map/ppermute | solution.py:332
  37.8 11.8 %collective-permute-start.9 = (bf16[40,3200]{1,0:T(8,128)(2,1)S(1)}, bf16[40,3200]{1,0:T(8,128)(2,1)S(1)}, u32[]{:S(2)}, u32[]{:S(2)}) collective-permute-start(bf16[40,3200]{1,0:T(8,128)(2,1)S(1)} %collective-permute-done.5.refs_1_), channel_id=1, source_target_pairs={{0,4},{4,8},{8,12},{12,14},{14,10},{10,6},{6,2},{2,0},{1,5},{5,9},... | collective-permute-start | bytes 768008 | tf_op jit(solution)/shard_map/ppermute | solution.py:332
  39.4 13.4 %collective-permute-start.13 = (bf16[40,3200]{1,0:T(8,128)(2,1)S(1)}, bf16[40,3200]{1,0:T(8,128)(2,1)S(1)}, u32[]{:S(2)}, u32[]{:S(2)}) collective-permute-start(bf16[40,3200]{1,0:T(8,128)(2,1)S(1)} %collective-permute-done.11.refs_3_), channel_id=1, source_target_pairs={{0,2},{4,0},{8,4},{12,8},{14,12},{10,14},{6,10},{2,6},{1,3},{5,1},... | collective-permute-start | bytes 768008 | tf_op jit(solution)/shard_map/ppermute | solution.py:335
  39.8 9.8 %collective-permute-start.10 = (bf16[32,3200]{1,0:T(8,128)(2,1)S(1)}, bf16[32,3200]{1,0:T(8,128)(2,1)S(1)}, u32[]{:S(2)}, u32[]{:S(2)}) collective-permute-start(bf16[32,3200]{1,0:T(8,128)(2,1)S(1)} %collective-permute-done.6.refs_2_), channel_id=1, source_target_pairs={{0,2},{4,0},{8,4},{12,8},{14,12},{10,14},{6,10},{2,6},{1,3},{5,1},... | collective-permute-start | bytes 614408 | tf_op jit(solution)/shard_map/ppermute | solution.py:335
  40.2 12.6 %collective-permute-start.12 = (bf16[32,3200]{1,0:T(8,128)(2,1)S(1)}, bf16[32,3200]{1,0:T(8,128)(2,1)S(1)}, u32[]{:S(2)}, u32[]{:S(2)}) collective-permute-start(bf16[32,3200]{1,0:T(8,128)(2,1)S(1)} %collective-permute-done.8.refs_0_), channel_id=1, source_target_pairs={{0,4},{4,8},{8,12},{12,14},{14,10},{10,6},{6,2},{2,0},{1,5},{5,9},... | collective-permute-start | bytes 614408 | tf_op jit(solution)/shard_map/ppermute | solution.py:332
  63.2 9.0 %collective-permute-start.16 = (bf16[40,3072]{1,0:T(8,128)(2,1)S(1)}, bf16[40,3072]{1,0:T(8,128)(2,1)S(1)}, u32[]{:S(2)}, u32[]{:S(2)}) collective-permute-start(bf16[40,3072]{1,0:T(8,128)(2,1)S(1)} %get-tuple-element.178), channel_id=1, source_target_pairs={{0,2},{4,0},{8,4},{12,8},{14,12},{10,14},{6,10},{2,6},{1,3},{5,1},... | collective-permute-start | bytes 737288 | tf_op jit(solution)/shard_map/ppermute | solution.py:335
  66.5 10.4 %collective-permute-start.21 = (bf16[32,3072]{1,0:T(8,128)(2,1)S(1)}, bf16[32,3072]{1,0:T(8,128)(2,1)S(1)}, u32[]{:S(2)}, u32[]{:S(2)}) collective-permute-start(bf16[32,3072]{1,0:T(8,128)(2,1)S(1)} %get-tuple-element.188), channel_id=1, source_target_pairs={{0,2},{4,0},{8,4},{12,8},{14,12},{10,14},{6,10},{2,6},{1,3},{5,1},... | collective-permute-start | bytes 589832 | tf_op jit(solution)/shard_map/ppermute | solution.py:335
  68.4 9.0 %collective-permute-start.20 = (bf16[40,3072]{1,0:T(8,128)(2,1)S(1)}, bf16[40,3072]{1,0:T(8,128)(2,1)S(1)}, u32[]{:S(2)}, u32[]{:S(2)}) collective-permute-start(bf16[40,3072]{1,0:T(8,128)(2,1)S(1)} %get-tuple-element.187), channel_id=1, source_target_pairs={{0,4},{4,8},{8,12},{12,14},{14,10},{10,6},{6,2},{2,0},{1,5},{5,9},... | collective-permute-start | bytes 737288 | tf_op jit(solution)/shard_map/ppermute | solution.py:332
  77.5 9.6 %collective-permute-start.26 = (bf16[40,3072]{1,0:T(8,128)(2,1)S(1)}, bf16[40,3072]{1,0:T(8,128)(2,1)S(1)}, u32[]{:S(2)}, u32[]{:S(2)}) collective-permute-start(bf16[40,3072]{1,0:T(8,128)(2,1)S(1)} %add_convert_fusion.2), channel_id=1, source_target_pairs={{0,4},{4,8},{8,12},{12,14},{14,10},{10,6},{6,2},{2,0},{1,5},{5,9},... | collective-permute-start | bytes 737288 | tf_op jit(solution)/shard_map/ppermute | solution.py:332
  87.1 7.9 %collective-permute-start.28 = (bf16[4,32,768]{2,1,0:T(8,128)(2,1)S(1)}, bf16[4,32,768]{2,1,0:T(8,128)(2,1)S(1)}, u32[]{:S(2)}, u32[]{:S(2)}) collective-permute-start(bf16[4,32,768]{2,1,0:T(8,128)(2,1)S(1)} %get-tuple-element.211), channel_id=1, source_target_pairs={{0,2},{2,0},{4,6},{6,4},{8,10},{10,8},{12,14},{14,12},{1,3},{3,1},... | collective-permute-start | bytes 589832 | tf_op jit(solution)/shard_map/ppermute | solution.py:430
  89.2 28.6 %collective-permute-start.30 = (bf16[32,3072]{1,0:T(8,128)(2,1)S(1)}, bf16[32,3072]{1,0:T(8,128)(2,1)S(1)}, u32[]{:S(2)}, u32[]{:S(2)}) collective-permute-start(bf16[32,3072]{1,0:T(8,128)(2,1)S(1)} %add_convert_fusion.5), channel_id=1, source_target_pairs={{0,2},{4,0},{8,4},{12,8},{14,12},{10,14},{6,10},{2,6},{1,3},{5,1},... | collective-permute-start | bytes 589832 | tf_op jit(solution)/shard_map/ppermute | solution.py:335
  89.4 9.8 %collective-permute-start.24 = (bf16[32,3072]{1,0:T(8,128)(2,1)S(1)}, bf16[32,3072]{1,0:T(8,128)(2,1)S(1)}, u32[]{:S(2)}, u32[]{:S(2)}) collective-permute-start(bf16[32,3072]{1,0:T(8,128)(2,1)S(1)} %add_convert_fusion.8), channel_id=1, source_target_pairs={{0,4},{4,8},{8,12},{12,14},{14,10},{10,6},{6,2},{2,0},{1,5},{5,9},... | collective-permute-start | bytes 589832 | tf_op jit(solution)/shard_map/ppermute | solution.py:332
  91.5 11.2 %collective-permute-start.25 = (bf16[40,3072]{1,0:T(8,128)(2,1)S(1)}, bf16[40,3072]{1,0:T(8,128)(2,1)S(1)}, u32[]{:S(2)}, u32[]{:S(2)}) collective-permute-start(bf16[40,3072]{1,0:T(8,128)(2,1)S(1)} %add_convert_fusion.3), channel_id=1, source_target_pairs={{0,2},{4,0},{8,4},{12,8},{14,12},{10,14},{6,10},{2,6},{1,3},{5,1},... | collective-permute-start | bytes 737288 | tf_op jit(solution)/shard_map/ppermute | solution.py:335
  91.6 26.2 %collective-permute-start.31 = (bf16[40,3072]{1,0:T(8,128)(2,1)S(1)}, bf16[40,3072]{1,0:T(8,128)(2,1)S(1)}, u32[]{:S(2)}, u32[]{:S(2)}) collective-permute-start(bf16[40,3072]{1,0:T(8,128)(2,1)S(1)} %add_convert_fusion.1), channel_id=1, source_target_pairs={{0,4},{4,8},{8,12},{12,14},{14,10},{10,6},{6,2},{2,0},{1,5},{5,9},... | collective-permute-start | bytes 737288 | tf_op jit(solution)/shard_map/ppermute | solution.py:332
  95.3 20.3 %collective-permute-start.36 = (bf16[128,768]{1,0:T(8,128)(2,1)S(1)}, bf16[128,768]{1,0:T(8,128)(2,1)S(1)}, u32[]{:S(2)}, u32[]{:S(2)}) collective-permute-start(bf16[128,768]{1,0:T(8,128)(2,1)S(1)} %lora_rows.1.lora_ref), channel_id=1, source_target_pairs={{0,1},{1,0},{2,3},{3,2},{4,5},{5,4},{6,7},{7,6},{8,9},{9,8},{10,11... | collective-permute-start | bytes 589832 | tf_op jit(solution)/shard_map/ppermute | solution.py:483
  102.9 16.8 %collective-permute-start.32 = (bf16[40,3072]{1,0:T(8,128)(2,1)S(1)}, bf16[40,3072]{1,0:T(8,128)(2,1)S(1)}, u32[]{:S(2)}, u32[]{:S(2)}) collective-permute-start(bf16[40,3072]{1,0:T(8,128)(2,1)S(1)} %add_convert_fusion), channel_id=1, source_target_pairs={{0,2},{4,0},{8,4},{12,8},{14,12},{10,14},{6,10},{2,6},{1,3},{5,1},... | collective-permute-start | bytes 737288 | tf_op jit(solution)/shard_map/ppermute | solution.py:335
  (28 other events, 252.7 us)

commit v10 on v8

--- a/solution.py
+++ b/solution.py
@@ -89,14 +89,6 @@
     cut = top.shape[0]
     top[...] = right_in[:cut, :]
     rest[...] = left_in[cut:, :]
-
-
-def merge_kernel(top_in, rest_in, own_right, own_left, right_out, left_out):
-    cut = top_in.shape[0]
-    right_out[:cut, :] = (top_in[...].astype(F32) + own_right[:cut, :].astype(F32)).astype(BF)
-    right_out[cut:, :] = own_right[cut:, :]
-    left_out[:cut, :] = own_left[:cut, :]
-    left_out[cut:, :] = (rest_in[...].astype(F32) + own_left[cut:, :].astype(F32)).astype(BF)
 
 
 def place_here(place):
@@ -225,11 +217,8 @@
             at = i * slot
             tile[:capacity, :] = sums[0][at : at + capacity]
             tile[capacity:, :] = sums[1][at : at + capacity]
-            if i < members - 1:
-                outs[i][:, t : t + TILE] = tile[...].astype(BF)
-            else:
-                outs[i][:, t : t + TILE] = tile[:cut, :].astype(BF)
-                outs[i + 1][:, t : t + TILE] = tile[cut:, :].astype(BF)
+            outs[2 * i][:, t : t + TILE] = tile[:cut, :].astype(BF)
+            outs[2 * i + 1][:, t : t + TILE] = tile[cut:, :].astype(BF)
 
 
 def adapter_kernel(capacity, choice_ref, tokens_ref, low_in, low_ref, keep_ref, send_ref):
@@ -258,8 +247,8 @@
 
 
 def finish_kernel(capacity, choice_ref, *refs):
-    parts, (low_ref, down_ref, out_ref, low_tall) = refs[:3], refs[3:]
-    half = parts[0].shape[1]
+    tops, rests, (low_ref, down_ref, out_ref, low_tall) = refs[:3], refs[3:6], refs[6:]
+    cut, half = tops[0].shape
     upper, lower = pick_rows(choice_ref[...], capacity)
     low = low_ref[...].astype(F32)[:capacity]
     zero = jnp.zeros_like(low)
@@ -269,11 +258,13 @@
     low_tall[:capacity, :] = zero
     low_tall[capacity:, :] = low
     low_lower = low_tall[...].astype(BF)
-    total = sum(x[...].astype(F32) for x in parts)
-    total += dot(low_upper, down_ref[:, :half]) + dot(low_lower, down_ref[:, half:])
-    total = total.astype(BF)
-    out_ref[:, :half] = dot(upper, total, TN).astype(BF)
-    out_ref[:, half:] = dot(lower, total, TN).astype(BF)
+    adapter = dot(low_upper, down_ref[:, :half]) + dot(low_lower, down_ref[:, half:])
+    top = sum(x[...].astype(F32) for x in tops) + adapter[:cut]
+    rest = sum(x[...].astype(F32) for x in rests) + adapter[cut:]
+    top, rest = top.astype(BF), rest.astype(BF)
+    for pick, at in ((upper, 0), (lower, half)):
+        picked = dot(pick[:cut], top, TN) + dot(pick[cut:], rest, TN)
+        out_ref[:, at : at + half] = picked.astype(BF)
 
 
 def in_hbm(x):
@@ -421,10 +412,10 @@
         [((n // 2, slot, rank), F32)] * 2,
         lows,
     )
-    *own, right_top, left_rest = call(
+    own = call(
         functools.partial(partial_kernel, capacity, slot, sizes, cut),
         "partials",
-        [((2 * capacity, half), BF)] * (n - 1) + [((h, half), BF) for h in heights],
+        [((h, half), BF) for h in heights] * n,
         [*dgates, *dups, gate_here, up_here],
         [
             pltpu.VMEM((n * slot, hidden), BF),
@@ -433,8 +424,6 @@
         ],
         (4 * n * slot * width * hidden, 4 * hidden * width),
     )
-    own = dict(zip(order[:-1], own))
-
     def add(a, b):
         return (a.astype(F32) + b.astype(F32)).astype(BF)
 
@@ -445,18 +434,22 @@
         shape = (count // parts,) + keep.shape[1:]
         return call(halve_kernel, "halve", [(shape, keep.dtype)] * parts, [keep, other])
 
-    low_keep, right_top, left_rest = lax.optimization_barrier((low_keep, right_top, left_rest))
-    right_top, left_rest = right(right_top), left(left_rest)
+    pair = exchange(low_keep, low_send, 1)
+    pair, own = lax.optimization_barrier((pair, own))
+    own = {r: (own[2 * i], own[2 * i + 1]) for i, r in enumerate(order)}
+    right_top, left_rest = right(own[middle][0]), left(own[middle][1])
+    right_rest, left_top = right(own[middle - 1][1]), left(own[1 - middle][0])
+    pair = exchange(*pair, 2)
+    right_top, left_rest, pair = lax.optimization_barrier((right_top, left_rest, pair))
+    for s in range(middle - 1, 0, -1):
+        right_top, left_rest = add(right_top, own[s][0]), add(left_rest, own[-s][1])
+        right_top, left_rest = right(right_top), left(left_rest)
+        if s > 1:
+            right_rest, left_top = add(right_rest, own[s - 1][1]), add(left_top, own[1 - s][0])
+            right_rest, left_top = right(right_rest), left(left_top)
     bits = [1 << i for i in range(n.bit_length() - 1)]
-    pair = [low_keep, low_send]
-    pair = exchange(*pair, bits[0])
-    right_top, left_rest, pair = lax.optimization_barrier((right_top, left_rest, pair))
-    going_right, going_left = call(
-        merge_kernel,
-        "first_add",
-        [((2 * capacity, half), BF)] * 2,
-        [right_top, left_rest, own[middle - 1], own[1 - middle]],
-    )
+    for bit in bits[2:]:
+        pair = exchange(*pair, bit)
 
     share = width // n
     part = rank // 2
@@ -498,20 +491,10 @@
         )
         return local, lax.ppermute(local, "dp", swap)
 
-    for hop, s in enumerate(range(middle - 1, 0, -1)):
-        going_right, going_left = right(going_right), left(going_left)
-        if hop == 0:
-            for bit in bits[1:]:
-                pair = exchange(*pair, bit)
-            low, pair = adapter_gradient(pair[0])
-        elif hop == 1:
-            pair = exchange(*pair, bits[0])
-            low_rows, pair = lax.optimization_barrier((low_rows, pair))
-        if s > 1:
-            going_right, going_left, pair = lax.optimization_barrier((going_right, going_left, pair))
-            going_right, going_left = add(going_right, own[s - 1]), add(going_left, own[1 - s])
+    low, pair = adapter_gradient(pair[0])
+    low_rows, _ = lax.optimization_barrier((low_rows, pair))
     lora, lora_there = lora_gradients()
-    for bit in bits[1:]:
+    for bit in bits:
         pair = exchange(*pair, bit)
     down = pair[0][0]
     there = lax.ppermute(down, "dp", swap)
@@ -526,7 +509,7 @@
         functools.partial(finish_kernel, capacity),
         "finish",
         [((own_count, width), BF)],
-        [choice, going_right, going_left, own[0], low, adapter_down_factor],
+        [choice, right_top, left_top, own[0][0], right_rest, left_rest, own[0][1], low, adapter_down_factor],
         [pltpu.VMEM((2 * capacity, rank), F32)],
         (4e8, 4.5e6),
     )

time: 126 us -> 111 us (0.88)
  waiting for transfers between devices: 67 us -> 39.2 us
  starting transfers between devices: 23.5 us -> 36 us
    ppermute x6, waiting for transfers between devices: 45.2 us -> 14.7 us  [exchange(): other = lax.ppermute(send, 'expert', [(e, e ^ bit) for e in range(n)])]
    ppermute x8 -> x11, starting transfers between devices: 9.18 us -> 14.3 us  [left(): return lax.ppermute(x, 'expert', to_left)]
    ppermute x8 -> x11, starting transfers between devices: 8.49 us -> 12.4 us  [right(): return lax.ppermute(x, 'expert', to_right)]
    ppermute x8 -> x11, waiting for transfers between devices: 10.7 us -> 13.9 us  [left(): return lax.ppermute(x, 'expert', to_left)]
    ppermute x6, starting transfers between devices: 5.57 us -> 8.67 us  [exchange(): other = lax.ppermute(send, 'expert', [(e, e ^ bit) for e in range(n)])]
    ppermute x8 -> x11, waiting for transfers between devices: 8.2 us -> 10.6 us  [right(): return lax.ppermute(x, 'expert', to_right)]
    ppermute x1, waiting for transfers between devices: 1.71 us -> 0.01 us  [adapter_gradient(): other = lax.ppermute(send, 'dp', swap)]
    pallas_call x21 -> x20, Pallas kernels: 26.5 us -> 26.8 us  [call(): pl.pallas_call(kernel, out_shape=[jax.ShapeDtypeStruct(shape, dtype) for...]
  transfers between devices with their start and end apart: 25 -> 31, of which waited for: 15 -> 16; matrix products, arithmetic and copies ran while one was open for 0% -> 1% of each run, Pallas kernels for 9% -> 18%
where the time goes in v10:
time: 111 us
  waiting for transfers between devices  39.2 us (35%)
  starting transfers between devices  36 us (32%)
  Pallas kernels  26.8 us (24%)
  local copies, waits for them, and re-layouts  7.54 us (7%)
    pallas_call x20, Pallas kernels, call(): pl.pallas_call(kernel, out_shape=[jax.ShapeDtypeStruct(shape, dtype) for...  26.8 us
    ppermute x6, waiting for transfers between devices, exchange(): other = lax.ppermute(send, 'expert', [(e, e ^ bit) for e in range(n)])  14.7 us
    ppermute x11, starting transfers between devices, left(): return lax.ppermute(x, 'expert', to_left)  14.3 us
    ppermute x11, waiting for transfers between devices, left(): return lax.ppermute(x, 'expert', to_left)  13.9 us
    ppermute x11, starting transfers between devices, right(): return lax.ppermute(x, 'expert', to_right)  12.4 us
    ppermute x11, waiting for transfers between devices, right(): return lax.ppermute(x, 'expert', to_right)  10.6 us
    ppermute x6, starting transfers between devices, exchange(): other = lax.ppermute(send, 'expert', [(e, e ^ bit) for e in range(n)])  8.67 us
    unnamed x34, local copies, waits for them, and re-layouts  7.54 us
  transfers between devices with their start and end apart: 31, of which 16 were waited for; matrix products, arithmetic and copies ran while one was open for 1% of the time, Pallas kernels for 18%

profile of v10, /device:TPU:0, one launch (start us, length us, event | category | flops | bytes accessed | tf_op | source)
XLA Modules:
  0.0 111.0 jit_solution(10388193469233638292)
XLA Ops:
  0.6 2.9 %prepare.1.refs_0_ = bf16[72,3200]{1,0:T(8,128)(2,1)S(1)} custom-call(s32[4,128]{1,0:T(4,128)} %bitcast.18, bf16[4,128]{1,0:T(4,128)(2,1)} %bitcast.27, bf16[128,6144]{1,0:T(8,128)(2,1)} %bitcast.26, bf16[128,6144]{1,0:T(8,128)(2,1)} %bitcast.12, bf16[64,6144]{1,0:T(8,128)(2,1)} %refs_7_.3), custom_call_target="tpu_custom_call" | custom-call | flops 400000000 | bytes 4500000 | tf_op jit(solution)/shard_map/prepare/pallas_call | solution.py:319
  3.6 3.0 %collective-permute-start.1 = (bf16[72,3200]{1,0:T(8,128)(2,1)S(1)}, bf16[72,3200]{1,0:T(8,128)(2,1)S(1)}, u32[]{:S(2)}, u32[]{:S(2)}) collective-permute-start(bf16[72,3200]{1,0:T(8,128)(2,1)S(1)} %prepare.1.refs_0_), channel_id=1, source_target_pairs={{0,2},{4,0},{8,4},{12,8},{14,12},{10,14},{6,10},{2,6},{1,3},{5,1},... | collective-permute-start | bytes 1382408 | tf_op jit(solution)/shard_map/ppermute | solution.py:335
  9.0 8.3 %collective-permute-done.1.refs_2_ = bf16[72,3200]{1,0:T(8,128)(2,1)S(1)} collective-permute-done((bf16[72,3200]{1,0:T(8,128)(2,1)S(1)}, bf16[72,3200]{1,0:T(8,128)(2,1)S(1)}, u32[]{:S(2)}, u32[]{:S(2)}) %collective-permute-start.1) | collective-permute-done | bytes 460832 | tf_op jit(solution)/shard_map/ppermute | solution.py:335
  19.0 1.6 %collective-permute-start.3 = (bf16[72,3200]{1,0:T(8,128)(2,1)S(1)}, bf16[72,3200]{1,0:T(8,128)(2,1)S(1)}, u32[]{:S(2)}, u32[]{:S(2)}) collective-permute-start(bf16[72,3200]{1,0:T(8,128)(2,1)S(1)} %collective-permute-done.1.refs_2_), channel_id=1, source_target_pairs={{0,2},{4,0},{8,4},{12,8},{14,12},{10,14},{6,10},{2,6},{1,3},{5,1},... | collective-permute-start | bytes 1382408 | tf_op jit(solution)/shard_map/ppermute | solution.py:335
  20.7 3.7 %copy-done = bf16[768,6144]{1,0:T(8,128)(2,1)S(1)} copy-done((bf16[768,6144]{1,0:T(8,128)(2,1)S(1)}, bf16[768,6144]{1,0:T(8,128)(2,1)}, u32[]{:S(2)}) %copy-start) | copy-done | bytes 9437208
  26.1 3.1 %hidden_rows.4 = (bf16[3,40,768]{2,1,0:T(8,128)(2,1)S(1)}, bf16[3,40,768]{2,1,0:T(8,128)(2,1)S(1)}, bf16[3,40,64]{2,1,0:T(8,128)(2,1)S(1)}, f32[40,64]{1,0:T(8,1...) custom-call(bf16[72,3200]{1,0:T(8,128)(2,1)S(1)} %prepare.1.refs_0_, ...), custom_call_target="tpu_custom_call" | custom-call | flops 2264924160 | bytes 9437184 | tf_op jit(solution)/shard_map/hidden_rows/pallas_call | solution.py:319
  30.2 1.5 %collective-permute-start.4 = (bf16[72,3200]{1,0:T(8,128)(2,1)S(1)}, bf16[72,3200]{1,0:T(8,128)(2,1)S(1)}, u32[]{:S(2)}, u32[]{:S(2)}) collective-permute-start(bf16[72,3200]{1,0:T(8,128)(2,1)S(1)} %collective-permute-done.2.refs_0_), channel_id=1, source_target_pairs={{0,4},{4,8},{8,12},{12,14},{14,10},{10,6},{6,2},{2,0},{1,5},{5,9},... | collective-permute-start | bytes 1382408 | tf_op jit(solution)/shard_map/ppermute | solution.py:332
  32.2 3.1 %hidden_rows.5 = (bf16[2,40,768]{2,1,0:T(8,128)(2,1)S(1)}, bf16[2,40,768]{2,1,0:T(8,128)(2,1)S(1)}, bf16[2,40,64]{2,1,0:T(8,128)(2,1)S(1)}, f32[40,64]{1,0:T(8,128)S(1)}, f32[40,64]{1,0:T(8,128)S(1)}) custom-call(bf16[72,3200]{1,0:T(8,128)(2,1)S(1)} %collective-permute-done.2.refs_0_, bf16[72,3200]{1,0:T(8,128)(2,1)S(1)} %collective-permute-done.3.refs_1_, ...), custom_call_target="tpu_custom_call" | custom-call | flops 2415919104 | bytes 9437184 | tf_op jit(solution)/shard_map/hidden_rows/pallas_call | solution.py:319
  35.3 5.1 %collective-permute-done.4.refs_0_.right_in = bf16[72,3200]{1,0:T(8,128)(2,1)S(1)} collective-permute-done((bf16[72,3200]{1,0:T(8,128)(2,1)S(1)}, bf16[72,3200]{1,0:T(8,128)(2,1)S(1)}, u32[]{:S(2)}, u32[]{:S(2)}) %collective-permute-start.4) | collective-permute-done | bytes 460832 | tf_op jit(solution)/shard_map/ppermute | solution.py:332
  40.4 1.9 %collective-permute-done.5.refs_1_.left_in = bf16[72,3200]{1,0:T(8,128)(2,1)S(1)} collective-permute-done((bf16[72,3200]{1,0:T(8,128)(2,1)S(1)}, bf16[72,3200]{1,0:T(8,128)(2,1)S(1)}, u32[]{:S(2)}, u32[]{:S(2)}) %collective-permute-start.5) | collective-permute-done | bytes 460832 | tf_op jit(solution)/shard_map/ppermute | solution.py:335
  42.9 1.5 %collective-permute-start.6 = (bf16[32,3200]{1,0:T(8,128)(2,1)S(1)}, bf16[32,3200]{1,0:T(8,128)(2,1)S(1)}, u32[]{:S(2)}, u32[]{:S(2)}) collective-permute-start(bf16[32,3200]{1,0:T(8,128)(2,1)S(1)} %get-tuple-element.125), channel_id=1, source_target_pairs={{0,4},{4,8},{8,12},{12,14},{14,10},{10,6},{6,2},{2,0},{1,5},{5,9},... | collective-permute-start | bytes 614408 | tf_op jit(solution)/shard_map/ppermute | solution.py:332
  44.5 3.1 %hidden_rows.6 = (bf16[2,40,768]{2,1,0:T(8,128)(2,1)S(1)}, bf16[2,40,768]{2,1,0:T(8,128)(2,1)S(1)}, bf16[2,40,64]{2,1,0:T(8,128)(2,1)S(1)}, f32[40,64]{1,0:T(8,128)S(1)}, f32[40,64]{1,0:T(8,128)S(1)}) custom-call(bf16[72,3200]{1,0:T(8,128)(2,1)S(1)} %collective-permute-done.4.refs_0_.right_in, bf16[72,3200]{1,0:T(8,128)(2,1)S(1)} %collective-permute-done.5.refs_1_.left_in, ...), custom_call_target="tpu_custom_call" | custom-call | flops 2415919104 | bytes 9437184 | tf_op jit(solution)/shard_map/hidden_rows/pallas_call | solution.py:319
  48.7 2.9 %hidden_rows.7 = (bf16[1,40,768]{2,1,0:T(8,128)(2,1)S(1)}, bf16[1,40,768]{2,1,0:T(8,128)(2,1)S(1)}, bf16[1,40,64]{2,1,0:T(8,128)(2,1)S(1)}, f32[40,64]{1,0:T(8,128)S(1)}) custom-call(bf16[32,3200]{1,0:T(8,128)(2,1)S(1)} %collective-permute-done.6.refs_0_, bf16[40,3200]{1,0:T(8,128)(2,1)S(1)} %collective-permute-done.7.refs_1_, ...), custom_call_target="tpu_custom_call" | custom-call | flops 1207959552 | bytes 9437184 | tf_op jit(solution)/shard_map/hidden_rows/pallas_call | solution.py:319
  53.4 6.5 %partials.1 = (bf16[32,3072]{1,0:T(8,128)(2,1)S(1)}, bf16[40,3072]{1,0:T(8,128)(2,1)S(1)}, bf16[32,3072]{1,0:T(8,128)(2,1)S(1)}, bf16[40,3072]{1,0:T(8,128)(2,1)...) custom-call(bf16[3,40,768]{2,1,0:T(8,128)(2,1)S(1)} %get-tuple-eleme, ...), custom_call_target="tpu_custom_call" | custom-call | flops 6039797760 | bytes 18874368 | tf_op jit(solution)/shard_map/partials/pallas_call | solution.py:319
  65.3 1.9 %collective-permute-done.11.theirs = f32[2,40,64]{2,1,0:T(8,128)S(1)} collective-permute-done((f32[2,40,64]{2,1,0:T(8,128)S(1)}, f32[2,40,64]{2,1,0:T(8,128)S(1)}, u32[]{:S(2)}, u32[]{:S(2)}) %collective-permute-start.11) | collective-permute-done | bytes 20512 | tf_op jit(solution)/shard_map/ppermute | solution.py:431
  68.7 2.7 %collective-permute-done.10 = bf16[40,3072]{1,0:T(8,128)(2,1)S(1)} collective-permute-done((bf16[40,3072]{1,0:T(8,128)(2,1)S(1)}, bf16[40,3072]{1,0:T(8,128)(2,1)S(1)}, u32[]{:S(2)}, u32[]{:S(2)}) %collective-permute-start.10) | collective-permute-done | bytes 245792 | tf_op jit(solution)/shard_map/ppermute | solution.py:335
  71.4 3.2 %collective-permute-start.24 = (f32[1,40,64]{2,1,0:T(8,128)S(1)}, f32[1,40,64]{2,1,0:T(8,128)S(1)}, u32[]{:S(2)}, u32[]{:S(2)}) collective-permute-start(f32[1,40,64]{2,1,0:T(8,128)S(1)} %get-tuple-element.183), channel_id=1, source_target_pairs={{0,8},{2,10},{4,12},{6,14},{8,0},{10,2},{12,4},{14,6},{1,9},{3,11}... | collective-permute-start | bytes 30728 | tf_op jit(solution)/shard_map/ppermute | solution.py:431
  84.4 2.1 %collective-permute-start.20 = (bf16[40,3072]{1,0:T(8,128)(2,1)S(1)}, bf16[40,3072]{1,0:T(8,128)(2,1)S(1)}, u32[]{:S(2)}, u32[]{:S(2)}) collective-permute-start(bf16[40,3072]{1,0:T(8,128)(2,1)S(1)} %add_convert_fusion.3), channel_id=1, source_target_pairs={{0,4},{4,8},{8,12},{12,14},{14,10},{10,6},{6,2},{2,0},{1,5},{5,9},... | collective-permute-start | bytes 737288 | tf_op jit(solution)/shard_map/ppermute | solution.py:332
  86.4 7.8 %collective-permute-done.26.theirs = bf16[4,32,768]{2,1,0:T(8,128)(2,1)S(1)} collective-permute-done((bf16[4,32,768]{2,1,0:T(8,128)(2,1)S(1)}, bf16[4,32,768]{2,1,0:T(8,128)(2,1)S(1)}, u32[]{:S(2)}, u32[]{:S(2)}) %collective-permute-start.26) | collective-permute-done | bytes 196640 | tf_op jit(solution)/shard_map/ppermute | solution.py:431
  94.4 2.5 %collective-permute-start.23 = (bf16[40,3072]{1,0:T(8,128)(2,1)S(1)}, bf16[40,3072]{1,0:T(8,128)(2,1)S(1)}, u32[]{:S(2)}, u32[]{:S(2)}) collective-permute-start(bf16[40,3072]{1,0:T(8,128)(2,1)S(1)} %add_convert_fusion), channel_id=1, source_target_pairs={{0,2},{4,0},{8,4},{12,8},{14,12},{10,14},{6,10},{2,6},{1,3},{5,1},... | collective-permute-start | bytes 737288 | tf_op jit(solution)/shard_map/ppermute | solution.py:335
  97.0 3.1 %collective-permute-done.27.theirs = bf16[2,32,768]{2,1,0:T(8,128)(2,1)S(1)} collective-permute-done((bf16[2,32,768]{2,1,0:T(8,128)(2,1)S(1)}, bf16[2,32,768]{2,1,0:T(8,128)(2,1)S(1)}, u32[]{:S(2)}, u32[]{:S(2)}) %collective-permute-start.27) | collective-permute-done | bytes 98336 | tf_op jit(solution)/shard_map/ppermute | solution.py:431
  100.1 1.9 %collective-permute-start.28 = (bf16[1,32,768]{2,1,0:T(8,128)(2,1)S(1)}, bf16[1,32,768]{2,1,0:T(8,128)(2,1)S(1)}, u32[]{:S(2)}, u32[]{:S(2)}) collective-permute-start(bf16[1,32,768]{2,1,0:T(8,128)(2,1)S(1)} %get-tuple-element.192), channel_id=1, source_target_pairs={{0,8},{2,10},{4,12},{6,14},{8,0},{10,2},{12,4},{14,6},{1,9},{3,11}... | collective-permute-start | bytes 147464 | tf_op jit(solution)/shard_map/ppermute | solution.py:431
  103.8 2.0 %collective-permute-done.28.theirs = bf16[1,32,768]{2,1,0:T(8,128)(2,1)S(1)} collective-permute-done((bf16[1,32,768]{2,1,0:T(8,128)(2,1)S(1)}, bf16[1,32,768]{2,1,0:T(8,128)(2,1)S(1)}, u32[]{:S(2)}, u32[]{:S(2)}) %collective-permute-start.28) | collective-permute-done | bytes 49184 | tf_op jit(solution)/shard_map/ppermute | solution.py:431
  107.8 2.4 %finish.1 = bf16[128,6144]{1,0:T(8,128)(2,1)} custom-call(s32[4,128]{1,0:T(4,128)S(1)} %bitcast.20, bf16[32,3072]{1,0:T(8,128)(2,1)S(1)} %collective-permute-done.14.refs_0_, bf16[32,3072]{1,0:T(8,128)(2,1)S(1)} %collective-permute-done.17.refs_1_, bf16[32,3072]{1,0:T(8,128)(2,1)S(1)} %get-tuple-element.173.refs_2_, ...), custom_call_target="tpu_custom_call" | custom-call | flops 400000000 | bytes 4500000 | tf_op jit(solution)/shard_map/finish/pallas_call | solution.py:319
  (104 shorter events, 32.3 us)
Async XLA Ops:
  3.6 13.6 %collective-permute-start.1 = (bf16[72,3200]{1,0:T(8,128)(2,1)S(1)}, bf16[72,3200]{1,0:T(8,128)(2,1)S(1)}, u32[]{:S(2)}, u32[]{:S(2)}) collective-permute-start(bf16[72,3200]{1,0:T(8,128)(2,1)S(1)} %prepare.1.refs_0_), channel_id=1, source_target_pairs={{0,2},{4,0},{8,4},{12,8},{14,12},{10,14},{6,10},{2,6},{1,3},{5,1},... | collective-permute-start | bytes 1382408 | tf_op jit(solution)/shard_map/ppermute | solution.py:335
  6.6 12.0 %collective-permute-start = (bf16[72,3200]{1,0:T(8,128)(2,1)S(1)}, bf16[72,3200]{1,0:T(8,128)(2,1)S(1)}, u32[]{:S(2)}, u32[]{:S(2)}) collective-permute-start(bf16[72,3200]{1,0:T(8,128)(2,1)S(1)} %prepare.1.refs_0_), channel_id=1, source_target_pairs={{0,4},{4,8},{8,12},{12,14},{14,10},{10,6},{6,2},{2,0},{1,5},{5,9},... | collective-permute-start | bytes 1382408 | tf_op jit(solution)/shard_map/ppermute | solution.py:332
  18.6 11.1 %collective-permute-start.2 = (bf16[72,3200]{1,0:T(8,128)(2,1)S(1)}, bf16[72,3200]{1,0:T(8,128)(2,1)S(1)}, u32[]{:S(2)}, u32[]{:S(2)}) collective-permute-start(bf16[72,3200]{1,0:T(8,128)(2,1)S(1)} %collective-permute-done.refs_1_), channel_id=1, source_target_pairs={{0,4},{4,8},{8,12},{12,14},{14,10},{10,6},{6,2},{2,0},{1,5},{5,9},... | collective-permute-start | bytes 1382408 | tf_op jit(solution)/shard_map/ppermute | solution.py:332
  19.0 11.1 %collective-permute-start.3 = (bf16[72,3200]{1,0:T(8,128)(2,1)S(1)}, bf16[72,3200]{1,0:T(8,128)(2,1)S(1)}, u32[]{:S(2)}, u32[]{:S(2)}) collective-permute-start(bf16[72,3200]{1,0:T(8,128)(2,1)S(1)} %collective-permute-done.1.refs_2_), channel_id=1, source_target_pairs={{0,2},{4,0},{8,4},{12,8},{14,12},{10,14},{6,10},{2,6},{1,3},{5,1},... | collective-permute-start | bytes 1382408 | tf_op jit(solution)/shard_map/ppermute | solution.py:335
  30.2 10.2 %collective-permute-start.4 = (bf16[72,3200]{1,0:T(8,128)(2,1)S(1)}, bf16[72,3200]{1,0:T(8,128)(2,1)S(1)}, u32[]{:S(2)}, u32[]{:S(2)}) collective-permute-start(bf16[72,3200]{1,0:T(8,128)(2,1)S(1)} %collective-permute-done.2.refs_0_), channel_id=1, source_target_pairs={{0,4},{4,8},{8,12},{12,14},{14,10},{10,6},{6,2},{2,0},{1,5},{5,9},... | collective-permute-start | bytes 1382408 | tf_op jit(solution)/shard_map/ppermute | solution.py:332
  31.7 10.6 %collective-permute-start.5 = (bf16[72,3200]{1,0:T(8,128)(2,1)S(1)}, bf16[72,3200]{1,0:T(8,128)(2,1)S(1)}, u32[]{:S(2)}, u32[]{:S(2)}) collective-permute-start(bf16[72,3200]{1,0:T(8,128)(2,1)S(1)} %collective-permute-done.3.refs_1_), channel_id=1, source_target_pairs={{0,2},{4,0},{8,4},{12,8},{14,12},{10,14},{6,10},{2,6},{1,3},{5,1},... | collective-permute-start | bytes 1382408 | tf_op jit(solution)/shard_map/ppermute | solution.py:335
  42.4 6.4 %collective-permute-start.7 = (bf16[40,3200]{1,0:T(8,128)(2,1)S(1)}, bf16[40,3200]{1,0:T(8,128)(2,1)S(1)}, u32[]{:S(2)}, u32[]{:S(2)}) collective-permute-start(bf16[40,3200]{1,0:T(8,128)(2,1)S(1)} %get-tuple-element.126), channel_id=1, source_target_pairs={{0,2},{4,0},{8,4},{12,8},{14,12},{10,14},{6,10},{2,6},{1,3},{5,1},... | collective-permute-start | bytes 768008 | tf_op jit(solution)/shard_map/ppermute | solution.py:335
  52.1 7.8 %collective-permute-start.8 = (f32[4,40,64]{2,1,0:T(8,128)S(1)}, f32[4,40,64]{2,1,0:T(8,128)S(1)}, u32[]{:S(2)}, u32[]{:S(2)}) collective-permute-start(f32[4,40,64]{2,1,0:T(8,128)S(1)} %get-tuple-element.133), channel_id=1, source_target_pairs={{0,2},{2,0},{4,6},{6,4},{8,10},{10,8},{12,14},{14,12},{1,3},{3,1},... | collective-permute-start | bytes 122888 | tf_op jit(solution)/shard_map/ppermute | solution.py:431
  59.9 7.2 %collective-permute-start.15 = (bf16[32,3072]{1,0:T(8,128)(2,1)S(1)}, bf16[32,3072]{1,0:T(8,128)(2,1)S(1)}, u32[]{:S(2)}, u32[]{:S(2)}) collective-permute-start(bf16[32,3072]{1,0:T(8,128)(2,1)S(1)} %get-tuple-element.170), channel_id=1, source_target_pairs={{0,2},{4,0},{8,4},{12,8},{14,12},{10,14},{6,10},{2,6},{1,3},{5,1},... | collective-permute-start | bytes 589832 | tf_op jit(solution)/shard_map/ppermute | solution.py:335
  60.8 6.3 %collective-permute-start.11 = (f32[2,40,64]{2,1,0:T(8,128)S(1)}, f32[2,40,64]{2,1,0:T(8,128)S(1)}, u32[]{:S(2)}, u32[]{:S(2)}) collective-permute-start(f32[2,40,64]{2,1,0:T(8,128)S(1)} %get-tuple-element.163), channel_id=1, source_target_pairs={{0,4},{2,6},{4,0},{6,2},{8,12},{10,14},{12,8},{14,10},{1,5},{3,7},... | collective-permute-start | bytes 61448 | tf_op jit(solution)/shard_map/ppermute | solution.py:431
  62.0 6.7 %collective-permute-start.9 = (bf16[32,3072]{1,0:T(8,128)(2,1)S(1)}, bf16[32,3072]{1,0:T(8,128)(2,1)S(1)}, u32[]{:S(2)}, u32[]{:S(2)}) collective-permute-start(bf16[32,3072]{1,0:T(8,128)(2,1)S(1)} %get-tuple-element.160), channel_id=1, source_target_pairs={{0,4},{4,8},{8,12},{12,14},{14,10},{10,6},{6,2},{2,0},{1,5},{5,9},... | collective-permute-start | bytes 589832 | tf_op jit(solution)/shard_map/ppermute | solution.py:332
  62.9 8.5 %collective-permute-start.10 = (bf16[40,3072]{1,0:T(8,128)(2,1)S(1)}, bf16[40,3072]{1,0:T(8,128)(2,1)S(1)}, u32[]{:S(2)}, u32[]{:S(2)}) collective-permute-start(bf16[40,3072]{1,0:T(8,128)(2,1)S(1)} %get-tuple-element.161), channel_id=1, source_target_pairs={{0,2},{4,0},{8,4},{12,8},{14,12},{10,14},{6,10},{2,6},{1,3},{5,1},... | collective-permute-start | bytes 737288 | tf_op jit(solution)/shard_map/ppermute | solution.py:335
  64.0 12.8 %collective-permute-start.18 = (bf16[40,3072]{1,0:T(8,128)(2,1)S(1)}, bf16[40,3072]{1,0:T(8,128)(2,1)S(1)}, u32[]{:S(2)}, u32[]{:S(2)}) collective-permute-start(bf16[40,3072]{1,0:T(8,128)(2,1)S(1)} %get-tuple-element.174), channel_id=1, source_target_pairs={{0,4},{4,8},{8,12},{12,14},{14,10},{10,6},{6,2},{2,0},{1,5},{5,9},... | collective-permute-start | bytes 737288 | tf_op jit(solution)/shard_map/ppermute | solution.py:332
  67.2 11.6 %collective-permute-start.16 = (bf16[32,3072]{1,0:T(8,128)(2,1)S(1)}, bf16[32,3072]{1,0:T(8,128)(2,1)S(1)}, u32[]{:S(2)}, u32[]{:S(2)}) collective-permute-start(bf16[32,3072]{1,0:T(8,128)(2,1)S(1)} %add_convert_fusion.6), channel_id=1, source_target_pairs={{0,2},{4,0},{8,4},{12,8},{14,12},{10,14},{6,10},{2,6},{1,3},{5,1},... | collective-permute-start | bytes 589832 | tf_op jit(solution)/shard_map/ppermute | solution.py:335
  71.4 6.6 %collective-permute-start.24 = (f32[1,40,64]{2,1,0:T(8,128)S(1)}, f32[1,40,64]{2,1,0:T(8,128)S(1)}, u32[]{:S(2)}, u32[]{:S(2)}) collective-permute-start(f32[1,40,64]{2,1,0:T(8,128)S(1)} %get-tuple-element.183), channel_id=1, source_target_pairs={{0,8},{2,10},{4,12},{6,14},{8,0},{10,2},{12,4},{14,6},{1,9},{3,11}... | collective-permute-start | bytes 30728 | tf_op jit(solution)/shard_map/ppermute | solution.py:431
  75.8 6.2 %collective-permute-start.21 = (bf16[40,3072]{1,0:T(8,128)(2,1)S(1)}, bf16[40,3072]{1,0:T(8,128)(2,1)S(1)}, u32[]{:S(2)}, u32[]{:S(2)}) collective-permute-start(bf16[40,3072]{1,0:T(8,128)(2,1)S(1)} %add_convert_fusion.2), channel_id=1, source_target_pairs={{0,2},{4,0},{8,4},{12,8},{14,12},{10,14},{6,10},{2,6},{1,3},{5,1},... | collective-permute-start | bytes 737288 | tf_op jit(solution)/shard_map/ppermute | solution.py:335
  76.9 7.4 %collective-permute-start.19 = (bf16[40,3072]{1,0:T(8,128)(2,1)S(1)}, bf16[40,3072]{1,0:T(8,128)(2,1)S(1)}, u32[]{:S(2)}, u32[]{:S(2)}) collective-permute-start(bf16[40,3072]{1,0:T(8,128)(2,1)S(1)} %add_convert_fusion.4), channel_id=1, source_target_pairs={{0,4},{4,8},{8,12},{12,14},{14,10},{10,6},{6,2},{2,0},{1,5},{5,9},... | collective-permute-start | bytes 737288 | tf_op jit(solution)/shard_map/ppermute | solution.py:332
  78.9 26.9 %collective-permute-start.17 = (bf16[32,3072]{1,0:T(8,128)(2,1)S(1)}, bf16[32,3072]{1,0:T(8,128)(2,1)S(1)}, u32[]{:S(2)}, u32[]{:S(2)}) collective-permute-start(bf16[32,3072]{1,0:T(8,128)(2,1)S(1)} %add_convert_fusion.5), channel_id=1, source_target_pairs={{0,2},{4,0},{8,4},{12,8},{14,12},{10,14},{6,10},{2,6},{1,3},{5,1},... | collective-permute-start | bytes 589832 | tf_op jit(solution)/shard_map/ppermute | solution.py:335
  80.4 21.6 %collective-permute-start.13 = (bf16[32,3072]{1,0:T(8,128)(2,1)S(1)}, bf16[32,3072]{1,0:T(8,128)(2,1)S(1)}, u32[]{:S(2)}, u32[]{:S(2)}) collective-permute-start(bf16[32,3072]{1,0:T(8,128)(2,1)S(1)} %add_convert_fusion.8), channel_id=1, source_target_pairs={{0,4},{4,8},{8,12},{12,14},{14,10},{10,6},{6,2},{2,0},{1,5},{5,9},... | collective-permute-start | bytes 589832 | tf_op jit(solution)/shard_map/ppermute | solution.py:332
  82.1 12.3 %collective-permute-start.22 = (bf16[40,3072]{1,0:T(8,128)(2,1)S(1)}, bf16[40,3072]{1,0:T(8,128)(2,1)S(1)}, u32[]{:S(2)}, u32[]{:S(2)}) collective-permute-start(bf16[40,3072]{1,0:T(8,128)(2,1)S(1)} %add_convert_fusion.1), channel_id=1, source_target_pairs={{0,2},{4,0},{8,4},{12,8},{14,12},{10,14},{6,10},{2,6},{1,3},{5,1},... | collective-permute-start | bytes 737288 | tf_op jit(solution)/shard_map/ppermute | solution.py:335
  83.2 11.0 %collective-permute-start.26 = (bf16[4,32,768]{2,1,0:T(8,128)(2,1)S(1)}, bf16[4,32,768]{2,1,0:T(8,128)(2,1)S(1)}, u32[]{:S(2)}, u32[]{:S(2)}) collective-permute-start(bf16[4,32,768]{2,1,0:T(8,128)(2,1)S(1)} %get-tuple-element.188), channel_id=1, source_target_pairs={{0,2},{2,0},{4,6},{6,4},{8,10},{10,8},{12,14},{14,12},{1,3},{3,1},... | collective-permute-start | bytes 589832 | tf_op jit(solution)/shard_map/ppermute | solution.py:431
  84.4 22.0 %collective-permute-start.20 = (bf16[40,3072]{1,0:T(8,128)(2,1)S(1)}, bf16[40,3072]{1,0:T(8,128)(2,1)S(1)}, u32[]{:S(2)}, u32[]{:S(2)}) collective-permute-start(bf16[40,3072]{1,0:T(8,128)(2,1)S(1)} %add_convert_fusion.3), channel_id=1, source_target_pairs={{0,4},{4,8},{8,12},{12,14},{14,10},{10,6},{6,2},{2,0},{1,5},{5,9},... | collective-permute-start | bytes 737288 | tf_op jit(solution)/shard_map/ppermute | solution.py:332
  94.3 5.8 %collective-permute-start.27 = (bf16[2,32,768]{2,1,0:T(8,128)(2,1)S(1)}, bf16[2,32,768]{2,1,0:T(8,128)(2,1)S(1)}, u32[]{:S(2)}, u32[]{:S(2)}) collective-permute-start(bf16[2,32,768]{2,1,0:T(8,128)(2,1)S(1)} %get-tuple-element.190), channel_id=1, source_target_pairs={{0,4},{2,6},{4,0},{6,2},{8,12},{10,14},{12,8},{14,10},{1,5},{3,7},... | collective-permute-start | bytes 294920 | tf_op jit(solution)/shard_map/ppermute | solution.py:431
  94.4 13.3 %collective-permute-start.23 = (bf16[40,3072]{1,0:T(8,128)(2,1)S(1)}, bf16[40,3072]{1,0:T(8,128)(2,1)S(1)}, u32[]{:S(2)}, u32[]{:S(2)}) collective-permute-start(bf16[40,3072]{1,0:T(8,128)(2,1)S(1)} %add_convert_fusion), channel_id=1, source_target_pairs={{0,2},{4,0},{8,4},{12,8},{14,12},{10,14},{6,10},{2,6},{1,3},{5,1},... | collective-permute-start | bytes 737288 | tf_op jit(solution)/shard_map/ppermute | solution.py:335
  (24 other events, 282.6 us)

commit v11 on v10

--- a/solution.py
+++ b/solution.py
@@ -96,7 +96,8 @@
     return me, sum(jnp.where(me == e, p, 0) for e, p in enumerate(place))
 
 
-def reorder_kernel(place, capacity, gate_in, up_in, gate_out, up_out, tall):
+def reorder_kernel(place, capacity, gate_in, up_in, *refs):
+    gate_out, up_out, tall = refs[-3:]
     count, slot, hidden = gate_out.shape
     _, here = place_here(place)
     live = lax.broadcasted_iota(jnp.int32, (slot, hidden), 0) < capacity
@@ -350,16 +351,17 @@
         (4e8, 4.5e6),
         in_specs=[pl.BlockSpec(memory_space=pl.ANY)] * 5,
     )
+    down_here, gate_here, up_here = in_vmem(down_weight), in_vmem(gate_weight), in_vmem(up_weight)
+    gate_factor, up_factor = in_vmem(adapter_gate_factor), in_vmem(adapter_up_factor)
     gate_rows, up_rows = call(
         functools.partial(reorder_kernel, place, capacity),
         "reorder",
         [((n, slot, hidden), BF)] * 2,
-        [stored_gate_rows[0], stored_up_rows[0]],
+        [stored_gate_rows[0], stored_up_rows[0], down_here, gate_factor, up_factor],
         [pltpu.VMEM((n * capacity + slot, hidden), F32)],
         (0, 8 * n * slot * hidden),
     )
 
-    down_here, gate_here, up_here = in_vmem(down_weight), in_vmem(gate_weight), in_vmem(up_weight)
     dgates, dups, low_rows, lows = [], [], [], []
     got = {0: (block,)}
 
@@ -373,7 +375,7 @@
             + [((size, slot, rank), BF)]
             + [((slot, rank), F32)] * size,
             [piece for r in group for piece in got[r]]
-            + [gate_rows, up_rows, down_here, adapter_gate_factor, adapter_up_factor],
+            + [gate_rows, up_rows, down_here, gate_factor, up_factor],
             [pltpu.VMEM((size * tall, half), BF)],
             (2 * size * tall * width * hidden, 2 * hidden * width),
         )
@@ -434,22 +436,6 @@
         shape = (count // parts,) + keep.shape[1:]
         return call(halve_kernel, "halve", [(shape, keep.dtype)] * parts, [keep, other])
 
-    pair = exchange(low_keep, low_send, 1)
-    pair, own = lax.optimization_barrier((pair, own))
-    own = {r: (own[2 * i], own[2 * i + 1]) for i, r in enumerate(order)}
-    right_top, left_rest = right(own[middle][0]), left(own[middle][1])
-    right_rest, left_top = right(own[middle - 1][1]), left(own[1 - middle][0])
-    pair = exchange(*pair, 2)
-    right_top, left_rest, pair = lax.optimization_barrier((right_top, left_rest, pair))
-    for s in range(middle - 1, 0, -1):
-        right_top, left_rest = add(right_top, own[s][0]), add(left_rest, own[-s][1])
-        right_top, left_rest = right(right_top), left(left_rest)
-        if s > 1:
-            right_rest, left_top = add(right_rest, own[s - 1][1]), add(left_top, own[1 - s][0])
-            right_rest, left_top = right(right_rest), left(left_top)
-    bits = [1 << i for i in range(n.bit_length() - 1)]
-    for bit in bits[2:]:
-        pair = exchange(*pair, bit)
 
     share = width // n
     part = rank // 2
@@ -491,20 +477,37 @@
         )
         return local, lax.ppermute(local, "dp", swap)
 
+    bits = [1 << i for i in range(n.bit_length() - 1)]
+    pair = exchange(low_keep, low_send, bits[0])
+    pair, own = lax.optimization_barrier((pair, own))
+    own = {r: (own[2 * i], own[2 * i + 1]) for i, r in enumerate(order)}
+    right_top, left_rest = right(own[middle][0]), left(own[middle][1])
+    pair = exchange(*pair, bits[1])
+    right_rest, left_top, pair = lax.optimization_barrier((own[middle - 1][1], own[1 - middle][0], pair))
+    right_rest, left_top = right(right_rest), left(left_top)
+    for bit in bits[2:]:
+        pair = exchange(*pair, bit)
     low, pair = adapter_gradient(pair[0])
+    done = 0
+    for s in range(middle - 1, 0, -1):
+        right_top, left_rest = add(right_top, own[s][0]), add(left_rest, own[-s][1])
+        if s == middle - 2:
+            keep, right_top, left_rest = lax.optimization_barrier((pair[0], right_top, left_rest))
+            pair = exchange(keep, pair[1], bits[done])
+            done += 1
+        right_top, left_rest = right(right_top), left(left_rest)
+        if s > 1:
+            right_rest, left_top = add(right_rest, own[s - 1][1]), add(left_top, own[1 - s][0])
+            right_rest, left_top = right(right_rest), left(left_top)
+    keep, right_rest, left_top = lax.optimization_barrier((pair[0], right_rest, left_top))
+    pair = exchange(keep, pair[1], bits[done])
+    done += 1
     low_rows, _ = lax.optimization_barrier((low_rows, pair))
     lora, lora_there = lora_gradients()
-    for bit in bits:
+    for bit in bits[done:]:
         pair = exchange(*pair, bit)
     down = pair[0][0]
     there = lax.ppermute(down, "dp", swap)
-    grad_down, grad_gate, grad_up = call(
-        join_kernel,
-        "join",
-        [((rank, hidden), F32)] * 3,
-        [down, there, lora, lora_there],
-    )
-
     (input_gradient,) = call(
         functools.partial(finish_kernel, capacity),
         "finish",
@@ -512,6 +515,13 @@
         [choice, right_top, left_top, own[0][0], right_rest, left_rest, own[0][1], low, adapter_down_factor],
         [pltpu.VMEM((2 * capacity, rank), F32)],
         (4e8, 4.5e6),
+    )
+    there, input_gradient = lax.optimization_barrier((there, input_gradient))
+    grad_down, grad_gate, grad_up = call(
+        join_kernel,
+        "join",
+        [((rank, hidden), F32)] * 3,
+        [down, there, lora, lora_there],
     )
     return (input_gradient[None], grad_down, grad_gate, grad_up)
 

time: 111 us -> 115 us (1.036)
  waiting for transfers between devices: 39.2 us -> 42.4 us
    ppermute x6, waiting for transfers between devices: 14.7 us -> 9.87 us  [exchange(): other = lax.ppermute(send, 'expert', [(e, e ^ bit) for e in range(n)])]
    ppermute x11, waiting for transfers between devices: 13.9 us -> 18.5 us  [left(): return lax.ppermute(x, 'expert', to_left)]
    ppermute x11, waiting for transfers between devices: 10.6 us -> 14 us  [right(): return lax.ppermute(x, 'expert', to_right)]
    ppermute x11, starting transfers between devices: 12.4 us -> 14.4 us  [right(): return lax.ppermute(x, 'expert', to_right)]
    unnamed x34 -> x30, local copies, waits for them, and re-layouts: 7.54 us -> 7.53 us
  transfers between devices with their start and end apart: 31 -> 31, of which waited for: 16 -> 15; matrix products, arithmetic and copies ran while one was open for 1% -> 0% of each run, Pallas kernels for 18% -> 17%
where the time goes in v11:
time: 115 us; the launch traced here: 114 us
  waiting for transfers between devices  42.4 us (37%)
  starting transfers between devices  36.1 us (31%)
  Pallas kernels  26.7 us (23%)
  local copies, waits for them, and re-layouts  7.53 us (7%)
    pallas_call x20, Pallas kernels, call(): pl.pallas_call(kernel, out_shape=[jax.ShapeDtypeStruct(shape, dtype) for...  26.7 us
    ppermute x11, waiting for transfers between devices, left(): return lax.ppermute(x, 'expert', to_left)  18.5 us
    ppermute x11, starting transfers between devices, right(): return lax.ppermute(x, 'expert', to_right)  14.4 us
    ppermute x11, waiting for transfers between devices, right(): return lax.ppermute(x, 'expert', to_right)  14 us
    ppermute x11, starting transfers between devices, left(): return lax.ppermute(x, 'expert', to_left)  13.8 us
    ppermute x6, waiting for transfers between devices, exchange(): other = lax.ppermute(send, 'expert', [(e, e ^ bit) for e in range(n)])  9.87 us
    ppermute x6, starting transfers between devices, exchange(): other = lax.ppermute(send, 'expert', [(e, e ^ bit) for e in range(n)])  7.65 us
    unnamed x30, local copies, waits for them, and re-layouts  7.53 us
  transfers between devices with their start and end apart: 31, of which 15 were waited for; matrix products, arithmetic and copies ran while one was open for 0% of the time, Pallas kernels for 17%

profile of v11, /device:TPU:0, one launch (start us, length us, event | category | flops | bytes accessed | tf_op | source)
XLA Modules:
  0.0 114.2 jit_solution(1568490546672109261)
XLA Ops:
  0.6 2.9 %prepare.1.refs_0_ = bf16[72,3200]{1,0:T(8,128)(2,1)S(1)} custom-call(s32[4,128]{1,0:T(4,128)} %bitcast.18, bf16[4,128]{1,0:T(4,128)(2,1)} %bitcast.27, bf16[128,6144]{1,0:T(8,128)(2,1)} %bitcast.26, bf16[128,6144]{1,0:T(8,128)(2,1)} %bitcast.12, bf16[64,6144]{1,0:T(8,128)(2,1)} %refs_7_.3), custom_call_target="tpu_custom_call" | custom-call | flops 400000000 | bytes 4500000 | tf_op jit(solution)/shard_map/prepare/pallas_call | solution.py:320
  3.6 3.0 %collective-permute-start.1 = (bf16[72,3200]{1,0:T(8,128)(2,1)S(1)}, bf16[72,3200]{1,0:T(8,128)(2,1)S(1)}, u32[]{:S(2)}, u32[]{:S(2)}) collective-permute-start(bf16[72,3200]{1,0:T(8,128)(2,1)S(1)} %prepare.1.refs_0_), channel_id=1, source_target_pairs={{0,2},{4,0},{8,4},{12,8},{14,12},{10,14},{6,10},{2,6},{1,3},{5,1},... | collective-permute-start | bytes 1382408 | tf_op jit(solution)/shard_map/ppermute | solution.py:336
  6.7 3.7 %copy-done = bf16[768,6144]{1,0:T(8,128)(2,1)S(1)} copy-done((bf16[768,6144]{1,0:T(8,128)(2,1)S(1)}, bf16[768,6144]{1,0:T(8,128)(2,1)}, u32[]{:S(2)}) %copy-start) | copy-done | bytes 9437208
  14.4 2.8 %collective-permute-done.1.refs_2_ = bf16[72,3200]{1,0:T(8,128)(2,1)S(1)} collective-permute-done((bf16[72,3200]{1,0:T(8,128)(2,1)S(1)}, bf16[72,3200]{1,0:T(8,128)(2,1)S(1)}, u32[]{:S(2)}, u32[]{:S(2)}) %collective-permute-start.1) | collective-permute-done | bytes 460832 | tf_op jit(solution)/shard_map/ppermute | solution.py:336
  20.6 3.0 %hidden_rows.4 = (bf16[3,40,768]{2,1,0:T(8,128)(2,1)S(1)}, bf16[3,40,768]{2,1,0:T(8,128)(2,1)S(1)}, bf16[3,40,64]{2,1,0:T(8,128)(2,1)S(1)}, f32[40,64]{1,0:T(8,1...) custom-call(bf16[72,3200]{1,0:T(8,128)(2,1)S(1)} %prepare.1.refs_0_, ...), custom_call_target="tpu_custom_call" | custom-call | flops 2264924160 | bytes 9437184 | tf_op jit(solution)/shard_map/hidden_rows/pallas_call | solution.py:320
  23.7 6.0 %collective-permute-done.2.refs_0_ = bf16[72,3200]{1,0:T(8,128)(2,1)S(1)} collective-permute-done((bf16[72,3200]{1,0:T(8,128)(2,1)S(1)}, bf16[72,3200]{1,0:T(8,128)(2,1)S(1)}, u32[]{:S(2)}, u32[]{:S(2)}) %collective-permute-start.2) | collective-permute-done | bytes 460832 | tf_op jit(solution)/shard_map/ppermute | solution.py:333
  32.2 3.1 %hidden_rows.5 = (bf16[2,40,768]{2,1,0:T(8,128)(2,1)S(1)}, bf16[2,40,768]{2,1,0:T(8,128)(2,1)S(1)}, bf16[2,40,64]{2,1,0:T(8,128)(2,1)S(1)}, f32[40,64]{1,0:T(8,128)S(1)}, f32[40,64]{1,0:T(8,128)S(1)}) custom-call(bf16[72,3200]{1,0:T(8,128)(2,1)S(1)} %collective-permute-done.2.refs_0_, bf16[72,3200]{1,0:T(8,128)(2,1)S(1)} %collective-permute-done.3.refs_1_, ...), custom_call_target="tpu_custom_call" | custom-call | flops 2415919104 | bytes 9437184 | tf_op jit(solution)/shard_map/hidden_rows/pallas_call | solution.py:320
  35.3 5.1 %collective-permute-done.4.refs_0_.right_in = bf16[72,3200]{1,0:T(8,128)(2,1)S(1)} collective-permute-done((bf16[72,3200]{1,0:T(8,128)(2,1)S(1)}, bf16[72,3200]{1,0:T(8,128)(2,1)S(1)}, u32[]{:S(2)}, u32[]{:S(2)}) %collective-permute-start.4) | collective-permute-done | bytes 460832 | tf_op jit(solution)/shard_map/ppermute | solution.py:333
  44.4 3.1 %hidden_rows.6 = (bf16[2,40,768]{2,1,0:T(8,128)(2,1)S(1)}, bf16[2,40,768]{2,1,0:T(8,128)(2,1)S(1)}, bf16[2,40,64]{2,1,0:T(8,128)(2,1)S(1)}, f32[40,64]{1,0:T(8,128)S(1)}, f32[40,64]{1,0:T(8,128)S(1)}) custom-call(bf16[72,3200]{1,0:T(8,128)(2,1)S(1)} %collective-permute-done.4.refs_0_.right_in, bf16[72,3200]{1,0:T(8,128)(2,1)S(1)} %collective-permute-done.5.refs_1_.left_in, ...), custom_call_target="tpu_custom_call" | custom-call | flops 2415919104 | bytes 9437184 | tf_op jit(solution)/shard_map/hidden_rows/pallas_call | solution.py:320
  48.7 2.9 %hidden_rows.7 = (bf16[1,40,768]{2,1,0:T(8,128)(2,1)S(1)}, bf16[1,40,768]{2,1,0:T(8,128)(2,1)S(1)}, bf16[1,40,64]{2,1,0:T(8,128)(2,1)S(1)}, f32[40,64]{1,0:T(8,128)S(1)}) custom-call(bf16[32,3200]{1,0:T(8,128)(2,1)S(1)} %collective-permute-done.6.refs_0_, bf16[40,3200]{1,0:T(8,128)(2,1)S(1)} %collective-permute-done.7.refs_1_, ...), custom_call_target="tpu_custom_call" | custom-call | flops 1207959552 | bytes 9437184 | tf_op jit(solution)/shard_map/hidden_rows/pallas_call | solution.py:320
  53.3 6.5 %partials.1 = (bf16[32,3072]{1,0:T(8,128)(2,1)S(1)}, bf16[40,3072]{1,0:T(8,128)(2,1)S(1)}, bf16[32,3072]{1,0:T(8,128)(2,1)S(1)}, bf16[40,3072]{1,0:T(8,128)(2,1)...) custom-call(bf16[3,40,768]{2,1,0:T(8,128)(2,1)S(1)} %get-tuple-eleme, ...), custom_call_target="tpu_custom_call" | custom-call | flops 6039797760 | bytes 18874368 | tf_op jit(solution)/shard_map/partials/pallas_call | solution.py:320
  63.2 2.8 %collective-permute-done.9.theirs = f32[2,40,64]{2,1,0:T(8,128)S(1)} collective-permute-done((f32[2,40,64]{2,1,0:T(8,128)S(1)}, f32[2,40,64]{2,1,0:T(8,128)S(1)}, u32[]{:S(2)}, u32[]{:S(2)}) %collective-permute-start.9) | collective-permute-done | bytes 20512 | tf_op jit(solution)/shard_map/ppermute | solution.py:433
  66.0 3.8 %collective-permute-start.10 = (f32[1,40,64]{2,1,0:T(8,128)S(1)}, f32[1,40,64]{2,1,0:T(8,128)S(1)}, u32[]{:S(2)}, u32[]{:S(2)}) collective-permute-start(f32[1,40,64]{2,1,0:T(8,128)S(1)} %get-tuple-element.175), channel_id=1, source_target_pairs={{0,8},{2,10},{4,12},{6,14},{8,0},{10,2},{12,4},{14,6},{1,9},{3,11}... | collective-permute-start | bytes 30728 | tf_op jit(solution)/shard_map/ppermute | solution.py:433
  71.6 2.0 %collective-permute-start.17 = (bf16[40,3072]{1,0:T(8,128)(2,1)S(1)}, bf16[40,3072]{1,0:T(8,128)(2,1)S(1)}, u32[]{:S(2)}, u32[]{:S(2)}) collective-permute-start(bf16[40,3072]{1,0:T(8,128)(2,1)S(1)} %get-tuple-element.188), channel_id=1, source_target_pairs={{0,4},{4,8},{8,12},{12,14},{14,10},{10,6},{6,2},{2,0},{1,5},{5,9},... | collective-permute-start | bytes 737288 | tf_op jit(solution)/shard_map/ppermute | solution.py:333
  75.3 3.3 %collective-permute-done.20 = bf16[32,3072]{1,0:T(8,128)(2,1)S(1)} collective-permute-done((bf16[32,3072]{1,0:T(8,128)(2,1)S(1)}, bf16[32,3072]{1,0:T(8,128)(2,1)S(1)}, u32[]{:S(2)}, u32[]{:S(2)}) %collective-permute-start.20) | collective-permute-done | bytes 196640 | tf_op jit(solution)/shard_map/ppermute | solution.py:336
  82.9 3.4 %collective-permute-done.21 = bf16[32,3072]{1,0:T(8,128)(2,1)S(1)} collective-permute-done((bf16[32,3072]{1,0:T(8,128)(2,1)S(1)}, bf16[32,3072]{1,0:T(8,128)(2,1)S(1)}, u32[]{:S(2)}, u32[]{:S(2)}) %collective-permute-start.21) | collective-permute-done | bytes 196640 | tf_op jit(solution)/shard_map/ppermute | solution.py:336
  88.4 3.0 %collective-permute-done.15 = bf16[40,3072]{1,0:T(8,128)(2,1)S(1)} collective-permute-done((bf16[40,3072]{1,0:T(8,128)(2,1)S(1)}, bf16[40,3072]{1,0:T(8,128)(2,1)S(1)}, u32[]{:S(2)}, u32[]{:S(2)}) %collective-permute-start.15) | collective-permute-done | bytes 245792 | tf_op jit(solution)/shard_map/ppermute | solution.py:336
  91.5 2.4 %collective-permute-start.26 = (bf16[32,3072]{1,0:T(8,128)(2,1)S(1)}, bf16[32,3072]{1,0:T(8,128)(2,1)S(1)}, u32[]{:S(2)}, u32[]{:S(2)}) collective-permute-start(bf16[32,3072]{1,0:T(8,128)(2,1)S(1)} %add_convert_fusion.8), channel_id=1, source_target_pairs={{0,4},{4,8},{8,12},{12,14},{14,10},{10,6},{6,2},{2,0},{1,5},{5,9},... | collective-permute-start | bytes 589832 | tf_op jit(solution)/shard_map/ppermute | solution.py:333
  93.9 2.1 %collective-permute-start.19 = (bf16[40,3072]{1,0:T(8,128)(2,1)S(1)}, bf16[40,3072]{1,0:T(8,128)(2,1)S(1)}, u32[]{:S(2)}, u32[]{:S(2)}) collective-permute-start(bf16[40,3072]{1,0:T(8,128)(2,1)S(1)} %add_convert_fusion.1), channel_id=1, source_target_pairs={{0,4},{4,8},{8,12},{12,14},{14,10},{10,6},{6,2},{2,0},{1,5},{5,9},... | collective-permute-start | bytes 737288 | tf_op jit(solution)/shard_map/ppermute | solution.py:333
  96.0 2.0 %collective-permute-done.16.theirs = bf16[4,32,768]{2,1,0:T(8,128)(2,1)S(1)} collective-permute-done((bf16[4,32,768]{2,1,0:T(8,128)(2,1)S(1)}, bf16[4,32,768]{2,1,0:T(8,128)(2,1)S(1)}, u32[]{:S(2)}, u32[]{:S(2)}) %collective-permute-start.16) | collective-permute-done | bytes 196640 | tf_op jit(solution)/shard_map/ppermute | solution.py:433
  98.1 3.7 %collective-permute-done.28 = bf16[40,3072]{1,0:T(8,128)(2,1)S(1)} collective-permute-done((bf16[40,3072]{1,0:T(8,128)(2,1)S(1)}, bf16[40,3072]{1,0:T(8,128)(2,1)S(1)}, u32[]{:S(2)}, u32[]{:S(2)}) %collective-permute-start.28) | collective-permute-done | bytes 245792 | tf_op jit(solution)/shard_map/ppermute | solution.py:336
  101.8 2.5 %collective-permute-start.29 = (bf16[40,3072]{1,0:T(8,128)(2,1)S(1)}, bf16[40,3072]{1,0:T(8,128)(2,1)S(1)}, u32[]{:S(2)}, u32[]{:S(2)}) collective-permute-start(bf16[40,3072]{1,0:T(8,128)(2,1)S(1)} %add_convert_fusion), channel_id=1, source_target_pairs={{0,2},{4,0},{8,4},{12,8},{14,12},{10,14},{6,10},{2,6},{1,3},{5,1},... | collective-permute-start | bytes 737288 | tf_op jit(solution)/shard_map/ppermute | solution.py:336
  105.8 5.1 %collective-permute-done.24.theirs = bf16[1,32,768]{2,1,0:T(8,128)(2,1)S(1)} collective-permute-done((bf16[1,32,768]{2,1,0:T(8,128)(2,1)S(1)}, bf16[1,32,768]{2,1,0:T(8,128)(2,1)S(1)}, u32[]{:S(2)}, u32[]{:S(2)}) %collective-permute-start.24) | collective-permute-done | bytes 49184 | tf_op jit(solution)/shard_map/ppermute | solution.py:433
  111.0 2.4 %finish.1 = bf16[128,6144]{1,0:T(8,128)(2,1)} custom-call(s32[4,128]{1,0:T(4,128)S(1)} %bitcast.20, bf16[32,3072]{1,0:T(8,128)(2,1)S(1)} %collective-permute-done.27.refs_0_, bf16[32,3072]{1,0:T(8,128)(2,1)S(1)} %collective-permute-done.22.refs_1_, bf16[32,3072]{1,0:T(8,128)(2,1)S(1)} %get-tuple-element.201.refs_2_, ...), custom_call_target="tpu_custom_call" | custom-call | flops 400000000 | bytes 4500000 | tf_op jit(solution)/shard_map/finish/pallas_call | solution.py:320
  (100 shorter events, 32.8 us)
Async XLA Ops:
  3.6 13.6 %collective-permute-start.1 = (bf16[72,3200]{1,0:T(8,128)(2,1)S(1)}, bf16[72,3200]{1,0:T(8,128)(2,1)S(1)}, u32[]{:S(2)}, u32[]{:S(2)}) collective-permute-start(bf16[72,3200]{1,0:T(8,128)(2,1)S(1)} %prepare.1.refs_0_), channel_id=1, source_target_pairs={{0,2},{4,0},{8,4},{12,8},{14,12},{10,14},{6,10},{2,6},{1,3},{5,1},... | collective-permute-start | bytes 1382408 | tf_op jit(solution)/shard_map/ppermute | solution.py:336
  6.6 12.0 %collective-permute-start = (bf16[72,3200]{1,0:T(8,128)(2,1)S(1)}, bf16[72,3200]{1,0:T(8,128)(2,1)S(1)}, u32[]{:S(2)}, u32[]{:S(2)}) collective-permute-start(bf16[72,3200]{1,0:T(8,128)(2,1)S(1)} %prepare.1.refs_0_), channel_id=1, source_target_pairs={{0,4},{4,8},{8,12},{12,14},{14,10},{10,6},{6,2},{2,0},{1,5},{5,9},... | collective-permute-start | bytes 1382408 | tf_op jit(solution)/shard_map/ppermute | solution.py:333
  18.6 11.1 %collective-permute-start.2 = (bf16[72,3200]{1,0:T(8,128)(2,1)S(1)}, bf16[72,3200]{1,0:T(8,128)(2,1)S(1)}, u32[]{:S(2)}, u32[]{:S(2)}) collective-permute-start(bf16[72,3200]{1,0:T(8,128)(2,1)S(1)} %collective-permute-done.refs_1_), channel_id=1, source_target_pairs={{0,4},{4,8},{8,12},{12,14},{14,10},{10,6},{6,2},{2,0},{1,5},{5,9},... | collective-permute-start | bytes 1382408 | tf_op jit(solution)/shard_map/ppermute | solution.py:333
  19.0 11.2 %collective-permute-start.3 = (bf16[72,3200]{1,0:T(8,128)(2,1)S(1)}, bf16[72,3200]{1,0:T(8,128)(2,1)S(1)}, u32[]{:S(2)}, u32[]{:S(2)}) collective-permute-start(bf16[72,3200]{1,0:T(8,128)(2,1)S(1)} %collective-permute-done.1.refs_2_), channel_id=1, source_target_pairs={{0,2},{4,0},{8,4},{12,8},{14,12},{10,14},{6,10},{2,6},{1,3},{5,1},... | collective-permute-start | bytes 1382408 | tf_op jit(solution)/shard_map/ppermute | solution.py:336
  30.2 10.2 %collective-permute-start.4 = (bf16[72,3200]{1,0:T(8,128)(2,1)S(1)}, bf16[72,3200]{1,0:T(8,128)(2,1)S(1)}, u32[]{:S(2)}, u32[]{:S(2)}) collective-permute-start(bf16[72,3200]{1,0:T(8,128)(2,1)S(1)} %collective-permute-done.2.refs_0_), channel_id=1, source_target_pairs={{0,4},{4,8},{8,12},{12,14},{14,10},{10,6},{6,2},{2,0},{1,5},{5,9},... | collective-permute-start | bytes 1382408 | tf_op jit(solution)/shard_map/ppermute | solution.py:333
  31.7 10.6 %collective-permute-start.5 = (bf16[72,3200]{1,0:T(8,128)(2,1)S(1)}, bf16[72,3200]{1,0:T(8,128)(2,1)S(1)}, u32[]{:S(2)}, u32[]{:S(2)}) collective-permute-start(bf16[72,3200]{1,0:T(8,128)(2,1)S(1)} %collective-permute-done.3.refs_1_), channel_id=1, source_target_pairs={{0,2},{4,0},{8,4},{12,8},{14,12},{10,14},{6,10},{2,6},{1,3},{5,1},... | collective-permute-start | bytes 1382408 | tf_op jit(solution)/shard_map/ppermute | solution.py:336
  52.0 7.8 %collective-permute-start.8 = (f32[4,40,64]{2,1,0:T(8,128)S(1)}, f32[4,40,64]{2,1,0:T(8,128)S(1)}, u32[]{:S(2)}, u32[]{:S(2)}) collective-permute-start(f32[4,40,64]{2,1,0:T(8,128)S(1)} %get-tuple-element.141), channel_id=1, source_target_pairs={{0,2},{2,0},{4,6},{6,4},{8,10},{10,8},{12,14},{14,12},{1,3},{3,1},... | collective-permute-start | bytes 122888 | tf_op jit(solution)/shard_map/ppermute | solution.py:433
  59.9 14.6 %collective-permute-start.12 = (bf16[32,3072]{1,0:T(8,128)(2,1)S(1)}, bf16[32,3072]{1,0:T(8,128)(2,1)S(1)}, u32[]{:S(2)}, u32[]{:S(2)}) collective-permute-start(bf16[32,3072]{1,0:T(8,128)(2,1)S(1)} %get-tuple-element.179), channel_id=1, source_target_pairs={{0,4},{4,8},{8,12},{12,14},{14,10},{10,6},{6,2},{2,0},{1,5},{5,9},... | collective-permute-start | bytes 589832 | tf_op jit(solution)/shard_map/ppermute | solution.py:333
  66.0 7.6 %collective-permute-start.10 = (f32[1,40,64]{2,1,0:T(8,128)S(1)}, f32[1,40,64]{2,1,0:T(8,128)S(1)}, u32[]{:S(2)}, u32[]{:S(2)}) collective-permute-start(f32[1,40,64]{2,1,0:T(8,128)S(1)} %get-tuple-element.175), channel_id=1, source_target_pairs={{0,8},{2,10},{4,12},{6,14},{8,0},{10,2},{12,4},{14,6},{1,9},{3,11}... | collective-permute-start | bytes 30728 | tf_op jit(solution)/shard_map/ppermute | solution.py:433
  69.8 10.5 %collective-permute-start.14 = (bf16[40,3072]{1,0:T(8,128)(2,1)S(1)}, bf16[40,3072]{1,0:T(8,128)(2,1)S(1)}, u32[]{:S(2)}, u32[]{:S(2)}) collective-permute-start(bf16[40,3072]{1,0:T(8,128)(2,1)S(1)} %get-tuple-element.182), channel_id=1, source_target_pairs={{0,2},{4,0},{8,4},{12,8},{14,12},{10,14},{6,10},{2,6},{1,3},{5,1},... | collective-permute-start | bytes 737288 | tf_op jit(solution)/shard_map/ppermute | solution.py:336
  71.6 7.1 %collective-permute-start.20 = (bf16[32,3072]{1,0:T(8,128)(2,1)S(1)}, bf16[32,3072]{1,0:T(8,128)(2,1)S(1)}, u32[]{:S(2)}, u32[]{:S(2)}) collective-permute-start(bf16[32,3072]{1,0:T(8,128)(2,1)S(1)} %get-tuple-element.191), channel_id=1, source_target_pairs={{0,2},{4,0},{8,4},{12,8},{14,12},{10,14},{6,10},{2,6},{1,3},{5,1},... | collective-permute-start | bytes 589832 | tf_op jit(solution)/shard_map/ppermute | solution.py:336
  71.6 9.0 %collective-permute-start.17 = (bf16[40,3072]{1,0:T(8,128)(2,1)S(1)}, bf16[40,3072]{1,0:T(8,128)(2,1)S(1)}, u32[]{:S(2)}, u32[]{:S(2)}) collective-permute-start(bf16[40,3072]{1,0:T(8,128)(2,1)S(1)} %get-tuple-element.188), channel_id=1, source_target_pairs={{0,4},{4,8},{8,12},{12,14},{14,10},{10,6},{6,2},{2,0},{1,5},{5,9},... | collective-permute-start | bytes 737288 | tf_op jit(solution)/shard_map/ppermute | solution.py:333
  74.4 13.9 %collective-permute-start.11 = (bf16[8,32,768]{2,1,0:T(8,128)(2,1)S(1)}, bf16[8,32,768]{2,1,0:T(8,128)(2,1)S(1)}, u32[]{:S(2)}, u32[]{:S(2)}) collective-permute-start(bf16[8,32,768]{2,1,0:T(8,128)(2,1)S(1)} %get-tuple-element.177), channel_id=1, source_target_pairs={{0,1},{1,0},{2,3},{3,2},{4,5},{5,4},{6,7},{7,6},{8,9},{9,8},{10,11... | collective-permute-start | bytes 1179656 | tf_op jit(solution)/shard_map/ppermute | solution.py:462
  74.5 8.4 %collective-permute-start.13 = (bf16[32,3072]{1,0:T(8,128)(2,1)S(1)}, bf16[32,3072]{1,0:T(8,128)(2,1)S(1)}, u32[]{:S(2)}, u32[]{:S(2)}) collective-permute-start(bf16[32,3072]{1,0:T(8,128)(2,1)S(1)} %add_convert_fusion.9), channel_id=1, source_target_pairs={{0,4},{4,8},{8,12},{12,14},{14,10},{10,6},{6,2},{2,0},{1,5},{5,9},... | collective-permute-start | bytes 589832 | tf_op jit(solution)/shard_map/ppermute | solution.py:333
  78.7 7.6 %collective-permute-start.21 = (bf16[32,3072]{1,0:T(8,128)(2,1)S(1)}, bf16[32,3072]{1,0:T(8,128)(2,1)S(1)}, u32[]{:S(2)}, u32[]{:S(2)}) collective-permute-start(bf16[32,3072]{1,0:T(8,128)(2,1)S(1)} %add_convert_fusion.7), channel_id=1, source_target_pairs={{0,2},{4,0},{8,4},{12,8},{14,12},{10,14},{6,10},{2,6},{1,3},{5,1},... | collective-permute-start | bytes 589832 | tf_op jit(solution)/shard_map/ppermute | solution.py:336
  80.4 11.0 %collective-permute-start.15 = (bf16[40,3072]{1,0:T(8,128)(2,1)S(1)}, bf16[40,3072]{1,0:T(8,128)(2,1)S(1)}, u32[]{:S(2)}, u32[]{:S(2)}) collective-permute-start(bf16[40,3072]{1,0:T(8,128)(2,1)S(1)} %add_convert_fusion.4), channel_id=1, source_target_pairs={{0,2},{4,0},{8,4},{12,8},{14,12},{10,14},{6,10},{2,6},{1,3},{5,1},... | collective-permute-start | bytes 737288 | tf_op jit(solution)/shard_map/ppermute | solution.py:336
  80.6 13.2 %collective-permute-start.18 = (bf16[40,3072]{1,0:T(8,128)(2,1)S(1)}, bf16[40,3072]{1,0:T(8,128)(2,1)S(1)}, u32[]{:S(2)}, u32[]{:S(2)}) collective-permute-start(bf16[40,3072]{1,0:T(8,128)(2,1)S(1)} %add_convert_fusion.2), channel_id=1, source_target_pairs={{0,4},{4,8},{8,12},{12,14},{14,10},{10,6},{6,2},{2,0},{1,5},{5,9},... | collective-permute-start | bytes 737288 | tf_op jit(solution)/shard_map/ppermute | solution.py:333
  86.3 18.1 %collective-permute-start.22 = (bf16[32,3072]{1,0:T(8,128)(2,1)S(1)}, bf16[32,3072]{1,0:T(8,128)(2,1)S(1)}, u32[]{:S(2)}, u32[]{:S(2)}) collective-permute-start(bf16[32,3072]{1,0:T(8,128)(2,1)S(1)} %add_convert_fusion.6), channel_id=1, source_target_pairs={{0,2},{4,0},{8,4},{12,8},{14,12},{10,14},{6,10},{2,6},{1,3},{5,1},... | collective-permute-start | bytes 589832 | tf_op jit(solution)/shard_map/ppermute | solution.py:336
  88.3 9.6 %collective-permute-start.16 = (bf16[4,32,768]{2,1,0:T(8,128)(2,1)S(1)}, bf16[4,32,768]{2,1,0:T(8,128)(2,1)S(1)}, u32[]{:S(2)}, u32[]{:S(2)}) collective-permute-start(bf16[4,32,768]{2,1,0:T(8,128)(2,1)S(1)} %get-tuple-element.186), channel_id=1, source_target_pairs={{0,2},{2,0},{4,6},{6,4},{8,10},{10,8},{12,14},{14,12},{1,3},{3,1},... | collective-permute-start | bytes 589832 | tf_op jit(solution)/shard_map/ppermute | solution.py:433
  91.5 12.9 %collective-permute-start.26 = (bf16[32,3072]{1,0:T(8,128)(2,1)S(1)}, bf16[32,3072]{1,0:T(8,128)(2,1)S(1)}, u32[]{:S(2)}, u32[]{:S(2)}) collective-permute-start(bf16[32,3072]{1,0:T(8,128)(2,1)S(1)} %add_convert_fusion.8), channel_id=1, source_target_pairs={{0,4},{4,8},{8,12},{12,14},{14,10},{10,6},{6,2},{2,0},{1,5},{5,9},... | collective-permute-start | bytes 589832 | tf_op jit(solution)/shard_map/ppermute | solution.py:333
  93.8 7.9 %collective-permute-start.28 = (bf16[40,3072]{1,0:T(8,128)(2,1)S(1)}, bf16[40,3072]{1,0:T(8,128)(2,1)S(1)}, u32[]{:S(2)}, u32[]{:S(2)}) collective-permute-start(bf16[40,3072]{1,0:T(8,128)(2,1)S(1)} %add_convert_fusion.3), channel_id=1, source_target_pairs={{0,2},{4,0},{8,4},{12,8},{14,12},{10,14},{6,10},{2,6},{1,3},{5,1},... | collective-permute-start | bytes 737288 | tf_op jit(solution)/shard_map/ppermute | solution.py:336
  93.9 10.6 %collective-permute-start.19 = (bf16[40,3072]{1,0:T(8,128)(2,1)S(1)}, bf16[40,3072]{1,0:T(8,128)(2,1)S(1)}, u32[]{:S(2)}, u32[]{:S(2)}) collective-permute-start(bf16[40,3072]{1,0:T(8,128)(2,1)S(1)} %add_convert_fusion.1), channel_id=1, source_target_pairs={{0,4},{4,8},{8,12},{12,14},{14,10},{10,6},{6,2},{2,0},{1,5},{5,9},... | collective-permute-start | bytes 737288 | tf_op jit(solution)/shard_map/ppermute | solution.py:333
  101.8 9.2 %collective-permute-start.29 = (bf16[40,3072]{1,0:T(8,128)(2,1)S(1)}, bf16[40,3072]{1,0:T(8,128)(2,1)S(1)}, u32[]{:S(2)}, u32[]{:S(2)}) collective-permute-start(bf16[40,3072]{1,0:T(8,128)(2,1)S(1)} %add_convert_fusion), channel_id=1, source_target_pairs={{0,2},{4,0},{8,4},{12,8},{14,12},{10,14},{6,10},{2,6},{1,3},{5,1},... | collective-permute-start | bytes 737288 | tf_op jit(solution)/shard_map/ppermute | solution.py:336
  104.9 8.5 %collective-permute-start.30 = (bf16[128,768]{1,0:T(8,128)(2,1)S(1)}, bf16[128,768]{1,0:T(8,128)(2,1)S(1)}, u32[]{:S(2)}, u32[]{:S(2)}) collective-permute-start(bf16[128,768]{1,0:T(8,128)(2,1)S(1)} %lora_rows.1.lora_ref), channel_id=1, source_target_pairs={{0,1},{1,0},{2,3},{3,2},{4,5},{5,4},{6,7},{7,6},{8,9},{9,8},{10,11... | collective-permute-start | bytes 589832 | tf_op jit(solution)/shard_map/ppermute | solution.py:478
  (22 other events, 235.1 us)

commit v12 on v11

--- a/solution.py
+++ b/solution.py
@@ -96,8 +96,7 @@
     return me, sum(jnp.where(me == e, p, 0) for e, p in enumerate(place))
 
 
-def reorder_kernel(place, capacity, gate_in, up_in, *refs):
-    gate_out, up_out, tall = refs[-3:]
+def reorder_kernel(place, capacity, gate_in, up_in, gate_out, up_out, tall):
     count, slot, hidden = gate_out.shape
     _, here = place_here(place)
     live = lax.broadcasted_iota(jnp.int32, (slot, hidden), 0) < capacity
@@ -351,17 +350,16 @@
         (4e8, 4.5e6),
         in_specs=[pl.BlockSpec(memory_space=pl.ANY)] * 5,
     )
-    down_here, gate_here, up_here = in_vmem(down_weight), in_vmem(gate_weight), in_vmem(up_weight)
-    gate_factor, up_factor = in_vmem(adapter_gate_factor), in_vmem(adapter_up_factor)
     gate_rows, up_rows = call(
         functools.partial(reorder_kernel, place, capacity),
         "reorder",
         [((n, slot, hidden), BF)] * 2,
-        [stored_gate_rows[0], stored_up_rows[0], down_here, gate_factor, up_factor],
+        [stored_gate_rows[0], stored_up_rows[0]],
         [pltpu.VMEM((n * capacity + slot, hidden), F32)],
         (0, 8 * n * slot * hidden),
     )
 
+    down_here, gate_here, up_here = in_vmem(down_weight), in_vmem(gate_weight), in_vmem(up_weight)
     dgates, dups, low_rows, lows = [], [], [], []
     got = {0: (block,)}
 
@@ -375,7 +373,7 @@
             + [((size, slot, rank), BF)]
             + [((slot, rank), F32)] * size,
             [piece for r in group for piece in got[r]]
-            + [gate_rows, up_rows, down_here, gate_factor, up_factor],
+            + [gate_rows, up_rows, down_here, adapter_gate_factor, adapter_up_factor],
             [pltpu.VMEM((size * tall, half), BF)],
             (2 * size * tall * width * hidden, 2 * hidden * width),
         )
@@ -436,6 +434,11 @@
         shape = (count // parts,) + keep.shape[1:]
         return call(halve_kernel, "halve", [(shape, keep.dtype)] * parts, [keep, other])
 
+    pair = exchange(low_keep, low_send, 1)
+    pair, own = lax.optimization_barrier((pair, own))
+    own = {r: (own[2 * i], own[2 * i + 1]) for i, r in enumerate(order)}
+    right_top, left_rest = right(own[middle][0]), left(own[middle][1])
+    right_rest, left_top = right(own[middle - 1][1]), left(own[1 - middle][0])
 
     share = width // n
     part = rank // 2
@@ -478,33 +481,27 @@
         return local, lax.ppermute(local, "dp", swap)
 
     bits = [1 << i for i in range(n.bit_length() - 1)]
-    pair = exchange(low_keep, low_send, bits[0])
-    pair, own = lax.optimization_barrier((pair, own))
-    own = {r: (own[2 * i], own[2 * i + 1]) for i, r in enumerate(order)}
-    right_top, left_rest = right(own[middle][0]), left(own[middle][1])
-    pair = exchange(*pair, bits[1])
-    right_rest, left_top, pair = lax.optimization_barrier((own[middle - 1][1], own[1 - middle][0], pair))
-    right_rest, left_top = right(right_rest), left(left_top)
+    keep, right_rest = lax.optimization_barrier((pair[0], right_rest))
+    pair = exchange(keep, pair[1], bits[1])
+    keep, right_top, left_rest = lax.optimization_barrier((pair[0], right_top, left_rest))
     for bit in bits[2:]:
-        pair = exchange(*pair, bit)
-    low, pair = adapter_gradient(pair[0])
-    done = 0
+        pair = exchange(keep, pair[1], bit)
+        keep = pair[0]
+    low, pair = adapter_gradient(keep)
     for s in range(middle - 1, 0, -1):
         right_top, left_rest = add(right_top, own[s][0]), add(left_rest, own[-s][1])
-        if s == middle - 2:
+        if s == 1:
             keep, right_top, left_rest = lax.optimization_barrier((pair[0], right_top, left_rest))
-            pair = exchange(keep, pair[1], bits[done])
-            done += 1
+            pair = exchange(keep, pair[1], bits[0])
         right_top, left_rest = right(right_top), left(left_rest)
         if s > 1:
             right_rest, left_top = add(right_rest, own[s - 1][1]), add(left_top, own[1 - s][0])
             right_rest, left_top = right(right_rest), left(left_top)
     keep, right_rest, left_top = lax.optimization_barrier((pair[0], right_rest, left_top))
-    pair = exchange(keep, pair[1], bits[done])
-    done += 1
+    pair = exchange(keep, pair[1], bits[1])
     low_rows, _ = lax.optimization_barrier((low_rows, pair))
     lora, lora_there = lora_gradients()
-    for bit in bits[done:]:
+    for bit in bits[2:]:
         pair = exchange(*pair, bit)
     down = pair[0][0]
     there = lax.ppermute(down, "dp", swap)

time: 115 us -> 114 us (level)
  starting transfers between devices: 36.1 us -> 30.5 us
  waiting for transfers between devices: 42.4 us -> 47.5 us
    ppermute x11, waiting for transfers between devices: 14 us -> 21 us  [right(): return lax.ppermute(x, 'expert', to_right)]
    ppermute x11, waiting for transfers between devices: 18.5 us -> 13.6 us  [left(): return lax.ppermute(x, 'expert', to_left)]
    ppermute x11, starting transfers between devices: 14.4 us -> 9.82 us  [right(): return lax.ppermute(x, 'expert', to_right)]
    ppermute x6, waiting for transfers between devices: 9.87 us -> 12.9 us  [exchange(): other = lax.ppermute(send, 'expert', [(e, e ^ bit) for e in range(n)])]
    unnamed x30 -> x34, local copies, waits for them, and re-layouts: 7.53 us -> 7.54 us
  transfers between devices with their start and end apart: 31 -> 31, of which waited for: 15 -> 15; matrix products, arithmetic and copies ran while one was open for 0% -> 1% of each run, Pallas kernels for 17% -> 17%
where the time goes in v12:
time: 114 us
  waiting for transfers between devices  47.5 us (42%)
  starting transfers between devices  30.5 us (27%)
  Pallas kernels  26.8 us (24%)
  local copies, waits for them, and re-layouts  7.54 us (7%)
    pallas_call x20, Pallas kernels, call(): pl.pallas_call(kernel, out_shape=[jax.ShapeDtypeStruct(shape, dtype) for...  26.8 us
    ppermute x11, waiting for transfers between devices, right(): return lax.ppermute(x, 'expert', to_right)  21 us
    ppermute x11, waiting for transfers between devices, left(): return lax.ppermute(x, 'expert', to_left)  13.6 us
    ppermute x6, waiting for transfers between devices, exchange(): other = lax.ppermute(send, 'expert', [(e, e ^ bit) for e in range(n)])  12.9 us
    ppermute x11, starting transfers between devices, left(): return lax.ppermute(x, 'expert', to_left)  12.9 us
    ppermute x11, starting transfers between devices, right(): return lax.ppermute(x, 'expert', to_right)  9.82 us
    unnamed x34, local copies, waits for them, and re-layouts  7.54 us
    ppermute x6, starting transfers between devices, exchange(): other = lax.ppermute(send, 'expert', [(e, e ^ bit) for e in range(n)])  7.53 us
  transfers between devices with their start and end apart: 31, of which 15 were waited for; matrix products, arithmetic and copies ran while one was open for 1% of the time, Pallas kernels for 17%

profile of v12, /device:TPU:0, one launch (start us, length us, event | category | flops | bytes accessed | tf_op | source)
XLA Modules:
  0.0 113.9 jit_solution(8374356601414628339)
XLA Ops:
  0.6 2.9 %prepare.1.refs_0_ = bf16[72,3200]{1,0:T(8,128)(2,1)S(1)} custom-call(s32[4,128]{1,0:T(4,128)} %bitcast.18, bf16[4,128]{1,0:T(4,128)(2,1)} %bitcast.27, bf16[128,6144]{1,0:T(8,128)(2,1)} %bitcast.26, bf16[128,6144]{1,0:T(8,128)(2,1)} %bitcast.12, bf16[64,6144]{1,0:T(8,128)(2,1)} %refs_7_.3), custom_call_target="tpu_custom_call" | custom-call | flops 400000000 | bytes 4500000 | tf_op jit(solution)/shard_map/prepare/pallas_call | solution.py:319
  3.6 3.0 %collective-permute-start.1 = (bf16[72,3200]{1,0:T(8,128)(2,1)S(1)}, bf16[72,3200]{1,0:T(8,128)(2,1)S(1)}, u32[]{:S(2)}, u32[]{:S(2)}) collective-permute-start(bf16[72,3200]{1,0:T(8,128)(2,1)S(1)} %prepare.1.refs_0_), channel_id=1, source_target_pairs={{0,2},{4,0},{8,4},{12,8},{14,12},{10,14},{6,10},{2,6},{1,3},{5,1},... | collective-permute-start | bytes 1382408 | tf_op jit(solution)/shard_map/ppermute | solution.py:335
  9.0 8.3 %collective-permute-done.1.refs_2_ = bf16[72,3200]{1,0:T(8,128)(2,1)S(1)} collective-permute-done((bf16[72,3200]{1,0:T(8,128)(2,1)S(1)}, bf16[72,3200]{1,0:T(8,128)(2,1)S(1)}, u32[]{:S(2)}, u32[]{:S(2)}) %collective-permute-start.1) | collective-permute-done | bytes 460832 | tf_op jit(solution)/shard_map/ppermute | solution.py:335
  19.0 1.6 %collective-permute-start.3 = (bf16[72,3200]{1,0:T(8,128)(2,1)S(1)}, bf16[72,3200]{1,0:T(8,128)(2,1)S(1)}, u32[]{:S(2)}, u32[]{:S(2)}) collective-permute-start(bf16[72,3200]{1,0:T(8,128)(2,1)S(1)} %collective-permute-done.1.refs_2_), channel_id=1, source_target_pairs={{0,2},{4,0},{8,4},{12,8},{14,12},{10,14},{6,10},{2,6},{1,3},{5,1},... | collective-permute-start | bytes 1382408 | tf_op jit(solution)/shard_map/ppermute | solution.py:335
  20.7 3.7 %copy-done = bf16[768,6144]{1,0:T(8,128)(2,1)S(1)} copy-done((bf16[768,6144]{1,0:T(8,128)(2,1)S(1)}, bf16[768,6144]{1,0:T(8,128)(2,1)}, u32[]{:S(2)}) %copy-start) | copy-done | bytes 9437208
  26.1 3.1 %hidden_rows.4 = (bf16[3,40,768]{2,1,0:T(8,128)(2,1)S(1)}, bf16[3,40,768]{2,1,0:T(8,128)(2,1)S(1)}, bf16[3,40,64]{2,1,0:T(8,128)(2,1)S(1)}, f32[40,64]{1,0:T(8,1...) custom-call(bf16[72,3200]{1,0:T(8,128)(2,1)S(1)} %prepare.1.refs_0_, ...), custom_call_target="tpu_custom_call" | custom-call | flops 2264924160 | bytes 9437184 | tf_op jit(solution)/shard_map/hidden_rows/pallas_call | solution.py:319
  32.2 3.1 %hidden_rows.5 = (bf16[2,40,768]{2,1,0:T(8,128)(2,1)S(1)}, bf16[2,40,768]{2,1,0:T(8,128)(2,1)S(1)}, bf16[2,40,64]{2,1,0:T(8,128)(2,1)S(1)}, f32[40,64]{1,0:T(8,128)S(1)}, f32[40,64]{1,0:T(8,128)S(1)}) custom-call(bf16[72,3200]{1,0:T(8,128)(2,1)S(1)} %collective-permute-done.2.refs_0_, bf16[72,3200]{1,0:T(8,128)(2,1)S(1)} %collective-permute-done.3.refs_1_, ...), custom_call_target="tpu_custom_call" | custom-call | flops 2415919104 | bytes 9437184 | tf_op jit(solution)/shard_map/hidden_rows/pallas_call | solution.py:319
  35.3 5.1 %collective-permute-done.4.refs_0_.right_in = bf16[72,3200]{1,0:T(8,128)(2,1)S(1)} collective-permute-done((bf16[72,3200]{1,0:T(8,128)(2,1)S(1)}, bf16[72,3200]{1,0:T(8,128)(2,1)S(1)}, u32[]{:S(2)}, u32[]{:S(2)}) %collective-permute-start.4) | collective-permute-done | bytes 460832 | tf_op jit(solution)/shard_map/ppermute | solution.py:332
  40.4 1.9 %collective-permute-done.5.refs_1_.left_in = bf16[72,3200]{1,0:T(8,128)(2,1)S(1)} collective-permute-done((bf16[72,3200]{1,0:T(8,128)(2,1)S(1)}, bf16[72,3200]{1,0:T(8,128)(2,1)S(1)}, u32[]{:S(2)}, u32[]{:S(2)}) %collective-permute-start.5) | collective-permute-done | bytes 460832 | tf_op jit(solution)/shard_map/ppermute | solution.py:335
  44.5 3.1 %hidden_rows.6 = (bf16[2,40,768]{2,1,0:T(8,128)(2,1)S(1)}, bf16[2,40,768]{2,1,0:T(8,128)(2,1)S(1)}, bf16[2,40,64]{2,1,0:T(8,128)(2,1)S(1)}, f32[40,64]{1,0:T(8,128)S(1)}, f32[40,64]{1,0:T(8,128)S(1)}) custom-call(bf16[72,3200]{1,0:T(8,128)(2,1)S(1)} %collective-permute-done.4.refs_0_.right_in, bf16[72,3200]{1,0:T(8,128)(2,1)S(1)} %collective-permute-done.5.refs_1_.left_in, ...), custom_call_target="tpu_custom_call" | custom-call | flops 2415919104 | bytes 9437184 | tf_op jit(solution)/shard_map/hidden_rows/pallas_call | solution.py:319
  48.7 2.9 %hidden_rows.7 = (bf16[1,40,768]{2,1,0:T(8,128)(2,1)S(1)}, bf16[1,40,768]{2,1,0:T(8,128)(2,1)S(1)}, bf16[1,40,64]{2,1,0:T(8,128)(2,1)S(1)}, f32[40,64]{1,0:T(8,128)S(1)}) custom-call(bf16[32,3200]{1,0:T(8,128)(2,1)S(1)} %collective-permute-done.6.refs_0_, bf16[40,3200]{1,0:T(8,128)(2,1)S(1)} %collective-permute-done.7.refs_1_, ...), custom_call_target="tpu_custom_call" | custom-call | flops 1207959552 | bytes 9437184 | tf_op jit(solution)/shard_map/hidden_rows/pallas_call | solution.py:319
  53.4 6.5 %partials.1 = (bf16[32,3072]{1,0:T(8,128)(2,1)S(1)}, bf16[40,3072]{1,0:T(8,128)(2,1)S(1)}, bf16[32,3072]{1,0:T(8,128)(2,1)S(1)}, bf16[40,3072]{1,0:T(8,128)(2,1)...) custom-call(bf16[3,40,768]{2,1,0:T(8,128)(2,1)S(1)} %get-tuple-eleme, ...), custom_call_target="tpu_custom_call" | custom-call | flops 6039797760 | bytes 18874368 | tf_op jit(solution)/shard_map/partials/pallas_call | solution.py:319
  62.9 2.4 %collective-permute-start.9 = (bf16[40,3072]{1,0:T(8,128)(2,1)S(1)}, bf16[40,3072]{1,0:T(8,128)(2,1)S(1)}, u32[]{:S(2)}, u32[]{:S(2)}) collective-permute-start(bf16[40,3072]{1,0:T(8,128)(2,1)S(1)} %get-tuple-element.170), channel_id=1, source_target_pairs={{0,4},{4,8},{8,12},{12,14},{14,10},{10,6},{6,2},{2,0},{1,5},{5,9},... | collective-permute-start | bytes 737288 | tf_op jit(solution)/shard_map/ppermute | solution.py:332
  65.3 2.3 %collective-permute-done.22 = bf16[32,3072]{1,0:T(8,128)(2,1)S(1)} collective-permute-done((bf16[32,3072]{1,0:T(8,128)(2,1)S(1)}, bf16[32,3072]{1,0:T(8,128)(2,1)S(1)}, u32[]{:S(2)}, u32[]{:S(2)}) %collective-permute-start.22) | collective-permute-done | bytes 196640 | tf_op jit(solution)/shard_map/ppermute | solution.py:335
  68.3 4.2 %collective-permute-done.9 = bf16[40,3072]{1,0:T(8,128)(2,1)S(1)} collective-permute-done((bf16[40,3072]{1,0:T(8,128)(2,1)S(1)}, bf16[40,3072]{1,0:T(8,128)(2,1)S(1)}, u32[]{:S(2)}, u32[]{:S(2)}) %collective-permute-start.9) | collective-permute-done | bytes 245792 | tf_op jit(solution)/shard_map/ppermute | solution.py:332
  72.5 4.8 %collective-permute-start.13 = (f32[1,40,64]{2,1,0:T(8,128)S(1)}, f32[1,40,64]{2,1,0:T(8,128)S(1)}, u32[]{:S(2)}, u32[]{:S(2)}) collective-permute-start(f32[1,40,64]{2,1,0:T(8,128)S(1)} %get-tuple-element.177), channel_id=1, source_target_pairs={{0,8},{2,10},{4,12},{6,14},{8,0},{10,2},{12,4},{14,6},{1,9},{3,11}... | collective-permute-start | bytes 30728 | tf_op jit(solution)/shard_map/ppermute | solution.py:431
  80.7 2.1 %collective-permute-start.24 = (bf16[32,3072]{1,0:T(8,128)(2,1)S(1)}, bf16[32,3072]{1,0:T(8,128)(2,1)S(1)}, u32[]{:S(2)}, u32[]{:S(2)}) collective-permute-start(bf16[32,3072]{1,0:T(8,128)(2,1)S(1)} %add_convert_fusion.5), channel_id=1, source_target_pairs={{0,2},{4,0},{8,4},{12,8},{14,12},{10,14},{6,10},{2,6},{1,3},{5,1},... | collective-permute-start | bytes 589832 | tf_op jit(solution)/shard_map/ppermute | solution.py:335
  82.7 3.1 %collective-permute-done.15 = bf16[32,3072]{1,0:T(8,128)(2,1)S(1)} collective-permute-done((bf16[32,3072]{1,0:T(8,128)(2,1)S(1)}, bf16[32,3072]{1,0:T(8,128)(2,1)S(1)}, u32[]{:S(2)}, u32[]{:S(2)}) %collective-permute-start.15) | collective-permute-done | bytes 196640 | tf_op jit(solution)/shard_map/ppermute | solution.py:332
  88.2 5.5 %collective-permute-done.16 = bf16[32,3072]{1,0:T(8,128)(2,1)S(1)} collective-permute-done((bf16[32,3072]{1,0:T(8,128)(2,1)S(1)}, bf16[32,3072]{1,0:T(8,128)(2,1)S(1)}, u32[]{:S(2)}, u32[]{:S(2)}) %collective-permute-start.16) | collective-permute-done | bytes 196640 | tf_op jit(solution)/shard_map/ppermute | solution.py:332
  94.7 5.0 %collective-permute-done.19.theirs = bf16[4,32,768]{2,1,0:T(8,128)(2,1)S(1)} collective-permute-done((bf16[4,32,768]{2,1,0:T(8,128)(2,1)S(1)}, bf16[4,32,768]{2,1,0:T(8,128)(2,1)S(1)}, u32[]{:S(2)}, u32[]{:S(2)}) %collective-permute-start.19) | collective-permute-done | bytes 196640 | tf_op jit(solution)/shard_map/ppermute | solution.py:431
  100.4 1.5 %collective-permute-start.28 = (bf16[32,3072]{1,0:T(8,128)(2,1)S(1)}, bf16[32,3072]{1,0:T(8,128)(2,1)S(1)}, u32[]{:S(2)}, u32[]{:S(2)}) collective-permute-start(bf16[32,3072]{1,0:T(8,128)(2,1)S(1)} %add_convert_fusion.7), channel_id=1, source_target_pairs={{0,4},{4,8},{8,12},{12,14},{14,10},{10,6},{6,2},{2,0},{1,5},{5,9},... | collective-permute-start | bytes 589832 | tf_op jit(solution)/shard_map/ppermute | solution.py:332
  101.9 2.5 %collective-permute-done.25.theirs = bf16[2,32,768]{2,1,0:T(8,128)(2,1)S(1)} collective-permute-done((bf16[2,32,768]{2,1,0:T(8,128)(2,1)S(1)}, bf16[2,32,768]{2,1,0:T(8,128)(2,1)S(1)}, u32[]{:S(2)}, u32[]{:S(2)}) %collective-permute-start.25) | collective-permute-done | bytes 98336 | tf_op jit(solution)/shard_map/ppermute | solution.py:431
  105.0 5.4 %collective-permute-done.26.theirs = bf16[1,32,768]{2,1,0:T(8,128)(2,1)S(1)} collective-permute-done((bf16[1,32,768]{2,1,0:T(8,128)(2,1)S(1)}, bf16[1,32,768]{2,1,0:T(8,128)(2,1)S(1)}, u32[]{:S(2)}, u32[]{:S(2)}) %collective-permute-start.26) | collective-permute-done | bytes 49184 | tf_op jit(solution)/shard_map/ppermute | solution.py:431
  110.6 2.4 %finish.1 = bf16[128,6144]{1,0:T(8,128)(2,1)} custom-call(s32[4,128]{1,0:T(4,128)S(1)} %bitcast.20, bf16[32,3072]{1,0:T(8,128)(2,1)S(1)} %collective-permute-done.28.refs_0_, bf16[32,3072]{1,0:T(8,128)(2,1)S(1)} %collective-permute-done.24.refs_1_, bf16[32,3072]{1,0:T(8,128)(2,1)S(1)} %get-tuple-element.204.refs_2_, ...), custom_call_target="tpu_custom_call" | custom-call | flops 400000000 | bytes 4500000 | tf_op jit(solution)/shard_map/finish/pallas_call | solution.py:319
  (104 shorter events, 26.5 us)
Async XLA Ops:
  3.6 13.6 %collective-permute-start.1 = (bf16[72,3200]{1,0:T(8,128)(2,1)S(1)}, bf16[72,3200]{1,0:T(8,128)(2,1)S(1)}, u32[]{:S(2)}, u32[]{:S(2)}) collective-permute-start(bf16[72,3200]{1,0:T(8,128)(2,1)S(1)} %prepare.1.refs_0_), channel_id=1, source_target_pairs={{0,2},{4,0},{8,4},{12,8},{14,12},{10,14},{6,10},{2,6},{1,3},{5,1},... | collective-permute-start | bytes 1382408 | tf_op jit(solution)/shard_map/ppermute | solution.py:335
  6.6 12.0 %collective-permute-start = (bf16[72,3200]{1,0:T(8,128)(2,1)S(1)}, bf16[72,3200]{1,0:T(8,128)(2,1)S(1)}, u32[]{:S(2)}, u32[]{:S(2)}) collective-permute-start(bf16[72,3200]{1,0:T(8,128)(2,1)S(1)} %prepare.1.refs_0_), channel_id=1, source_target_pairs={{0,4},{4,8},{8,12},{12,14},{14,10},{10,6},{6,2},{2,0},{1,5},{5,9},... | collective-permute-start | bytes 1382408 | tf_op jit(solution)/shard_map/ppermute | solution.py:332
  18.6 11.1 %collective-permute-start.2 = (bf16[72,3200]{1,0:T(8,128)(2,1)S(1)}, bf16[72,3200]{1,0:T(8,128)(2,1)S(1)}, u32[]{:S(2)}, u32[]{:S(2)}) collective-permute-start(bf16[72,3200]{1,0:T(8,128)(2,1)S(1)} %collective-permute-done.refs_1_), channel_id=1, source_target_pairs={{0,4},{4,8},{8,12},{12,14},{14,10},{10,6},{6,2},{2,0},{1,5},{5,9},... | collective-permute-start | bytes 1382408 | tf_op jit(solution)/shard_map/ppermute | solution.py:332
  19.0 11.1 %collective-permute-start.3 = (bf16[72,3200]{1,0:T(8,128)(2,1)S(1)}, bf16[72,3200]{1,0:T(8,128)(2,1)S(1)}, u32[]{:S(2)}, u32[]{:S(2)}) collective-permute-start(bf16[72,3200]{1,0:T(8,128)(2,1)S(1)} %collective-permute-done.1.refs_2_), channel_id=1, source_target_pairs={{0,2},{4,0},{8,4},{12,8},{14,12},{10,14},{6,10},{2,6},{1,3},{5,1},... | collective-permute-start | bytes 1382408 | tf_op jit(solution)/shard_map/ppermute | solution.py:335
  30.2 10.2 %collective-permute-start.4 = (bf16[72,3200]{1,0:T(8,128)(2,1)S(1)}, bf16[72,3200]{1,0:T(8,128)(2,1)S(1)}, u32[]{:S(2)}, u32[]{:S(2)}) collective-permute-start(bf16[72,3200]{1,0:T(8,128)(2,1)S(1)} %collective-permute-done.2.refs_0_), channel_id=1, source_target_pairs={{0,4},{4,8},{8,12},{12,14},{14,10},{10,6},{6,2},{2,0},{1,5},{5,9},... | collective-permute-start | bytes 1382408 | tf_op jit(solution)/shard_map/ppermute | solution.py:332
  31.7 10.6 %collective-permute-start.5 = (bf16[72,3200]{1,0:T(8,128)(2,1)S(1)}, bf16[72,3200]{1,0:T(8,128)(2,1)S(1)}, u32[]{:S(2)}, u32[]{:S(2)}) collective-permute-start(bf16[72,3200]{1,0:T(8,128)(2,1)S(1)} %collective-permute-done.3.refs_1_), channel_id=1, source_target_pairs={{0,2},{4,0},{8,4},{12,8},{14,12},{10,14},{6,10},{2,6},{1,3},{5,1},... | collective-permute-start | bytes 1382408 | tf_op jit(solution)/shard_map/ppermute | solution.py:335
  52.1 7.8 %collective-permute-start.8 = (f32[4,40,64]{2,1,0:T(8,128)S(1)}, f32[4,40,64]{2,1,0:T(8,128)S(1)}, u32[]{:S(2)}, u32[]{:S(2)}) collective-permute-start(f32[4,40,64]{2,1,0:T(8,128)S(1)} %get-tuple-element.142), channel_id=1, source_target_pairs={{0,2},{2,0},{4,6},{6,4},{8,10},{10,8},{12,14},{14,12},{1,3},{3,1},... | collective-permute-start | bytes 122888 | tf_op jit(solution)/shard_map/ppermute | solution.py:431
  59.9 7.6 %collective-permute-start.22 = (bf16[32,3072]{1,0:T(8,128)(2,1)S(1)}, bf16[32,3072]{1,0:T(8,128)(2,1)S(1)}, u32[]{:S(2)}, u32[]{:S(2)}) collective-permute-start(bf16[32,3072]{1,0:T(8,128)(2,1)S(1)} %get-tuple-element.195), channel_id=1, source_target_pairs={{0,2},{4,0},{8,4},{12,8},{14,12},{10,14},{6,10},{2,6},{1,3},{5,1},... | collective-permute-start | bytes 589832 | tf_op jit(solution)/shard_map/ppermute | solution.py:335
  60.8 11.7 %collective-permute-start.10 = (f32[2,40,64]{2,1,0:T(8,128)S(1)}, f32[2,40,64]{2,1,0:T(8,128)S(1)}, u32[]{:S(2)}, u32[]{:S(2)}) collective-permute-start(f32[2,40,64]{2,1,0:T(8,128)S(1)} %get-tuple-element.172), channel_id=1, source_target_pairs={{0,4},{2,6},{4,0},{6,2},{8,12},{10,14},{12,8},{14,10},{1,5},{3,7},... | collective-permute-start | bytes 61448 | tf_op jit(solution)/shard_map/ppermute | solution.py:431
  62.0 15.5 %collective-permute-start.11 = (bf16[32,3072]{1,0:T(8,128)(2,1)S(1)}, bf16[32,3072]{1,0:T(8,128)(2,1)S(1)}, u32[]{:S(2)}, u32[]{:S(2)}) collective-permute-start(bf16[32,3072]{1,0:T(8,128)(2,1)S(1)} %get-tuple-element.174), channel_id=1, source_target_pairs={{0,4},{4,8},{8,12},{12,14},{14,10},{10,6},{6,2},{2,0},{1,5},{5,9},... | collective-permute-start | bytes 589832 | tf_op jit(solution)/shard_map/ppermute | solution.py:332
  62.9 9.6 %collective-permute-start.9 = (bf16[40,3072]{1,0:T(8,128)(2,1)S(1)}, bf16[40,3072]{1,0:T(8,128)(2,1)S(1)}, u32[]{:S(2)}, u32[]{:S(2)}) collective-permute-start(bf16[40,3072]{1,0:T(8,128)(2,1)S(1)} %get-tuple-element.170), channel_id=1, source_target_pairs={{0,4},{4,8},{8,12},{12,14},{14,10},{10,6},{6,2},{2,0},{1,5},{5,9},... | collective-permute-start | bytes 737288 | tf_op jit(solution)/shard_map/ppermute | solution.py:332
  65.3 12.2 %collective-permute-start.12 = (bf16[40,3072]{1,0:T(8,128)(2,1)S(1)}, bf16[40,3072]{1,0:T(8,128)(2,1)S(1)}, u32[]{:S(2)}, u32[]{:S(2)}) collective-permute-start(bf16[40,3072]{1,0:T(8,128)(2,1)S(1)} %get-tuple-element.175), channel_id=1, source_target_pairs={{0,2},{4,0},{8,4},{12,8},{14,12},{10,14},{6,10},{2,6},{1,3},{5,1},... | collective-permute-start | bytes 737288 | tf_op jit(solution)/shard_map/ppermute | solution.py:335
  67.6 13.0 %collective-permute-start.23 = (bf16[32,3072]{1,0:T(8,128)(2,1)S(1)}, bf16[32,3072]{1,0:T(8,128)(2,1)S(1)}, u32[]{:S(2)}, u32[]{:S(2)}) collective-permute-start(bf16[32,3072]{1,0:T(8,128)(2,1)S(1)} %add_convert_fusion.6), channel_id=1, source_target_pairs={{0,2},{4,0},{8,4},{12,8},{14,12},{10,14},{6,10},{2,6},{1,3},{5,1},... | collective-permute-start | bytes 589832 | tf_op jit(solution)/shard_map/ppermute | solution.py:335
  77.4 8.6 %collective-permute-start.20 = (bf16[40,3072]{1,0:T(8,128)(2,1)S(1)}, bf16[40,3072]{1,0:T(8,128)(2,1)S(1)}, u32[]{:S(2)}, u32[]{:S(2)}) collective-permute-start(bf16[40,3072]{1,0:T(8,128)(2,1)S(1)} %add_convert_fusion.1), channel_id=1, source_target_pairs={{0,4},{4,8},{8,12},{12,14},{14,10},{10,6},{6,2},{2,0},{1,5},{5,9},... | collective-permute-start | bytes 737288 | tf_op jit(solution)/shard_map/ppermute | solution.py:332
  77.6 8.3 %collective-permute-start.15 = (bf16[32,3072]{1,0:T(8,128)(2,1)S(1)}, bf16[32,3072]{1,0:T(8,128)(2,1)S(1)}, u32[]{:S(2)}, u32[]{:S(2)}) collective-permute-start(bf16[32,3072]{1,0:T(8,128)(2,1)S(1)} %add_convert_fusion.9), channel_id=1, source_target_pairs={{0,4},{4,8},{8,12},{12,14},{14,10},{10,6},{6,2},{2,0},{1,5},{5,9},... | collective-permute-start | bytes 589832 | tf_op jit(solution)/shard_map/ppermute | solution.py:332
  78.2 8.6 %collective-permute-start.17 = (bf16[40,3072]{1,0:T(8,128)(2,1)S(1)}, bf16[40,3072]{1,0:T(8,128)(2,1)S(1)}, u32[]{:S(2)}, u32[]{:S(2)}) collective-permute-start(bf16[40,3072]{1,0:T(8,128)(2,1)S(1)} %add_convert_fusion.4), channel_id=1, source_target_pairs={{0,2},{4,0},{8,4},{12,8},{14,12},{10,14},{6,10},{2,6},{1,3},{5,1},... | collective-permute-start | bytes 737288 | tf_op jit(solution)/shard_map/ppermute | solution.py:335
  80.5 13.3 %collective-permute-start.14 = (bf16[8,32,768]{2,1,0:T(8,128)(2,1)S(1)}, bf16[8,32,768]{2,1,0:T(8,128)(2,1)S(1)}, u32[]{:S(2)}, u32[]{:S(2)}) collective-permute-start(bf16[8,32,768]{2,1,0:T(8,128)(2,1)S(1)} %get-tuple-element.179), channel_id=1, source_target_pairs={{0,1},{1,0},{2,3},{3,2},{4,5},{5,4},{6,7},{7,6},{8,9},{9,8},{10,11... | collective-permute-start | bytes 1179656 | tf_op jit(solution)/shard_map/ppermute | solution.py:465
  80.7 21.2 %collective-permute-start.24 = (bf16[32,3072]{1,0:T(8,128)(2,1)S(1)}, bf16[32,3072]{1,0:T(8,128)(2,1)S(1)}, u32[]{:S(2)}, u32[]{:S(2)}) collective-permute-start(bf16[32,3072]{1,0:T(8,128)(2,1)S(1)} %add_convert_fusion.5), channel_id=1, source_target_pairs={{0,2},{4,0},{8,4},{12,8},{14,12},{10,14},{6,10},{2,6},{1,3},{5,1},... | collective-permute-start | bytes 589832 | tf_op jit(solution)/shard_map/ppermute | solution.py:335
  85.9 7.9 %collective-permute-start.16 = (bf16[32,3072]{1,0:T(8,128)(2,1)S(1)}, bf16[32,3072]{1,0:T(8,128)(2,1)S(1)}, u32[]{:S(2)}, u32[]{:S(2)}) collective-permute-start(bf16[32,3072]{1,0:T(8,128)(2,1)S(1)} %add_convert_fusion.8), channel_id=1, source_target_pairs={{0,4},{4,8},{8,12},{12,14},{14,10},{10,6},{6,2},{2,0},{1,5},{5,9},... | collective-permute-start | bytes 589832 | tf_op jit(solution)/shard_map/ppermute | solution.py:332
  86.0 15.9 %collective-permute-start.21 = (bf16[40,3072]{1,0:T(8,128)(2,1)S(1)}, bf16[40,3072]{1,0:T(8,128)(2,1)S(1)}, u32[]{:S(2)}, u32[]{:S(2)}) collective-permute-start(bf16[40,3072]{1,0:T(8,128)(2,1)S(1)} %add_convert_fusion), channel_id=1, source_target_pairs={{0,4},{4,8},{8,12},{12,14},{14,10},{10,6},{6,2},{2,0},{1,5},{5,9},... | collective-permute-start | bytes 737288 | tf_op jit(solution)/shard_map/ppermute | solution.py:332
  86.9 7.8 %collective-permute-start.18 = (bf16[40,3072]{1,0:T(8,128)(2,1)S(1)}, bf16[40,3072]{1,0:T(8,128)(2,1)S(1)}, u32[]{:S(2)}, u32[]{:S(2)}) collective-permute-start(bf16[40,3072]{1,0:T(8,128)(2,1)S(1)} %add_convert_fusion.3), channel_id=1, source_target_pairs={{0,2},{4,0},{8,4},{12,8},{14,12},{10,14},{6,10},{2,6},{1,3},{5,1},... | collective-permute-start | bytes 737288 | tf_op jit(solution)/shard_map/ppermute | solution.py:335
  99.8 10.8 %collective-permute-start.29 = (bf16[40,3072]{1,0:T(8,128)(2,1)S(1)}, bf16[40,3072]{1,0:T(8,128)(2,1)S(1)}, u32[]{:S(2)}, u32[]{:S(2)}) collective-permute-start(bf16[40,3072]{1,0:T(8,128)(2,1)S(1)} %add_convert_fusion.2), channel_id=1, source_target_pairs={{0,2},{4,0},{8,4},{12,8},{14,12},{10,14},{6,10},{2,6},{1,3},{5,1},... | collective-permute-start | bytes 737288 | tf_op jit(solution)/shard_map/ppermute | solution.py:335
  100.4 10.2 %collective-permute-start.28 = (bf16[32,3072]{1,0:T(8,128)(2,1)S(1)}, bf16[32,3072]{1,0:T(8,128)(2,1)S(1)}, u32[]{:S(2)}, u32[]{:S(2)}) collective-permute-start(bf16[32,3072]{1,0:T(8,128)(2,1)S(1)} %add_convert_fusion.7), channel_id=1, source_target_pairs={{0,4},{4,8},{8,12},{12,14},{14,10},{10,6},{6,2},{2,0},{1,5},{5,9},... | collective-permute-start | bytes 589832 | tf_op jit(solution)/shard_map/ppermute | solution.py:332
  104.8 8.2 %collective-permute-start.30 = (bf16[128,768]{1,0:T(8,128)(2,1)S(1)}, bf16[128,768]{1,0:T(8,128)(2,1)S(1)}, u32[]{:S(2)}, u32[]{:S(2)}) collective-permute-start(bf16[128,768]{1,0:T(8,128)(2,1)S(1)} %lora_rows.1.lora_ref), channel_id=1, source_target_pairs={{0,1},{1,0},{2,3},{3,2},{4,5},{5,4},{6,7},{7,6},{8,9},{9,8},{10,11... | collective-permute-start | bytes 589832 | tf_op jit(solution)/shard_map/ppermute | solution.py:481
  (24 other events, 290.9 us)

commit v13 on v10

--- a/solution.py
+++ b/solution.py
@@ -96,7 +96,8 @@
     return me, sum(jnp.where(me == e, p, 0) for e, p in enumerate(place))
 
 
-def reorder_kernel(place, capacity, gate_in, up_in, gate_out, up_out, tall):
+def reorder_kernel(place, capacity, gate_in, up_in, *refs):
+    gate_out, up_out, tall = refs[-3:]
     count, slot, hidden = gate_out.shape
     _, here = place_here(place)
     live = lax.broadcasted_iota(jnp.int32, (slot, hidden), 0) < capacity
@@ -108,24 +109,6 @@
             at = jnp.where(2 * away < count, 2 * away, 2 * (count - away) - 1)
             rows = tall[e * capacity : e * capacity + slot, :]
             target[at] = jnp.where(live, rows, 0.0).astype(BF)
-
-
-def low_order_kernel(ring, place, order, *refs):
-    lows, (keep, send) = refs[:-2], refs[-2:]
-    count = len(ring)
-    me, here = place_here(place)
-    for low, r in zip(lows, order):
-        spot = lax.rem(here + r + count, count)
-        owner = sum(jnp.where(spot == i, e, 0) for i, e in enumerate(ring))
-        key = owner ^ me
-
-        @pl.when(key % 2 == 0)
-        def _(low=low, key=key):
-            keep[key // 2] = low[...]
-
-        @pl.when(key % 2 == 1)
-        def _(low=low, key=key):
-            send[key // 2] = low[...]
 
 
 def halve_kernel(ours, theirs, *outs):
@@ -221,9 +204,10 @@
             outs[2 * i + 1][:, t : t + TILE] = tile[cut:, :].astype(BF)
 
 
-def adapter_kernel(capacity, choice_ref, tokens_ref, low_in, low_ref, keep_ref, send_ref):
+def adapter_kernel(capacity, choice_ref, tokens_ref, *refs):
+    lows, (low_ref, keep_ref, send_ref) = refs[:-3], refs[-3:]
     count, part, share = keep_ref.shape
-    low = low_in[0].astype(BF)
+    low = sum(x[...] for x in lows).astype(BF)
     low_ref[...] = low
     upper, _ = pick_rows(choice_ref[...], capacity)
     low = dot(upper[: low.shape[0]], low, TN).astype(BF)
@@ -350,16 +334,17 @@
         (4e8, 4.5e6),
         in_specs=[pl.BlockSpec(memory_space=pl.ANY)] * 5,
     )
+    down_here, gate_here, up_here = in_vmem(down_weight), in_vmem(gate_weight), in_vmem(up_weight)
+    gate_factor, up_factor = in_vmem(adapter_gate_factor), in_vmem(adapter_up_factor)
     gate_rows, up_rows = call(
         functools.partial(reorder_kernel, place, capacity),
         "reorder",
         [((n, slot, hidden), BF)] * 2,
-        [stored_gate_rows[0], stored_up_rows[0]],
+        [stored_gate_rows[0], stored_up_rows[0], down_here, gate_factor, up_factor],
         [pltpu.VMEM((n * capacity + slot, hidden), F32)],
         (0, 8 * n * slot * hidden),
     )
 
-    down_here, gate_here, up_here = in_vmem(down_weight), in_vmem(gate_weight), in_vmem(up_weight)
     dgates, dups, low_rows, lows = [], [], [], []
     got = {0: (block,)}
 
@@ -373,7 +358,7 @@
             + [((size, slot, rank), BF)]
             + [((slot, rank), F32)] * size,
             [piece for r in group for piece in got[r]]
-            + [gate_rows, up_rows, down_here, adapter_gate_factor, adapter_up_factor],
+            + [gate_rows, up_rows, down_here, gate_factor, up_factor],
             [pltpu.VMEM((size * tall, half), BF)],
             (2 * size * tall * width * hidden, 2 * hidden * width),
         )
@@ -381,6 +366,10 @@
         dups.append(results[1])
         low_rows.append(results[2])
         lows.extend(results[3:])
+
+    def to_owner(at):
+        r = order[at]
+        lows[at] = lax.ppermute(lows[at], "expert", [(ring[i], ring[(i + r) % n]) for i in range(n)])
 
     going_right = going_left = block
     for s in range(1, middle):
@@ -390,28 +379,29 @@
                 (going_right, going_left, gate_rows, up_rows)
             )
         else:
+            before = len(lows)
             hidden_pass(passes[s - 2])
-            going_right, going_left, dgates[-1], dups[-1] = lax.optimization_barrier(
-                (going_right, going_left, dgates[-1], dups[-1])
+            for at in range(max(before, 1), len(lows)):
+                to_owner(at)
+            going_right, going_left, dgates[-1], dups[-1], lows[before:] = lax.optimization_barrier(
+                (going_right, going_left, dgates[-1], dups[-1], lows[before:])
             )
         got[-s], got[s] = (going_right,), (going_left,)
     right_top, left_rest = call(
         cut_kernel, "cut", [((h, wide), BF) for h in heights], [going_right, going_left]
     )
     right_top, left_rest = right(right_top), left(left_rest)
+    before = len(lows)
     hidden_pass(passes[-2])
+    for at in range(max(before, 1), len(lows)):
+        to_owner(at)
     right_top, left_rest, dgates[-1], dups[-1] = lax.optimization_barrier(
         (right_top, left_rest, dgates[-1], dups[-1])
     )
     got[middle] = (right_top, left_rest)
     hidden_pass(passes[-1])
-
-    low_keep, low_send = call(
-        functools.partial(low_order_kernel, ring, place, order),
-        "low_order",
-        [((n // 2, slot, rank), F32)] * 2,
-        lows,
-    )
+    to_owner(n - 1)
+
     own = call(
         functools.partial(partial_kernel, capacity, slot, sizes, cut),
         "partials",
@@ -434,13 +424,10 @@
         shape = (count // parts,) + keep.shape[1:]
         return call(halve_kernel, "halve", [(shape, keep.dtype)] * parts, [keep, other])
 
-    pair = exchange(low_keep, low_send, 1)
-    pair, own = lax.optimization_barrier((pair, own))
+    lows, own = lax.optimization_barrier((lows, own))
     own = {r: (own[2 * i], own[2 * i + 1]) for i, r in enumerate(order)}
     right_top, left_rest = right(own[middle][0]), left(own[middle][1])
     right_rest, left_top = right(own[middle - 1][1]), left(own[1 - middle][0])
-    pair = exchange(*pair, 2)
-    right_top, left_rest, pair = lax.optimization_barrier((right_top, left_rest, pair))
     for s in range(middle - 1, 0, -1):
         right_top, left_rest = add(right_top, own[s][0]), add(left_rest, own[-s][1])
         right_top, left_rest = right(right_top), left(left_rest)
@@ -448,26 +435,24 @@
             right_rest, left_top = add(right_rest, own[s - 1][1]), add(left_top, own[1 - s][0])
             right_rest, left_top = right(right_rest), left(left_top)
     bits = [1 << i for i in range(n.bit_length() - 1)]
-    for bit in bits[2:]:
-        pair = exchange(*pair, bit)
 
     share = width // n
     part = rank // 2
     swap = [(0, 1), (1, 0)]
 
-    def adapter_gradient(low_total):
+    def adapter_gradient():
         if share % 128 == 0:
             low, keep, send = call(
                 functools.partial(adapter_kernel, capacity),
                 "adapter_gradient",
                 [((slot, rank), BF)] + [((n, part, share), BF)] * 2,
-                [choice, tokens, low_total],
+                [choice, tokens, *lows],
                 work=(2 * own_count * rank * width, 2 * own_count * width),
             )
         else:
             me, core = lax.axis_index("expert"), lax.axis_index("dp")
             upper, _ = pick_rows(choice, capacity)
-            low = low_total[0].astype(BF)
+            low = sum(lows).astype(BF)
             low_tokens = dot(upper[:slot], low, TN).astype(BF)
             down = dot(low_tokens, tokens, TN).astype(BF).reshape(rank, n, share)
             down = down.transpose(1, 0, 2)[jnp.arange(n, dtype=jnp.int32) ^ me]
@@ -491,7 +476,7 @@
         )
         return local, lax.ppermute(local, "dp", swap)
 
-    low, pair = adapter_gradient(pair[0])
+    low, pair = adapter_gradient()
     low_rows, _ = lax.optimization_barrier((low_rows, pair))
     lora, lora_there = lora_gradients()
     for bit in bits:

time: 111 us -> 116 us (1.045)
  starting transfers between devices: 36 us -> 41.9 us
    ppermute x0 -> x7, starting transfers between devices: none -> 11.7 us  [to_owner(): lax.ppermute(lows[at], 'expert', [(ring[i], ring[(i + r) % n]) for i in r...]
    ppermute x0 -> x7, waiting for transfers between devices: none -> 10.3 us  [to_owner(): lax.ppermute(lows[at], 'expert', [(ring[i], ring[(i + r) % n]) for i in r...]
    ppermute x6 -> x3, starting transfers between devices: 8.67 us -> 2.45 us  [exchange(): other = lax.ppermute(send, 'expert', [(e, e ^ bit) for e in range(n)])]
    ppermute x11, waiting for transfers between devices: 13.9 us -> 7.99 us  [left(): return lax.ppermute(x, 'expert', to_left)]
    ppermute x6 -> x3, waiting for transfers between devices: 14.7 us -> 10.1 us  [exchange(): other = lax.ppermute(send, 'expert', [(e, e ^ bit) for e in range(n)])]
    ppermute x11, starting transfers between devices: 14.3 us -> 16.5 us  [left(): return lax.ppermute(x, 'expert', to_left)]
    ppermute x11, waiting for transfers between devices: 10.6 us -> 8.68 us  [right(): return lax.ppermute(x, 'expert', to_right)]
    ppermute x11, starting transfers between devices: 12.4 us -> 11.1 us  [right(): return lax.ppermute(x, 'expert', to_right)]
  transfers between devices with their start and end apart: 31 -> 35, of which waited for: 16 -> 14; matrix products, arithmetic and copies ran while one was open for 1% -> 0% of each run, Pallas kernels for 18% -> 18%
where the time goes in v13:
time: 116 us
  starting transfers between devices  41.9 us (36%)
  waiting for transfers between devices  38.3 us (33%)
  Pallas kernels  26.2 us (23%)
  local copies, waits for them, and re-layouts  7.54 us (6%)
    pallas_call x16, Pallas kernels, call(): pl.pallas_call(kernel, out_shape=[jax.ShapeDtypeStruct(shape, dtype) for...  26.2 us
    ppermute x11, starting transfers between devices, left(): return lax.ppermute(x, 'expert', to_left)  16.5 us
    ppermute x7, starting transfers between devices, to_owner(): lax.ppermute(lows[at], 'expert', [(ring[i], ring[(i + r) % n]) for i in r...  11.7 us
    ppermute x11, starting transfers between devices, right(): return lax.ppermute(x, 'expert', to_right)  11.1 us
    ppermute x7, waiting for transfers between devices, to_owner(): lax.ppermute(lows[at], 'expert', [(ring[i], ring[(i + r) % n]) for i in r...  10.3 us
    ppermute x3, waiting for transfers between devices, exchange(): other = lax.ppermute(send, 'expert', [(e, e ^ bit) for e in range(n)])  10.1 us
    ppermute x11, waiting for transfers between devices, right(): return lax.ppermute(x, 'expert', to_right)  8.68 us
    ppermute x11, waiting for transfers between devices, left(): return lax.ppermute(x, 'expert', to_left)  7.99 us
  transfers between devices with their start and end apart: 35, of which 14 were waited for; matrix products, arithmetic and copies ran while one was open for 0% of the time, Pallas kernels for 18%

profile of v13, /device:TPU:0, one launch (start us, length us, event | category | flops | bytes accessed | tf_op | source)
XLA Modules:
  0.0 115.5 jit_solution(9704835339571231730)
XLA Ops:
  0.6 2.9 %prepare.1.refs_0_ = bf16[72,3200]{1,0:T(8,128)(2,1)S(1)} custom-call(s32[4,128]{1,0:T(4,128)} %bitcast.18, bf16[4,128]{1,0:T(4,128)(2,1)} %bitcast.27, bf16[128,6144]{1,0:T(8,128)(2,1)} %bitcast.26, bf16[128,6144]{1,0:T(8,128)(2,1)} %bitcast.12, bf16[64,6144]{1,0:T(8,128)(2,1)} %refs_7_.3), custom_call_target="tpu_custom_call" | custom-call | flops 400000000 | bytes 4500000 | tf_op jit(solution)/shard_map/prepare/pallas_call | solution.py:303
  3.6 3.0 %collective-permute-start.1 = (bf16[72,3200]{1,0:T(8,128)(2,1)S(1)}, bf16[72,3200]{1,0:T(8,128)(2,1)S(1)}, u32[]{:S(2)}, u32[]{:S(2)}) collective-permute-start(bf16[72,3200]{1,0:T(8,128)(2,1)S(1)} %prepare.1.refs_0_), channel_id=1, source_target_pairs={{0,2},{4,0},{8,4},{12,8},{14,12},{10,14},{6,10},{2,6},{1,3},{5,1},... | collective-permute-start | bytes 1382408 | tf_op jit(solution)/shard_map/ppermute | solution.py:319
  6.7 3.7 %copy-done = bf16[768,6144]{1,0:T(8,128)(2,1)S(1)} copy-done((bf16[768,6144]{1,0:T(8,128)(2,1)S(1)}, bf16[768,6144]{1,0:T(8,128)(2,1)}, u32[]{:S(2)}) %copy-start) | copy-done | bytes 9437208
  14.4 2.8 %collective-permute-done.1.refs_2_ = bf16[72,3200]{1,0:T(8,128)(2,1)S(1)} collective-permute-done((bf16[72,3200]{1,0:T(8,128)(2,1)S(1)}, bf16[72,3200]{1,0:T(8,128)(2,1)S(1)}, u32[]{:S(2)}, u32[]{:S(2)}) %collective-permute-start.1) | collective-permute-done | bytes 460832 | tf_op jit(solution)/shard_map/ppermute | solution.py:319
  20.6 3.0 %hidden_rows.4 = (bf16[3,40,768]{2,1,0:T(8,128)(2,1)S(1)}, bf16[3,40,768]{2,1,0:T(8,128)(2,1)S(1)}, bf16[3,40,64]{2,1,0:T(8,128)(2,1)S(1)}, f32[40,64]{1,0:T(8,1...) custom-call(bf16[72,3200]{1,0:T(8,128)(2,1)S(1)} %prepare.1.refs_0_, ...), custom_call_target="tpu_custom_call" | custom-call | flops 2264924160 | bytes 9437184 | tf_op jit(solution)/shard_map/hidden_rows/pallas_call | solution.py:303
  25.7 4.9 %collective-permute-done.4.refs_1_ = f32[40,64]{1,0:T(8,128)S(1)} collective-permute-done((f32[40,64]{1,0:T(8,128)S(1)}, f32[40,64]{1,0:T(8,128)S(1)}, u32[]{:S(2)}, u32[]{:S(2)}) %collective-permute-start.4) | collective-permute-done | bytes 10272 | tf_op jit(solution)/shard_map/ppermute | solution.py:372
  32.7 3.1 %hidden_rows.5 = (bf16[2,40,768]{2,1,0:T(8,128)(2,1)S(1)}, bf16[2,40,768]{2,1,0:T(8,128)(2,1)S(1)}, bf16[2,40,64]{2,1,0:T(8,128)(2,1)S(1)}, f32[40,64]{1,0:T(8,128)S(1)}, f32[40,64]{1,0:T(8,128)S(1)}) custom-call(bf16[72,3200]{1,0:T(8,128)(2,1)S(1)} %collective-permute-done.2.refs_0_, bf16[72,3200]{1,0:T(8,128)(2,1)S(1)} %collective-permute-done.3.refs_1_, ...), custom_call_target="tpu_custom_call" | custom-call | flops 2415919104 | bytes 9437184 | tf_op jit(solution)/shard_map/hidden_rows/pallas_call | solution.py:303
  35.8 2.4 %collective-permute-start.8 = (f32[40,64]{1,0:T(8,128)S(1)}, f32[40,64]{1,0:T(8,128)S(1)}, u32[]{:S(2)}, u32[]{:S(2)}) collective-permute-start(f32[40,64]{1,0:T(8,128)S(1)} %get-tuple-element.123), channel_id=1, source_target_pairs={{0,6},{4,2},{8,0},{12,4},{14,8},{10,12},{6,14},{2,10},{1,7},{5,3},... | collective-permute-start | bytes 30728 | tf_op jit(solution)/shard_map/ppermute | solution.py:372
  38.8 5.4 %collective-permute-done.8.refs_3_ = f32[40,64]{1,0:T(8,128)S(1)} collective-permute-done((f32[40,64]{1,0:T(8,128)S(1)}, f32[40,64]{1,0:T(8,128)S(1)}, u32[]{:S(2)}, u32[]{:S(2)}) %collective-permute-start.8) | collective-permute-done | bytes 10272 | tf_op jit(solution)/shard_map/ppermute | solution.py:372
  44.6 2.2 %collective-permute-start.12 = (bf16[32,3200]{1,0:T(8,128)(2,1)S(1)}, bf16[32,3200]{1,0:T(8,128)(2,1)S(1)}, u32[]{:S(2)}, u32[]{:S(2)}) collective-permute-start(bf16[32,3200]{1,0:T(8,128)(2,1)S(1)} %get-tuple-element.131), channel_id=1, source_target_pairs={{0,4},{4,8},{8,12},{12,14},{14,10},{10,6},{6,2},{2,0},{1,5},{5,9},... | collective-permute-start | bytes 614408 | tf_op jit(solution)/shard_map/ppermute | solution.py:316
  46.9 3.1 %hidden_rows.6 = (bf16[2,40,768]{2,1,0:T(8,128)(2,1)S(1)}, bf16[2,40,768]{2,1,0:T(8,128)(2,1)S(1)}, bf16[2,40,64]{2,1,0:T(8,128)(2,1)S(1)}, f32[40,64]{1,0:T(8,128)S(1)}, f32[40,64]{1,0:T(8,128)S(1)}) custom-call(bf16[72,3200]{1,0:T(8,128)(2,1)S(1)} %collective-permute-done.6.refs_0_.right_in, bf16[72,3200]{1,0:T(8,128)(2,1)S(1)} %collective-permute-done.7.refs_1_.left_in, ...), custom_call_target="tpu_custom_call" | custom-call | flops 2415919104 | bytes 9437184 | tf_op jit(solution)/shard_map/hidden_rows/pallas_call | solution.py:303
  50.0 3.3 %collective-permute-start.10 = (f32[40,64]{1,0:T(8,128)S(1)}, f32[40,64]{1,0:T(8,128)S(1)}, u32[]{:S(2)}, u32[]{:S(2)}) collective-permute-start(f32[40,64]{1,0:T(8,128)S(1)} %get-tuple-element.129), channel_id=1, source_target_pairs={{0,10},{4,6},{8,2},{12,0},{14,4},{10,8},{6,12},{2,14},{1,11},{5,7}... | collective-permute-start | bytes 30728 | tf_op jit(solution)/shard_map/ppermute | solution.py:372
  53.9 2.9 %hidden_rows.7 = (bf16[1,40,768]{2,1,0:T(8,128)(2,1)S(1)}, bf16[1,40,768]{2,1,0:T(8,128)(2,1)S(1)}, bf16[1,40,64]{2,1,0:T(8,128)(2,1)S(1)}, f32[40,64]{1,0:T(8,128)S(1)}) custom-call(bf16[32,3200]{1,0:T(8,128)(2,1)S(1)} %collective-permute-done.12.refs_0_, bf16[40,3200]{1,0:T(8,128)(2,1)S(1)} %collective-permute-done.13.refs_1_, ...), custom_call_target="tpu_custom_call" | custom-call | flops 1207959552 | bytes 9437184 | tf_op jit(solution)/shard_map/hidden_rows/pallas_call | solution.py:303
  56.7 2.8 %collective-permute-start.14 = (f32[40,64]{1,0:T(8,128)S(1)}, f32[40,64]{1,0:T(8,128)S(1)}, u32[]{:S(2)}, u32[]{:S(2)}) collective-permute-start(f32[40,64]{1,0:T(8,128)S(1)} %get-tuple-element.137), channel_id=1, source_target_pairs={{0,14},{4,10},{8,6},{12,2},{14,0},{10,4},{6,8},{2,12},{1,15},{5,11... | collective-permute-start | bytes 30728 | tf_op jit(solution)/shard_map/ppermute | solution.py:372
  59.6 6.5 %partials.1 = (bf16[32,3072]{1,0:T(8,128)(2,1)S(1)}, bf16[40,3072]{1,0:T(8,128)(2,1)S(1)}, bf16[32,3072]{1,0:T(8,128)(2,1)S(1)}, bf16[40,3072]{1,0:T(8,128)(2,1)...) custom-call(bf16[3,40,768]{2,1,0:T(8,128)(2,1)S(1)} %get-tuple-eleme, ...), custom_call_target="tpu_custom_call" | custom-call | flops 6039797760 | bytes 18874368 | tf_op jit(solution)/shard_map/partials/pallas_call | solution.py:303
  81.1 4.0 %collective-permute-done.26 = bf16[40,3072]{1,0:T(8,128)(2,1)S(1)} collective-permute-done((bf16[40,3072]{1,0:T(8,128)(2,1)S(1)}, bf16[40,3072]{1,0:T(8,128)(2,1)S(1)}, u32[]{:S(2)}, u32[]{:S(2)}) %collective-permute-start.26) | collective-permute-done | bytes 245792 | tf_op jit(solution)/shard_map/ppermute | solution.py:319
  85.1 2.2 %collective-permute-start.21 = (bf16[32,3072]{1,0:T(8,128)(2,1)S(1)}, bf16[32,3072]{1,0:T(8,128)(2,1)S(1)}, u32[]{:S(2)}, u32[]{:S(2)}) collective-permute-start(bf16[32,3072]{1,0:T(8,128)(2,1)S(1)} %add_convert_fusion.5), channel_id=1, source_target_pairs={{0,2},{4,0},{8,4},{12,8},{14,12},{10,14},{6,10},{2,6},{1,3},{5,1},... | collective-permute-start | bytes 589832 | tf_op jit(solution)/shard_map/ppermute | solution.py:319
  87.4 2.0 %collective-permute-done.30.theirs = bf16[4,32,768]{2,1,0:T(8,128)(2,1)S(1)} collective-permute-done((bf16[4,32,768]{2,1,0:T(8,128)(2,1)S(1)}, bf16[4,32,768]{2,1,0:T(8,128)(2,1)S(1)}, u32[]{:S(2)}, u32[]{:S(2)}) %collective-permute-start.30) | collective-permute-done | bytes 196640 | tf_op jit(solution)/shard_map/ppermute | solution.py:421
  89.3 2.2 %collective-permute-start.27 = (bf16[40,3072]{1,0:T(8,128)(2,1)S(1)}, bf16[40,3072]{1,0:T(8,128)(2,1)S(1)}, u32[]{:S(2)}, u32[]{:S(2)}) collective-permute-start(bf16[40,3072]{1,0:T(8,128)(2,1)S(1)} %add_convert_fusion.1), channel_id=1, source_target_pairs={{0,2},{4,0},{8,4},{12,8},{14,12},{10,14},{6,10},{2,6},{1,3},{5,1},... | collective-permute-start | bytes 737288 | tf_op jit(solution)/shard_map/ppermute | solution.py:319
  91.7 6.4 %collective-permute-done.31.theirs = bf16[2,32,768]{2,1,0:T(8,128)(2,1)S(1)} collective-permute-done((bf16[2,32,768]{2,1,0:T(8,128)(2,1)S(1)}, bf16[2,32,768]{2,1,0:T(8,128)(2,1)S(1)}, u32[]{:S(2)}, u32[]{:S(2)}) %collective-permute-start.31) | collective-permute-done | bytes 98336 | tf_op jit(solution)/shard_map/ppermute | solution.py:421
  99.5 2.5 %collective-permute-start.28 = (bf16[40,3072]{1,0:T(8,128)(2,1)S(1)}, bf16[40,3072]{1,0:T(8,128)(2,1)S(1)}, u32[]{:S(2)}, u32[]{:S(2)}) collective-permute-start(bf16[40,3072]{1,0:T(8,128)(2,1)S(1)} %add_convert_fusion), channel_id=1, source_target_pairs={{0,2},{4,0},{8,4},{12,8},{14,12},{10,14},{6,10},{2,6},{1,3},{5,1},... | collective-permute-start | bytes 737288 | tf_op jit(solution)/shard_map/ppermute | solution.py:319
  103.8 2.5 %collective-permute-start.18 = (bf16[32,3072]{1,0:T(8,128)(2,1)S(1)}, bf16[32,3072]{1,0:T(8,128)(2,1)S(1)}, u32[]{:S(2)}, u32[]{:S(2)}) collective-permute-start(bf16[32,3072]{1,0:T(8,128)(2,1)S(1)} %add_convert_fusion.7), channel_id=1, source_target_pairs={{0,4},{4,8},{8,12},{12,14},{14,10},{10,6},{6,2},{2,0},{1,5},{5,9},... | collective-permute-start | bytes 589832 | tf_op jit(solution)/shard_map/ppermute | solution.py:316
  108.4 4.7 %collective-permute-done.18.refs_0_ = bf16[32,3072]{1,0:T(8,128)(2,1)S(1)} collective-permute-done((bf16[32,3072]{1,0:T(8,128)(2,1)S(1)}, bf16[32,3072]{1,0:T(8,128)(2,1)S(1)}, u32[]{:S(2)}, u32[]{:S(2)}) %collective-permute-start.18) | collective-permute-done | bytes 196640 | tf_op jit(solution)/shard_map/ppermute | solution.py:316
  113.1 2.4 %finish.1 = bf16[128,6144]{1,0:T(8,128)(2,1)} custom-call(s32[4,128]{1,0:T(4,128)S(1)} %bitcast.20, bf16[32,3072]{1,0:T(8,128)(2,1)S(1)} %collective-permute-done.18.refs_0_, bf16[32,3072]{1,0:T(8,128)(2,1)S(1)} %collective-permute-done.21.refs_1_, bf16[32,3072]{1,0:T(8,128)(2,1)S(1)} %get-tuple-element.169.refs_2_, ...), custom_call_target="tpu_custom_call" | custom-call | flops 400000000 | bytes 4500000 | tf_op jit(solution)/shard_map/finish/pallas_call | solution.py:303
  (104 shorter events, 33.7 us)
Async XLA Ops:
  3.6 13.6 %collective-permute-start.1 = (bf16[72,3200]{1,0:T(8,128)(2,1)S(1)}, bf16[72,3200]{1,0:T(8,128)(2,1)S(1)}, u32[]{:S(2)}, u32[]{:S(2)}) collective-permute-start(bf16[72,3200]{1,0:T(8,128)(2,1)S(1)} %prepare.1.refs_0_), channel_id=1, source_target_pairs={{0,2},{4,0},{8,4},{12,8},{14,12},{10,14},{6,10},{2,6},{1,3},{5,1},... | collective-permute-start | bytes 1382408 | tf_op jit(solution)/shard_map/ppermute | solution.py:319
  6.6 12.0 %collective-permute-start = (bf16[72,3200]{1,0:T(8,128)(2,1)S(1)}, bf16[72,3200]{1,0:T(8,128)(2,1)S(1)}, u32[]{:S(2)}, u32[]{:S(2)}) collective-permute-start(bf16[72,3200]{1,0:T(8,128)(2,1)S(1)} %prepare.1.refs_0_), channel_id=1, source_target_pairs={{0,4},{4,8},{8,12},{12,14},{14,10},{10,6},{6,2},{2,0},{1,5},{5,9},... | collective-permute-start | bytes 1382408 | tf_op jit(solution)/shard_map/ppermute | solution.py:316
  18.6 12.0 %collective-permute-start.2 = (bf16[72,3200]{1,0:T(8,128)(2,1)S(1)}, bf16[72,3200]{1,0:T(8,128)(2,1)S(1)}, u32[]{:S(2)}, u32[]{:S(2)}) collective-permute-start(bf16[72,3200]{1,0:T(8,128)(2,1)S(1)} %collective-permute-done.refs_1_), channel_id=1, source_target_pairs={{0,4},{4,8},{8,12},{12,14},{14,10},{10,6},{6,2},{2,0},{1,5},{5,9},... | collective-permute-start | bytes 1382408 | tf_op jit(solution)/shard_map/ppermute | solution.py:316
  19.0 11.6 %collective-permute-start.3 = (bf16[72,3200]{1,0:T(8,128)(2,1)S(1)}, bf16[72,3200]{1,0:T(8,128)(2,1)S(1)}, u32[]{:S(2)}, u32[]{:S(2)}) collective-permute-start(bf16[72,3200]{1,0:T(8,128)(2,1)S(1)} %collective-permute-done.1.refs_2_), channel_id=1, source_target_pairs={{0,2},{4,0},{8,4},{12,8},{14,12},{10,14},{6,10},{2,6},{1,3},{5,1},... | collective-permute-start | bytes 1382408 | tf_op jit(solution)/shard_map/ppermute | solution.py:319
  30.6 13.5 %collective-permute-start.6 = (bf16[72,3200]{1,0:T(8,128)(2,1)S(1)}, bf16[72,3200]{1,0:T(8,128)(2,1)S(1)}, u32[]{:S(2)}, u32[]{:S(2)}) collective-permute-start(bf16[72,3200]{1,0:T(8,128)(2,1)S(1)} %collective-permute-done.2.refs_0_), channel_id=1, source_target_pairs={{0,4},{4,8},{8,12},{12,14},{14,10},{10,6},{6,2},{2,0},{1,5},{5,9},... | collective-permute-start | bytes 1382408 | tf_op jit(solution)/shard_map/ppermute | solution.py:316
  32.2 12.0 %collective-permute-start.7 = (bf16[72,3200]{1,0:T(8,128)(2,1)S(1)}, bf16[72,3200]{1,0:T(8,128)(2,1)S(1)}, u32[]{:S(2)}, u32[]{:S(2)}) collective-permute-start(bf16[72,3200]{1,0:T(8,128)(2,1)S(1)} %collective-permute-done.3.refs_1_), channel_id=1, source_target_pairs={{0,2},{4,0},{8,4},{12,8},{14,12},{10,14},{6,10},{2,6},{1,3},{5,1},... | collective-permute-start | bytes 1382408 | tf_op jit(solution)/shard_map/ppermute | solution.py:319
  35.8 8.4 %collective-permute-start.8 = (f32[40,64]{1,0:T(8,128)S(1)}, f32[40,64]{1,0:T(8,128)S(1)}, u32[]{:S(2)}, u32[]{:S(2)}) collective-permute-start(f32[40,64]{1,0:T(8,128)S(1)} %get-tuple-element.123), channel_id=1, source_target_pairs={{0,6},{4,2},{8,0},{12,4},{14,8},{10,12},{6,14},{2,10},{1,7},{5,3},... | collective-permute-start | bytes 30728 | tf_op jit(solution)/shard_map/ppermute | solution.py:372
  44.2 9.7 %collective-permute-start.13 = (bf16[40,3200]{1,0:T(8,128)(2,1)S(1)}, bf16[40,3200]{1,0:T(8,128)(2,1)S(1)}, u32[]{:S(2)}, u32[]{:S(2)}) collective-permute-start(bf16[40,3200]{1,0:T(8,128)(2,1)S(1)} %get-tuple-element.132), channel_id=1, source_target_pairs={{0,2},{4,0},{8,4},{12,8},{14,12},{10,14},{6,10},{2,6},{1,3},{5,1},... | collective-permute-start | bytes 768008 | tf_op jit(solution)/shard_map/ppermute | solution.py:319
  44.6 9.2 %collective-permute-start.12 = (bf16[32,3200]{1,0:T(8,128)(2,1)S(1)}, bf16[32,3200]{1,0:T(8,128)(2,1)S(1)}, u32[]{:S(2)}, u32[]{:S(2)}) collective-permute-start(bf16[32,3200]{1,0:T(8,128)(2,1)S(1)} %get-tuple-element.131), channel_id=1, source_target_pairs={{0,4},{4,8},{8,12},{12,14},{14,10},{10,6},{6,2},{2,0},{1,5},{5,9},... | collective-permute-start | bytes 614408 | tf_op jit(solution)/shard_map/ppermute | solution.py:316
  50.0 16.2 %collective-permute-start.10 = (f32[40,64]{1,0:T(8,128)S(1)}, f32[40,64]{1,0:T(8,128)S(1)}, u32[]{:S(2)}, u32[]{:S(2)}) collective-permute-start(f32[40,64]{1,0:T(8,128)S(1)} %get-tuple-element.129), channel_id=1, source_target_pairs={{0,10},{4,6},{8,2},{12,0},{14,4},{10,8},{6,12},{2,14},{1,11},{5,7}... | collective-permute-start | bytes 30728 | tf_op jit(solution)/shard_map/ppermute | solution.py:372
  53.3 12.9 %collective-permute-start.11 = (f32[40,64]{1,0:T(8,128)S(1)}, f32[40,64]{1,0:T(8,128)S(1)}, u32[]{:S(2)}, u32[]{:S(2)}) collective-permute-start(f32[40,64]{1,0:T(8,128)S(1)} %get-tuple-element.130), channel_id=1, source_target_pairs={{0,12},{4,14},{8,10},{12,6},{14,2},{10,0},{6,4},{2,8},{1,13},{5,15... | collective-permute-start | bytes 30728 | tf_op jit(solution)/shard_map/ppermute | solution.py:372
  56.7 9.5 %collective-permute-start.14 = (f32[40,64]{1,0:T(8,128)S(1)}, f32[40,64]{1,0:T(8,128)S(1)}, u32[]{:S(2)}, u32[]{:S(2)}) collective-permute-start(f32[40,64]{1,0:T(8,128)S(1)} %get-tuple-element.137), channel_id=1, source_target_pairs={{0,14},{4,10},{8,6},{12,2},{14,0},{10,4},{6,8},{2,12},{1,15},{5,11... | collective-permute-start | bytes 30728 | tf_op jit(solution)/shard_map/ppermute | solution.py:372
  72.0 7.9 %collective-permute-start.16 = (bf16[32,3072]{1,0:T(8,128)(2,1)S(1)}, bf16[32,3072]{1,0:T(8,128)(2,1)S(1)}, u32[]{:S(2)}, u32[]{:S(2)}) collective-permute-start(bf16[32,3072]{1,0:T(8,128)(2,1)S(1)} %add_convert_fusion.9), channel_id=1, source_target_pairs={{0,4},{4,8},{8,12},{12,14},{14,10},{10,6},{6,2},{2,0},{1,5},{5,9},... | collective-permute-start | bytes 589832 | tf_op jit(solution)/shard_map/ppermute | solution.py:316
  73.1 7.9 %collective-permute-start.20 = (bf16[32,3072]{1,0:T(8,128)(2,1)S(1)}, bf16[32,3072]{1,0:T(8,128)(2,1)S(1)}, u32[]{:S(2)}, u32[]{:S(2)}) collective-permute-start(bf16[32,3072]{1,0:T(8,128)(2,1)S(1)} %add_convert_fusion.6), channel_id=1, source_target_pairs={{0,2},{4,0},{8,4},{12,8},{14,12},{10,14},{6,10},{2,6},{1,3},{5,1},... | collective-permute-start | bytes 589832 | tf_op jit(solution)/shard_map/ppermute | solution.py:319
  74.8 16.8 %collective-permute-start.23 = (bf16[40,3072]{1,0:T(8,128)(2,1)S(1)}, bf16[40,3072]{1,0:T(8,128)(2,1)S(1)}, u32[]{:S(2)}, u32[]{:S(2)}) collective-permute-start(bf16[40,3072]{1,0:T(8,128)(2,1)S(1)} %add_convert_fusion.4), channel_id=1, source_target_pairs={{0,4},{4,8},{8,12},{12,14},{14,10},{10,6},{6,2},{2,0},{1,5},{5,9},... | collective-permute-start | bytes 737288 | tf_op jit(solution)/shard_map/ppermute | solution.py:316
  76.0 9.1 %collective-permute-start.26 = (bf16[40,3072]{1,0:T(8,128)(2,1)S(1)}, bf16[40,3072]{1,0:T(8,128)(2,1)S(1)}, u32[]{:S(2)}, u32[]{:S(2)}) collective-permute-start(bf16[40,3072]{1,0:T(8,128)(2,1)S(1)} %add_convert_fusion.2), channel_id=1, source_target_pairs={{0,2},{4,0},{8,4},{12,8},{14,12},{10,14},{6,10},{2,6},{1,3},{5,1},... | collective-permute-start | bytes 737288 | tf_op jit(solution)/shard_map/ppermute | solution.py:319
  77.2 12.2 %collective-permute-start.30 = (bf16[4,32,768]{2,1,0:T(8,128)(2,1)S(1)}, bf16[4,32,768]{2,1,0:T(8,128)(2,1)S(1)}, u32[]{:S(2)}, u32[]{:S(2)}) collective-permute-start(bf16[4,32,768]{2,1,0:T(8,128)(2,1)S(1)} %get-tuple-element.190), channel_id=1, source_target_pairs={{0,2},{2,0},{4,6},{6,4},{8,10},{10,8},{12,14},{14,12},{1,3},{3,1},... | collective-permute-start | bytes 589832 | tf_op jit(solution)/shard_map/ppermute | solution.py:421
  79.9 26.4 %collective-permute-start.34 = (bf16[128,768]{1,0:T(8,128)(2,1)S(1)}, bf16[128,768]{1,0:T(8,128)(2,1)S(1)}, u32[]{:S(2)}, u32[]{:S(2)}) collective-permute-start(bf16[128,768]{1,0:T(8,128)(2,1)S(1)} %lora_rows.1.lora_ref), channel_id=1, source_target_pairs={{0,1},{1,0},{2,3},{3,2},{4,5},{5,4},{6,7},{7,6},{8,9},{9,8},{10,11... | collective-permute-start | bytes 589832 | tf_op jit(solution)/shard_map/ppermute | solution.py:477
  81.0 18.5 %collective-permute-start.17 = (bf16[32,3072]{1,0:T(8,128)(2,1)S(1)}, bf16[32,3072]{1,0:T(8,128)(2,1)S(1)}, u32[]{:S(2)}, u32[]{:S(2)}) collective-permute-start(bf16[32,3072]{1,0:T(8,128)(2,1)S(1)} %add_convert_fusion.8), channel_id=1, source_target_pairs={{0,4},{4,8},{8,12},{12,14},{14,10},{10,6},{6,2},{2,0},{1,5},{5,9},... | collective-permute-start | bytes 589832 | tf_op jit(solution)/shard_map/ppermute | solution.py:316
  85.1 23.3 %collective-permute-start.21 = (bf16[32,3072]{1,0:T(8,128)(2,1)S(1)}, bf16[32,3072]{1,0:T(8,128)(2,1)S(1)}, u32[]{:S(2)}, u32[]{:S(2)}) collective-permute-start(bf16[32,3072]{1,0:T(8,128)(2,1)S(1)} %add_convert_fusion.5), channel_id=1, source_target_pairs={{0,2},{4,0},{8,4},{12,8},{14,12},{10,14},{6,10},{2,6},{1,3},{5,1},... | collective-permute-start | bytes 589832 | tf_op jit(solution)/shard_map/ppermute | solution.py:319
  89.3 8.9 %collective-permute-start.27 = (bf16[40,3072]{1,0:T(8,128)(2,1)S(1)}, bf16[40,3072]{1,0:T(8,128)(2,1)S(1)}, u32[]{:S(2)}, u32[]{:S(2)}) collective-permute-start(bf16[40,3072]{1,0:T(8,128)(2,1)S(1)} %add_convert_fusion.1), channel_id=1, source_target_pairs={{0,2},{4,0},{8,4},{12,8},{14,12},{10,14},{6,10},{2,6},{1,3},{5,1},... | collective-permute-start | bytes 737288 | tf_op jit(solution)/shard_map/ppermute | solution.py:319
  98.2 10.2 %collective-permute-start.24 = (bf16[40,3072]{1,0:T(8,128)(2,1)S(1)}, bf16[40,3072]{1,0:T(8,128)(2,1)S(1)}, u32[]{:S(2)}, u32[]{:S(2)}) collective-permute-start(bf16[40,3072]{1,0:T(8,128)(2,1)S(1)} %add_convert_fusion.3), channel_id=1, source_target_pairs={{0,4},{4,8},{8,12},{12,14},{14,10},{10,6},{6,2},{2,0},{1,5},{5,9},... | collective-permute-start | bytes 737288 | tf_op jit(solution)/shard_map/ppermute | solution.py:316
  99.5 13.5 %collective-permute-start.28 = (bf16[40,3072]{1,0:T(8,128)(2,1)S(1)}, bf16[40,3072]{1,0:T(8,128)(2,1)S(1)}, u32[]{:S(2)}, u32[]{:S(2)}) collective-permute-start(bf16[40,3072]{1,0:T(8,128)(2,1)S(1)} %add_convert_fusion), channel_id=1, source_target_pairs={{0,2},{4,0},{8,4},{12,8},{14,12},{10,14},{6,10},{2,6},{1,3},{5,1},... | collective-permute-start | bytes 737288 | tf_op jit(solution)/shard_map/ppermute | solution.py:319
  103.8 9.3 %collective-permute-start.18 = (bf16[32,3072]{1,0:T(8,128)(2,1)S(1)}, bf16[32,3072]{1,0:T(8,128)(2,1)S(1)}, u32[]{:S(2)}, u32[]{:S(2)}) collective-permute-start(bf16[32,3072]{1,0:T(8,128)(2,1)S(1)} %add_convert_fusion.7), channel_id=1, source_target_pairs={{0,4},{4,8},{8,12},{12,14},{14,10},{10,6},{6,2},{2,0},{1,5},{5,9},... | collective-permute-start | bytes 589832 | tf_op jit(solution)/shard_map/ppermute | solution.py:316
  (26 other events, 263.0 us)

commit v14 on v13

--- a/solution.py
+++ b/solution.py
@@ -428,12 +428,6 @@
     own = {r: (own[2 * i], own[2 * i + 1]) for i, r in enumerate(order)}
     right_top, left_rest = right(own[middle][0]), left(own[middle][1])
     right_rest, left_top = right(own[middle - 1][1]), left(own[1 - middle][0])
-    for s in range(middle - 1, 0, -1):
-        right_top, left_rest = add(right_top, own[s][0]), add(left_rest, own[-s][1])
-        right_top, left_rest = right(right_top), left(left_rest)
-        if s > 1:
-            right_rest, left_top = add(right_rest, own[s - 1][1]), add(left_top, own[1 - s][0])
-            right_rest, left_top = right(right_rest), left(left_top)
     bits = [1 << i for i in range(n.bit_length() - 1)]
 
     share = width // n
@@ -477,10 +471,28 @@
         return local, lax.ppermute(local, "dp", swap)
 
     low, pair = adapter_gradient()
+    pair = exchange(*pair, bits[0])
+    for s in range(middle - 1, 0, -1):
+        right_top, left_rest = add(right_top, own[s][0]), add(left_rest, own[-s][1])
+        right_top, left_rest = right(right_top), left(left_rest)
+        if s > 1:
+            right_rest, left_top = add(right_rest, own[s - 1][1]), add(left_top, own[1 - s][0])
+            right_rest, left_top = right(right_rest), left(left_top)
+    keep, right_rest, left_top = lax.optimization_barrier((pair[0], right_rest, left_top))
+    pair = exchange(keep, pair[1], bits[1])
     low_rows, _ = lax.optimization_barrier((low_rows, pair))
+    (input_gradient,) = call(
+        functools.partial(finish_kernel, capacity),
+        "finish",
+        [((own_count, width), BF)],
+        [choice, right_top, left_top, own[0][0], right_rest, left_rest, own[0][1], low, adapter_down_factor],
+        [pltpu.VMEM((2 * capacity, rank), F32)],
+        (4e8, 4.5e6),
+    )
     lora, lora_there = lora_gradients()
-    for bit in bits:
-        pair = exchange(*pair, bit)
+    for bit in bits[2:]:
+        keep, input_gradient = lax.optimization_barrier((pair[0], input_gradient))
+        pair = exchange(keep, pair[1], bit)
     down = pair[0][0]
     there = lax.ppermute(down, "dp", swap)
     grad_down, grad_gate, grad_up = call(
@@ -488,15 +500,6 @@
         "join",
         [((rank, hidden), F32)] * 3,
         [down, there, lora, lora_there],
-    )
-
-    (input_gradient,) = call(
-        functools.partial(finish_kernel, capacity),
-        "finish",
-        [((own_count, width), BF)],
-        [choice, right_top, left_top, own[0][0], right_rest, left_rest, own[0][1], low, adapter_down_factor],
-        [pltpu.VMEM((2 * capacity, rank), F32)],
-        (4e8, 4.5e6),
     )
     return (input_gradient[None], grad_down, grad_gate, grad_up)
 

time: 116 us -> 110 us (0.948)
  waiting for transfers between devices: 38.3 us -> 35.2 us
  starting transfers between devices: 41.9 us -> 39.7 us
    ppermute x3, waiting for transfers between devices: 10.1 us -> 2.14 us  [exchange(): other = lax.ppermute(send, 'expert', [(e, e ^ bit) for e in range(n)])]
    ppermute x11, waiting for transfers between devices: 7.99 us -> 14.3 us  [left(): return lax.ppermute(x, 'expert', to_left)]
    ppermute x11, starting transfers between devices: 16.5 us -> 14.3 us  [left(): return lax.ppermute(x, 'expert', to_left)]
    ppermute x11, waiting for transfers between devices: 8.68 us -> 7.25 us  [right(): return lax.ppermute(x, 'expert', to_right)]
  transfers between devices with their start and end apart: 35 -> 35, of which waited for: 14 -> 12; matrix products, arithmetic and copies ran while one was open for 0% -> 0% of each run, Pallas kernels for 18% -> 20%
where the time goes in v14:
time: 110 us
  starting transfers between devices  39.7 us (36%)
  waiting for transfers between devices  35.2 us (32%)
  Pallas kernels  26.2 us (24%)
  local copies, waits for them, and re-layouts  7.54 us (7%)
    pallas_call x16, Pallas kernels, call(): pl.pallas_call(kernel, out_shape=[jax.ShapeDtypeStruct(shape, dtype) for...  26.2 us
    ppermute x11, starting transfers between devices, left(): return lax.ppermute(x, 'expert', to_left)  14.3 us
    ppermute x11, waiting for transfers between devices, left(): return lax.ppermute(x, 'expert', to_left)  14.3 us
    ppermute x7, starting transfers between devices, to_owner(): lax.ppermute(lows[at], 'expert', [(ring[i], ring[(i + r) % n]) for i in r...  11.7 us
    ppermute x11, starting transfers between devices, right(): return lax.ppermute(x, 'expert', to_right)  10.8 us
    ppermute x7, waiting for transfers between devices, to_owner(): lax.ppermute(lows[at], 'expert', [(ring[i], ring[(i + r) % n]) for i in r...  10.3 us
    unnamed x30, local copies, waits for them, and re-layouts  7.54 us
    ppermute x11, waiting for transfers between devices, right(): return lax.ppermute(x, 'expert', to_right)  7.25 us
  transfers between devices with their start and end apart: 35, of which 12 were waited for; matrix products, arithmetic and copies ran while one was open for 0% of the time, Pallas kernels for 20%

profile of v14, /device:TPU:0, one launch (start us, length us, event | category | flops | bytes accessed | tf_op | source)
XLA Modules:
  0.0 110.1 jit_solution(9145678459110250091)
XLA Ops:
  0.6 2.9 %prepare.1.refs_0_ = bf16[72,3200]{1,0:T(8,128)(2,1)S(1)} custom-call(s32[4,128]{1,0:T(4,128)} %bitcast.18, bf16[4,128]{1,0:T(4,128)(2,1)} %bitcast.27, bf16[128,6144]{1,0:T(8,128)(2,1)} %bitcast.26, bf16[128,6144]{1,0:T(8,128)(2,1)} %bitcast.12, bf16[64,6144]{1,0:T(8,128)(2,1)} %refs_7_.3), custom_call_target="tpu_custom_call" | custom-call | flops 400000000 | bytes 4500000 | tf_op jit(solution)/shard_map/prepare/pallas_call | solution.py:303
  3.6 3.0 %collective-permute-start.1 = (bf16[72,3200]{1,0:T(8,128)(2,1)S(1)}, bf16[72,3200]{1,0:T(8,128)(2,1)S(1)}, u32[]{:S(2)}, u32[]{:S(2)}) collective-permute-start(bf16[72,3200]{1,0:T(8,128)(2,1)S(1)} %prepare.1.refs_0_), channel_id=1, source_target_pairs={{0,2},{4,0},{8,4},{12,8},{14,12},{10,14},{6,10},{2,6},{1,3},{5,1},... | collective-permute-start | bytes 1382408 | tf_op jit(solution)/shard_map/ppermute | solution.py:319
  6.7 3.7 %copy-done = bf16[768,6144]{1,0:T(8,128)(2,1)S(1)} copy-done((bf16[768,6144]{1,0:T(8,128)(2,1)S(1)}, bf16[768,6144]{1,0:T(8,128)(2,1)}, u32[]{:S(2)}) %copy-start) | copy-done | bytes 9437208
  14.4 2.8 %collective-permute-done.1.refs_2_ = bf16[72,3200]{1,0:T(8,128)(2,1)S(1)} collective-permute-done((bf16[72,3200]{1,0:T(8,128)(2,1)S(1)}, bf16[72,3200]{1,0:T(8,128)(2,1)S(1)}, u32[]{:S(2)}, u32[]{:S(2)}) %collective-permute-start.1) | collective-permute-done | bytes 460832 | tf_op jit(solution)/shard_map/ppermute | solution.py:319
  19.0 1.6 %collective-permute-start.3 = (bf16[72,3200]{1,0:T(8,128)(2,1)S(1)}, bf16[72,3200]{1,0:T(8,128)(2,1)S(1)}, u32[]{:S(2)}, u32[]{:S(2)}) collective-permute-start(bf16[72,3200]{1,0:T(8,128)(2,1)S(1)} %collective-permute-done.1.refs_2_), channel_id=1, source_target_pairs={{0,2},{4,0},{8,4},{12,8},{14,12},{10,14},{6,10},{2,6},{1,3},{5,1},... | collective-permute-start | bytes 1382408 | tf_op jit(solution)/shard_map/ppermute | solution.py:319
  20.6 3.0 %hidden_rows.4 = (bf16[3,40,768]{2,1,0:T(8,128)(2,1)S(1)}, bf16[3,40,768]{2,1,0:T(8,128)(2,1)S(1)}, bf16[3,40,64]{2,1,0:T(8,128)(2,1)S(1)}, f32[40,64]{1,0:T(8,1...) custom-call(bf16[72,3200]{1,0:T(8,128)(2,1)S(1)} %prepare.1.refs_0_, ...), custom_call_target="tpu_custom_call" | custom-call | flops 2264924160 | bytes 9437184 | tf_op jit(solution)/shard_map/hidden_rows/pallas_call | solution.py:303
  23.7 1.6 %collective-permute-start.4 = (f32[40,64]{1,0:T(8,128)S(1)}, f32[40,64]{1,0:T(8,128)S(1)}, u32[]{:S(2)}, u32[]{:S(2)}) collective-permute-start(f32[40,64]{1,0:T(8,128)S(1)} %get-tuple-element.119), channel_id=1, source_target_pairs={{0,2},{4,0},{8,4},{12,8},{14,12},{10,14},{6,10},{2,6},{1,3},{5,1},... | collective-permute-start | bytes 30728 | tf_op jit(solution)/shard_map/ppermute | solution.py:372
  25.7 4.9 %collective-permute-done.4.refs_1_ = f32[40,64]{1,0:T(8,128)S(1)} collective-permute-done((f32[40,64]{1,0:T(8,128)S(1)}, f32[40,64]{1,0:T(8,128)S(1)}, u32[]{:S(2)}, u32[]{:S(2)}) %collective-permute-start.4) | collective-permute-done | bytes 10272 | tf_op jit(solution)/shard_map/ppermute | solution.py:372
  32.7 3.1 %hidden_rows.5 = (bf16[2,40,768]{2,1,0:T(8,128)(2,1)S(1)}, bf16[2,40,768]{2,1,0:T(8,128)(2,1)S(1)}, bf16[2,40,64]{2,1,0:T(8,128)(2,1)S(1)}, f32[40,64]{1,0:T(8,128)S(1)}, f32[40,64]{1,0:T(8,128)S(1)}) custom-call(bf16[72,3200]{1,0:T(8,128)(2,1)S(1)} %collective-permute-done.2.refs_0_, bf16[72,3200]{1,0:T(8,128)(2,1)S(1)} %collective-permute-done.3.refs_1_, ...), custom_call_target="tpu_custom_call" | custom-call | flops 2415919104 | bytes 9437184 | tf_op jit(solution)/shard_map/hidden_rows/pallas_call | solution.py:303
  35.8 2.4 %collective-permute-start.8 = (f32[40,64]{1,0:T(8,128)S(1)}, f32[40,64]{1,0:T(8,128)S(1)}, u32[]{:S(2)}, u32[]{:S(2)}) collective-permute-start(f32[40,64]{1,0:T(8,128)S(1)} %get-tuple-element.128), channel_id=1, source_target_pairs={{0,6},{4,2},{8,0},{12,4},{14,8},{10,12},{6,14},{2,10},{1,7},{5,3},... | collective-permute-start | bytes 30728 | tf_op jit(solution)/shard_map/ppermute | solution.py:372
  38.8 5.4 %collective-permute-done.8.refs_3_ = f32[40,64]{1,0:T(8,128)S(1)} collective-permute-done((f32[40,64]{1,0:T(8,128)S(1)}, f32[40,64]{1,0:T(8,128)S(1)}, u32[]{:S(2)}, u32[]{:S(2)}) %collective-permute-start.8) | collective-permute-done | bytes 10272 | tf_op jit(solution)/shard_map/ppermute | solution.py:372
  44.6 2.2 %collective-permute-start.12 = (bf16[32,3200]{1,0:T(8,128)(2,1)S(1)}, bf16[32,3200]{1,0:T(8,128)(2,1)S(1)}, u32[]{:S(2)}, u32[]{:S(2)}) collective-permute-start(bf16[32,3200]{1,0:T(8,128)(2,1)S(1)} %get-tuple-element.136), channel_id=1, source_target_pairs={{0,4},{4,8},{8,12},{12,14},{14,10},{10,6},{6,2},{2,0},{1,5},{5,9},... | collective-permute-start | bytes 614408 | tf_op jit(solution)/shard_map/ppermute | solution.py:316
  46.9 3.1 %hidden_rows.6 = (bf16[2,40,768]{2,1,0:T(8,128)(2,1)S(1)}, bf16[2,40,768]{2,1,0:T(8,128)(2,1)S(1)}, bf16[2,40,64]{2,1,0:T(8,128)(2,1)S(1)}, f32[40,64]{1,0:T(8,128)S(1)}, f32[40,64]{1,0:T(8,128)S(1)}) custom-call(bf16[72,3200]{1,0:T(8,128)(2,1)S(1)} %collective-permute-done.6.refs_0_.right_in, bf16[72,3200]{1,0:T(8,128)(2,1)S(1)} %collective-permute-done.7.refs_1_.left_in, ...), custom_call_target="tpu_custom_call" | custom-call | flops 2415919104 | bytes 9437184 | tf_op jit(solution)/shard_map/hidden_rows/pallas_call | solution.py:303
  50.0 3.3 %collective-permute-start.10 = (f32[40,64]{1,0:T(8,128)S(1)}, f32[40,64]{1,0:T(8,128)S(1)}, u32[]{:S(2)}, u32[]{:S(2)}) collective-permute-start(f32[40,64]{1,0:T(8,128)S(1)} %get-tuple-element.134), channel_id=1, source_target_pairs={{0,10},{4,6},{8,2},{12,0},{14,4},{10,8},{6,12},{2,14},{1,11},{5,7}... | collective-permute-start | bytes 30728 | tf_op jit(solution)/shard_map/ppermute | solution.py:372
  53.9 2.9 %hidden_rows.7 = (bf16[1,40,768]{2,1,0:T(8,128)(2,1)S(1)}, bf16[1,40,768]{2,1,0:T(8,128)(2,1)S(1)}, bf16[1,40,64]{2,1,0:T(8,128)(2,1)S(1)}, f32[40,64]{1,0:T(8,128)S(1)}) custom-call(bf16[32,3200]{1,0:T(8,128)(2,1)S(1)} %collective-permute-done.12.refs_0_, bf16[40,3200]{1,0:T(8,128)(2,1)S(1)} %collective-permute-done.13.refs_1_, ...), custom_call_target="tpu_custom_call" | custom-call | flops 1207959552 | bytes 9437184 | tf_op jit(solution)/shard_map/hidden_rows/pallas_call | solution.py:303
  56.7 2.8 %collective-permute-start.14 = (f32[40,64]{1,0:T(8,128)S(1)}, f32[40,64]{1,0:T(8,128)S(1)}, u32[]{:S(2)}, u32[]{:S(2)}) collective-permute-start(f32[40,64]{1,0:T(8,128)S(1)} %get-tuple-element.142), channel_id=1, source_target_pairs={{0,14},{4,10},{8,6},{12,2},{14,0},{10,4},{6,8},{2,12},{1,15},{5,11... | collective-permute-start | bytes 30728 | tf_op jit(solution)/shard_map/ppermute | solution.py:372
  59.6 6.5 %partials.1 = (bf16[32,3072]{1,0:T(8,128)(2,1)S(1)}, bf16[40,3072]{1,0:T(8,128)(2,1)S(1)}, bf16[32,3072]{1,0:T(8,128)(2,1)S(1)}, bf16[40,3072]{1,0:T(8,128)(2,1)...) custom-call(bf16[3,40,768]{2,1,0:T(8,128)(2,1)S(1)} %get-tuple-eleme, ...), custom_call_target="tpu_custom_call" | custom-call | flops 6039797760 | bytes 18874368 | tf_op jit(solution)/shard_map/partials/pallas_call | solution.py:303
  74.2 1.8 %collective-permute-done.17 = bf16[40,3072]{1,0:T(8,128)(2,1)S(1)} collective-permute-done((bf16[40,3072]{1,0:T(8,128)(2,1)S(1)}, bf16[40,3072]{1,0:T(8,128)(2,1)S(1)}, u32[]{:S(2)}, u32[]{:S(2)}) %collective-permute-start.17) | collective-permute-done | bytes 245792 | tf_op jit(solution)/shard_map/ppermute | solution.py:316
  83.1 3.0 %collective-permute-done.29 = bf16[40,3072]{1,0:T(8,128)(2,1)S(1)} collective-permute-done((bf16[40,3072]{1,0:T(8,128)(2,1)S(1)}, bf16[40,3072]{1,0:T(8,128)(2,1)S(1)}, u32[]{:S(2)}, u32[]{:S(2)}) %collective-permute-start.29) | collective-permute-done | bytes 245792 | tf_op jit(solution)/shard_map/ppermute | solution.py:319
  88.4 2.1 %collective-permute-done.16.theirs = bf16[4,32,768]{2,1,0:T(8,128)(2,1)S(1)} collective-permute-done((bf16[4,32,768]{2,1,0:T(8,128)(2,1)S(1)}, bf16[4,32,768]{2,1,0:T(8,128)(2,1)S(1)}, u32[]{:S(2)}, u32[]{:S(2)}) %collective-permute-start.16) | collective-permute-done | bytes 196640 | tf_op jit(solution)/shard_map/ppermute | solution.py:421
  90.7 6.5 %collective-permute-done.30 = bf16[40,3072]{1,0:T(8,128)(2,1)S(1)} collective-permute-done((bf16[40,3072]{1,0:T(8,128)(2,1)S(1)}, bf16[40,3072]{1,0:T(8,128)(2,1)S(1)}, u32[]{:S(2)}, u32[]{:S(2)}) %collective-permute-start.30) | collective-permute-done | bytes 245792 | tf_op jit(solution)/shard_map/ppermute | solution.py:319
  97.3 2.5 %collective-permute-start.31 = (bf16[40,3072]{1,0:T(8,128)(2,1)S(1)}, bf16[40,3072]{1,0:T(8,128)(2,1)S(1)}, u32[]{:S(2)}, u32[]{:S(2)}) collective-permute-start(bf16[40,3072]{1,0:T(8,128)(2,1)S(1)} %add_convert_fusion), channel_id=1, source_target_pairs={{0,2},{4,0},{8,4},{12,8},{14,12},{10,14},{6,10},{2,6},{1,3},{5,1},... | collective-permute-start | bytes 737288 | tf_op jit(solution)/shard_map/ppermute | solution.py:319
  101.5 4.1 %collective-permute-done.27.refs_0_ = bf16[32,3072]{1,0:T(8,128)(2,1)S(1)} collective-permute-done((bf16[32,3072]{1,0:T(8,128)(2,1)S(1)}, bf16[32,3072]{1,0:T(8,128)(2,1)S(1)}, u32[]{:S(2)}, u32[]{:S(2)}) %collective-permute-start.27) | collective-permute-done | bytes 196640 | tf_op jit(solution)/shard_map/ppermute | solution.py:316
  105.6 2.4 %finish.1 = bf16[128,6144]{1,0:T(8,128)(2,1)} custom-call(s32[4,128]{1,0:T(4,128)S(1)} %bitcast.20, bf16[32,3072]{1,0:T(8,128)(2,1)S(1)} %collective-permute-done.27.refs_0_, bf16[32,3072]{1,0:T(8,128)(2,1)S(1)} %collective-permute-done.22.refs_1_, bf16[32,3072]{1,0:T(8,128)(2,1)S(1)} %get-tuple-element.194.refs_2_, ...), custom_call_target="tpu_custom_call" | custom-call | flops 400000000 | bytes 4500000 | tf_op jit(solution)/shard_map/finish/pallas_call | solution.py:303
  (104 shorter events, 31.5 us)
Async XLA Ops:
  3.6 13.6 %collective-permute-start.1 = (bf16[72,3200]{1,0:T(8,128)(2,1)S(1)}, bf16[72,3200]{1,0:T(8,128)(2,1)S(1)}, u32[]{:S(2)}, u32[]{:S(2)}) collective-permute-start(bf16[72,3200]{1,0:T(8,128)(2,1)S(1)} %prepare.1.refs_0_), channel_id=1, source_target_pairs={{0,2},{4,0},{8,4},{12,8},{14,12},{10,14},{6,10},{2,6},{1,3},{5,1},... | collective-permute-start | bytes 1382408 | tf_op jit(solution)/shard_map/ppermute | solution.py:319
  6.6 12.0 %collective-permute-start = (bf16[72,3200]{1,0:T(8,128)(2,1)S(1)}, bf16[72,3200]{1,0:T(8,128)(2,1)S(1)}, u32[]{:S(2)}, u32[]{:S(2)}) collective-permute-start(bf16[72,3200]{1,0:T(8,128)(2,1)S(1)} %prepare.1.refs_0_), channel_id=1, source_target_pairs={{0,4},{4,8},{8,12},{12,14},{14,10},{10,6},{6,2},{2,0},{1,5},{5,9},... | collective-permute-start | bytes 1382408 | tf_op jit(solution)/shard_map/ppermute | solution.py:316
  18.6 12.0 %collective-permute-start.2 = (bf16[72,3200]{1,0:T(8,128)(2,1)S(1)}, bf16[72,3200]{1,0:T(8,128)(2,1)S(1)}, u32[]{:S(2)}, u32[]{:S(2)}) collective-permute-start(bf16[72,3200]{1,0:T(8,128)(2,1)S(1)} %collective-permute-done.refs_1_), channel_id=1, source_target_pairs={{0,4},{4,8},{8,12},{12,14},{14,10},{10,6},{6,2},{2,0},{1,5},{5,9},... | collective-permute-start | bytes 1382408 | tf_op jit(solution)/shard_map/ppermute | solution.py:316
  19.0 11.6 %collective-permute-start.3 = (bf16[72,3200]{1,0:T(8,128)(2,1)S(1)}, bf16[72,3200]{1,0:T(8,128)(2,1)S(1)}, u32[]{:S(2)}, u32[]{:S(2)}) collective-permute-start(bf16[72,3200]{1,0:T(8,128)(2,1)S(1)} %collective-permute-done.1.refs_2_), channel_id=1, source_target_pairs={{0,2},{4,0},{8,4},{12,8},{14,12},{10,14},{6,10},{2,6},{1,3},{5,1},... | collective-permute-start | bytes 1382408 | tf_op jit(solution)/shard_map/ppermute | solution.py:319
  30.6 13.5 %collective-permute-start.6 = (bf16[72,3200]{1,0:T(8,128)(2,1)S(1)}, bf16[72,3200]{1,0:T(8,128)(2,1)S(1)}, u32[]{:S(2)}, u32[]{:S(2)}) collective-permute-start(bf16[72,3200]{1,0:T(8,128)(2,1)S(1)} %collective-permute-done.2.refs_0_), channel_id=1, source_target_pairs={{0,4},{4,8},{8,12},{12,14},{14,10},{10,6},{6,2},{2,0},{1,5},{5,9},... | collective-permute-start | bytes 1382408 | tf_op jit(solution)/shard_map/ppermute | solution.py:316
  32.2 12.0 %collective-permute-start.7 = (bf16[72,3200]{1,0:T(8,128)(2,1)S(1)}, bf16[72,3200]{1,0:T(8,128)(2,1)S(1)}, u32[]{:S(2)}, u32[]{:S(2)}) collective-permute-start(bf16[72,3200]{1,0:T(8,128)(2,1)S(1)} %collective-permute-done.3.refs_1_), channel_id=1, source_target_pairs={{0,2},{4,0},{8,4},{12,8},{14,12},{10,14},{6,10},{2,6},{1,3},{5,1},... | collective-permute-start | bytes 1382408 | tf_op jit(solution)/shard_map/ppermute | solution.py:319
  35.8 8.4 %collective-permute-start.8 = (f32[40,64]{1,0:T(8,128)S(1)}, f32[40,64]{1,0:T(8,128)S(1)}, u32[]{:S(2)}, u32[]{:S(2)}) collective-permute-start(f32[40,64]{1,0:T(8,128)S(1)} %get-tuple-element.128), channel_id=1, source_target_pairs={{0,6},{4,2},{8,0},{12,4},{14,8},{10,12},{6,14},{2,10},{1,7},{5,3},... | collective-permute-start | bytes 30728 | tf_op jit(solution)/shard_map/ppermute | solution.py:372
  44.2 9.7 %collective-permute-start.13 = (bf16[40,3200]{1,0:T(8,128)(2,1)S(1)}, bf16[40,3200]{1,0:T(8,128)(2,1)S(1)}, u32[]{:S(2)}, u32[]{:S(2)}) collective-permute-start(bf16[40,3200]{1,0:T(8,128)(2,1)S(1)} %get-tuple-element.137), channel_id=1, source_target_pairs={{0,2},{4,0},{8,4},{12,8},{14,12},{10,14},{6,10},{2,6},{1,3},{5,1},... | collective-permute-start | bytes 768008 | tf_op jit(solution)/shard_map/ppermute | solution.py:319
  44.6 9.2 %collective-permute-start.12 = (bf16[32,3200]{1,0:T(8,128)(2,1)S(1)}, bf16[32,3200]{1,0:T(8,128)(2,1)S(1)}, u32[]{:S(2)}, u32[]{:S(2)}) collective-permute-start(bf16[32,3200]{1,0:T(8,128)(2,1)S(1)} %get-tuple-element.136), channel_id=1, source_target_pairs={{0,4},{4,8},{8,12},{12,14},{14,10},{10,6},{6,2},{2,0},{1,5},{5,9},... | collective-permute-start | bytes 614408 | tf_op jit(solution)/shard_map/ppermute | solution.py:316
  50.0 16.2 %collective-permute-start.10 = (f32[40,64]{1,0:T(8,128)S(1)}, f32[40,64]{1,0:T(8,128)S(1)}, u32[]{:S(2)}, u32[]{:S(2)}) collective-permute-start(f32[40,64]{1,0:T(8,128)S(1)} %get-tuple-element.134), channel_id=1, source_target_pairs={{0,10},{4,6},{8,2},{12,0},{14,4},{10,8},{6,12},{2,14},{1,11},{5,7}... | collective-permute-start | bytes 30728 | tf_op jit(solution)/shard_map/ppermute | solution.py:372
  53.3 12.9 %collective-permute-start.11 = (f32[40,64]{1,0:T(8,128)S(1)}, f32[40,64]{1,0:T(8,128)S(1)}, u32[]{:S(2)}, u32[]{:S(2)}) collective-permute-start(f32[40,64]{1,0:T(8,128)S(1)} %get-tuple-element.135), channel_id=1, source_target_pairs={{0,12},{4,14},{8,10},{12,6},{14,2},{10,0},{6,4},{2,8},{1,13},{5,15... | collective-permute-start | bytes 30728 | tf_op jit(solution)/shard_map/ppermute | solution.py:372
  56.7 9.5 %collective-permute-start.14 = (f32[40,64]{1,0:T(8,128)S(1)}, f32[40,64]{1,0:T(8,128)S(1)}, u32[]{:S(2)}, u32[]{:S(2)}) collective-permute-start(f32[40,64]{1,0:T(8,128)S(1)} %get-tuple-element.142), channel_id=1, source_target_pairs={{0,14},{4,10},{8,6},{12,2},{14,0},{10,4},{6,8},{2,12},{1,15},{5,11... | collective-permute-start | bytes 30728 | tf_op jit(solution)/shard_map/ppermute | solution.py:372
  72.0 8.9 %collective-permute-start.21 = (bf16[32,3072]{1,0:T(8,128)(2,1)S(1)}, bf16[32,3072]{1,0:T(8,128)(2,1)S(1)}, u32[]{:S(2)}, u32[]{:S(2)}) collective-permute-start(bf16[32,3072]{1,0:T(8,128)(2,1)S(1)} %add_convert_fusion.9), channel_id=1, source_target_pairs={{0,2},{4,0},{8,4},{12,8},{14,12},{10,14},{6,10},{2,6},{1,3},{5,1},... | collective-permute-start | bytes 589832 | tf_op jit(solution)/shard_map/ppermute | solution.py:319
  73.2 8.7 %collective-permute-start.25 = (bf16[32,3072]{1,0:T(8,128)(2,1)S(1)}, bf16[32,3072]{1,0:T(8,128)(2,1)S(1)}, u32[]{:S(2)}, u32[]{:S(2)}) collective-permute-start(bf16[32,3072]{1,0:T(8,128)(2,1)S(1)} %add_convert_fusion.7), channel_id=1, source_target_pairs={{0,4},{4,8},{8,12},{12,14},{14,10},{10,6},{6,2},{2,0},{1,5},{5,9},... | collective-permute-start | bytes 589832 | tf_op jit(solution)/shard_map/ppermute | solution.py:316
  76.0 11.2 %collective-permute-start.18 = (bf16[40,3072]{1,0:T(8,128)(2,1)S(1)}, bf16[40,3072]{1,0:T(8,128)(2,1)S(1)}, u32[]{:S(2)}, u32[]{:S(2)}) collective-permute-start(bf16[40,3072]{1,0:T(8,128)(2,1)S(1)} %add_convert_fusion.4), channel_id=1, source_target_pairs={{0,4},{4,8},{8,12},{12,14},{14,10},{10,6},{6,2},{2,0},{1,5},{5,9},... | collective-permute-start | bytes 737288 | tf_op jit(solution)/shard_map/ppermute | solution.py:316
  77.1 9.0 %collective-permute-start.29 = (bf16[40,3072]{1,0:T(8,128)(2,1)S(1)}, bf16[40,3072]{1,0:T(8,128)(2,1)S(1)}, u32[]{:S(2)}, u32[]{:S(2)}) collective-permute-start(bf16[40,3072]{1,0:T(8,128)(2,1)S(1)} %add_convert_fusion.2), channel_id=1, source_target_pairs={{0,2},{4,0},{8,4},{12,8},{14,12},{10,14},{6,10},{2,6},{1,3},{5,1},... | collective-permute-start | bytes 737288 | tf_op jit(solution)/shard_map/ppermute | solution.py:319
  78.3 12.2 %collective-permute-start.16 = (bf16[4,32,768]{2,1,0:T(8,128)(2,1)S(1)}, bf16[4,32,768]{2,1,0:T(8,128)(2,1)S(1)}, u32[]{:S(2)}, u32[]{:S(2)}) collective-permute-start(bf16[4,32,768]{2,1,0:T(8,128)(2,1)S(1)} %get-tuple-element.178), channel_id=1, source_target_pairs={{0,2},{2,0},{4,6},{6,4},{8,10},{10,8},{12,14},{14,12},{1,3},{3,1},... | collective-permute-start | bytes 589832 | tf_op jit(solution)/shard_map/ppermute | solution.py:421
  80.9 19.0 %collective-permute-start.22 = (bf16[32,3072]{1,0:T(8,128)(2,1)S(1)}, bf16[32,3072]{1,0:T(8,128)(2,1)S(1)}, u32[]{:S(2)}, u32[]{:S(2)}) collective-permute-start(bf16[32,3072]{1,0:T(8,128)(2,1)S(1)} %add_convert_fusion.8), channel_id=1, source_target_pairs={{0,2},{4,0},{8,4},{12,8},{14,12},{10,14},{6,10},{2,6},{1,3},{5,1},... | collective-permute-start | bytes 589832 | tf_op jit(solution)/shard_map/ppermute | solution.py:319
  81.9 17.9 %collective-permute-start.26 = (bf16[32,3072]{1,0:T(8,128)(2,1)S(1)}, bf16[32,3072]{1,0:T(8,128)(2,1)S(1)}, u32[]{:S(2)}, u32[]{:S(2)}) collective-permute-start(bf16[32,3072]{1,0:T(8,128)(2,1)S(1)} %add_convert_fusion.6), channel_id=1, source_target_pairs={{0,4},{4,8},{8,12},{12,14},{14,10},{10,6},{6,2},{2,0},{1,5},{5,9},... | collective-permute-start | bytes 589832 | tf_op jit(solution)/shard_map/ppermute | solution.py:316
  86.2 11.0 %collective-permute-start.30 = (bf16[40,3072]{1,0:T(8,128)(2,1)S(1)}, bf16[40,3072]{1,0:T(8,128)(2,1)S(1)}, u32[]{:S(2)}, u32[]{:S(2)}) collective-permute-start(bf16[40,3072]{1,0:T(8,128)(2,1)S(1)} %add_convert_fusion.1), channel_id=1, source_target_pairs={{0,2},{4,0},{8,4},{12,8},{14,12},{10,14},{6,10},{2,6},{1,3},{5,1},... | collective-permute-start | bytes 737288 | tf_op jit(solution)/shard_map/ppermute | solution.py:319
  87.2 12.7 %collective-permute-start.19 = (bf16[40,3072]{1,0:T(8,128)(2,1)S(1)}, bf16[40,3072]{1,0:T(8,128)(2,1)S(1)}, u32[]{:S(2)}, u32[]{:S(2)}) collective-permute-start(bf16[40,3072]{1,0:T(8,128)(2,1)S(1)} %add_convert_fusion.3), channel_id=1, source_target_pairs={{0,4},{4,8},{8,12},{12,14},{14,10},{10,6},{6,2},{2,0},{1,5},{5,9},... | collective-permute-start | bytes 737288 | tf_op jit(solution)/shard_map/ppermute | solution.py:316
  90.6 9.4 %collective-permute-start.23 = (bf16[2,32,768]{2,1,0:T(8,128)(2,1)S(1)}, bf16[2,32,768]{2,1,0:T(8,128)(2,1)S(1)}, u32[]{:S(2)}, u32[]{:S(2)}) collective-permute-start(bf16[2,32,768]{2,1,0:T(8,128)(2,1)S(1)} %get-tuple-element.187), channel_id=1, source_target_pairs={{0,4},{2,6},{4,0},{6,2},{8,12},{10,14},{12,8},{14,10},{1,5},{3,7},... | collective-permute-start | bytes 294920 | tf_op jit(solution)/shard_map/ppermute | solution.py:421
  97.3 8.3 %collective-permute-start.31 = (bf16[40,3072]{1,0:T(8,128)(2,1)S(1)}, bf16[40,3072]{1,0:T(8,128)(2,1)S(1)}, u32[]{:S(2)}, u32[]{:S(2)}) collective-permute-start(bf16[40,3072]{1,0:T(8,128)(2,1)S(1)} %add_convert_fusion), channel_id=1, source_target_pairs={{0,2},{4,0},{8,4},{12,8},{14,12},{10,14},{6,10},{2,6},{1,3},{5,1},... | collective-permute-start | bytes 737288 | tf_op jit(solution)/shard_map/ppermute | solution.py:319
  100.4 7.7 %collective-permute-start.34 = (bf16[128,768]{1,0:T(8,128)(2,1)S(1)}, bf16[128,768]{1,0:T(8,128)(2,1)S(1)}, u32[]{:S(2)}, u32[]{:S(2)}) collective-permute-start(bf16[128,768]{1,0:T(8,128)(2,1)S(1)} %lora_rows.1.lora_ref), channel_id=1, source_target_pairs={{0,1},{1,0},{2,3},{3,2},{4,5},{5,4},{6,7},{7,6},{8,9},{9,8},{10,11... | collective-permute-start | bytes 589832 | tf_op jit(solution)/shard_map/ppermute | solution.py:471
  (26 other events, 260.1 us)

commit v15 on v14

--- a/solution.py
+++ b/solution.py
@@ -393,14 +393,14 @@
     right_top, left_rest = right(right_top), left(left_rest)
     before = len(lows)
     hidden_pass(passes[-2])
-    for at in range(max(before, 1), len(lows)):
-        to_owner(at)
     right_top, left_rest, dgates[-1], dups[-1] = lax.optimization_barrier(
         (right_top, left_rest, dgates[-1], dups[-1])
     )
     got[middle] = (right_top, left_rest)
     hidden_pass(passes[-1])
-    to_owner(n - 1)
+    lows[before:] = lax.optimization_barrier(lows[before:])
+    for at in range(max(before, 1), n):
+        to_owner(at)
 
     own = call(
         functools.partial(partial_kernel, capacity, slot, sizes, cut),

time: 110 us -> 112 us (1.018)
  waiting for transfers between devices: 35.2 us -> 36.4 us
    ppermute x11, starting transfers between devices: 14.3 us -> 16.1 us  [left(): return lax.ppermute(x, 'expert', to_left)]
    ppermute x3, starting transfers between devices: 2.63 us -> 1.5 us  [exchange(): other = lax.ppermute(send, 'expert', [(e, e ^ bit) for e in range(n)])]
  transfers between devices with their start and end apart: 35 -> 35, of which waited for: 12 -> 14; matrix products, arithmetic and copies ran while one was open for 0% -> 0% of each run, Pallas kernels for 20% -> 18%
where the time goes in v15:
time: 112 us
  starting transfers between devices  40.1 us (36%)
  waiting for transfers between devices  36.4 us (32%)
  Pallas kernels  26.2 us (23%)
  local copies, waits for them, and re-layouts  7.54 us (7%)
    pallas_call x16, Pallas kernels, call(): pl.pallas_call(kernel, out_shape=[jax.ShapeDtypeStruct(shape, dtype) for...  26.2 us
    ppermute x11, starting transfers between devices, left(): return lax.ppermute(x, 'expert', to_left)  16.1 us
    ppermute x11, waiting for transfers between devices, left(): return lax.ppermute(x, 'expert', to_left)  15.4 us
    ppermute x7, starting transfers between devices, to_owner(): lax.ppermute(lows[at], 'expert', [(ring[i], ring[(i + r) % n]) for i in r...  12.3 us
    ppermute x7, waiting for transfers between devices, to_owner(): lax.ppermute(lows[at], 'expert', [(ring[i], ring[(i + r) % n]) for i in r...  10.3 us
    ppermute x11, starting transfers between devices, right(): return lax.ppermute(x, 'expert', to_right)  10 us
    ppermute x11, waiting for transfers between devices, right(): return lax.ppermute(x, 'expert', to_right)  7.77 us
    unnamed x30, local copies, waits for them, and re-layouts  7.54 us
  transfers between devices with their start and end apart: 35, of which 14 were waited for; matrix products, arithmetic and copies ran while one was open for 0% of the time, Pallas kernels for 18%

profile of v15, /device:TPU:0, one launch (start us, length us, event | category | flops | bytes accessed | tf_op | source)
XLA Modules:
  0.0 111.8 jit_solution(16421892254422225607)
XLA Ops:
  0.6 2.9 %prepare.1.refs_0_ = bf16[72,3200]{1,0:T(8,128)(2,1)S(1)} custom-call(s32[4,128]{1,0:T(4,128)} %bitcast.18, bf16[4,128]{1,0:T(4,128)(2,1)} %bitcast.27, bf16[128,6144]{1,0:T(8,128)(2,1)} %bitcast.26, bf16[128,6144]{1,0:T(8,128)(2,1)} %bitcast.12, bf16[64,6144]{1,0:T(8,128)(2,1)} %refs_7_.3), custom_call_target="tpu_custom_call" | custom-call | flops 400000000 | bytes 4500000 | tf_op jit(solution)/shard_map/prepare/pallas_call | solution.py:303
  3.6 3.0 %collective-permute-start.1 = (bf16[72,3200]{1,0:T(8,128)(2,1)S(1)}, bf16[72,3200]{1,0:T(8,128)(2,1)S(1)}, u32[]{:S(2)}, u32[]{:S(2)}) collective-permute-start(bf16[72,3200]{1,0:T(8,128)(2,1)S(1)} %prepare.1.refs_0_), channel_id=1, source_target_pairs={{0,2},{4,0},{8,4},{12,8},{14,12},{10,14},{6,10},{2,6},{1,3},{5,1},... | collective-permute-start | bytes 1382408 | tf_op jit(solution)/shard_map/ppermute | solution.py:319
  6.7 3.7 %copy-done = bf16[768,6144]{1,0:T(8,128)(2,1)S(1)} copy-done((bf16[768,6144]{1,0:T(8,128)(2,1)S(1)}, bf16[768,6144]{1,0:T(8,128)(2,1)}, u32[]{:S(2)}) %copy-start) | copy-done | bytes 9437208
  14.4 2.8 %collective-permute-done.1.refs_2_ = bf16[72,3200]{1,0:T(8,128)(2,1)S(1)} collective-permute-done((bf16[72,3200]{1,0:T(8,128)(2,1)S(1)}, bf16[72,3200]{1,0:T(8,128)(2,1)S(1)}, u32[]{:S(2)}, u32[]{:S(2)}) %collective-permute-start.1) | collective-permute-done | bytes 460832 | tf_op jit(solution)/shard_map/ppermute | solution.py:319
  19.0 1.6 %collective-permute-start.3 = (bf16[72,3200]{1,0:T(8,128)(2,1)S(1)}, bf16[72,3200]{1,0:T(8,128)(2,1)S(1)}, u32[]{:S(2)}, u32[]{:S(2)}) collective-permute-start(bf16[72,3200]{1,0:T(8,128)(2,1)S(1)} %collective-permute-done.1.refs_2_), channel_id=1, source_target_pairs={{0,2},{4,0},{8,4},{12,8},{14,12},{10,14},{6,10},{2,6},{1,3},{5,1},... | collective-permute-start | bytes 1382408 | tf_op jit(solution)/shard_map/ppermute | solution.py:319
  20.6 3.0 %hidden_rows.4 = (bf16[3,40,768]{2,1,0:T(8,128)(2,1)S(1)}, bf16[3,40,768]{2,1,0:T(8,128)(2,1)S(1)}, bf16[3,40,64]{2,1,0:T(8,128)(2,1)S(1)}, f32[40,64]{1,0:T(8,1...) custom-call(bf16[72,3200]{1,0:T(8,128)(2,1)S(1)} %prepare.1.refs_0_, ...), custom_call_target="tpu_custom_call" | custom-call | flops 2264924160 | bytes 9437184 | tf_op jit(solution)/shard_map/hidden_rows/pallas_call | solution.py:303
  25.7 4.9 %collective-permute-done.4.refs_1_ = f32[40,64]{1,0:T(8,128)S(1)} collective-permute-done((f32[40,64]{1,0:T(8,128)S(1)}, f32[40,64]{1,0:T(8,128)S(1)}, u32[]{:S(2)}, u32[]{:S(2)}) %collective-permute-start.4) | collective-permute-done | bytes 10272 | tf_op jit(solution)/shard_map/ppermute | solution.py:372
  32.7 3.1 %hidden_rows.5 = (bf16[2,40,768]{2,1,0:T(8,128)(2,1)S(1)}, bf16[2,40,768]{2,1,0:T(8,128)(2,1)S(1)}, bf16[2,40,64]{2,1,0:T(8,128)(2,1)S(1)}, f32[40,64]{1,0:T(8,128)S(1)}, f32[40,64]{1,0:T(8,128)S(1)}) custom-call(bf16[72,3200]{1,0:T(8,128)(2,1)S(1)} %collective-permute-done.2.refs_0_, bf16[72,3200]{1,0:T(8,128)(2,1)S(1)} %collective-permute-done.3.refs_1_, ...), custom_call_target="tpu_custom_call" | custom-call | flops 2415919104 | bytes 9437184 | tf_op jit(solution)/shard_map/hidden_rows/pallas_call | solution.py:303
  35.8 2.4 %collective-permute-start.8 = (f32[40,64]{1,0:T(8,128)S(1)}, f32[40,64]{1,0:T(8,128)S(1)}, u32[]{:S(2)}, u32[]{:S(2)}) collective-permute-start(f32[40,64]{1,0:T(8,128)S(1)} %get-tuple-element.131), channel_id=1, source_target_pairs={{0,6},{4,2},{8,0},{12,4},{14,8},{10,12},{6,14},{2,10},{1,7},{5,3},... | collective-permute-start | bytes 30728 | tf_op jit(solution)/shard_map/ppermute | solution.py:372
  38.8 5.4 %collective-permute-done.8.refs_3_ = f32[40,64]{1,0:T(8,128)S(1)} collective-permute-done((f32[40,64]{1,0:T(8,128)S(1)}, f32[40,64]{1,0:T(8,128)S(1)}, u32[]{:S(2)}, u32[]{:S(2)}) %collective-permute-start.8) | collective-permute-done | bytes 10272 | tf_op jit(solution)/shard_map/ppermute | solution.py:372
  44.6 2.2 %collective-permute-start.10 = (bf16[32,3200]{1,0:T(8,128)(2,1)S(1)}, bf16[32,3200]{1,0:T(8,128)(2,1)S(1)}, u32[]{:S(2)}, u32[]{:S(2)}) collective-permute-start(bf16[32,3200]{1,0:T(8,128)(2,1)S(1)} %get-tuple-element.139), channel_id=1, source_target_pairs={{0,4},{4,8},{8,12},{12,14},{14,10},{10,6},{6,2},{2,0},{1,5},{5,9},... | collective-permute-start | bytes 614408 | tf_op jit(solution)/shard_map/ppermute | solution.py:316
  46.9 3.1 %hidden_rows.6 = (bf16[2,40,768]{2,1,0:T(8,128)(2,1)S(1)}, bf16[2,40,768]{2,1,0:T(8,128)(2,1)S(1)}, bf16[2,40,64]{2,1,0:T(8,128)(2,1)S(1)}, f32[40,64]{1,0:T(8,128)S(1)}, f32[40,64]{1,0:T(8,128)S(1)}) custom-call(bf16[72,3200]{1,0:T(8,128)(2,1)S(1)} %collective-permute-done.6.refs_0_.right_in, bf16[72,3200]{1,0:T(8,128)(2,1)S(1)} %collective-permute-done.7.refs_1_.left_in, ...), custom_call_target="tpu_custom_call" | custom-call | flops 2415919104 | bytes 9437184 | tf_op jit(solution)/shard_map/hidden_rows/pallas_call | solution.py:303
  51.1 2.9 %hidden_rows.7 = (bf16[1,40,768]{2,1,0:T(8,128)(2,1)S(1)}, bf16[1,40,768]{2,1,0:T(8,128)(2,1)S(1)}, bf16[1,40,64]{2,1,0:T(8,128)(2,1)S(1)}, f32[40,64]{1,0:T(8,128)S(1)}) custom-call(bf16[32,3200]{1,0:T(8,128)(2,1)S(1)} %collective-permute-done.10.refs_0_, bf16[40,3200]{1,0:T(8,128)(2,1)S(1)} %collective-permute-done.11.refs_1_, ...), custom_call_target="tpu_custom_call" | custom-call | flops 1207959552 | bytes 9437184 | tf_op jit(solution)/shard_map/hidden_rows/pallas_call | solution.py:303
  54.0 3.4 %collective-permute-start.12 = (f32[40,64]{1,0:T(8,128)S(1)}, f32[40,64]{1,0:T(8,128)S(1)}, u32[]{:S(2)}, u32[]{:S(2)}) collective-permute-start(f32[40,64]{1,0:T(8,128)S(1)} %get-tuple-element.146), channel_id=1, source_target_pairs={{0,10},{4,6},{8,2},{12,0},{14,4},{10,8},{6,12},{2,14},{1,11},{5,7}... | collective-permute-start | bytes 30728 | tf_op jit(solution)/shard_map/ppermute | solution.py:372
  57.8 3.4 %collective-permute-start.14 = (f32[40,64]{1,0:T(8,128)S(1)}, f32[40,64]{1,0:T(8,128)S(1)}, u32[]{:S(2)}, u32[]{:S(2)}) collective-permute-start(f32[40,64]{1,0:T(8,128)S(1)} %get-tuple-element.148), channel_id=1, source_target_pairs={{0,14},{4,10},{8,6},{12,2},{14,0},{10,4},{6,8},{2,12},{1,15},{5,11... | collective-permute-start | bytes 30728 | tf_op jit(solution)/shard_map/ppermute | solution.py:372
  61.3 6.5 %partials.1 = (bf16[32,3072]{1,0:T(8,128)(2,1)S(1)}, bf16[40,3072]{1,0:T(8,128)(2,1)S(1)}, bf16[32,3072]{1,0:T(8,128)(2,1)S(1)}, bf16[40,3072]{1,0:T(8,128)(2,1)...) custom-call(bf16[3,40,768]{2,1,0:T(8,128)(2,1)S(1)} %get-tuple-eleme, ...), custom_call_target="tpu_custom_call" | custom-call | flops 6039797760 | bytes 18874368 | tf_op jit(solution)/shard_map/partials/pallas_call | solution.py:303
  81.6 2.5 %collective-permute-start.22 = (bf16[32,3072]{1,0:T(8,128)(2,1)S(1)}, bf16[32,3072]{1,0:T(8,128)(2,1)S(1)}, u32[]{:S(2)}, u32[]{:S(2)}) collective-permute-start(bf16[32,3072]{1,0:T(8,128)(2,1)S(1)} %add_convert_fusion.8), channel_id=1, source_target_pairs={{0,2},{4,0},{8,4},{12,8},{14,12},{10,14},{6,10},{2,6},{1,3},{5,1},... | collective-permute-start | bytes 589832 | tf_op jit(solution)/shard_map/ppermute | solution.py:319
  84.2 3.5 %collective-permute-done.29 = bf16[40,3072]{1,0:T(8,128)(2,1)S(1)} collective-permute-done((bf16[40,3072]{1,0:T(8,128)(2,1)S(1)}, bf16[40,3072]{1,0:T(8,128)(2,1)S(1)}, u32[]{:S(2)}, u32[]{:S(2)}) %collective-permute-start.29) | collective-permute-done | bytes 245792 | tf_op jit(solution)/shard_map/ppermute | solution.py:319
  87.8 1.6 %collective-permute-start.30 = (bf16[40,3072]{1,0:T(8,128)(2,1)S(1)}, bf16[40,3072]{1,0:T(8,128)(2,1)S(1)}, u32[]{:S(2)}, u32[]{:S(2)}) collective-permute-start(bf16[40,3072]{1,0:T(8,128)(2,1)S(1)} %add_convert_fusion.1), channel_id=1, source_target_pairs={{0,2},{4,0},{8,4},{12,8},{14,12},{10,14},{6,10},{2,6},{1,3},{5,1},... | collective-permute-start | bytes 737288 | tf_op jit(solution)/shard_map/ppermute | solution.py:319
  90.0 1.7 %collective-permute-done.16.theirs = bf16[4,32,768]{2,1,0:T(8,128)(2,1)S(1)} collective-permute-done((bf16[4,32,768]{2,1,0:T(8,128)(2,1)S(1)}, bf16[4,32,768]{2,1,0:T(8,128)(2,1)S(1)}, u32[]{:S(2)}, u32[]{:S(2)}) %collective-permute-start.16) | collective-permute-done | bytes 196640 | tf_op jit(solution)/shard_map/ppermute | solution.py:421
  91.8 7.0 %collective-permute-done.30 = bf16[40,3072]{1,0:T(8,128)(2,1)S(1)} collective-permute-done((bf16[40,3072]{1,0:T(8,128)(2,1)S(1)}, bf16[40,3072]{1,0:T(8,128)(2,1)S(1)}, u32[]{:S(2)}, u32[]{:S(2)}) %collective-permute-start.30) | collective-permute-done | bytes 245792 | tf_op jit(solution)/shard_map/ppermute | solution.py:319
  98.9 2.5 %collective-permute-start.31 = (bf16[40,3072]{1,0:T(8,128)(2,1)S(1)}, bf16[40,3072]{1,0:T(8,128)(2,1)S(1)}, u32[]{:S(2)}, u32[]{:S(2)}) collective-permute-start(bf16[40,3072]{1,0:T(8,128)(2,1)S(1)} %add_convert_fusion), channel_id=1, source_target_pairs={{0,2},{4,0},{8,4},{12,8},{14,12},{10,14},{6,10},{2,6},{1,3},{5,1},... | collective-permute-start | bytes 737288 | tf_op jit(solution)/shard_map/ppermute | solution.py:319
  102.6 4.7 %collective-permute-done.27.refs_0_ = bf16[32,3072]{1,0:T(8,128)(2,1)S(1)} collective-permute-done((bf16[32,3072]{1,0:T(8,128)(2,1)S(1)}, bf16[32,3072]{1,0:T(8,128)(2,1)S(1)}, u32[]{:S(2)}, u32[]{:S(2)}) %collective-permute-start.27) | collective-permute-done | bytes 196640 | tf_op jit(solution)/shard_map/ppermute | solution.py:316
  107.2 2.4 %finish.1 = bf16[128,6144]{1,0:T(8,128)(2,1)} custom-call(s32[4,128]{1,0:T(4,128)S(1)} %bitcast.20, bf16[32,3072]{1,0:T(8,128)(2,1)S(1)} %collective-permute-done.27.refs_0_, bf16[32,3072]{1,0:T(8,128)(2,1)S(1)} %collective-permute-done.22.refs_1_, bf16[32,3072]{1,0:T(8,128)(2,1)S(1)} %get-tuple-element.200.refs_2_, ...), custom_call_target="tpu_custom_call" | custom-call | flops 400000000 | bytes 4500000 | tf_op jit(solution)/shard_map/finish/pallas_call | solution.py:303
  (104 shorter events, 30.5 us)
Async XLA Ops:
  3.6 13.6 %collective-permute-start.1 = (bf16[72,3200]{1,0:T(8,128)(2,1)S(1)}, bf16[72,3200]{1,0:T(8,128)(2,1)S(1)}, u32[]{:S(2)}, u32[]{:S(2)}) collective-permute-start(bf16[72,3200]{1,0:T(8,128)(2,1)S(1)} %prepare.1.refs_0_), channel_id=1, source_target_pairs={{0,2},{4,0},{8,4},{12,8},{14,12},{10,14},{6,10},{2,6},{1,3},{5,1},... | collective-permute-start | bytes 1382408 | tf_op jit(solution)/shard_map/ppermute | solution.py:319
  6.6 12.0 %collective-permute-start = (bf16[72,3200]{1,0:T(8,128)(2,1)S(1)}, bf16[72,3200]{1,0:T(8,128)(2,1)S(1)}, u32[]{:S(2)}, u32[]{:S(2)}) collective-permute-start(bf16[72,3200]{1,0:T(8,128)(2,1)S(1)} %prepare.1.refs_0_), channel_id=1, source_target_pairs={{0,4},{4,8},{8,12},{12,14},{14,10},{10,6},{6,2},{2,0},{1,5},{5,9},... | collective-permute-start | bytes 1382408 | tf_op jit(solution)/shard_map/ppermute | solution.py:316
  18.6 12.0 %collective-permute-start.2 = (bf16[72,3200]{1,0:T(8,128)(2,1)S(1)}, bf16[72,3200]{1,0:T(8,128)(2,1)S(1)}, u32[]{:S(2)}, u32[]{:S(2)}) collective-permute-start(bf16[72,3200]{1,0:T(8,128)(2,1)S(1)} %collective-permute-done.refs_1_), channel_id=1, source_target_pairs={{0,4},{4,8},{8,12},{12,14},{14,10},{10,6},{6,2},{2,0},{1,5},{5,9},... | collective-permute-start | bytes 1382408 | tf_op jit(solution)/shard_map/ppermute | solution.py:316
  19.0 11.6 %collective-permute-start.3 = (bf16[72,3200]{1,0:T(8,128)(2,1)S(1)}, bf16[72,3200]{1,0:T(8,128)(2,1)S(1)}, u32[]{:S(2)}, u32[]{:S(2)}) collective-permute-start(bf16[72,3200]{1,0:T(8,128)(2,1)S(1)} %collective-permute-done.1.refs_2_), channel_id=1, source_target_pairs={{0,2},{4,0},{8,4},{12,8},{14,12},{10,14},{6,10},{2,6},{1,3},{5,1},... | collective-permute-start | bytes 1382408 | tf_op jit(solution)/shard_map/ppermute | solution.py:319
  30.6 13.5 %collective-permute-start.6 = (bf16[72,3200]{1,0:T(8,128)(2,1)S(1)}, bf16[72,3200]{1,0:T(8,128)(2,1)S(1)}, u32[]{:S(2)}, u32[]{:S(2)}) collective-permute-start(bf16[72,3200]{1,0:T(8,128)(2,1)S(1)} %collective-permute-done.2.refs_0_), channel_id=1, source_target_pairs={{0,4},{4,8},{8,12},{12,14},{14,10},{10,6},{6,2},{2,0},{1,5},{5,9},... | collective-permute-start | bytes 1382408 | tf_op jit(solution)/shard_map/ppermute | solution.py:316
  32.2 12.0 %collective-permute-start.7 = (bf16[72,3200]{1,0:T(8,128)(2,1)S(1)}, bf16[72,3200]{1,0:T(8,128)(2,1)S(1)}, u32[]{:S(2)}, u32[]{:S(2)}) collective-permute-start(bf16[72,3200]{1,0:T(8,128)(2,1)S(1)} %collective-permute-done.3.refs_1_), channel_id=1, source_target_pairs={{0,2},{4,0},{8,4},{12,8},{14,12},{10,14},{6,10},{2,6},{1,3},{5,1},... | collective-permute-start | bytes 1382408 | tf_op jit(solution)/shard_map/ppermute | solution.py:319
  35.8 8.4 %collective-permute-start.8 = (f32[40,64]{1,0:T(8,128)S(1)}, f32[40,64]{1,0:T(8,128)S(1)}, u32[]{:S(2)}, u32[]{:S(2)}) collective-permute-start(f32[40,64]{1,0:T(8,128)S(1)} %get-tuple-element.131), channel_id=1, source_target_pairs={{0,6},{4,2},{8,0},{12,4},{14,8},{10,12},{6,14},{2,10},{1,7},{5,3},... | collective-permute-start | bytes 30728 | tf_op jit(solution)/shard_map/ppermute | solution.py:372
  54.0 13.9 %collective-permute-start.12 = (f32[40,64]{1,0:T(8,128)S(1)}, f32[40,64]{1,0:T(8,128)S(1)}, u32[]{:S(2)}, u32[]{:S(2)}) collective-permute-start(f32[40,64]{1,0:T(8,128)S(1)} %get-tuple-element.146), channel_id=1, source_target_pairs={{0,10},{4,6},{8,2},{12,0},{14,4},{10,8},{6,12},{2,14},{1,11},{5,7}... | collective-permute-start | bytes 30728 | tf_op jit(solution)/shard_map/ppermute | solution.py:372
  57.3 10.5 %collective-permute-start.13 = (f32[40,64]{1,0:T(8,128)S(1)}, f32[40,64]{1,0:T(8,128)S(1)}, u32[]{:S(2)}, u32[]{:S(2)}) collective-permute-start(f32[40,64]{1,0:T(8,128)S(1)} %get-tuple-element.147), channel_id=1, source_target_pairs={{0,12},{4,14},{8,10},{12,6},{14,2},{10,0},{6,4},{2,8},{1,13},{5,15... | collective-permute-start | bytes 30728 | tf_op jit(solution)/shard_map/ppermute | solution.py:372
  57.8 10.0 %collective-permute-start.14 = (f32[40,64]{1,0:T(8,128)S(1)}, f32[40,64]{1,0:T(8,128)S(1)}, u32[]{:S(2)}, u32[]{:S(2)}) collective-permute-start(f32[40,64]{1,0:T(8,128)S(1)} %get-tuple-element.148), channel_id=1, source_target_pairs={{0,14},{4,10},{8,6},{12,2},{14,0},{10,4},{6,8},{2,12},{1,15},{5,11... | collective-permute-start | bytes 30728 | tf_op jit(solution)/shard_map/ppermute | solution.py:372
  70.5 8.2 %collective-permute-start.28 = (bf16[40,3072]{1,0:T(8,128)(2,1)S(1)}, bf16[40,3072]{1,0:T(8,128)(2,1)S(1)}, u32[]{:S(2)}, u32[]{:S(2)}) collective-permute-start(bf16[40,3072]{1,0:T(8,128)(2,1)S(1)} %get-tuple-element.202), channel_id=1, source_target_pairs={{0,2},{4,0},{8,4},{12,8},{14,12},{10,14},{6,10},{2,6},{1,3},{5,1},... | collective-permute-start | bytes 737288 | tf_op jit(solution)/shard_map/ppermute | solution.py:319
  73.6 7.9 %collective-permute-start.21 = (bf16[32,3072]{1,0:T(8,128)(2,1)S(1)}, bf16[32,3072]{1,0:T(8,128)(2,1)S(1)}, u32[]{:S(2)}, u32[]{:S(2)}) collective-permute-start(bf16[32,3072]{1,0:T(8,128)(2,1)S(1)} %add_convert_fusion.9), channel_id=1, source_target_pairs={{0,2},{4,0},{8,4},{12,8},{14,12},{10,14},{6,10},{2,6},{1,3},{5,1},... | collective-permute-start | bytes 589832 | tf_op jit(solution)/shard_map/ppermute | solution.py:319
  74.3 9.8 %collective-permute-start.25 = (bf16[32,3072]{1,0:T(8,128)(2,1)S(1)}, bf16[32,3072]{1,0:T(8,128)(2,1)S(1)}, u32[]{:S(2)}, u32[]{:S(2)}) collective-permute-start(bf16[32,3072]{1,0:T(8,128)(2,1)S(1)} %add_convert_fusion.7), channel_id=1, source_target_pairs={{0,4},{4,8},{8,12},{12,14},{14,10},{10,6},{6,2},{2,0},{1,5},{5,9},... | collective-permute-start | bytes 589832 | tf_op jit(solution)/shard_map/ppermute | solution.py:316
  77.2 12.2 %collective-permute-start.18 = (bf16[40,3072]{1,0:T(8,128)(2,1)S(1)}, bf16[40,3072]{1,0:T(8,128)(2,1)S(1)}, u32[]{:S(2)}, u32[]{:S(2)}) collective-permute-start(bf16[40,3072]{1,0:T(8,128)(2,1)S(1)} %add_convert_fusion.4), channel_id=1, source_target_pairs={{0,4},{4,8},{8,12},{12,14},{14,10},{10,6},{6,2},{2,0},{1,5},{5,9},... | collective-permute-start | bytes 737288 | tf_op jit(solution)/shard_map/ppermute | solution.py:316
  78.8 8.9 %collective-permute-start.29 = (bf16[40,3072]{1,0:T(8,128)(2,1)S(1)}, bf16[40,3072]{1,0:T(8,128)(2,1)S(1)}, u32[]{:S(2)}, u32[]{:S(2)}) collective-permute-start(bf16[40,3072]{1,0:T(8,128)(2,1)S(1)} %add_convert_fusion.2), channel_id=1, source_target_pairs={{0,2},{4,0},{8,4},{12,8},{14,12},{10,14},{6,10},{2,6},{1,3},{5,1},... | collective-permute-start | bytes 737288 | tf_op jit(solution)/shard_map/ppermute | solution.py:319
  80.0 11.7 %collective-permute-start.16 = (bf16[4,32,768]{2,1,0:T(8,128)(2,1)S(1)}, bf16[4,32,768]{2,1,0:T(8,128)(2,1)S(1)}, u32[]{:S(2)}, u32[]{:S(2)}) collective-permute-start(bf16[4,32,768]{2,1,0:T(8,128)(2,1)S(1)} %get-tuple-element.184), channel_id=1, source_target_pairs={{0,2},{2,0},{4,6},{6,4},{8,10},{10,8},{12,14},{14,12},{1,3},{3,1},... | collective-permute-start | bytes 589832 | tf_op jit(solution)/shard_map/ppermute | solution.py:421
  81.6 20.0 %collective-permute-start.22 = (bf16[32,3072]{1,0:T(8,128)(2,1)S(1)}, bf16[32,3072]{1,0:T(8,128)(2,1)S(1)}, u32[]{:S(2)}, u32[]{:S(2)}) collective-permute-start(bf16[32,3072]{1,0:T(8,128)(2,1)S(1)} %add_convert_fusion.8), channel_id=1, source_target_pairs={{0,2},{4,0},{8,4},{12,8},{14,12},{10,14},{6,10},{2,6},{1,3},{5,1},... | collective-permute-start | bytes 589832 | tf_op jit(solution)/shard_map/ppermute | solution.py:319
  84.2 17.3 %collective-permute-start.26 = (bf16[32,3072]{1,0:T(8,128)(2,1)S(1)}, bf16[32,3072]{1,0:T(8,128)(2,1)S(1)}, u32[]{:S(2)}, u32[]{:S(2)}) collective-permute-start(bf16[32,3072]{1,0:T(8,128)(2,1)S(1)} %add_convert_fusion.6), channel_id=1, source_target_pairs={{0,4},{4,8},{8,12},{12,14},{14,10},{10,6},{6,2},{2,0},{1,5},{5,9},... | collective-permute-start | bytes 589832 | tf_op jit(solution)/shard_map/ppermute | solution.py:316
  87.8 11.1 %collective-permute-start.30 = (bf16[40,3072]{1,0:T(8,128)(2,1)S(1)}, bf16[40,3072]{1,0:T(8,128)(2,1)S(1)}, u32[]{:S(2)}, u32[]{:S(2)}) collective-permute-start(bf16[40,3072]{1,0:T(8,128)(2,1)S(1)} %add_convert_fusion.1), channel_id=1, source_target_pairs={{0,2},{4,0},{8,4},{12,8},{14,12},{10,14},{6,10},{2,6},{1,3},{5,1},... | collective-permute-start | bytes 737288 | tf_op jit(solution)/shard_map/ppermute | solution.py:319
  89.4 12.1 %collective-permute-start.19 = (bf16[40,3072]{1,0:T(8,128)(2,1)S(1)}, bf16[40,3072]{1,0:T(8,128)(2,1)S(1)}, u32[]{:S(2)}, u32[]{:S(2)}) collective-permute-start(bf16[40,3072]{1,0:T(8,128)(2,1)S(1)} %add_convert_fusion.3), channel_id=1, source_target_pairs={{0,4},{4,8},{8,12},{12,14},{14,10},{10,6},{6,2},{2,0},{1,5},{5,9},... | collective-permute-start | bytes 737288 | tf_op jit(solution)/shard_map/ppermute | solution.py:316
  91.7 9.9 %collective-permute-start.23 = (bf16[2,32,768]{2,1,0:T(8,128)(2,1)S(1)}, bf16[2,32,768]{2,1,0:T(8,128)(2,1)S(1)}, u32[]{:S(2)}, u32[]{:S(2)}) collective-permute-start(bf16[2,32,768]{2,1,0:T(8,128)(2,1)S(1)} %get-tuple-element.193), channel_id=1, source_target_pairs={{0,4},{2,6},{4,0},{6,2},{8,12},{10,14},{12,8},{14,10},{1,5},{3,7},... | collective-permute-start | bytes 294920 | tf_op jit(solution)/shard_map/ppermute | solution.py:421
  98.9 8.3 %collective-permute-start.31 = (bf16[40,3072]{1,0:T(8,128)(2,1)S(1)}, bf16[40,3072]{1,0:T(8,128)(2,1)S(1)}, u32[]{:S(2)}, u32[]{:S(2)}) collective-permute-start(bf16[40,3072]{1,0:T(8,128)(2,1)S(1)} %add_convert_fusion), channel_id=1, source_target_pairs={{0,2},{4,0},{8,4},{12,8},{14,12},{10,14},{6,10},{2,6},{1,3},{5,1},... | collective-permute-start | bytes 737288 | tf_op jit(solution)/shard_map/ppermute | solution.py:319
  102.0 7.7 %collective-permute-start.34 = (bf16[128,768]{1,0:T(8,128)(2,1)S(1)}, bf16[128,768]{1,0:T(8,128)(2,1)S(1)}, u32[]{:S(2)}, u32[]{:S(2)}) collective-permute-start(bf16[128,768]{1,0:T(8,128)(2,1)S(1)} %lora_rows.1.lora_ref), channel_id=1, source_target_pairs={{0,1},{1,0},{2,3},{3,2},{4,5},{5,4},{6,7},{7,6},{8,9},{9,8},{10,11... | collective-permute-start | bytes 589832 | tf_op jit(solution)/shard_map/ppermute | solution.py:471
  102.1 7.6 %collective-permute-start.32 = (bf16[1,32,768]{2,1,0:T(8,128)(2,1)S(1)}, bf16[1,32,768]{2,1,0:T(8,128)(2,1)S(1)}, u32[]{:S(2)}, u32[]{:S(2)}) collective-permute-start(bf16[1,32,768]{2,1,0:T(8,128)(2,1)S(1)} %get-tuple-element.210), channel_id=1, source_target_pairs={{0,8},{2,10},{4,12},{6,14},{8,0},{10,2},{12,4},{14,6},{1,9},{3,11}... | collective-permute-start | bytes 147464 | tf_op jit(solution)/shard_map/ppermute | solution.py:421
  (26 other events, 269.6 us)
